TPU v7x, 32 devices: a whole 2x2x4 slice. The times are simulated.
32 devices in a mesh: group: 2 (over x), ccd: 16 (over z, y, core).
Axes of the slice: x: 2, y: 2, z: 4, core: 2. Of those that a mesh axis runs over, the one named last changes fastest.
Arguments:
- images: float32 [4, 4096, 512], P(None, ('group', 'ccd')), parts along dimension 1, may hold values from -6 to 6
- basis_taps: float32 [2, 9, 11], replicated, may hold values from -1.75 to 1.75
- psf_coef: float32 [4, 10, 9, 3], P(None, 'group'), parts along dimension 1, may hold values from -3 to 3
- affine: float32 [4, 10, 2, 2], P(None, 'group'), parts along dimension 1, may hold values from -0.5 to 0.5
- visit_weight: bfloat16 [4, 10], P(None, 'group'), parts along dimension 1, may hold values from 0.25 to 4
- block_patch: int32 [32, 16, 1], P(('group', 'ccd')), parts along dimension 0, may hold values from 0 to 15; in each aligned block of 16 rows (0 to 15, 16 to 31, ..., all dimensions but the last counted through in order) at most 2 rows name the same one
- block_slot: int32 [32, 16], P(('group', 'ccd')), parts along dimension 0, may hold values from 0 to 15
- patch_owner: int32 [32], P('group'), parts along dimension 0, may hold values from 0 to 15, each once
Outputs:
- coadd: float32 [32, 512, 512], P(('group', 'ccd')), parts along dimension 0
There are 2 independent parts, one for each index of `group`. A program takes and returns all parts, laid end to end along the dimension named above; an argument that names none is the same for every part. Nothing has to cross between parts.
Inputs may be any that keep to these rules, and one draw needn't show every extreme that they name: `block_patch`: among the 16 blocks of one band no patch is named more than 2 times, and in every draw some band names some patch exactly 2 times. `patch_owner`: each device index along ccd owns exactly one patch.
All inputs are finite; a program needn't handle non-finite values.
Results may differ from a plain program's by a relative error of at most 0.0029.
Values may be sent and summed in bfloat16 or wider, within the bound.
No kernel may reach another device: no remote copies, remote signals or barrier semaphores. Data moves between devices by JAX's collectives and lax.ppermute only.
A program may use at most 64 MiB of HBM per device.

v0:
```python
import functools

import jax
import jax.numpy as jnp
from jax import lax
from jax.experimental import pallas as pl
from jax.experimental.pallas import tpu as pltpu
from jax.sharding import PartitionSpec as P

V = 4
BLOCK = 128
BLKC = 4
SPLIT = 4
TAPS = 11
NBASIS = 9
PSIDE = 4
CELLS = PSIDE * PSIDE
CAP = 2

HALF = TAPS // 2
WARP = 3
RIM = HALF + WARP
HEIGHT = SPLIT * BLOCK
WIDTH = BLKC * BLOCK
PARTS = 2
ROWS = BLOCK // PARTS
RAW = ROWS + 2 * RIM
MATCH = ROWS + 8
DEPTH = -(-TAPS * RAW // 128) * 128
MARGIN = 128
F32 = jnp.float32
BF16 = jnp.bfloat16


def sin_pi(t):
    whole = jnp.round(t)
    f = t - whole
    odd = whole - 2.0 * jnp.floor(0.5 * whole)
    f2 = f * f
    out = 0.0
    for c in (
        0.00046630280576761, -0.0073704309457144, 0.0821458866111282,
        -0.599264529320792, 2.55016403987734, -5.16771278004997, 3.14159265358979,
    ):
        out = out * f2 + c
    return f * out * (1.0 - 2.0 * odd)


def lanczos(t):
    zero = t == 0.0
    safe = jnp.where(zero, 1.0, t)
    pt = jnp.pi * safe
    value = 3.0 * sin_pi(safe) * sin_pi(safe / 3.0) / (pt * pt)
    return jnp.where(jnp.abs(t) < 3.0, jnp.where(zero, 1.0, value), 0.0)


def split(x):
    high = x.astype(BF16)
    return high, (x - high.astype(F32)).astype(BF16)


def iota(shape, dim):
    return lax.broadcasted_iota(jnp.int32, shape, dim)


def warp_kernel(
    part,
    place, patch, owner, taps, psf, affine, image, rim, out,
    basis, padded, shifted, framed, ready, seen, sem,
):
    visit = pl.program_id(0)
    visits = pl.num_programs(0)
    top_row = place[1] + part * ROWS
    inside = place[2 + part]

    @pl.when(visit == 0)
    def _():
        lane = iota((TAPS, DEPTH), 1)
        tap = iota((TAPS, DEPTH), 0)
        seg = lane // RAW
        rows = jnp.dot(taps[0], (lane - seg * RAW == tap).astype(F32),
                       precision=lax.Precision.HIGHEST, preferred_element_type=F32)
        cols = jnp.dot(taps[1], (seg == tap).astype(F32),
                       precision=lax.Precision.HIGHEST, preferred_element_type=F32)
        basis[...] = rows * cols
        padded[...] = jnp.zeros_like(padded)
        framed[...] = jnp.zeros_like(framed)
        shifted[:, TAPS * RAW:, :] = jnp.zeros((2, DEPTH - TAPS * RAW, WIDTH), BF16)

    edge = jnp.where(inside > 0, rim[0], 0.0)
    if part == 0:
        raw = jnp.concatenate([edge, image[0, : ROWS + RIM]], axis=0)
    else:
        raw = jnp.concatenate([image[0, BLOCK - ROWS - RIM :], edge], axis=0)
    for term, value in enumerate(split(raw)):
        padded[term, :, MARGIN : MARGIN + WIDTH] = value
    for term in range(2):
        for u in range(TAPS):
            start = MARGIN + u - HALF
            shifted[term, u * RAW : (u + 1) * RAW, :] = padded[term, :, start : start + WIDTH]

    kernels = lax.dot_general(
        psf[0, 0], basis[...], (((0,), (0,)), ((), ())),
        precision=lax.Precision.HIGHEST, preferred_element_type=F32,
    )
    bands = []
    for c in range(3):
        first = jnp.broadcast_to(kernels[c : c + 1], (8, DEPTH))
        first = pltpu.roll(first, 0, 1, stride=1, stride_axis=0)
        bands.append(
            jnp.concatenate(
                [first] + [pltpu.roll(first, 8 * a, 1) for a in range(1, MATCH // 8)], axis=0
            )
        )
    match_row = (top_row - WARP + iota((MATCH, 1), 0)).astype(F32)
    row_pos = (2.0 * match_row + 1.0) / HEIGHT - 1.0
    level = bands[0] + row_pos * bands[1]
    level_hi, level_lo = split(level)
    slope_hi, slope_lo = split(bands[2])
    both_hi = jnp.concatenate([level_hi, slope_hi], axis=0)
    both_lo = jnp.concatenate([level_lo, slope_lo], axis=0)
    high, low = shifted[0], shifted[1]
    terms = jnp.dot(both_hi, high, preferred_element_type=F32)
    terms = terms + jnp.dot(both_lo, high, preferred_element_type=F32)
    terms = terms + jnp.dot(both_hi, low, preferred_element_type=F32)
    col_pos = (2.0 * iota((1, WIDTH), 1).astype(F32) + 1.0) / WIDTH - 1.0
    matched = terms[:MATCH] + col_pos * terms[MATCH:]

    a = affine[0, 0]
    out_row = iota((ROWS, MATCH), 0)
    in_row = iota((ROWS, MATCH), 1)
    row = (top_row + out_row).astype(F32)
    shift = a[0:1, 0:1] + a[0:1, 1:2] * (row - (HEIGHT - 1) / 2.0) / HEIGHT
    step = in_row - out_row - WARP
    keep = jnp.abs(step) <= WARP
    outer = in_row < WARP if part == 0 else in_row >= ROWS + WARP
    keep = keep & (jnp.logical_not(outer) | (inside > 0))
    weights = jnp.where(keep, lanczos(shift - step.astype(F32)), 0.0)
    weights_hi, weights_lo = split(weights)
    matched_hi, matched_lo = split(matched)
    warped = jnp.dot(weights_hi, matched_hi, preferred_element_type=F32)
    warped = warped + jnp.dot(weights_lo, matched_hi, preferred_element_type=F32)
    warped = warped + jnp.dot(weights_hi, matched_lo, preferred_element_type=F32)

    framed[:, MARGIN : MARGIN + WIDTH] = warped
    col = iota((8, WIDTH), 1).astype(F32)
    col_shift = a[1:2, 0:1] + a[1:2, 1:2] * (col - (WIDTH - 1) / 2.0) / WIDTH
    col_weights = lanczos(col_shift - (iota((8, WIDTH), 0) - WARP).astype(F32))
    total = jnp.zeros((ROWS, WIDTH), F32)
    for s in range(2 * WARP + 1):
        start = MARGIN + s - WARP
        total = total + col_weights[s : s + 1] * framed[:, start : start + WIDTH]
    result = total.astype(BF16)

    @pl.when(visit == 0)
    def _():
        def clear(p, _):
            seen[p] = 0
            return 0

        lax.fori_loop(0, owner.shape[0], clear, 0)

    for j in range(BLKC):
        block = visit * BLKC + j
        ready[block] = result[:, j * BLOCK : (j + 1) * BLOCK]
        p = patch[0, block]
        rank = seen[p]
        seen[p] = rank + 1
        pltpu.make_async_copy(ready.at[block], out.at[owner[p], rank], sem.at[block]).start()

    @pl.when(visit == visits - 1)
    def _():
        for block in range(V * BLKC):
            pltpu.make_async_copy(ready.at[block], out.at[0, 0], sem.at[block]).wait()


def warp(part, place, patch, owner, taps, psf, affine, images, rim, devices):
    smem = pl.BlockSpec(memory_space=pltpu.SMEM)
    return pl.pallas_call(
        functools.partial(warp_kernel, part),
        grid_spec=pltpu.PrefetchScalarGridSpec(
            num_scalar_prefetch=1,
            grid=(V,),
            in_specs=[
                smem,
                smem,
                pl.BlockSpec((2, NBASIS, TAPS), lambda v, place: (0, 0, 0)),
                pl.BlockSpec((1, 1, NBASIS, 3), lambda v, place: (v, place[0], 0, 0)),
                pl.BlockSpec((1, 1, 2, 2), lambda v, place: (v, place[0], 0, 0)),
                pl.BlockSpec((1, BLOCK, WIDTH), lambda v, place: (v, 0, 0)),
                pl.BlockSpec((1, RIM, WIDTH), lambda v, place: (v, 0, 0)),
            ],
            out_specs=pl.BlockSpec(memory_space=pl.ANY),
            scratch_shapes=[
                pltpu.VMEM((NBASIS, DEPTH), F32),
                pltpu.VMEM((2, RAW, WIDTH + 2 * MARGIN), BF16),
                pltpu.VMEM((2, DEPTH, WIDTH), BF16),
                pltpu.VMEM((ROWS, WIDTH + 2 * MARGIN), F32),
                pltpu.VMEM((V * BLKC, ROWS, BLOCK), BF16),
                pltpu.SMEM((owner.shape[0],), jnp.int32),
                pltpu.SemaphoreType.DMA((V * BLKC,)),
            ],
        ),
        out_shape=jax.ShapeDtypeStruct((devices, CAP, ROWS, BLOCK), BF16),
        compiler_params=pltpu.CompilerParams(vmem_limit_bytes=32 << 20),
        cost_estimate=pl.CostEstimate(
            flops=V * 2 * 3 * 2 * MATCH * DEPTH * WIDTH,
            bytes_accessed=V * (BLOCK * WIDTH * 4 + ROWS * WIDTH * 2),
            transcendentals=0,
        ),
        name="match_warp_" + str(part),
    )(place, patch, owner, taps, psf, affine, images, rim)


def table_kernel(place, names, weights, owner, cell_out, weight_out, sum_out):
    devices = names.shape[0]
    me = place[4]

    def find(p, mine):
        return jnp.where(owner[p] == me, p, mine)

    mine = lax.fori_loop(0, owner.shape[0], find, 0)
    for c in range(CELLS):
        sum_out[c] = 0.0

    def source(s, _):
        cell_out[s * CAP] = -1
        cell_out[s * CAP + 1] = -1
        ccd = (s + SPLIT // 2) // SPLIT
        rank = 0
        for e in range(V * BLKC):
            name = names[s, e]
            hit = name // CELLS == mine

            @pl.when(hit)
            def _(rank=rank, name=name, e=e):
                cell = name % CELLS
                weight = weights[e // BLKC, ccd]
                cell_out[s * CAP + rank] = cell
                weight_out[s * CAP + rank] = weight
                sum_out[cell] += weight

            rank = rank + hit.astype(jnp.int32)
        return 0

    lax.fori_loop(0, devices, source, 0)


def table(place, names, weights, owner):
    smem = pl.BlockSpec(memory_space=pltpu.SMEM)
    devices = names.shape[0]
    return pl.pallas_call(
        table_kernel,
        in_specs=[smem] * 4,
        out_specs=[smem] * 3,
        out_shape=[
            jax.ShapeDtypeStruct((devices * CAP,), jnp.int32),
            jax.ShapeDtypeStruct((devices * CAP,), F32),
            jax.ShapeDtypeStruct((CELLS,), F32),
        ],
        name="contents",
    )(place, names, weights, owner)


def coadd_kernel(cell, weight, sums, got, *refs):
    out = refs[-1]
    out[...] = jnp.zeros_like(out)

    def add(k, _):
        c = cell[k]

        @pl.when(c >= 0)
        def _():
            r = c // PSIDE
            lanes = pl.ds(pl.multiple_of(c % PSIDE * BLOCK, BLOCK), BLOCK)
            out[r, 0, :, lanes] += weight[k] * got[k].astype(F32)

        return 0

    lax.fori_loop(0, got.shape[0], add, 0)
    for c in range(CELLS):
        lanes = slice(c % PSIDE * BLOCK, (c % PSIDE + 1) * BLOCK)
        total = jnp.maximum(jnp.full((1, BLOCK), sums[c], F32), 1.0)
        out[c // PSIDE, 0, :, lanes] = out[c // PSIDE, 0, :, lanes] / total


def coadd(part, cell, weight, sums, got, before):
    smem = pl.BlockSpec(memory_space=pltpu.SMEM)
    got = got.reshape(-1, ROWS, BLOCK)
    args = [cell, weight, sums, got]
    specs = [smem] * 3 + [pl.BlockSpec(got.shape, lambda i: (0, 0, 0))]
    alias = {}
    if before is not None:
        alias = {len(args): 0}
        args.append(before)
        specs.append(pl.BlockSpec(memory_space=pl.ANY))
    return pl.pallas_call(
        coadd_kernel,
        grid=(1,),
        in_specs=specs,
        out_specs=pl.BlockSpec((PSIDE, 1, ROWS, WIDTH), lambda i: (0, part, 0, 0)),
        out_shape=jax.ShapeDtypeStruct((PSIDE, PARTS, ROWS, PSIDE * BLOCK), F32),
        input_output_aliases=alias,
        compiler_params=pltpu.CompilerParams(vmem_limit_bytes=32 << 20),
        name="coadd_" + str(part),
    )(*args)


def shards(
    images, basis_taps, psf_coef, affine, visit_weight, block_patch, block_slot, patch_owner
):
    band = lax.axis_index("ccd")
    devices = lax.axis_size("ccd")
    shifted = band + SPLIT // 2
    quarter = shifted % SPLIT
    place = jnp.stack(
        [
            shifted // SPLIT,
            quarter * BLOCK,
            ((quarter > 0) & (band > 0)).astype(jnp.int32),
            ((quarter < SPLIT - 1) & (band < devices - 1)).astype(jnp.int32),
            band,
        ]
    ).astype(jnp.int32)
    down = [(i, i + 1) for i in range(devices - 1)]
    up = [(i + 1, i) for i in range(devices - 1)]
    above = lax.ppermute(images[:, BLOCK - RIM :], "ccd", down)
    below = lax.ppermute(images[:, :RIM], "ccd", up)
    patch = block_patch[:, :, 0]
    names = lax.all_gather(patch * CELLS + block_slot, "ccd", axis=0, tiled=True)
    cell, weight, sums = table(place, names, visit_weight.astype(F32), patch_owner)
    result = None
    sent = [
        warp(part, place, patch, patch_owner, basis_taps, psf_coef, affine, images, rim, devices)
        for part, rim in enumerate((above, below))
    ]
    for part, blocks in enumerate(sent):
        got = lax.all_to_all(blocks, "ccd", split_axis=0, concat_axis=0, tiled=True)
        result = coadd(part, cell, weight, sums, got, result)
    return result.reshape(1, PSIDE * BLOCK, PSIDE * BLOCK)


def solution(mesh):
    placed = (
        P(None, ("group", "ccd"), None),
        P(),
        P(None, "group", None, None),
        P(None, "group", None, None),
        P(None, "group"),
        P(("group", "ccd"), None, None),
        P(("group", "ccd"), None),
        P("group"),
    )
    return jax.shard_map(
        shards,
        mesh=mesh,
        in_specs=placed,
        out_specs=P(("group", "ccd"), None, None),
        check_vma=False,
    )
```

profile of v0, /device:TPU:0, one launch (start us, length us, event | category | flops | bytes accessed | tf_op | source)
XLA Modules:
  0.0 87.3 jit_solution(1059349640559715917)
XLA Ops:
  0.0 0.9 %fusion = (f32[4,8,512]{2,1,0:T(8,128)S(1)}, f32[4,8,512]{2,1,0:T(8,128)S(1)}) fusion(f32[4,128,512]{2,1,0:T(8,128)} %image.3), kind=kLoop, calls=%fused_computation.1 | loop fusion | bytes 262144 | tf_op jit(solution)/shard_map/slice | solution.py:327
  0.9 2.4 %collective-permute-start.1 = (f32[4,8,512]{2,1,0:T(8,128)S(1)}, f32[4,8,512]{2,1,0:T(8,128)S(1)}, u32[]{:S(2)}, u32[]{:S(2)}) collective-permute-start(f32[4,8,512]{2,1,0:T(8,128)S(1)} %get-tuple-element.11), channel_id=1, source_target_pairs={{0,1},{1,2},{2,3},{3,4},{4,5},{5,6},{6,7},{7,8},{8,9},{9,10},{10,1... | collective-permute-start | bytes 196616 | tf_op jit(solution)/shard_map/ppermute | solution.py:327
  3.3 0.0 copy-start.9
  3.3 0.0 copy-start.10
  3.3 0.0 copy-start.8
  3.3 0.7 copy-done.9
  4.0 0.0 copy-done.10
  4.0 0.1 copy.19.affine
  4.1 0.2 copy.18.psf
  4.4 0.1 stack.31.place
  4.5 0.0 collective-permute-done.1.rim
  4.5 0.6 copy-done.6
  5.1 0.0 copy-done.7
  5.1 1.2 %copy-done = f32[4,128,512]{2,1,0:T(8,128)S(1)} copy-done((f32[4,128,512]{2,1,0:T(8,128)S(1)}, f32[4,128,512]{2,1,0:T(8,128)}, u32[]{:S(2)}) %copy-start) | copy-done | bytes 1048600
  6.3 9.1 %match_warp_0.1 = bf16[16,2,64,128]{3,2,1,0:T(8,128)(2,1)} custom-call(s32[5]{0:T(128)S(1)} %stack.31.place, s32[1,16]{1,0:T(1,128)S(1)} %bitcast.15, s32[16]{0:T(128)S(1)} %copy-done.6, f32[2,9,11]{2,1,0:T(8,128)S(1)} %copy.17.taps, f32[4,5,9,3]{3,2,1,0:T(8,128)S(1)} %copy.18.psf, f32[4,5,2,2]{3,2,1,0:T(2,128)S(1)} %copy.19.affine, ...), custom_call_target="tpu_custom_call" | custom-call | flops 1585446912 | bytes 1310720 | tf_op jit(solution)/shard_map/match_warp_0/pallas_call | solution.py:179
  15.4 0.0 copy-start.1
  15.4 8.9 %all-to-all-start.1 = ((bf16[16,2,64,128]{3,2,1,0:T(8,128)(2,1)}), bf16[16,2,64,128]{3,2,1,0:T(8,128)(2,1)S(1)}, u32[]{:S(2)}, u32[]{:S(2)}) async-start(bf16[16,2,64,128]{3,2,1,0:T(8,128)(2,1)} %match_warp_0.1), calls=%async_computation.1 | async-start | bytes 1048576 | tf_op jit(solution)/shard_map/all_to_all | solution.py:338
  24.3 1.3 %collective-permute-start = (f32[4,8,512]{2,1,0:T(8,128)S(1)}, f32[4,8,512]{2,1,0:T(8,128)S(1)}, u32[]{:S(2)}, u32[]{:S(2)}) collective-permute-start(f32[4,8,512]{2,1,0:T(8,128)S(1)} %get-tuple-element.12), channel_id=1, source_target_pairs={{1,0},{2,1},{3,2},{4,3},{5,4},{6,5},{7,6},{8,7},{9,8},{10,9},{11,1... | collective-permute-start | bytes 196616 | tf_op jit(solution)/shard_map/ppermute | solution.py:328
  25.6 1.8 %collective-permute-done.rim = f32[4,8,512]{2,1,0:T(8,128)S(1)} collective-permute-done((f32[4,8,512]{2,1,0:T(8,128)S(1)}, f32[4,8,512]{2,1,0:T(8,128)S(1)}, u32[]{:S(2)}, u32[]{:S(2)}) %collective-permute-start) | collective-permute-done | bytes 65568 | tf_op jit(solution)/shard_map/ppermute | solution.py:328
  27.5 9.1 %match_warp_1.1 = bf16[16,2,64,128]{3,2,1,0:T(8,128)(2,1)} custom-call(s32[5]{0:T(128)S(1)} %stack.31.place, s32[1,16]{1,0:T(1,128)S(1)} %bitcast.16, s32[16]{0:T(128)S(1)} %copy-done.6, f32[2,9,11]{2,1,0:T(8,128)S(1)} %copy.17.taps, f32[4,5,9,3]{3,2,1,0:T(8,128)S(1)} %copy.18.psf, f32[4,5,2,2]{3,2,1,0:T(2,128)S(1)} %copy.19.affine, ...), custom_call_target="tpu_custom_call" | custom-call | flops 1585446912 | bytes 1310720 | tf_op jit(solution)/shard_map/match_warp_1/pallas_call | solution.py:179
  36.6 0.0 copy-start.11
  36.6 2.2 %all-to-all-done.1 = bf16[16,2,64,128]{3,2,1,0:T(8,128)(2,1)S(1)} async-done(((bf16[16,2,64,128]{3,2,1,0:T(8,128)(2,1)}), bf16[16,2,64,128]{3,2,1,0:T(8,128)(2,1)S(1)}, u32[]{:S(2)}, u32[]{:S(2)}) %all-to-all-start.1) | async-done | bytes 524320 | tf_op jit(solution)/shard_map/all_to_all | solution.py:338
  38.8 12.9 %all-to-all-start = ((bf16[16,2,64,128]{3,2,1,0:T(8,128)(2,1)}), bf16[16,2,64,128]{3,2,1,0:T(8,128)(2,1)S(1)}, u32[]{:S(2)}, u32[]{:S(2)}) async-start(bf16[16,2,64,128]{3,2,1,0:T(8,128)(2,1)} %match_warp_1.1), calls=%async_computation | async-start | bytes 1048576 | tf_op jit(solution)/shard_map/all_to_all | solution.py:338
  51.8 0.0 copy-start.12
  51.8 0.6 convert_element_type.2.weights
  52.3 0.1 copy-done.12
  52.4 25.1 %all-gather = s32[16,1,16]{2,1,0:T(1,128)} all-gather(s32[1,1,16]{2,1,0:T(1,128)S(1)} %add_bitcast_fusion), channel_id=1, replica_groups=mesh['group'=2,'ccd'=16] {'ccd'}, dimensions={0}, use_global_device_ids=true | all-gather | bytes 1088 | tf_op jit(solution)/shard_map/all_gather | solution.py:330
  77.5 4.6 %contents.1 = (s32[32]{0:T(128)}, f32[32]{0:T(128)}, f32[16]{0:T(128)}) custom-call(s32[5]{0:T(128)} %copy-done.2, s32[16,16]{1,0:T(8,128)} %bitcast.17, f32[4,5]{1,0:T(4,128)} %convert_element_type.2.weights, s32[16]{0:T(128)} %owner.5), custom_call_target="tpu_custom_call" | custom-call | tf_op jit(solution)/shard_map/contents/pallas_call | solution.py:252
  82.2 0.6 copy-done.3
  82.8 0.0 copy-done.5
  82.8 2.2 %coadd_0.1.refs_0_ = f32[4,2,64,512]{3,2,1,0:T(8,128)} custom-call(s32[32]{0:T(128)S(1)} %copy-done.3, f32[32]{0:T(128)S(1)} %copy-done.4, f32[16]{0:T(128)S(1)} %copy-done.5, bf16[32,64,128]{2,1,0:T(8,128)(2,1)S(1)} %bitcast.13), custom_call_target="tpu_custom_call" | custom-call | tf_op jit(solution)/shard_map/coadd_0/pallas_call | solution.py:297
  85.1 2.2 %coadd_1.1 = f32[4,2,64,512]{3,2,1,0:T(8,128)} custom-call(s32[32]{0:T(128)S(1)} %copy-done.3, f32[32]{0:T(128)S(1)} %copy-done.4, f32[16]{0:T(128)S(1)} %copy-done.5, bf16[32,64,128]{2,1,0:T(8,128)(2,1)S(1)} %bitcast.14, f32[4,2,64,512]{3,2,1,0:T(8,128)} %coadd_0.1.refs_0_), custom_call_target="tpu_custom_call", output_to_operand_aliasing={{}: (4, {})} | custom-call | tf_op jit(solution)/shard_map/coadd_1/pallas_call | solution.py:297
  (15 shorter events, 0.0 us)
Async XLA Ops:
  0.9 3.6 %collective-permute-start.1 = (f32[4,8,512]{2,1,0:T(8,128)S(1)}, f32[4,8,512]{2,1,0:T(8,128)S(1)}, u32[]{:S(2)}, u32[]{:S(2)}) collective-permute-start(f32[4,8,512]{2,1,0:T(8,128)S(1)} %get-tuple-element.11), channel_id=1, source_target_pairs={{0,1},{1,2},{2,3},{3,4},{4,5},{5,6},{6,7},{7,8},{8,9},{9,10},{10,1... | collective-permute-start | bytes 196616 | tf_op jit(solution)/shard_map/ppermute | solution.py:327
  3.3 0.7 copy-start.9
  3.3 0.7 copy-start.10
  3.3 0.8 copy-start.8
  4.4 23.0 %copy-start.2 = (s32[5]{0:T(128)}, s32[5]{0:T(128)S(1)}, u32[]{:S(2)}) copy-start(s32[5]{0:T(128)S(1)} %stack.31.place) | copy-start | bytes 64
  4.4 0.7 copy-start.6
  4.5 0.7 copy-start.7
  5.1 1.2 %copy-start = (f32[4,128,512]{2,1,0:T(8,128)S(1)}, f32[4,128,512]{2,1,0:T(8,128)}, u32[]{:S(2)}) copy-start(f32[4,128,512]{2,1,0:T(8,128)} %image.3) | copy-start | bytes 3145732
  15.4 12.1 %copy-start.1 = (f32[4,128,512]{2,1,0:T(8,128)S(1)}, f32[4,128,512]{2,1,0:T(8,128)}, u32[]{:S(2)}) copy-start(f32[4,128,512]{2,1,0:T(8,128)} %image.3) | copy-start | bytes 3145732
  15.4 23.4 %all-to-all-start.1 = ((bf16[16,2,64,128]{3,2,1,0:T(8,128)(2,1)}), bf16[16,2,64,128]{3,2,1,0:T(8,128)(2,1)S(1)}, u32[]{:S(2)}, u32[]{:S(2)}) async-start(bf16[16,2,64,128]{3,2,1,0:T(8,128)(2,1)} %match_warp_0.1), calls=%async_computation.1 | async-start | bytes 1048576 | tf_op jit(solution)/shard_map/all_to_all | solution.py:338
  24.3 3.1 %collective-permute-start = (f32[4,8,512]{2,1,0:T(8,128)S(1)}, f32[4,8,512]{2,1,0:T(8,128)S(1)}, u32[]{:S(2)}, u32[]{:S(2)}) collective-permute-start(f32[4,8,512]{2,1,0:T(8,128)S(1)} %get-tuple-element.12), channel_id=1, source_target_pairs={{1,0},{2,1},{3,2},{4,3},{5,4},{6,5},{7,6},{8,7},{9,8},{10,9},{11,1... | collective-permute-start | bytes 196616 | tf_op jit(solution)/shard_map/ppermute | solution.py:328
  36.6 15.2 %copy-start.11 = (bf16[4,5]{1,0:T(4,128)(2,1)S(1)}, bf16[4,5]{1,0:T(4,128)(2,1)}, u32[]{:S(2)}) copy-start(bf16[4,5]{1,0:T(4,128)(2,1)} %param.12) | copy-start | bytes 124
  38.8 46.3 %all-to-all-start = ((bf16[16,2,64,128]{3,2,1,0:T(8,128)(2,1)}), bf16[16,2,64,128]{3,2,1,0:T(8,128)(2,1)S(1)}, u32[]{:S(2)}, u32[]{:S(2)}) async-start(bf16[16,2,64,128]{3,2,1,0:T(8,128)(2,1)} %match_warp_1.1), calls=%async_computation | async-start | bytes 1048576 | tf_op jit(solution)/shard_map/all_to_all | solution.py:338
  51.8 0.7 copy-start.12
  82.1 0.7 copy-start.3
  82.2 0.7 copy-start.4
  82.2 0.7 copy-start.5
where the time goes:
time: 87.7 us; the launch traced here: 87.3 us
  Pallas kernels  27.2 us (31%)
  starting transfers between devices  25.5 us (29%)
  blocking collectives  25.1 us (29%)
  local copies, waits for them, and re-layouts  4.65 us (5%)
  waiting for transfers between devices  4.06 us (5%)
    all_gather x1, blocking collectives, shards(): lax.all_gather(patch * CELLS + block_slot, 'ccd', axis=0, tiled=True)  25.1 us
    all_to_all x2, starting transfers between devices, shards(): got = lax.all_to_all(blocks, 'ccd', split_axis=0, concat_axis=0, tiled=True)  21.8 us
    pallas_call x2, Pallas kernels, warp(): pl.pallas_call(functools.partial(warp_kernel, part), grid_spec=pltpu.Pref...  18.1 us
    pallas_call x1, Pallas kernels, table(): pl.pallas_call(table_kernel, in_specs=[smem] * 4, out_specs=[smem] * 3, o...  4.62 us
    pallas_call x2, Pallas kernels, coadd(): pl.pallas_call(coadd_kernel, grid=(1,), in_specs=specs, out_specs=pl.Bloc...  4.46 us
    unnamed x29, local copies, waits for them, and re-layouts  3.69 us
    ppermute x1, starting transfers between devices, shards(): above = lax.ppermute(images[:, BLOCK - RIM:], 'ccd', down)  2.36 us
    all_to_all x2, waiting for transfers between devices, shards(): got = lax.all_to_all(blocks, 'ccd', split_axis=0, concat_axis=0, tiled=True)  2.21 us
  transfers between devices with their start and end apart: 4, of which 2 were waited for; matrix products, arithmetic and copies ran while one was open for 1% of the time, Pallas kernels for 18%

commit v1 on v0

v1 whole, which is shorter than its diff:
```python
import functools

import jax
import jax.numpy as jnp
from jax import lax
from jax.experimental import pallas as pl
from jax.experimental.pallas import tpu as pltpu
from jax.sharding import PartitionSpec as P

V = 4
BLOCK = 128
BLKC = 4
SPLIT = 4
TAPS = 11
NBASIS = 9
PSIDE = 4
CELLS = PSIDE * PSIDE
CAP = 2

HALF = TAPS // 2
WARP = 3
RIM = HALF + WARP
HEIGHT = SPLIT * BLOCK
WIDTH = BLKC * BLOCK
PARTS = 2
ROWS = BLOCK // PARTS
RAW = ROWS + 2 * RIM
MATCH = ROWS + 8
STRIP = 24
STEP = -(-(STRIP + TAPS - 1) // 8) * 8
BAND = -(-9 * STEP // 128) * 128
TALL = MATCH - STRIP + STEP
LABEL = 16
F32 = jnp.float32
BF16 = jnp.bfloat16


def sin_pi(t):
    whole = jnp.round(t)
    f = t - whole
    odd = whole - 2.0 * jnp.floor(0.5 * whole)
    f2 = f * f
    out = 0.0
    for c in (
        0.00046630280576761, -0.0073704309457144, 0.0821458866111282,
        -0.599264529320792, 2.55016403987734, -5.16771278004997, 3.14159265358979,
    ):
        out = out * f2 + c
    return f * out * (1.0 - 2.0 * odd)


def lanczos(t):
    zero = t == 0.0
    safe = jnp.where(zero, 1.0, t)
    pt = jnp.pi * safe
    value = 3.0 * sin_pi(safe) * sin_pi(safe / 3.0) / (pt * pt)
    return jnp.where(jnp.abs(t) < 3.0, jnp.where(zero, 1.0, value), 0.0)


def iota(shape, dim):
    return lax.broadcasted_iota(jnp.int32, shape, dim)


def rolled(x, shift):
    return x if shift == 0 else pltpu.roll(x, -shift % x.shape[1], 1)


def prepare_kernel(place, taps, psf, affine, bands_out, rows_out, cols_out, row_taps):
    visit = pl.program_id(0)
    lane = iota((1, BAND), 1)
    seg = lane // STEP
    tap = lane - seg * STEP

    @pl.when(visit == 0)
    def _():
        onehot = (tap == iota((TAPS, BAND), 0)) & (seg < 9)
        row_taps[...] = jnp.dot(
            taps[0], onehot.astype(F32),
            precision=lax.Precision.HIGHEST, preferred_element_type=F32,
        )

    p = psf[0, 0]
    r = row_taps[...]
    first = seg < 3
    term = jnp.where(first, p[:, 0:1], jnp.where(seg < 6, p[:, 1:2], p[:, 2:3]))
    row_move = jnp.where(first, (tap - HALF).astype(F32) * (2.0 / HEIGHT), 0.0)
    plain = r * (term - row_move * p[:, 1:2])
    moved = r * jnp.where(first, p[:, 2:3], 0.0)

    def over_bases(x):
        return lax.dot_general(
            taps[1], x, (((0,), (0,)), ((), ())),
            precision=lax.Precision.HIGHEST, preferred_element_type=F32,
        )

    col_move = (iota((TAPS, 1), 0) - HALF).astype(F32) * (2.0 / WIDTH)
    kernels = over_bases(plain) - col_move * over_bases(moved)
    low_lanes = seg % 3 == 2
    parts = []
    for u in range(TAPS):
        x = jnp.broadcast_to(kernels[u : u + 1], (8, BAND))
        x = pltpu.roll(x, 0, 1, stride=1, stride_axis=0)
        x = jnp.concatenate([x] + [pltpu.roll(x, 8 * k, 1) for k in range(1, STRIP // 8)], axis=0)
        high = x.astype(BF16).astype(F32)
        parts.append(jnp.where(low_lanes, x - high, high))
    bands_out[0] = jnp.concatenate(parts, axis=0).astype(BF16)

    a = affine[0, 0]
    out_row = iota((BLOCK, 128), 0)
    local = out_row % ROWS
    in_row = iota((BLOCK, 128), 1)
    row = (place[1] + out_row).astype(F32)
    shift = a[0:1, 0:1] + a[0:1, 1:2] * (row - (HEIGHT - 1) / 2.0) / HEIGHT
    step = in_row - local - WARP
    band_row = out_row + step
    keep = jnp.abs(step) <= WARP
    keep = keep & ((band_row >= 0) | (place[2] > 0)) & ((band_row < BLOCK) | (place[3] > 0))
    weights = jnp.where(keep, lanczos(shift - step.astype(F32)), 0.0)
    high = weights.astype(BF16).astype(F32)
    zero = jnp.zeros_like(weights)
    wide = jnp.concatenate([high, zero], axis=1)
    low = jnp.concatenate([weights - high, zero], axis=1)
    wide = wide + pltpu.roll(wide, MATCH, 1) + pltpu.roll(low, 2 * MATCH, 1)
    rows_out[0] = wide.astype(BF16)

    col = iota((8, WIDTH), 1)
    offset = iota((8, WIDTH), 0) - WARP
    col_shift = a[1:2, 0:1] + a[1:2, 1:2] * (col.astype(F32) - (WIDTH - 1) / 2.0) / WIDTH
    within = (col + offset >= 0) & (col + offset < WIDTH)
    cols_out[0] = jnp.where(within, lanczos(col_shift - offset.astype(F32)), 0.0)


def prepare(place, taps, psf, affine):
    return pl.pallas_call(
        prepare_kernel,
        grid_spec=pltpu.PrefetchScalarGridSpec(
            num_scalar_prefetch=1,
            grid=(V,),
            in_specs=[
                pl.BlockSpec((2, NBASIS, TAPS), lambda v, place: (0, 0, 0)),
                pl.BlockSpec((1, 1, NBASIS, 3), lambda v, place: (v, place[0], 0, 0)),
                pl.BlockSpec((1, 1, 2, 2), lambda v, place: (v, place[0], 0, 0)),
            ],
            out_specs=[
                pl.BlockSpec((1, TAPS * STRIP, BAND), lambda v, place: (v, 0, 0)),
                pl.BlockSpec((1, BLOCK, 256), lambda v, place: (v, 0, 0)),
                pl.BlockSpec((1, 8, WIDTH), lambda v, place: (v, 0, 0)),
            ],
            scratch_shapes=[pltpu.VMEM((NBASIS, BAND), F32)],
        ),
        out_shape=[
            jax.ShapeDtypeStruct((V, TAPS * STRIP, BAND), BF16),
            jax.ShapeDtypeStruct((V, BLOCK, 256), BF16),
            jax.ShapeDtypeStruct((V, 8, WIDTH), F32),
        ],
        compiler_params=pltpu.CompilerParams(vmem_limit_bytes=32 << 20),
        cost_estimate=pl.CostEstimate(flops=1 << 30, bytes_accessed=1 << 20, transcendentals=0),
        name="prepare",
    )(place, taps, psf, affine)


def warp_kernel(
    part,
    place, patch, slot, owner, weight, bands, row_weights, col_weights, image, rim, out,
    terms, ready, seen, sem, *extra,
):
    visit = pl.program_id(0)
    visits = pl.num_programs(0)
    top_row = place[1] + part * ROWS
    inside = place[2 + part]

    edge = jnp.where(inside > 0, rim[0], 0.0)
    empty = jnp.zeros((TALL - RAW, WIDTH), F32)
    if part == 0:
        raw = jnp.concatenate([edge, image[0, : ROWS + RIM], empty], axis=0)
    else:
        raw = jnp.concatenate([image[0, BLOCK - ROWS - RIM :], edge, empty], axis=0)
    raw_row = (top_row - RIM + iota((TALL, 1), 0)).astype(F32)
    row_pos = (2.0 * raw_row + 1.0) / HEIGHT - 1.0
    col_pos = (2.0 * iota((1, WIDTH), 1).astype(F32) + 1.0) / WIDTH - 1.0
    for c, value in enumerate((raw, raw * row_pos, raw * col_pos)):
        high = value.astype(BF16).astype(F32)
        terms[c, 0] = high
        terms[c, 1] = value - high

    lane = iota((1, 128), 1)
    strips = []
    for k in range(MATCH // STRIP):
        rows = slice(k * STRIP, k * STRIP + STEP)
        stack = [terms[c, h, rows] for c in range(3) for h in (0, 1, 0)]
        stack.append(jnp.zeros((BAND - 9 * STEP, WIDTH), F32))
        columns = jnp.concatenate(stack, axis=0).astype(BF16)
        taps = jnp.dot(bands[0], columns, preferred_element_type=F32)
        total = None
        for u in range(TAPS):
            move = u - HALF
            value = rolled(taps[u * STRIP : (u + 1) * STRIP], move)
            if move < 0:
                head = jnp.where(lane >= -move, value[:, :128], 0.0)
                value = jnp.concatenate([head, value[:, 128:]], axis=1)
            if move > 0:
                tail = jnp.where(lane < 128 - move, value[:, WIDTH - 128 :], 0.0)
                value = jnp.concatenate([value[:, : WIDTH - 128], tail], axis=1)
            total = value if total is None else total + value
        strips.append(total)
    matched = jnp.concatenate(strips, axis=0)

    high = matched.astype(BF16).astype(F32)
    columns = jnp.concatenate(
        [high, matched - high, high, jnp.zeros((256 - 3 * MATCH, WIDTH), F32)], axis=0
    ).astype(BF16)
    warped = jnp.dot(row_weights[0], columns, preferred_element_type=F32)

    col = col_weights[0]
    total = None
    for s in range(2 * WARP + 1):
        value = col[s : s + 1] * rolled(warped, s - WARP)
        total = value if total is None else total + value
    result = total.astype(BF16)

    @pl.when(visit == 0)
    def _():
        def clear(p, _):
            seen[p] = 0
            return 0

        lax.fori_loop(0, owner.shape[0], clear, 0)
        if extra:
            extra[0][...] = jnp.zeros_like(extra[0])

    for j in range(BLKC):
        block = visit * BLKC + j
        ready[block] = result[:, j * BLOCK : (j + 1) * BLOCK]
        p = patch[0, block]
        rank = seen[p]
        seen[p] = rank + 1
        to = out.at[owner[p], pl.ds(pl.multiple_of(rank * ROWS, ROWS), ROWS)]
        pltpu.make_async_copy(ready.at[block], to, sem.at[block]).start()
        if extra:
            label = extra[0]
            at = rank * 2
            label[owner[p], pl.ds(at, 1), :] = jnp.full((1, BLOCK), weight[visit, place[0]], F32)
            label[owner[p], pl.ds(at + 1, 1), :] = jnp.full((1, BLOCK), slot[0, block].astype(F32), F32)

    @pl.when(visit == visits - 1)
    def _():
        if extra:
            label, label_ready, label_sem = extra
            label_ready[...] = label[...].astype(BF16)
            copy = pltpu.make_async_copy(
                label_ready, out.at[:, pl.ds(CAP * ROWS, LABEL)], label_sem
            )
            copy.start()
            copy.wait()
        for block in range(V * BLKC):
            pltpu.make_async_copy(ready.at[block], out.at[0, pl.ds(0, ROWS)], sem.at[block]).wait()


def warp(part, place, patch, slot, owner, weight, ready, images, rim, devices):
    smem = pl.BlockSpec(memory_space=pltpu.SMEM)
    rows = CAP * ROWS
    scratch = [
        pltpu.VMEM((3, 2, TALL, WIDTH), F32),
        pltpu.VMEM((V * BLKC, ROWS, BLOCK), BF16),
        pltpu.SMEM((owner.shape[0],), jnp.int32),
        pltpu.SemaphoreType.DMA((V * BLKC,)),
    ]
    if part == 0:
        rows += LABEL
        scratch += [
            pltpu.VMEM((devices, LABEL, BLOCK), F32),
            pltpu.VMEM((devices, LABEL, BLOCK), BF16),
            pltpu.SemaphoreType.DMA(()),
        ]
    return pl.pallas_call(
        functools.partial(warp_kernel, part),
        grid_spec=pltpu.PrefetchScalarGridSpec(
            num_scalar_prefetch=1,
            grid=(V,),
            in_specs=[
                smem,
                smem,
                smem,
                smem,
                pl.BlockSpec((1, TAPS * STRIP, BAND), lambda v, place: (v, 0, 0)),
                pl.BlockSpec((1, ROWS, 256), lambda v, place: (v, part, 0)),
                pl.BlockSpec((1, 8, WIDTH), lambda v, place: (v, 0, 0)),
                pl.BlockSpec((1, BLOCK, WIDTH), lambda v, place: (v, 0, 0)),
                pl.BlockSpec((1, RIM, WIDTH), lambda v, place: (v, 0, 0)),
            ],
            out_specs=pl.BlockSpec(memory_space=pl.ANY),
            scratch_shapes=scratch,
        ),
        out_shape=jax.ShapeDtypeStruct((devices, rows, BLOCK), BF16),
        compiler_params=pltpu.CompilerParams(vmem_limit_bytes=32 << 20),
        cost_estimate=pl.CostEstimate(
            flops=V * 2 * 2 * MATCH * TAPS * BAND * WIDTH,
            bytes_accessed=V * (BLOCK * WIDTH * 4 + ROWS * WIDTH * 2),
            transcendentals=0,
        ),
        name="match_warp_" + str(part),
    )(place, patch, slot, owner, weight, *ready, images, rim)


def coadd_kernel(labels, got, *refs):
    out, sums = refs[-2:]
    out[...] = jnp.zeros_like(out)
    for c in range(CELLS):
        sums[c] = 0.0

    def add(k, _):
        source, rank = k // CAP, k % CAP
        weight = labels[source, rank * 2]

        @pl.when(weight > 0.0)
        def _():
            c = labels[source, rank * 2 + 1].astype(jnp.int32)
            sums[c] += weight
            lanes = pl.ds(pl.multiple_of(c % PSIDE * BLOCK, BLOCK), BLOCK)
            rows = pl.ds(pl.multiple_of(rank * ROWS, ROWS), ROWS)
            out[c // PSIDE, 0, :, lanes] += weight * got[source, rows].astype(F32)

        return 0

    lax.fori_loop(0, got.shape[0] * CAP, add, 0)
    for c in range(CELLS):
        lanes = slice(c % PSIDE * BLOCK, (c % PSIDE + 1) * BLOCK)
        total = jnp.maximum(jnp.full((1, BLOCK), sums[c], F32), 1.0)
        out[c // PSIDE, 0, :, lanes] = out[c // PSIDE, 0, :, lanes] / total


def coadd(part, labels, got, before):
    smem = pl.BlockSpec(memory_space=pltpu.SMEM)
    args = [labels, got]
    specs = [smem, pl.BlockSpec((got.shape[0], CAP * ROWS, BLOCK), lambda i: (0, 0, 0))]
    alias = {}
    if before is not None:
        alias = {len(args): 0}
        args.append(before)
        specs.append(pl.BlockSpec(memory_space=pl.ANY))
    return pl.pallas_call(
        coadd_kernel,
        grid=(1,),
        in_specs=specs,
        out_specs=pl.BlockSpec((PSIDE, 1, ROWS, WIDTH), lambda i: (0, part, 0, 0)),
        out_shape=jax.ShapeDtypeStruct((PSIDE, PARTS, ROWS, PSIDE * BLOCK), F32),
        scratch_shapes=[pltpu.SMEM((CELLS,), F32)],
        input_output_aliases=alias,
        compiler_params=pltpu.CompilerParams(vmem_limit_bytes=32 << 20),
        name="coadd_" + str(part),
    )(*args)


def shards(
    images, basis_taps, psf_coef, affine, visit_weight, block_patch, block_slot, patch_owner
):
    band = lax.axis_index("ccd")
    devices = lax.axis_size("ccd")
    shifted = band + SPLIT // 2
    quarter = shifted % SPLIT
    place = jnp.stack(
        [
            shifted // SPLIT,
            quarter * BLOCK,
            ((quarter > 0) & (band > 0)).astype(jnp.int32),
            ((quarter < SPLIT - 1) & (band < devices - 1)).astype(jnp.int32),
            band,
        ]
    ).astype(jnp.int32)
    down = [(i, i + 1) for i in range(devices - 1)]
    up = [(i + 1, i) for i in range(devices - 1)]
    above = lax.ppermute(images[:, BLOCK - RIM :], "ccd", down)
    below = lax.ppermute(images[:, :RIM], "ccd", up)
    patch = block_patch[:, :, 0]
    weight = visit_weight.astype(F32)
    ready = prepare(place, basis_taps, psf_coef, affine)
    sent = [
        warp(part, place, patch, block_slot, patch_owner, weight, ready, images, rim, devices)
        for part, rim in enumerate((above, below))
    ]
    result = labels = None
    for part, blocks in enumerate(sent):
        got = lax.all_to_all(blocks, "ccd", split_axis=0, concat_axis=0, tiled=True)
        if part == 0:
            labels = got[:, CAP * ROWS : CAP * ROWS + 2 * CAP, 0].astype(F32)
        result = coadd(part, labels, got, result)
    return result.reshape(1, PSIDE * BLOCK, PSIDE * BLOCK)


def solution(mesh):
    placed = (
        P(None, ("group", "ccd"), None),
        P(),
        P(None, "group", None, None),
        P(None, "group", None, None),
        P(None, "group"),
        P(("group", "ccd"), None, None),
        P(("group", "ccd"), None),
        P("group"),
    )
    return jax.shard_map(
        shards,
        mesh=mesh,
        in_specs=placed,
        out_specs=P(("group", "ccd"), None, None),
        check_vma=False,
    )
```

time: 87.7 us -> 66.7 us (0.76)
  blocking collectives: 25.1 us -> 0 us
  waiting for transfers between devices: 4.06 us -> 19.2 us
  Pallas kernels: 27.2 us -> 22.1 us
  starting transfers between devices: 25.5 us -> 21.9 us
  local copies, waits for them, and re-layouts: 4.65 us -> 2.87 us
    all_gather x1 -> x0, blocking collectives: 25.1 us -> none  [shards(): lax.all_gather(patch * CELLS + block_slot, 'ccd', axis=0, tiled=True)]
    all_to_all x2, waiting for transfers between devices: 2.21 us -> 17.3 us  [shards(): got = lax.all_to_all(blocks, 'ccd', split_axis=0, concat_axis=0, tiled=True)]
    pallas_call x2, Pallas kernels: 18.1 us -> 13.7 us  [warp(): pl.pallas_call(functools.partial(warp_kernel, part), grid_spec=pltpu.Pref...]
    all_to_all x2, starting transfers between devices: 21.8 us -> 18.2 us  [shards(): got = lax.all_to_all(blocks, 'ccd', split_axis=0, concat_axis=0, tiled=True)]
    unnamed x29 -> x19, local copies, waits for them, and re-layouts: 3.69 us -> 1.72 us
    pallas_call x1, Pallas kernels: 4.62 us -> 3.3 us  [prepare(): pl.pallas_call(prepare_kernel, grid_spec=pltpu.PrefetchScalarGridSpec(num...]
  transfers between devices with their start and end apart: 4 -> 4, of which waited for: 2 -> 3; matrix products, arithmetic and copies ran while one was open for 1% -> 1% of each run, Pallas kernels for 18% -> 19%
where the time goes in v1:
time: 66.7 us; the launch traced here: 66.2 us
  Pallas kernels  22.1 us (33%)
  starting transfers between devices  21.9 us (33%)
  waiting for transfers between devices  19.2 us (29%)
  local copies, waits for them, and re-layouts  2.87 us (4%)
    all_to_all x2, starting transfers between devices, shards(): got = lax.all_to_all(blocks, 'ccd', split_axis=0, concat_axis=0, tiled=True)  18.2 us
    all_to_all x2, waiting for transfers between devices, shards(): got = lax.all_to_all(blocks, 'ccd', split_axis=0, concat_axis=0, tiled=True)  17.3 us
    pallas_call x2, Pallas kernels, warp(): pl.pallas_call(functools.partial(warp_kernel, part), grid_spec=pltpu.Pref...  13.7 us
    pallas_call x2, Pallas kernels, coadd(): pl.pallas_call(coadd_kernel, grid=(1,), in_specs=specs, out_specs=pl.Bloc...  5.08 us
    pallas_call x1, Pallas kernels, prepare(): pl.pallas_call(prepare_kernel, grid_spec=pltpu.PrefetchScalarGridSpec(num...  3.3 us
    ppermute x1, starting transfers between devices, shards(): above = lax.ppermute(images[:, BLOCK - RIM:], 'ccd', down)  2.36 us
    ppermute x1, waiting for transfers between devices, shards(): below = lax.ppermute(images[:, :RIM], 'ccd', up)  1.85 us
    unnamed x19, local copies, waits for them, and re-layouts  1.72 us
  transfers between devices with their start and end apart: 4, of which 3 were waited for; matrix products, arithmetic and copies ran while one was open for 1% of the time, Pallas kernels for 19%

profile of v1, /device:TPU:0, one launch (start us, length us, event | category | flops | bytes accessed | tf_op | source)
XLA Modules:
  0.0 66.2 jit_solution(8090613691034049368)
XLA Ops:
  0.0 0.9 %fusion = (f32[4,8,512]{2,1,0:T(8,128)S(1)}, f32[4,8,512]{2,1,0:T(8,128)S(1)}) fusion(f32[4,128,512]{2,1,0:T(8,128)} %image.3), kind=kLoop, calls=%fused_computation.1 | loop fusion | bytes 262144 | tf_op jit(solution)/shard_map/slice | solution.py:373
  0.9 2.4 %collective-permute-start = (f32[4,8,512]{2,1,0:T(8,128)S(1)}, f32[4,8,512]{2,1,0:T(8,128)S(1)}, u32[]{:S(2)}, u32[]{:S(2)}) collective-permute-start(f32[4,8,512]{2,1,0:T(8,128)S(1)} %get-tuple-element.12), channel_id=1, source_target_pairs={{0,1},{1,2},{2,3},{3,4},{4,5},{5,6},{6,7},{7,8},{8,9},{9,10},{10,1... | collective-permute-start | bytes 196616 | tf_op jit(solution)/shard_map/ppermute | solution.py:372
  3.3 0.0 copy-start.5
  3.3 0.0 copy-start.7
  3.3 0.0 copy-start.6
  3.3 0.0 copy-start.4
  3.3 0.6 copy-done.7
  4.0 0.0 copy-done.5
  4.0 0.0 copy-done.6
  4.0 0.1 copy.18.affine
  4.1 0.2 copy.17.psf
  4.4 0.1 stack.31.place
  4.5 3.3 %prepare.1 = (bf16[4,264,384]{2,1,0:T(8,128)(2,1)S(1)}, bf16[4,128,256]{2,1,0:T(8,128)(2,1)S(1)}, f32[4,8,512]{2,1,0:T(8,128)S(1)}) custom-call(s32[5]{0:T(128)S(1)} %stack.31.place, f32[2,9,11]{2,1,0:T(8,128)S(1)} %copy.16.taps, f32[4,5,9,3]{3,2,1,0:T(8,128)S(1)} %copy.17.psf, f32[4,5,2,2]{3,2,1,0:T(2,128)S(1)} %copy.18.affine), custom_call_target="tpu_custom_call" | custom-call | flops 1073741824 | bytes 1048576 | tf_op jit(solution)/shard_map/prepare/pallas_call | solution.py:134
  7.8 0.0 collective-permute-done.rim
  7.8 0.0 copy-start.1
  7.8 0.0 copy-start.2
  7.8 0.0 copy-start.3
  7.8 0.6 copy-done.1
  8.4 0.0 copy-done.2
  8.5 0.0 copy-done.3
  8.5 6.9 %match_warp_0.1 = bf16[16,144,128]{2,1,0:T(8,128)(2,1)} custom-call(s32[5]{0:T(128)S(1)} %stack.31.place, s32[1,16]{1,0:T(1,128)S(1)} %bitcast.8, s32[1,16]{1,0:T(1,128)S(1)} %copy-done.2, s32[16]{0:T(128)S(1)} %copy-done.3, f32[4,5]{1,0:T(4,128)S(1)} %convert_element_type.10.weight, bf16[4,264,384]{2,1,0:T(8,128)(2,1)S(1)} %get-tuple-element.8.bands, ...), custom_call_target="tpu_custom_call" | custom-call | flops 2491416576 | bytes 1310720 | tf_op jit(solution)/shard_map/match_warp_0/pallas_call | solution.py:275
  15.4 7.2 %all-to-all-start = ((bf16[16,144,128]{2,1,0:T(8,128)(2,1)}), bf16[16,144,128]{2,1,0:T(8,128)(2,1)S(1)}, u32[]{:S(2)}, u32[]{:S(2)}) async-start(bf16[16,144,128]{2,1,0:T(8,128)(2,1)} %match_warp_0.1), calls=%async_computation | async-start | bytes 1179648 | tf_op jit(solution)/shard_map/all_to_all | solution.py:383
  22.6 1.3 %collective-permute-start.1 = (f32[4,8,512]{2,1,0:T(8,128)S(1)}, f32[4,8,512]{2,1,0:T(8,128)S(1)}, u32[]{:S(2)}, u32[]{:S(2)}) collective-permute-start(f32[4,8,512]{2,1,0:T(8,128)S(1)} %get-tuple-element.11), channel_id=1, source_target_pairs={{1,0},{2,1},{3,2},{4,3},{5,4},{6,5},{7,6},{8,7},{9,8},{10,9},{11,1... | collective-permute-start | bytes 196616 | tf_op jit(solution)/shard_map/ppermute | solution.py:373
  23.9 1.8 %collective-permute-done.1.rim = f32[4,8,512]{2,1,0:T(8,128)S(1)} collective-permute-done((f32[4,8,512]{2,1,0:T(8,128)S(1)}, f32[4,8,512]{2,1,0:T(8,128)S(1)}, u32[]{:S(2)}, u32[]{:S(2)}) %collective-permute-start.1) | collective-permute-done | bytes 65568 | tf_op jit(solution)/shard_map/ppermute | solution.py:373
  25.8 6.8 %match_warp_1.1 = bf16[16,128,128]{2,1,0:T(8,128)(2,1)} custom-call(s32[5]{0:T(128)S(1)} %stack.31.place, s32[1,16]{1,0:T(1,128)S(1)} %bitcast.9, s32[1,16]{1,0:T(1,128)S(1)} %copy-done.2, s32[16]{0:T(128)S(1)} %copy-done.3, f32[4,5]{1,0:T(4,128)S(1)} %convert_element_type.10.weight, bf16[4,264,384]{2,1,0:T(8,128)(2,1)S(1)} %get-tuple-element.8.bands, ...), custom_call_target="tpu_custom_call" | custom-call | flops 2491416576 | bytes 1310720 | tf_op jit(solution)/shard_map/match_warp_1/pallas_call | solution.py:275
  32.6 5.6 %all-to-all-done.got = bf16[16,144,128]{2,1,0:T(8,128)(2,1)S(1)} async-done(((bf16[16,144,128]{2,1,0:T(8,128)(2,1)}), bf16[16,144,128]{2,1,0:T(8,128)(2,1)S(1)}, u32[]{:S(2)}, u32[]{:S(2)}) %all-to-all-start) | async-done | bytes 589856 | tf_op jit(solution)/shard_map/all_to_all | solution.py:383
  38.2 11.0 %all-to-all-start.1 = ((bf16[16,128,128]{2,1,0:T(8,128)(2,1)}), bf16[16,128,128]{2,1,0:T(8,128)(2,1)S(1)}, u32[]{:S(2)}, u32[]{:S(2)}) async-start(bf16[16,128,128]{2,1,0:T(8,128)(2,1)} %match_warp_1.1), calls=%async_computation.1 | async-start | bytes 1048576 | tf_op jit(solution)/shard_map/all_to_all | solution.py:383
  49.2 0.1 copy.19
  49.3 0.1 copy.21.labels
  49.4 2.5 %coadd_0.1.refs_0_ = f32[4,2,64,512]{3,2,1,0:T(8,128)} custom-call(f32[16,4]{1,0:T(8,128)S(1)} %copy.21.labels, bf16[16,144,128]{2,1,0:T(8,128)(2,1)S(1)} %all-to-all-done.got), custom_call_target="tpu_custom_call" | custom-call | tf_op jit(solution)/shard_map/coadd_0/pallas_call | solution.py:341
  51.9 11.7 %all-to-all-done.1.got = bf16[16,128,128]{2,1,0:T(8,128)(2,1)S(1)} async-done(((bf16[16,128,128]{2,1,0:T(8,128)(2,1)}), bf16[16,128,128]{2,1,0:T(8,128)(2,1)S(1)}, u32[]{:S(2)}, u32[]{:S(2)}) %all-to-all-start.1) | async-done | bytes 524320 | tf_op jit(solution)/shard_map/all_to_all | solution.py:383
  63.7 2.5 %coadd_1.1 = f32[4,2,64,512]{3,2,1,0:T(8,128)} custom-call(f32[16,4]{1,0:T(8,128)S(1)} %copy.21.labels, bf16[16,128,128]{2,1,0:T(8,128)(2,1)S(1)} %all-to-all-done.1.got, f32[4,2,64,512]{3,2,1,0:T(8,128)} %coadd_0.1.refs_0_), custom_call_target="tpu_custom_call", output_to_operand_aliasing={{}: (2, {})} | custom-call | tf_op jit(solution)/shard_map/coadd_1/pallas_call | solution.py:341
  (6 shorter events, 0.0 us)
Async XLA Ops:
  0.9 6.9 %collective-permute-start = (f32[4,8,512]{2,1,0:T(8,128)S(1)}, f32[4,8,512]{2,1,0:T(8,128)S(1)}, u32[]{:S(2)}, u32[]{:S(2)}) collective-permute-start(f32[4,8,512]{2,1,0:T(8,128)S(1)} %get-tuple-element.12), channel_id=1, source_target_pairs={{0,1},{1,2},{2,3},{3,4},{4,5},{5,6},{6,7},{7,8},{8,9},{9,10},{10,1... | collective-permute-start | bytes 196616 | tf_op jit(solution)/shard_map/ppermute | solution.py:372
  3.3 0.7 %copy-start.5 = (f32[2,9,11]{2,0,1:T(2,128)S(1)}, f32[2,9,11]{2,0,1:T(2,128)}, u32[]{:S(2)}) copy-start(f32[2,9,11]{2,0,1:T(2,128)} %param.9) | copy-start | bytes 2380
  3.3 0.7 %copy-start.7 = (bf16[4,5]{1,0:T(4,128)(2,1)S(1)}, bf16[4,5]{1,0:T(4,128)(2,1)}, u32[]{:S(2)}) copy-start(bf16[4,5]{1,0:T(4,128)(2,1)} %param.12) | copy-start | bytes 124
  3.3 0.7 %copy-start.6 = (f32[4,5,2,2]{1,3,2,0:T(2,128)S(1)}, f32[4,5,2,2]{1,3,2,0:T(2,128)}, u32[]{:S(2)}) copy-start(f32[4,5,2,2]{1,3,2,0:T(2,128)} %param.11) | copy-start | bytes 964
  3.3 0.8 %copy-start.4 = (f32[4,5,9,3]{2,0,3,1:T(4,128)S(1)}, f32[4,5,9,3]{2,0,3,1:T(4,128)}, u32[]{:S(2)}) copy-start(f32[4,5,9,3]{2,0,3,1:T(4,128)} %param.10) | copy-start | bytes 6484
  4.5 3.4 %copy-start = (f32[4,128,512]{2,1,0:T(8,128)S(1)}, f32[4,128,512]{2,1,0:T(8,128)}, u32[]{:S(2)}) copy-start(f32[4,128,512]{2,1,0:T(8,128)} %image.3) | copy-start | bytes 3145732
  7.8 0.7 copy-start.1
  7.8 0.7 %copy-start.2 = (s32[1,16]{1,0:T(1,128)S(1)}, s32[1,16]{1,0:T(1,128)}, u32[]{:S(2)}) copy-start(s32[1,16]{1,0:T(1,128)} %slot.3) | copy-start | bytes 196
  7.8 0.7 %copy-start.3 = (s32[16]{0:T(128)S(1)}, s32[16]{0:T(128)}, u32[]{:S(2)}) copy-start(s32[16]{0:T(128)} %owner.3) | copy-start | bytes 196
  15.4 22.8 %all-to-all-start = ((bf16[16,144,128]{2,1,0:T(8,128)(2,1)}), bf16[16,144,128]{2,1,0:T(8,128)(2,1)S(1)}, u32[]{:S(2)}, u32[]{:S(2)}) async-start(bf16[16,144,128]{2,1,0:T(8,128)(2,1)} %match_warp_0.1), calls=%async_computation | async-start | bytes 1179648 | tf_op jit(solution)/shard_map/all_to_all | solution.py:383
  22.6 3.1 %collective-permute-start.1 = (f32[4,8,512]{2,1,0:T(8,128)S(1)}, f32[4,8,512]{2,1,0:T(8,128)S(1)}, u32[]{:S(2)}, u32[]{:S(2)}) collective-permute-start(f32[4,8,512]{2,1,0:T(8,128)S(1)} %get-tuple-element.11), channel_id=1, source_target_pairs={{1,0},{2,1},{3,2},{4,3},{5,4},{6,5},{7,6},{8,7},{9,8},{10,9},{11,1... | collective-permute-start | bytes 196616 | tf_op jit(solution)/shard_map/ppermute | solution.py:373
  38.2 25.5 %all-to-all-start.1 = ((bf16[16,128,128]{2,1,0:T(8,128)(2,1)}), bf16[16,128,128]{2,1,0:T(8,128)(2,1)S(1)}, u32[]{:S(2)}, u32[]{:S(2)}) async-start(bf16[16,128,128]{2,1,0:T(8,128)(2,1)} %match_warp_1.1), calls=%async_computation.1 | async-start | bytes 1048576 | tf_op jit(solution)/shard_map/all_to_all | solution.py:383

commit v2 on v1

v2 whole, which is shorter than its diff:
```python
import jax
import jax.numpy as jnp
import numpy as np
from jax import lax
from jax.experimental import pallas as pl
from jax.experimental.pallas import tpu as pltpu
from jax.sharding import PartitionSpec as P

V = 4
BLOCK = 128
BLKC = 4
SPLIT = 4
TAPS = 11
NBASIS = 9
PSIDE = 4
CELLS = PSIDE * PSIDE
CAP = 2

HALF = TAPS // 2
WARP = 3
RIM = HALF + WARP
HEIGHT = SPLIT * BLOCK
WIDTH = BLKC * BLOCK
LANES = 128
LANE_BLOCKS = WIDTH // LANES
STRIP = 16
STEP = 32
STRIPS = -(-(BLOCK + 2 * WARP) // STRIP)
GROUPS = 6
BAND = 256
TALL = (STRIPS - 1) * STRIP + STEP
HALVES = 2
ROWS = BLOCK // HALVES
MATCH = ROWS + 8
LABEL = 16
F32 = jnp.float32
BF16 = jnp.bfloat16


def sin_pi(t):
    whole = jnp.round(t)
    f = t - whole
    odd = whole - 2.0 * jnp.floor(0.5 * whole)
    f2 = f * f
    out = 0.0
    for c in (
        0.00046630280576761, -0.0073704309457144, 0.0821458866111282,
        -0.599264529320792, 2.55016403987734, -5.16771278004997, 3.14159265358979,
    ):
        out = out * f2 + c
    return f * out * (1.0 - 2.0 * odd)


def lanczos(t):
    zero = t == 0.0
    safe = jnp.where(zero, 1.0, t)
    pt = jnp.pi * safe
    value = 3.0 * sin_pi(safe) * sin_pi(safe / 3.0) / (pt * pt)
    return jnp.where(jnp.abs(t) < 3.0, jnp.where(zero, 1.0, value), 0.0)


def iota(shape, dim):
    return lax.broadcasted_iota(jnp.int32, shape, dim)


def deinterleave():
    order = np.arange(WIDTH).reshape(LANES, LANE_BLOCKS).T.reshape(-1)
    return (np.arange(WIDTH)[:, None] == order[None, :]).astype(np.float32)


def column_at(lane):
    return lane % LANES * LANE_BLOCKS + lane // LANES


def prepare_kernel(place, taps, psf, affine, level_out, slope_out, rows_out, cols_out):
    lane = iota((1, BAND), 1)
    seg = lane // STEP
    tap = lane - seg * STEP
    row_taps, col_taps = taps[:, 0], taps[:, 1]
    onehot = (tap == iota((TAPS, BAND), 0)) & (seg < GROUPS)
    r = jnp.dot(
        row_taps, onehot.astype(F32),
        precision=lax.Precision.HIGHEST, preferred_element_type=F32,
    )
    is_level = seg < 3
    low_lanes = seg % 3 == 2
    ccd_lane = iota((1, 1, affine.shape[3]), 2) == place[0]

    turned = lax.dot_general(
        (iota((TAPS, STRIP), 0) == iota((TAPS, STRIP), 1)).astype(F32), col_taps,
        (((0,), (1,)), ((), ())),
        precision=lax.Precision.HIGHEST, preferred_element_type=F32,
    )
    kernels = jnp.dot(
        jnp.concatenate(
            [turned * psf[0, c, v : v + 1, :] for v in range(V) for c in range(3)], axis=0
        ),
        r, precision=lax.Precision.HIGHEST, preferred_element_type=F32,
    )

    col_move = (iota((STRIP, 1), 0) - HALF).astype(F32) * (2.0 / WIDTH)
    for visit in range(V):
        const, by_row, by_col = (
            kernels[(visit * 3 + c) * STRIP : (visit * 3 + c + 1) * STRIP] for c in range(3)
        )
        const = jnp.where(is_level, const - col_move * by_col, by_col)
        by_row = jnp.where(is_level, by_row, 0.0)
        for u in range(TAPS):
            x = jnp.broadcast_to(const[u : u + 1], (8, BAND))
            x = pltpu.roll(x, 0, 1, stride=1, stride_axis=0)
            x = jnp.concatenate([x, pltpu.roll(x, 8, 1)], axis=0)
            y = jnp.broadcast_to(by_row[u : u + 1, :LANES], (8, LANES))
            y = pltpu.roll(y, 0, 1, stride=1, stride_axis=0)
            y = jnp.concatenate([y, pltpu.roll(y, 8, 1)], axis=0)
            at = slice(u * STRIP, (u + 1) * STRIP)
            level_out[visit, 0, at] = x[:, :LANES]
            level_out[visit, 1, at] = y
            high = x.astype(BF16).astype(F32)
            slope_out[visit, at] = jnp.where(low_lanes, x - high, high)[:, LANES:].astype(BF16)

        a = jnp.sum(jnp.where(ccd_lane, affine[visit], 0.0), axis=2, keepdims=True)
        out_row = iota((BLOCK, LANES), 0)
        local = out_row % ROWS
        in_row = iota((BLOCK, LANES), 1)
        row = (place[1] + out_row).astype(F32)
        shift = a[0, 0:1] + a[0, 1:2] * (row - (HEIGHT - 1) / 2.0) / HEIGHT
        step = in_row - local - WARP
        band_row = out_row + step
        keep = jnp.abs(step) <= WARP
        keep = keep & ((band_row >= 0) | (place[2] > 0)) & ((band_row < BLOCK) | (place[3] > 0))
        weights = jnp.where(keep, lanczos(shift - step.astype(F32)), 0.0)
        high = weights.astype(BF16).astype(F32)
        zero = jnp.zeros_like(weights)
        wide = jnp.concatenate([high, zero], axis=1)
        low = jnp.concatenate([weights - high, zero], axis=1)
        wide = wide + pltpu.roll(wide, MATCH, 1) + pltpu.roll(low, 2 * MATCH, 1)
        rows_out[visit] = wide.astype(BF16)

        lanes = iota((8, WIDTH), 1)
        offset = iota((8, WIDTH), 0) - WARP
        block = lanes // LANES
        carry = (block + offset + LANE_BLOCKS) // LANE_BLOCKS - 1
        from_lane = lanes % LANES - carry
        col = (from_lane * LANE_BLOCKS + block).astype(F32)
        col_shift = a[1, 0:1] + a[1, 1:2] * (col - (WIDTH - 1) / 2.0) / WIDTH
        within = (from_lane >= 0) & (from_lane < LANES) & (offset <= WARP)
        cols_out[visit] = jnp.where(within, lanczos(col_shift - offset.astype(F32)), 0.0)


def prepare(place, taps, psf, affine):
    ccds = affine.shape[1]
    return pl.pallas_call(
        prepare_kernel,
        grid_spec=pltpu.PrefetchScalarGridSpec(
            num_scalar_prefetch=1,
            grid=(1,),
            in_specs=[
                pl.BlockSpec((NBASIS, 2, TAPS), lambda i, place: (0, 0, 0)),
                pl.BlockSpec((1, 3, V, NBASIS), lambda i, place: (place[0], 0, 0, 0)),
                pl.BlockSpec((V, 2, 2, ccds), lambda i, place: (0, 0, 0, 0)),
            ],
            out_specs=[
                pl.BlockSpec((V, 2, TAPS * STRIP, LANES), lambda i, place: (0, 0, 0, 0)),
                pl.BlockSpec((V, TAPS * STRIP, BAND - LANES), lambda i, place: (0, 0, 0)),
                pl.BlockSpec((V, BLOCK, 256), lambda i, place: (0, 0, 0)),
                pl.BlockSpec((V, 8, WIDTH), lambda i, place: (0, 0, 0)),
            ],
        ),
        out_shape=[
            jax.ShapeDtypeStruct((V, 2, TAPS * STRIP, LANES), F32),
            jax.ShapeDtypeStruct((V, TAPS * STRIP, BAND - LANES), BF16),
            jax.ShapeDtypeStruct((V, BLOCK, 256), BF16),
            jax.ShapeDtypeStruct((V, 8, WIDTH), F32),
        ],
        compiler_params=pltpu.CompilerParams(vmem_limit_bytes=32 << 20),
        cost_estimate=pl.CostEstimate(flops=1 << 30, bytes_accessed=1 << 20, transcendentals=0),
        name="prepare",
    )(place, taps.transpose(1, 0, 2), psf.transpose(1, 3, 0, 2), affine.transpose(0, 2, 3, 1))


def lane_block(x, v):
    return x[:, v * LANES : (v + 1) * LANES]


def warp_kernel(
    place, patch, slot, owner, weight, level, slope, row_weights, col_weights, sort, unsort,
    image, above, below, out,
    terms, ready, seen, label, label_ready, sem, label_sem,
):
    visit = pl.program_id(0)
    visits = pl.num_programs(0)
    top_row = place[1]

    @pl.when(visit == 0)
    def _():
        terms[:, BLOCK + 2 * RIM :] = jnp.zeros((4, TALL - BLOCK - 2 * RIM, WIDTH), BF16)

    raw = jnp.concatenate(
        [jnp.where(place[2] > 0, above[0], 0.0), image[0], jnp.where(place[3] > 0, below[0], 0.0)],
        axis=0,
    )
    raw_high = raw.astype(BF16)
    raw_low = (raw - raw_high.astype(F32)).astype(BF16)
    tall = BLOCK + 2 * RIM
    sorted_terms = jnp.dot(
        jnp.concatenate([raw_high, raw_low], axis=0), sort[...], preferred_element_type=F32
    )
    high, low = sorted_terms[:tall], sorted_terms[tall:]
    col_pos = (2.0 * column_at(iota((1, WIDTH), 1)).astype(F32) + 1.0) / WIDTH - 1.0
    tilted = (high + low) * col_pos
    tilted_high = tilted.astype(BF16)
    terms[0, :tall] = high.astype(BF16)
    terms[1, :tall] = low.astype(BF16)
    terms[2, :tall] = tilted_high
    terms[3, :tall] = (tilted - tilted_high.astype(F32)).astype(BF16)

    lane = iota((1, LANES), 1)
    low_lanes = (lane // STEP) % 3 == 2
    level_lanes = lane < 3 * STEP
    strip_row = (iota((TAPS * STRIP, 1), 0) % STRIP).astype(F32)
    filler = jnp.zeros((BAND - GROUPS * STEP, WIDTH), BF16)
    strips = []
    for k in range(STRIPS):
        match_row = (top_row + (k * STRIP - WARP)).astype(F32) + strip_row
        row_pos = (2.0 * match_row + 1.0) / HEIGHT - 1.0
        x = level[0, 0] + row_pos * level[0, 1]
        x = jnp.where(low_lanes, x - x.astype(BF16).astype(F32), x)
        matrix = jnp.concatenate([x.astype(BF16), slope[0]], axis=1)
        rows = slice(k * STRIP, k * STRIP + STEP)
        columns = jnp.concatenate(
            [terms[h, rows] for h in (0, 1, 0, 2, 3, 2)] + [filler], axis=0
        )
        taps = jnp.dot(matrix, columns, preferred_element_type=F32)
        out_blocks = []
        for v in range(LANE_BLOCKS):
            total = None
            for q in range(-(HALF // LANE_BLOCKS) - 1, HALF // LANE_BLOCKS + 2):
                part = None
                for u in range(TAPS):
                    if (v + u - HALF) // LANE_BLOCKS != q:
                        continue
                    w = (v + u - HALF) % LANE_BLOCKS
                    piece = lane_block(taps[u * STRIP : (u + 1) * STRIP], w)
                    part = piece if part is None else part + piece
                if part is None:
                    continue
                if q:
                    part = pltpu.roll(part, -q % LANES, 1)
                    part = jnp.where((lane + q >= 0) & (lane + q < LANES), part, 0.0)
                total = part if total is None else total + part
            out_blocks.append(total)
        strips.append(jnp.concatenate(out_blocks, axis=1))
    matched = jnp.concatenate(strips, axis=0)

    high = matched.astype(BF16).astype(F32)
    low = matched - high
    empty = jnp.zeros((256 - 3 * MATCH, WIDTH), F32)
    halves = []
    for h in range(HALVES):
        rows = slice(h * ROWS, h * ROWS + MATCH)
        columns = jnp.concatenate([high[rows], low[rows], high[rows], empty], axis=0).astype(BF16)
        halves.append(
            jnp.dot(
                row_weights[0, h * ROWS : (h + 1) * ROWS], columns, preferred_element_type=F32
            )
        )
    warped = jnp.concatenate(halves, axis=0)
    col = col_weights[0]
    out_blocks = []
    for v in range(LANE_BLOCKS):
        total = None
        for q in (-1, 0, 1):
            part = None
            for s in range(2 * WARP + 1):
                if (v + s - WARP) // LANE_BLOCKS != q:
                    continue
                w = (v + s - WARP) % LANE_BLOCKS
                piece = lane_block(col[s : s + 1], v) * lane_block(warped, w)
                part = piece if part is None else part + piece
            if part is None:
                continue
            if q:
                part = pltpu.roll(part, -q % LANES, 1)
            total = part if total is None else total + part
        out_blocks.append(total.astype(BF16))
    result = jnp.dot(
        jnp.concatenate(out_blocks, axis=1), unsort[...], preferred_element_type=F32
    ).astype(BF16)

    @pl.when(visit == 0)
    def _():
        def clear(p, _):
            seen[p] = 0
            return 0

        lax.fori_loop(0, owner.shape[0], clear, 0)
        label[...] = jnp.zeros_like(label)

    for j in range(BLKC):
        block = visit * BLKC + j
        ready[block] = result[:, j * BLOCK : (j + 1) * BLOCK]
        p = patch[0, block]
        rank = seen[p]
        seen[p] = rank + 1
        to = out.at[owner[p], pl.ds(pl.multiple_of(rank * BLOCK, BLOCK), BLOCK)]
        pltpu.make_async_copy(ready.at[block], to, sem.at[block]).start()
        at = rank * 2
        label[owner[p], pl.ds(at, 1), :] = jnp.full((1, BLOCK), weight[visit, place[0]], F32)
        label[owner[p], pl.ds(at + 1, 1), :] = jnp.full((1, BLOCK), slot[0, block].astype(F32), F32)

    @pl.when(visit == visits - 1)
    def _():
        label_ready[...] = label[...].astype(BF16)
        copy = pltpu.make_async_copy(label_ready, out.at[:, pl.ds(CAP * BLOCK, LABEL)], label_sem)
        copy.start()
        copy.wait()
        for block in range(V * BLKC):
            pltpu.make_async_copy(ready.at[block], out.at[0, pl.ds(0, BLOCK)], sem.at[block]).wait()


def warp(place, patch, slot, owner, weight, ready, images, above, below, devices):
    smem = pl.BlockSpec(memory_space=pltpu.SMEM)
    sort = deinterleave()
    whole = pl.BlockSpec((WIDTH, WIDTH), lambda v, place: (0, 0))
    return pl.pallas_call(
        warp_kernel,
        grid_spec=pltpu.PrefetchScalarGridSpec(
            num_scalar_prefetch=1,
            grid=(V,),
            in_specs=[
                smem,
                smem,
                smem,
                smem,
                pl.BlockSpec((1, 2, TAPS * STRIP, LANES), lambda v, place: (v, 0, 0, 0)),
                pl.BlockSpec((1, TAPS * STRIP, BAND - LANES), lambda v, place: (v, 0, 0)),
                pl.BlockSpec((1, BLOCK, 256), lambda v, place: (v, 0, 0)),
                pl.BlockSpec((1, 8, WIDTH), lambda v, place: (v, 0, 0)),
                whole,
                whole,
                pl.BlockSpec((1, BLOCK, WIDTH), lambda v, place: (v, 0, 0)),
                pl.BlockSpec((1, RIM, WIDTH), lambda v, place: (v, 0, 0)),
                pl.BlockSpec((1, RIM, WIDTH), lambda v, place: (v, 0, 0)),
            ],
            out_specs=pl.BlockSpec(memory_space=pl.ANY),
            scratch_shapes=[
                pltpu.VMEM((4, TALL, WIDTH), BF16),
                pltpu.VMEM((V * BLKC, BLOCK, BLOCK), BF16),
                pltpu.SMEM((owner.shape[0],), jnp.int32),
                pltpu.VMEM((devices, LABEL, BLOCK), F32),
                pltpu.VMEM((devices, LABEL, BLOCK), BF16),
                pltpu.SemaphoreType.DMA((V * BLKC,)),
                pltpu.SemaphoreType.DMA(()),
            ],
        ),
        out_shape=jax.ShapeDtypeStruct((devices, CAP * BLOCK + LABEL, BLOCK), BF16),
        compiler_params=pltpu.CompilerParams(vmem_limit_bytes=32 << 20),
        cost_estimate=pl.CostEstimate(
            flops=V * 2 * STRIPS * TAPS * STRIP * BAND * WIDTH,
            bytes_accessed=V * (BLOCK * WIDTH * 6),
            transcendentals=0,
        ),
        name="match_warp",
    )(
        place, patch, slot, owner, weight, *ready,
        jnp.asarray(sort, BF16), jnp.asarray(sort.T, BF16), images, above, below,
    )


def coadd_kernel(labels, got, out, sums):
    out[...] = jnp.zeros_like(out)
    for c in range(CELLS):
        sums[c] = 0.0

    def add(k, _):
        source, rank = k // CAP, k % CAP
        weight = labels[source, rank * 2]

        @pl.when(weight > 0.0)
        def _():
            c = labels[source, rank * 2 + 1].astype(jnp.int32)
            sums[c] += weight
            lanes = pl.ds(pl.multiple_of(c % PSIDE * BLOCK, BLOCK), BLOCK)
            rows = pl.ds(pl.multiple_of(rank * BLOCK, BLOCK), BLOCK)
            out[c // PSIDE, :, lanes] += weight * got[source, rows].astype(F32)

        return 0

    lax.fori_loop(0, got.shape[0] * CAP, add, 0)
    for c in range(CELLS):
        lanes = slice(c % PSIDE * BLOCK, (c % PSIDE + 1) * BLOCK)
        inverse = 1.0 / jnp.maximum(jnp.full((1, BLOCK), sums[c], F32), 1.0)
        out[c // PSIDE, :, lanes] = out[c // PSIDE, :, lanes] * inverse


def coadd(labels, got):
    smem = pl.BlockSpec(memory_space=pltpu.SMEM)
    return pl.pallas_call(
        coadd_kernel,
        grid=(1,),
        in_specs=[smem, pl.BlockSpec((got.shape[0], CAP * BLOCK, BLOCK), lambda i: (0, 0, 0))],
        out_specs=pl.BlockSpec((PSIDE, BLOCK, WIDTH), lambda i: (0, 0, 0)),
        out_shape=jax.ShapeDtypeStruct((PSIDE, BLOCK, PSIDE * BLOCK), F32),
        scratch_shapes=[pltpu.SMEM((CELLS,), F32)],
        compiler_params=pltpu.CompilerParams(vmem_limit_bytes=32 << 20),
        name="coadd",
    )(labels, got)


def shards(
    images, basis_taps, psf_coef, affine, visit_weight, block_patch, block_slot, patch_owner
):
    band = lax.axis_index("ccd")
    devices = lax.axis_size("ccd")
    shifted = band + SPLIT // 2
    quarter = shifted % SPLIT
    place = jnp.stack(
        [
            shifted // SPLIT,
            quarter * BLOCK,
            ((quarter > 0) & (band > 0)).astype(jnp.int32),
            ((quarter < SPLIT - 1) & (band < devices - 1)).astype(jnp.int32),
            band,
        ]
    ).astype(jnp.int32)
    down = [(i, i + 1) for i in range(devices - 1)]
    up = [(i + 1, i) for i in range(devices - 1)]
    above = lax.ppermute(images[:, BLOCK - RIM :], "ccd", down)
    below = lax.ppermute(images[:, :RIM], "ccd", up)
    patch = block_patch[:, :, 0]
    weight = visit_weight.astype(F32)
    ready = prepare(place, basis_taps, psf_coef, affine)
    sent = warp(
        place, patch, block_slot, patch_owner, weight, ready, images, above, below, devices
    )
    got = lax.all_to_all(sent, "ccd", split_axis=0, concat_axis=0, tiled=True)
    labels = got[:, CAP * BLOCK : CAP * BLOCK + 2 * CAP, 0].astype(F32)
    result = coadd(labels, got)
    return result.reshape(1, PSIDE * BLOCK, PSIDE * BLOCK)


def solution(mesh):
    placed = (
        P(None, ("group", "ccd"), None),
        P(),
        P(None, "group", None, None),
        P(None, "group", None, None),
        P(None, "group"),
        P(("group", "ccd"), None, None),
        P(("group", "ccd"), None),
        P("group"),
    )
    return jax.shard_map(
        shards,
        mesh=mesh,
        in_specs=placed,
        out_specs=P(("group", "ccd"), None, None),
        check_vma=False,
    )
```

time: 66.7 us -> 58.3 us (0.87)
  blocking collectives: 0 us -> 36.3 us
  waiting for transfers between devices: 19.2 us -> 0.01 us
  starting transfers between devices: 21.9 us -> 4.33 us
  Pallas kernels: 22.1 us -> 13 us
  other arithmetic: 0.01 us -> 0.69 us
    all_to_all x0 -> x1, blocking collectives: none -> 36.3 us  [shards(): got = lax.all_to_all(sent, 'ccd', split_axis=0, concat_axis=0, tiled=True)]
    all_to_all x2 -> x0, starting transfers between devices: 18.2 us -> none  [shards(): got = lax.all_to_all(blocks, 'ccd', split_axis=0, concat_axis=0, tiled=True)]
    all_to_all x2 -> x0, waiting for transfers between devices: 17.3 us -> none  [shards(): got = lax.all_to_all(blocks, 'ccd', split_axis=0, concat_axis=0, tiled=True)]
    pallas_call x4 -> x2, Pallas kernels: 18.8 us -> 11 us  [the longest x1 8.18 us: warp(): pl.pallas_call(warp_kernel, grid_spec=pltpu.PrefetchScalarGridSpec(num_sc...]
    ppermute x1, waiting for transfers between devices: 1.85 us -> 0.01 us  [shards(): below = lax.ppermute(images[:, :RIM], 'ccd', up)]
    pallas_call x1, Pallas kernels: 3.3 us -> 2 us  [prepare(): pl.pallas_call(prepare_kernel, grid_spec=pltpu.PrefetchScalarGridSpec(num...]
    convert_element_type x1, other arithmetic: 0.01 us -> 0.68 us  [shards(): weight = visit_weight.astype(F32)]
    ppermute x1, starting transfers between devices: 2.36 us -> 3.03 us  [shards(): above = lax.ppermute(images[:, BLOCK - RIM:], 'ccd', down)]
  transfers between devices with their start and end apart: 4 -> 2, of which waited for: 3 -> 0; matrix products, arithmetic and copies ran while one was open for 1% -> 1% of each run, Pallas kernels for 19% -> 3%
where the time goes in v2:
time: 58.3 us; the launch traced here: 57.8 us
  blocking collectives  36.3 us (62%)
  Pallas kernels  13 us (22%)
  starting transfers between devices  4.33 us (7%)
  local copies, waits for them, and re-layouts  3.33 us (6%)
  other arithmetic  0.69 us (1%)
    all_to_all x1, blocking collectives, shards(): got = lax.all_to_all(sent, 'ccd', split_axis=0, concat_axis=0, tiled=True)  36.3 us
    pallas_call x1, Pallas kernels, warp(): pl.pallas_call(warp_kernel, grid_spec=pltpu.PrefetchScalarGridSpec(num_sc...  8.18 us
    ppermute x1, starting transfers between devices, shards(): above = lax.ppermute(images[:, BLOCK - RIM:], 'ccd', down)  3.03 us
    pallas_call x1, Pallas kernels, coadd(): pl.pallas_call(coadd_kernel, grid=(1,), in_specs=[smem, pl.BlockSpec((got...  2.86 us
    unnamed x18, local copies, waits for them, and re-layouts  2.18 us
    pallas_call x1, Pallas kernels, prepare(): pl.pallas_call(prepare_kernel, grid_spec=pltpu.PrefetchScalarGridSpec(num...  2 us
    ppermute x1, starting transfers between devices, shards(): below = lax.ppermute(images[:, :RIM], 'ccd', up)  1.29 us
  transfers between devices with their start and end apart: 2, of which 0 were waited for; matrix products, arithmetic and copies ran while one was open for 1% of the time, Pallas kernels for 3%

profile of v2, /device:TPU:0, one launch (start us, length us, event | category | flops | bytes accessed | tf_op | source)
XLA Modules:
  0.0 57.8 jit_solution(9061499897316419295)
XLA Ops:
  0.0 0.9 %fusion = (f32[4,8,512]{2,1,0:T(8,128)S(1)}, f32[4,8,512]{2,1,0:T(8,128)S(1)}) fusion(f32[4,128,512]{2,1,0:T(8,128)} %image.1), kind=kLoop, calls=%fused_computation.1 | loop fusion | bytes 262144 | tf_op jit(solution)/shard_map/slice | solution.py:429
  0.9 1.3 %collective-permute-start.1 = (f32[4,8,512]{2,1,0:T(8,128)S(1)}, f32[4,8,512]{2,1,0:T(8,128)S(1)}, u32[]{:S(2)}, u32[]{:S(2)}) collective-permute-start(f32[4,8,512]{2,1,0:T(8,128)S(1)} %get-tuple-element.13), channel_id=1, source_target_pairs={{1,0},{2,1},{3,2},{4,3},{5,4},{6,5},{7,6},{8,7},{9,8},{10,9},{11,1... | collective-permute-start | bytes 196616 | tf_op jit(solution)/shard_map/ppermute | solution.py:429
  2.2 3.0 %collective-permute-start = (f32[4,8,512]{2,1,0:T(8,128)S(1)}, f32[4,8,512]{2,1,0:T(8,128)S(1)}, u32[]{:S(2)}, u32[]{:S(2)}) collective-permute-start(f32[4,8,512]{2,1,0:T(8,128)S(1)} %get-tuple-element.14), channel_id=1, source_target_pairs={{0,1},{1,2},{2,3},{3,4},{4,5},{5,6},{6,7},{7,8},{8,9},{9,10},{10,1... | collective-permute-start | bytes 196616 | tf_op jit(solution)/shard_map/ppermute | solution.py:428
  5.3 0.7 %convert_element_type.10.weight = f32[4,5]{1,0:T(4,128)S(1)} convert(bf16[4,5]{1,0:T(4,128)(2,1)} %param.14) | non-fusion elementwise | flops 20 | bytes 120 | tf_op jit(solution)/shard_map/convert_element_type | solution.py:431
  5.9 0.1 stack.31.place
  6.0 0.0 copy-start.1
  6.0 0.8 %copy-done.1 = f32[4,5,9,3]{2,0,3,1:T(4,128)S(1)} copy-done((f32[4,5,9,3]{2,0,3,1:T(4,128)S(1)}, f32[4,5,9,3]{2,0,3,1:T(4,128)}, u32[]{:S(2)}) %copy-start.1) | copy-done | bytes 2184
  6.8 0.0 copy-start.2
  6.8 0.7 %copy-done.2 = f32[2,9,11]{2,0,1:T(2,128)S(1)} copy-done((f32[2,9,11]{2,0,1:T(2,128)S(1)}, f32[2,9,11]{2,0,1:T(2,128)}, u32[]{:S(2)}) %copy-start.2) | copy-done | bytes 816
  7.5 0.0 copy-start.3
  7.5 0.7 %copy-done.3 = f32[4,5,2,2]{1,3,2,0:T(2,128)S(1)} copy-done((f32[4,5,2,2]{1,3,2,0:T(2,128)S(1)}, f32[4,5,2,2]{1,3,2,0:T(2,128)}, u32[]{:S(2)}) %copy-start.3) | copy-done | bytes 344
  8.2 0.0 copy-start
  8.2 0.0 copy-start.4
  8.2 0.0 copy-start.5
  8.2 0.0 copy-start.6
  8.2 0.0 copy-start.7
  8.2 0.0 copy-start.8
  8.2 2.0 %prepare.1 = (f32[4,2,176,128]{3,2,1,0:T(8,128)S(1)}, bf16[4,176,128]{2,1,0:T(8,128)(2,1)S(1)}, bf16[4,128,256]{2,1,0:T(8,128)(2,1)S(1)}, f32[4,8,512]{2,1,0:T(8,128)S(1)}) custom-call(s32[5]{0:T(128)S(1)} %stack.31.place, f32[9,2,11]{2,1,0:T(2,128)S(1)} %bitcast.12, f32[5,3,4,9]{3,2,1,0:T(4,128)S(1)} %bitcast.11, f32[4,2,2,5]{3,2,1,0:T(2,128)S(1)} %bitcast.13), custom_call_target="tpu_custom_call" | custom-call | flops 1073741824 | bytes 1048576 | tf_op jit(solution)/shard_map/prepare/pallas_call | solution.py:152
  10.2 0.0 collective-permute-done.1.below
  10.2 0.0 collective-permute-done.above
  10.2 0.0 copy-done
  10.2 0.0 copy-done.4
  10.3 0.0 copy-done.5
  10.3 0.0 copy-done.6
  10.3 0.0 copy-done.7
  10.3 0.0 copy-done.8
  10.3 8.2 %match_warp.1 = bf16[16,272,128]{2,1,0:T(8,128)(2,1)S(1)} custom-call(s32[5]{0:T(128)S(1)} %stack.31.place, s32[1,16]{1,0:T(1,128)S(1)} %bitcast.14, s32[1,16]{1,0:T(1,128)S(1)} %copy-done.5, s32[16]{0:T(128)S(1)} %copy-done.6, f32[4,5]{1,0:T(4,128)S(1)} %convert_element_type.10.weight, f32[4,2,176,128]{3,2,1,0:T(8,128)S(1)} %get-tuple-element.9.level, ...), custom_call_target="tpu_custom_call" | custom-call | flops 1660944384 | bytes 1572864 | tf_op jit(solution)/shard_map/match_warp/pallas_call | solution.py:325
  18.5 36.3 %all_to_all.5.got = bf16[16,272,128]{2,1,0:T(8,128)(2,1)S(1)} all-to-all(bf16[16,272,128]{2,1,0:T(8,128)(2,1)S(1)} %match_warp.1), channel_id=1, replica_groups=mesh['group'=2,'ccd'=16] {'ccd'}, dimensions={0} | all-to-all | bytes 2228224 | tf_op jit(solution)/shard_map/all_to_all | solution.py:436
  54.8 0.1 copy.13
  54.9 0.1 copy.14.labels
  55.0 2.9 %coadd.1 = f32[4,128,512]{2,1,0:T(8,128)} custom-call(f32[16,4]{1,0:T(8,128)S(1)} %copy.14.labels, bf16[16,272,128]{2,1,0:T(8,128)(2,1)S(1)} %all_to_all.5.got), custom_call_target="tpu_custom_call" | custom-call | tf_op jit(solution)/shard_map/coadd/pallas_call | solution.py:398
  (1 shorter events, 0.0 us)
Async XLA Ops:
  0.9 9.3 %collective-permute-start.1 = (f32[4,8,512]{2,1,0:T(8,128)S(1)}, f32[4,8,512]{2,1,0:T(8,128)S(1)}, u32[]{:S(2)}, u32[]{:S(2)}) collective-permute-start(f32[4,8,512]{2,1,0:T(8,128)S(1)} %get-tuple-element.13), channel_id=1, source_target_pairs={{1,0},{2,1},{3,2},{4,3},{5,4},{6,5},{7,6},{8,7},{9,8},{10,9},{11,1... | collective-permute-start | bytes 196616 | tf_op jit(solution)/shard_map/ppermute | solution.py:429
  2.2 8.0 %collective-permute-start = (f32[4,8,512]{2,1,0:T(8,128)S(1)}, f32[4,8,512]{2,1,0:T(8,128)S(1)}, u32[]{:S(2)}, u32[]{:S(2)}) collective-permute-start(f32[4,8,512]{2,1,0:T(8,128)S(1)} %get-tuple-element.14), channel_id=1, source_target_pairs={{0,1},{1,2},{2,3},{3,4},{4,5},{5,6},{6,7},{7,8},{8,9},{9,10},{10,1... | collective-permute-start | bytes 196616 | tf_op jit(solution)/shard_map/ppermute | solution.py:428
  6.0 0.8 %copy-start.1 = (f32[4,5,9,3]{2,0,3,1:T(4,128)S(1)}, f32[4,5,9,3]{2,0,3,1:T(4,128)}, u32[]{:S(2)}) copy-start(f32[4,5,9,3]{2,0,3,1:T(4,128)} %param.12) | copy-start | bytes 6484
  6.8 0.7 %copy-start.2 = (f32[2,9,11]{2,0,1:T(2,128)S(1)}, f32[2,9,11]{2,0,1:T(2,128)}, u32[]{:S(2)}) copy-start(f32[2,9,11]{2,0,1:T(2,128)} %param.11) | copy-start | bytes 2380
  7.5 0.7 %copy-start.3 = (f32[4,5,2,2]{1,3,2,0:T(2,128)S(1)}, f32[4,5,2,2]{1,3,2,0:T(2,128)}, u32[]{:S(2)}) copy-start(f32[4,5,2,2]{1,3,2,0:T(2,128)} %param.13) | copy-start | bytes 964
  8.2 2.1 %copy-start = (f32[4,128,512]{2,1,0:T(8,128)S(1)}, f32[4,128,512]{2,1,0:T(8,128)}, u32[]{:S(2)}) copy-start(f32[4,128,512]{2,1,0:T(8,128)} %image.1) | copy-start | bytes 3145732
  8.2 2.1 %copy-start.4 = (s32[1,16,1]{1,2,0:T(1,128)S(1)}, s32[1,16,1]{1,2,0:T(1,128)}, u32[]{:S(2)}) copy-start(s32[1,16,1]{1,2,0:T(1,128)} %param.15) | copy-start | bytes 196
  8.2 2.1 %copy-start.5 = (s32[1,16]{1,0:T(1,128)S(1)}, s32[1,16]{1,0:T(1,128)}, u32[]{:S(2)}) copy-start(s32[1,16]{1,0:T(1,128)} %slot.1) | copy-start | bytes 196
  8.2 2.1 %copy-start.6 = (s32[16]{0:T(128)S(1)}, s32[16]{0:T(128)}, u32[]{:S(2)}) copy-start(s32[16]{0:T(128)} %owner.1) | copy-start | bytes 196
  8.2 2.1 %copy-start.7 = (bf16[512,512]{1,0:T(8,128)(2,1)S(1)}, bf16[512,512]{1,0:T(8,128)(2,1)}, u32[]{:S(2)}) copy-start(bf16[512,512]{1,0:T(8,128)(2,1)} %constant.42.clone.unsort) | copy-start | bytes 1572868
  8.2 2.1 %copy-start.8 = (bf16[512,512]{1,0:T(8,128)(2,1)S(1)}, bf16[512,512]{1,0:T(8,128)(2,1)}, u32[]{:S(2)}) copy-start(bf16[512,512]{1,0:T(8,128)(2,1)} %constant.41.clone.sort) | copy-start | bytes 1572868

commit v3 on v2

--- a/solution.py
+++ b/solution.py
@@ -14,7 +14,6 @@
 NBASIS = 9
 PSIDE = 4
 CELLS = PSIDE * PSIDE
-CAP = 2
 
 HALF = TAPS // 2
 WARP = 3
@@ -32,6 +31,7 @@
 HALVES = 2
 ROWS = BLOCK // HALVES
 MATCH = ROWS + 8
+SHARED = 2
 LABEL = 16
 F32 = jnp.float32
 BF16 = jnp.bfloat16
@@ -72,7 +72,19 @@
     return lane % LANES * LANE_BLOCKS + lane // LANES
 
 
-def prepare_kernel(place, taps, psf, affine, level_out, slope_out, rows_out, cols_out):
+def prepare_kernel(
+    place, taps_in, psf_in, affine_in, level_out, slope_out, rows_out, cols_out,
+    taps, psf, affine, sems,
+):
+    copies = [
+        pltpu.make_async_copy(taps_in, taps, sems.at[0]),
+        pltpu.make_async_copy(psf_in.at[pl.ds(place[0], 1)], psf, sems.at[1]),
+        pltpu.make_async_copy(affine_in, affine, sems.at[2]),
+    ]
+    for copy in copies:
+        copy.start()
+    for copy in copies:
+        copy.wait()
     lane = iota((1, BAND), 1)
     seg = lane // STEP
     tap = lane - seg * STEP
@@ -154,16 +166,18 @@
         grid_spec=pltpu.PrefetchScalarGridSpec(
             num_scalar_prefetch=1,
             grid=(1,),
-            in_specs=[
-                pl.BlockSpec((NBASIS, 2, TAPS), lambda i, place: (0, 0, 0)),
-                pl.BlockSpec((1, 3, V, NBASIS), lambda i, place: (place[0], 0, 0, 0)),
-                pl.BlockSpec((V, 2, 2, ccds), lambda i, place: (0, 0, 0, 0)),
-            ],
+            in_specs=[pl.BlockSpec(memory_space=pltpu.HBM)] * 3,
             out_specs=[
                 pl.BlockSpec((V, 2, TAPS * STRIP, LANES), lambda i, place: (0, 0, 0, 0)),
                 pl.BlockSpec((V, TAPS * STRIP, BAND - LANES), lambda i, place: (0, 0, 0)),
                 pl.BlockSpec((V, BLOCK, 256), lambda i, place: (0, 0, 0)),
                 pl.BlockSpec((V, 8, WIDTH), lambda i, place: (0, 0, 0)),
+            ],
+            scratch_shapes=[
+                pltpu.VMEM((NBASIS, 2, TAPS), F32),
+                pltpu.VMEM((1, 3, V, NBASIS), F32),
+                pltpu.VMEM((V, 2, 2, ccds), F32),
+                pltpu.SemaphoreType.DMA((3,)),
             ],
         ),
         out_shape=[
@@ -184,8 +198,8 @@
 
 def warp_kernel(
     place, patch, slot, owner, weight, level, slope, row_weights, col_weights, sort, unsort,
-    image, above, below, out,
-    terms, ready, seen, label, label_ready, sem, label_sem,
+    image, above, below, first_out, shared_out, rest_out,
+    terms, ready, seen, order, label, sem, label_sem,
 ):
     visit = pl.program_id(0)
     visits = pl.num_programs(0)
@@ -294,28 +308,55 @@
             return 0
 
         lax.fori_loop(0, owner.shape[0], clear, 0)
-        label[...] = jnp.zeros_like(label)
+        order[V * BLKC] = 0
 
     for j in range(BLKC):
         block = visit * BLKC + j
         ready[block] = result[:, j * BLOCK : (j + 1) * BLOCK]
         p = patch[0, block]
-        rank = seen[p]
-        seen[p] = rank + 1
-        to = out.at[owner[p], pl.ds(pl.multiple_of(rank * BLOCK, BLOCK), BLOCK)]
-        pltpu.make_async_copy(ready.at[block], to, sem.at[block]).start()
-        at = rank * 2
-        label[owner[p], pl.ds(at, 1), :] = jnp.full((1, BLOCK), weight[visit, place[0]], F32)
-        label[owner[p], pl.ds(at + 1, 1), :] = jnp.full((1, BLOCK), slot[0, block].astype(F32), F32)
+        again = seen[p] > 0
+        place_in_rest = order[V * BLKC]
+        seen[p] = 1
+        order[block] = jnp.where(again, place_in_rest + 1, 0)
+        order[V * BLKC] = place_in_rest + again.astype(jnp.int32)
+        share = again & (place_in_rest < SHARED)
+
+        def send(to):
+            pltpu.make_async_copy(ready.at[block], to, sem.at[block]).start()
+
+        @pl.when(jnp.logical_not(again))
+        def _():
+            send(first_out.at[owner[p]])
+
+        @pl.when(share)
+        def _():
+            send(shared_out.at[0, pl.ds(pl.multiple_of(place_in_rest * BLOCK, BLOCK), BLOCK)])
+
+        @pl.when(again & jnp.logical_not(share))
+        def _():
+            send(rest_out.at[owner[p]])
 
     @pl.when(visit == visits - 1)
     def _():
-        label_ready[...] = label[...].astype(BF16)
-        copy = pltpu.make_async_copy(label_ready, out.at[:, pl.ds(CAP * BLOCK, LABEL)], label_sem)
+        lane = iota((1, LANES), 1)
+        blocks = V * BLKC
+        row = jnp.zeros((1, LANES), F32)
+        ccd = iota(weight.shape, 1) == place[0]
+        own = jnp.sum(jnp.where(ccd, weight[...].astype(F32), 0.0), axis=1, keepdims=True)
+        for e in range(blocks):
+            row = jnp.where(lane == e, patch[0, e].astype(F32), row)
+            row = jnp.where(lane == blocks + e, slot[0, e].astype(F32), row)
+            row = jnp.where(lane == 2 * blocks + e, own[e // BLKC : e // BLKC + 1], row)
+            row = jnp.where(lane == 3 * blocks + e, order[e].astype(F32), row)
+        row = jnp.where(lane == 4 * blocks, order[blocks].astype(F32), row)
+        label[...] = jnp.broadcast_to(row, (LABEL, LANES)).astype(BF16)
+        copy = pltpu.make_async_copy(
+            label, shared_out.at[0, pl.ds(SHARED * BLOCK, LABEL)], label_sem
+        )
         copy.start()
         copy.wait()
-        for block in range(V * BLKC):
-            pltpu.make_async_copy(ready.at[block], out.at[0, pl.ds(0, BLOCK)], sem.at[block]).wait()
+        for block in range(blocks):
+            pltpu.make_async_copy(ready.at[block], first_out.at[0], sem.at[block]).wait()
 
 
 def warp(place, patch, slot, owner, weight, ready, images, above, below, devices):
@@ -331,7 +372,7 @@
                 smem,
                 smem,
                 smem,
-                smem,
+                pl.BlockSpec(weight.shape, lambda v, place: (0, 0)),
                 pl.BlockSpec((1, 2, TAPS * STRIP, LANES), lambda v, place: (v, 0, 0, 0)),
                 pl.BlockSpec((1, TAPS * STRIP, BAND - LANES), lambda v, place: (v, 0, 0)),
                 pl.BlockSpec((1, BLOCK, 256), lambda v, place: (v, 0, 0)),
@@ -342,18 +383,22 @@
                 pl.BlockSpec((1, RIM, WIDTH), lambda v, place: (v, 0, 0)),
                 pl.BlockSpec((1, RIM, WIDTH), lambda v, place: (v, 0, 0)),
             ],
-            out_specs=pl.BlockSpec(memory_space=pl.ANY),
+            out_specs=[pl.BlockSpec(memory_space=pl.ANY)] * 3,
             scratch_shapes=[
                 pltpu.VMEM((4, TALL, WIDTH), BF16),
                 pltpu.VMEM((V * BLKC, BLOCK, BLOCK), BF16),
                 pltpu.SMEM((owner.shape[0],), jnp.int32),
-                pltpu.VMEM((devices, LABEL, BLOCK), F32),
-                pltpu.VMEM((devices, LABEL, BLOCK), BF16),
+                pltpu.SMEM((V * BLKC + 1,), jnp.int32),
+                pltpu.VMEM((LABEL, LANES), BF16),
                 pltpu.SemaphoreType.DMA((V * BLKC,)),
                 pltpu.SemaphoreType.DMA(()),
             ],
         ),
-        out_shape=jax.ShapeDtypeStruct((devices, CAP * BLOCK + LABEL, BLOCK), BF16),
+        out_shape=[
+            jax.ShapeDtypeStruct((devices, BLOCK, BLOCK), BF16),
+            jax.ShapeDtypeStruct((1, SHARED * BLOCK + LABEL, BLOCK), BF16),
+            jax.ShapeDtypeStruct((devices, BLOCK, BLOCK), BF16),
+        ],
         compiler_params=pltpu.CompilerParams(vmem_limit_bytes=32 << 20),
         cost_estimate=pl.CostEstimate(
             flops=V * 2 * STRIPS * TAPS * STRIP * BAND * WIDTH,
@@ -367,44 +412,89 @@
     )
 
 
-def coadd_kernel(labels, got, out, sums):
+def coadd_kernel(place, owner, first, shared, *refs):
+    rest = refs[0] if len(refs) == 6 else None
+    out, table, numbers, sums, sem = refs[-5:]
+    devices = first.shape[0]
+    me = place[4]
+
+    def find(p, mine):
+        return jnp.where(owner[p] == me, p, mine)
+
+    mine = lax.fori_loop(0, owner.shape[0], find, 0)
+
+    blocks = V * BLKC
+    label = shared[:, SHARED * BLOCK : SHARED * BLOCK + LABEL].astype(F32)[:, 0]
+    lane = iota(label.shape, 1)
+    slots, weights, orders = (pltpu.roll(label, LANES - k * blocks, 1) for k in (1, 2, 3))
+    match = (lane < blocks) & (label == mine.astype(F32))
+    one = match & (orders == 0.0)
+    two = match & (orders > 0.0)
+    found = jnp.zeros_like(label)
+    for k, (which, value) in enumerate(
+        ((one, weights), (one, slots), (two, weights), (two, slots), (two, orders))
+    ):
+        column = jnp.sum(jnp.where(which, value, 0.0), axis=1, keepdims=True)
+        found = jnp.where(lane == k, column, found)
+    table[...] = found
+    copy = pltpu.make_async_copy(table, numbers, sem)
+    copy.start()
     out[...] = jnp.zeros_like(out)
     for c in range(CELLS):
         sums[c] = 0.0
-
-    def add(k, _):
-        source, rank = k // CAP, k % CAP
-        weight = labels[source, rank * 2]
-
-        @pl.when(weight > 0.0)
+    copy.wait()
+
+    def add(weight, cell, block):
+        c = cell.astype(jnp.int32)
+        sums[c] += weight
+        lanes = pl.ds(pl.multiple_of(c % PSIDE * BLOCK, BLOCK), BLOCK)
+        out[c // PSIDE, :, lanes] += weight * block.astype(F32)
+
+    def source(s, _):
+        @pl.when(numbers[s, 0] > 0.0)
         def _():
-            c = labels[source, rank * 2 + 1].astype(jnp.int32)
-            sums[c] += weight
-            lanes = pl.ds(pl.multiple_of(c % PSIDE * BLOCK, BLOCK), BLOCK)
-            rows = pl.ds(pl.multiple_of(rank * BLOCK, BLOCK), BLOCK)
-            out[c // PSIDE, :, lanes] += weight * got[source, rows].astype(F32)
+            add(numbers[s, 0], numbers[s, 1], first[s])
+
+        second = numbers[s, 4].astype(jnp.int32) - 1
+
+        @pl.when((second >= 0) & (second < SHARED))
+        def _():
+            rows = pl.ds(pl.multiple_of(second * BLOCK, BLOCK), BLOCK)
+            add(numbers[s, 2], numbers[s, 3], shared[s, rows])
+
+        if rest is not None:
+
+            @pl.when(second >= SHARED)
+            def _():
+                add(numbers[s, 2], numbers[s, 3], rest[s])
 
         return 0
 
-    lax.fori_loop(0, got.shape[0] * CAP, add, 0)
+    lax.fori_loop(0, devices, source, 0)
     for c in range(CELLS):
         lanes = slice(c % PSIDE * BLOCK, (c % PSIDE + 1) * BLOCK)
         inverse = 1.0 / jnp.maximum(jnp.full((1, BLOCK), sums[c], F32), 1.0)
         out[c // PSIDE, :, lanes] = out[c // PSIDE, :, lanes] * inverse
 
 
-def coadd(labels, got):
+def coadd(place, owner, *got):
     smem = pl.BlockSpec(memory_space=pltpu.SMEM)
+    devices = got[0].shape[0]
     return pl.pallas_call(
         coadd_kernel,
         grid=(1,),
-        in_specs=[smem, pl.BlockSpec((got.shape[0], CAP * BLOCK, BLOCK), lambda i: (0, 0, 0))],
+        in_specs=[smem, smem] + [pl.BlockSpec(x.shape, lambda i: (0, 0, 0)) for x in got],
         out_specs=pl.BlockSpec((PSIDE, BLOCK, WIDTH), lambda i: (0, 0, 0)),
         out_shape=jax.ShapeDtypeStruct((PSIDE, BLOCK, PSIDE * BLOCK), F32),
-        scratch_shapes=[pltpu.SMEM((CELLS,), F32)],
+        scratch_shapes=[
+            pltpu.VMEM((devices, LANES), F32),
+            pltpu.SMEM((devices, LANES), F32),
+            pltpu.SMEM((CELLS,), F32),
+            pltpu.SemaphoreType.DMA(()),
+        ],
         compiler_params=pltpu.CompilerParams(vmem_limit_bytes=32 << 20),
-        name="coadd",
-    )(labels, got)
+        name="coadd_" + str(len(got)),
+    )(place, owner, *got)
 
 
 def shards(
@@ -428,14 +518,22 @@
     above = lax.ppermute(images[:, BLOCK - RIM :], "ccd", down)
     below = lax.ppermute(images[:, :RIM], "ccd", up)
     patch = block_patch[:, :, 0]
-    weight = visit_weight.astype(F32)
     ready = prepare(place, basis_taps, psf_coef, affine)
-    sent = warp(
-        place, patch, block_slot, patch_owner, weight, ready, images, above, below, devices
-    )
-    got = lax.all_to_all(sent, "ccd", split_axis=0, concat_axis=0, tiled=True)
-    labels = got[:, CAP * BLOCK : CAP * BLOCK + 2 * CAP, 0].astype(F32)
-    result = coadd(labels, got)
+    first, shared, rest = warp(
+        place, patch, block_slot, patch_owner, visit_weight, ready, images, above, below, devices
+    )
+    shared = lax.all_gather(shared, "ccd", axis=0, tiled=True)
+    first = lax.all_to_all(first, "ccd", split_axis=0, concat_axis=0, tiled=True)
+    seconds = jnp.max(shared[:, SHARED * BLOCK, 4 * V * BLKC])
+
+    def more(first, shared, rest):
+        rest = lax.all_to_all(rest, "ccd", split_axis=0, concat_axis=0, tiled=True)
+        return coadd(place, patch_owner, first, shared, rest)
+
+    def all_here(first, shared, rest):
+        return coadd(place, patch_owner, first, shared)
+
+    result = lax.cond(seconds > SHARED, more, all_here, first, shared, rest)
     return result.reshape(1, PSIDE * BLOCK, PSIDE * BLOCK)
 
 

time: 58.3 us -> 81.5 us (1.40)
  blocking collectives: 36.3 us -> 0 us
  waiting for transfers between devices: 0.01 us -> 35.6 us
  between operations: 0.15 us -> 14.2 us
  starting transfers between devices: 4.33 us -> 12.3 us
    all_to_all x1 -> x0, blocking collectives: 36.3 us -> none  [shards(): got = lax.all_to_all(sent, 'ccd', split_axis=0, concat_axis=0, tiled=True)]
    all_gather x0 -> x1, waiting for transfers between devices: none -> 35.5 us  [shards(): shared = lax.all_gather(shared, 'ccd', axis=0, tiled=True)]
    all_to_all x0 -> x1, starting transfers between devices: none -> 8 us  [shards(): lax.all_to_all(first, 'ccd', split_axis=0, concat_axis=0, tiled=True)]
    reduce_max x0 -> x1, other arithmetic: none -> 1.47 us  [shards(): seconds = jnp.max(shared[:, SHARED * BLOCK, 4 * V * BLKC])]
    unnamed x18 -> x22, local copies, waits for them, and re-layouts: 2.18 us -> 3.15 us
  transfers between devices with their start and end apart: 2 -> 4, of which waited for: 0 -> 1; matrix products, arithmetic and copies ran while one was open for 1% -> 2% of each run, Pallas kernels for 3% -> 3%
where the time goes in v3:
time: 81.5 us; the launch traced here: 80.9 us
  waiting for transfers between devices  35.6 us (44%)
  between operations  14.2 us (17%)
  Pallas kernels  13.2 us (16%)
  starting transfers between devices  12.3 us (15%)
  local copies, waits for them, and re-layouts  4.11 us (5%)
  other arithmetic  1.47 us (2%)
    all_gather x1, waiting for transfers between devices, shards(): shared = lax.all_gather(shared, 'ccd', axis=0, tiled=True)  35.5 us
    pallas_call x1, Pallas kernels, warp(): pl.pallas_call(warp_kernel, grid_spec=pltpu.PrefetchScalarGridSpec(num_sc...  8.06 us
    all_to_all x1, starting transfers between devices, shards(): lax.all_to_all(first, 'ccd', split_axis=0, concat_axis=0, tiled=True)  8 us
    unnamed x22, local copies, waits for them, and re-layouts  3.15 us
    pallas_call x1, Pallas kernels, coadd(): pl.pallas_call(coadd_kernel, grid=(1,), in_specs=[smem, smem] + [pl.Block...  3.09 us
    ppermute x1, starting transfers between devices, shards(): above = lax.ppermute(images[:, BLOCK - RIM:], 'ccd', down)  3.03 us
    pallas_call x1, Pallas kernels, prepare(): pl.pallas_call(prepare_kernel, grid_spec=pltpu.PrefetchScalarGridSpec(num...  2.06 us
  transfers between devices with their start and end apart: 4, of which 1 were waited for; matrix products, arithmetic and copies ran while one was open for 2% of the time, Pallas kernels for 3%

profile of v3, /device:TPU:0, one launch (start us, length us, event | category | flops | bytes accessed | tf_op | source)
XLA Modules:
  0.0 80.9 jit_solution(66441434554407251)
XLA Ops:
  6.5 0.0 all-gather.2.cloned.1.call-start
  6.5 0.9 %fusion = (f32[4,8,512]{2,1,0:T(8,128)S(1)}, f32[4,8,512]{2,1,0:T(8,128)S(1)}) fusion(f32[4,128,512]{2,1,0:T(8,128)} %image.1), kind=kLoop, calls=%fused_computation.1 | loop fusion | bytes 262144 | tf_op jit(solution)/shard_map/slice | solution.py:519
  7.4 1.3 %collective-permute-start.1 = (f32[4,8,512]{2,1,0:T(8,128)S(1)}, f32[4,8,512]{2,1,0:T(8,128)S(1)}, u32[]{:S(2)}, u32[]{:S(2)}) collective-permute-start(f32[4,8,512]{2,1,0:T(8,128)S(1)} %get-tuple-element.51), channel_id=1, source_target_pairs={{1,0},{2,1},{3,2},{4,3},{5,4},{6,5},{7,6},{8,7},{9,8},{10,9},{11,1... | collective-permute-start | bytes 196616 | tf_op jit(solution)/shard_map/ppermute | solution.py:519
  8.7 3.0 %collective-permute-start = (f32[4,8,512]{2,1,0:T(8,128)S(1)}, f32[4,8,512]{2,1,0:T(8,128)S(1)}, u32[]{:S(2)}, u32[]{:S(2)}) collective-permute-start(f32[4,8,512]{2,1,0:T(8,128)S(1)} %get-tuple-element.52), channel_id=1, source_target_pairs={{0,1},{1,2},{2,3},{3,4},{4,5},{5,6},{6,7},{7,8},{8,9},{9,10},{10,1... | collective-permute-start | bytes 196616 | tf_op jit(solution)/shard_map/ppermute | solution.py:518
  11.8 0.1 stack.31.place
  11.9 0.0 copy-start.1
  11.9 0.8 copy-done.1
  12.6 0.7 copy-done.2
  13.3 0.7 copy-done.3
  14.0 0.0 copy-start.7
  14.0 0.0 copy-start.8
  14.1 0.0 copy-start.10
  14.1 2.1 %prepare.1 = (f32[4,2,176,128]{3,2,1,0:T(8,128)S(1)}, bf16[4,176,128]{2,1,0:T(8,128)(2,1)S(1)}, bf16[4,128,256]{2,1,0:T(8,128)(2,1)S(1)}, f32[4,8,512]{2,1,0:T(8,128)S(1)}) custom-call(s32[5]{0:T(128)S(1)} %stack.31.place, f32[9,2,11]{2,1,0:T(2,128)S(1)} %bitcast.12, f32[5,3,4,9]{3,2,1,0:T(4,128)S(1)} %bitcast.11, f32[4,2,2,5]{3,2,1,0:T(2,128)S(1)} %bitcast.13), custom_call_target="tpu_custom_call" | custom-call | flops 1073741824 | bytes 1048576 | tf_op jit(solution)/shard_map/prepare/pallas_call | solution.py:164
  16.1 0.0 collective-permute-done.1.below
  16.1 0.0 collective-permute-done.above
  16.2 0.0 copy-done
  16.2 0.0 copy-done.4
  16.2 0.0 copy-done.5
  16.2 0.0 copy-done.6
  16.2 0.0 copy-done.7
  16.2 0.0 copy-done.8
  16.2 0.0 copy-done.10
  16.2 8.1 %match_warp.1 = (bf16[16,128,128]{2,1,0:T(8,128)(2,1)}, bf16[1,272,128]{2,1,0:T(8,128)(2,1)}, bf16[16,128,128]{2,1,0:T(8,128)(2,1)S(1)}) custom-call(s32[5]{0:T(128)S(1)} %stack.31.place, s32[1,16]{1,0:T(1,128)S(1)} %bitcast.14, s32[1,16]{1,0:T(1,128)S(1)} %copy-done.6, s32[16]{0:T(128)S(1)} %copy-done.10, bf16[4,5]{1,0:T(4,128)(2,1)S(1)} %copy-done.4, ...), custom_call_target="tpu_custom_call" | custom-call | flops 1660944384 | bytes 1572864 | tf_op jit(solution)/shard_map/match_warp/pallas_call | solution.py:366
  24.3 0.0 all-gather.2.cloned.1.call-update
  24.3 8.0 %all-to-all-start.1 = ((bf16[16,128,128]{2,1,0:T(8,128)(2,1)}), bf16[16,128,128]{2,1,0:T(8,128)(2,1)S(1)}, u32[]{:S(2)}, u32[]{:S(2)}) async-start(bf16[16,128,128]{2,1,0:T(8,128)(2,1)} %get-tuple-element.48), calls=%async_computation.1 | async-start | bytes 1048576 | tf_op jit(solution)/shard_map/all_to_all | solution.py:526
  32.3 35.5 %all-gather.2.cloned.1.call-done = bf16[16,272,128]{2,1,0:T(8,128)(2,1)} async-done(((bf16[1,272,128]{2,1,0:T(8,128)(2,1)}), bf16[16,272,128]{2,1,0:T(8,128)(2,1)}) %all-gather.2.cloned.1.call-update) | async-done | bytes 1114128 | tf_op jit(solution)/shard_map/all_gather | solution.py:525
  67.9 1.5 %slice_reduce_fusion = bf16[]{:T(256)} fusion(bf16[16,272,128]{2,1,0:T(8,128)(2,1)} %all-gather.2.cloned.1.call-done), kind=kLoop, calls=%fused_computation | loop fusion | flops 15 | bytes 34 | tf_op jit(solution)/shard_map/reduce_max | solution.py:527
  69.9 0.0 all-to-all-done.1
  70.0 3.1 %conditional.1 = (f32[1,512,512]{2,1,0:T(8,128)S(1)}) conditional(s32[]{:T(128)} %convert_element_type.2, (s32[5]{0:T(128)S(1)}, s32[16]{0:T(128)S(1)}, bf16[16,128,128]{2,1,0:T(8,128)(2,1)S(1)}, bf16[16,272,128]{2,1,0:T(8,128)(2,1)}) %tuple.23, (bf16[16,128,128]{2,1,0:T(8,128)(2,1)S(1)}, s32[5]{0:T(128)S(1)}, s32[16]{0:T(128)S(1)}, ...), branch_computations={%region_1.2_spmd, %region_2.3_spmd} | conditional | bytes 1048584 | solution.py:536
  70.0 3.1 %coadd_2.1 = f32[4,128,512]{2,1,0:T(8,128)S(1)} custom-call(s32[5]{0:T(128)S(1)} %get-tuple-element.27.place, s32[16]{0:T(128)S(1)} %get-tuple-element.28.owner, bf16[16,128,128]{2,1,0:T(8,128)(2,1)S(1)} %get-tuple-element.29.first, bf16[16,272,128]{2,1,0:T(8,128)(2,1)} %get-tuple-element.30.shared), custom_call_target="tpu_custom_call" | custom-call | tf_op jit(solution)/shard_map/cond/branch_0_fun/coadd_2/pallas_call | solution.py:483
  73.1 0.0 copy-start.9
  73.1 1.0 %copy-done.9 = f32[1,512,512]{2,1,0:T(8,128)} copy-done((f32[1,512,512]{2,1,0:T(8,128)}, f32[1,512,512]{2,1,0:T(8,128)S(1)}, u32[]{:S(2)}) %copy-start.9) | copy-done | bytes 1048600
  (6 shorter events, 0.0 us)
Async XLA Ops:
  6.5 61.3 %all-gather.2.cloned.1.call-start = ((), (), s32[]{:S(2)}) async-start(), calls=%async_computation.2 | async-start | bytes 1183744 | tf_op jit(solution)/shard_map/all_gather | solution.py:525
  7.4 8.7 %collective-permute-start.1 = (f32[4,8,512]{2,1,0:T(8,128)S(1)}, f32[4,8,512]{2,1,0:T(8,128)S(1)}, u32[]{:S(2)}, u32[]{:S(2)}) collective-permute-start(f32[4,8,512]{2,1,0:T(8,128)S(1)} %get-tuple-element.51), channel_id=1, source_target_pairs={{1,0},{2,1},{3,2},{4,3},{5,4},{6,5},{7,6},{8,7},{9,8},{10,9},{11,1... | collective-permute-start | bytes 196616 | tf_op jit(solution)/shard_map/ppermute | solution.py:519
  8.7 7.4 %collective-permute-start = (f32[4,8,512]{2,1,0:T(8,128)S(1)}, f32[4,8,512]{2,1,0:T(8,128)S(1)}, u32[]{:S(2)}, u32[]{:S(2)}) collective-permute-start(f32[4,8,512]{2,1,0:T(8,128)S(1)} %get-tuple-element.52), channel_id=1, source_target_pairs={{0,1},{1,2},{2,3},{3,4},{4,5},{5,6},{6,7},{7,8},{8,9},{9,10},{10,1... | collective-permute-start | bytes 196616 | tf_op jit(solution)/shard_map/ppermute | solution.py:518
  11.9 0.8 copy-start.1
  12.6 0.7 copy-start.2
  13.3 0.7 copy-start.3
  14.0 2.1 %copy-start = (f32[4,128,512]{2,1,0:T(8,128)S(1)}, f32[4,128,512]{2,1,0:T(8,128)}, u32[]{:S(2)}) copy-start(f32[4,128,512]{2,1,0:T(8,128)} %image.1) | copy-start | bytes 3145732
  14.0 2.1 %copy-start.4 = (bf16[4,5]{1,0:T(4,128)(2,1)S(1)}, bf16[4,5]{1,0:T(4,128)(2,1)}, u32[]{:S(2)}) copy-start(bf16[4,5]{1,0:T(4,128)(2,1)} %weight.1) | copy-start | bytes 124
  14.0 2.2 %copy-start.5 = (s32[1,16,1]{1,2,0:T(1,128)S(1)}, s32[1,16,1]{1,2,0:T(1,128)}, u32[]{:S(2)}) copy-start(s32[1,16,1]{1,2,0:T(1,128)} %param.17) | copy-start | bytes 196
  14.0 2.2 %copy-start.6 = (s32[1,16]{1,0:T(1,128)S(1)}, s32[1,16]{1,0:T(1,128)}, u32[]{:S(2)}) copy-start(s32[1,16]{1,0:T(1,128)} %slot.1) | copy-start | bytes 196
  14.0 2.2 %copy-start.7 = (bf16[512,512]{1,0:T(8,128)(2,1)S(1)}, bf16[512,512]{1,0:T(8,128)(2,1)}, u32[]{:S(2)}) copy-start(bf16[512,512]{1,0:T(8,128)(2,1)} %constant.46.clone.unsort) | copy-start | bytes 1572868
  14.0 2.2 %copy-start.8 = (bf16[512,512]{1,0:T(8,128)(2,1)S(1)}, bf16[512,512]{1,0:T(8,128)(2,1)}, u32[]{:S(2)}) copy-start(bf16[512,512]{1,0:T(8,128)(2,1)} %constant.45.clone.sort) | copy-start | bytes 1572868
  14.1 2.2 %copy-start.10 = (s32[16]{0:T(128)S(1)}, s32[16]{0:T(128)}, u32[]{:S(2)}) copy-start(s32[16]{0:T(128)} %owner.1) | copy-start | bytes 196
  24.3 45.6 %all-to-all-start.1 = ((bf16[16,128,128]{2,1,0:T(8,128)(2,1)}), bf16[16,128,128]{2,1,0:T(8,128)(2,1)S(1)}, u32[]{:S(2)}, u32[]{:S(2)}) async-start(bf16[16,128,128]{2,1,0:T(8,128)(2,1)} %get-tuple-element.48), calls=%async_computation.1 | async-start | bytes 1048576 | tf_op jit(solution)/shard_map/all_to_all | solution.py:526
  73.1 1.0 %copy-start.9 = (f32[1,512,512]{2,1,0:T(8,128)}, f32[1,512,512]{2,1,0:T(8,128)S(1)}, u32[]{:S(2)}) copy-start(f32[1,512,512]{2,1,0:T(8,128)S(1)} %get-tuple-element.60) | copy-start | bytes 3145732
Sparse Core Ops, SparseCore 0:
  24.4 43.3 all-gather.1

commit v4 on v2

v4 whole, which is shorter than its diff:
```python
import jax
import jax.numpy as jnp
import numpy as np
from jax import lax
from jax.experimental import pallas as pl
from jax.experimental.pallas import tpu as pltpu
from jax.sharding import PartitionSpec as P

V = 4
BLOCK = 128
BLKC = 4
SPLIT = 4
TAPS = 11
NBASIS = 9
PSIDE = 4
CELLS = PSIDE * PSIDE
CAP = 2

HALF = TAPS // 2
WARP = 3
RIM = HALF + WARP
HEIGHT = SPLIT * BLOCK
WIDTH = BLKC * BLOCK
LANES = 128
LANE_BLOCKS = WIDTH // LANES
STRIP = 16
STEP = 32
STRIPS = -(-(BLOCK + 2 * WARP) // STRIP)
GROUPS = 6
BAND = 256
TALL = (STRIPS - 1) * STRIP + STEP
HALVES = 2
TOGETHER = 2
ROWS = BLOCK // HALVES
MATCH = ROWS + 8
LABEL = 16
F32 = jnp.float32
BF16 = jnp.bfloat16


def sin_pi(t):
    whole = jnp.round(t)
    f = t - whole
    odd = whole - 2.0 * jnp.floor(0.5 * whole)
    f2 = f * f
    out = 0.0
    for c in (
        0.00046630280576761, -0.0073704309457144, 0.0821458866111282,
        -0.599264529320792, 2.55016403987734, -5.16771278004997, 3.14159265358979,
    ):
        out = out * f2 + c
    return f * out * (1.0 - 2.0 * odd)


def lanczos(t):
    zero = t == 0.0
    safe = jnp.where(zero, 1.0, t)
    pt = jnp.pi * safe
    value = 3.0 * sin_pi(safe) * sin_pi(safe / 3.0) / (pt * pt)
    return jnp.where(jnp.abs(t) < 3.0, jnp.where(zero, 1.0, value), 0.0)


def iota(shape, dim):
    return lax.broadcasted_iota(jnp.int32, shape, dim)


def deinterleave():
    order = np.arange(WIDTH).reshape(LANES, LANE_BLOCKS).T.reshape(-1)
    return (np.arange(WIDTH)[:, None] == order[None, :]).astype(np.float32)


def column_at(lane):
    return lane % LANES * LANE_BLOCKS + lane // LANES


def prepare_kernel(
    place, taps_in, psf_in, affine_in, level_out, slope_out, rows_out, cols_out,
    taps, psf, affine, sems,
):
    copies = [
        pltpu.make_async_copy(taps_in, taps, sems.at[0]),
        pltpu.make_async_copy(psf_in.at[pl.ds(place[0], 1)], psf, sems.at[1]),
        pltpu.make_async_copy(affine_in, affine, sems.at[2]),
    ]
    for copy in copies:
        copy.start()
    for copy in copies:
        copy.wait()
    lane = iota((1, BAND), 1)
    seg = lane // STEP
    tap = lane - seg * STEP
    row_taps, col_taps = taps[:, 0], taps[:, 1]
    onehot = (tap == iota((TAPS, BAND), 0)) & (seg < GROUPS)
    r = jnp.dot(
        row_taps, onehot.astype(F32),
        precision=lax.Precision.HIGHEST, preferred_element_type=F32,
    )
    is_level = seg < 3
    low_lanes = seg % 3 == 2
    ccd_lane = iota((1, 1, affine.shape[3]), 2) == place[0]

    turned = lax.dot_general(
        (iota((TAPS, STRIP), 0) == iota((TAPS, STRIP), 1)).astype(F32), col_taps,
        (((0,), (1,)), ((), ())),
        precision=lax.Precision.HIGHEST, preferred_element_type=F32,
    )
    kernels = jnp.dot(
        jnp.concatenate(
            [turned * psf[0, c, v : v + 1, :] for v in range(V) for c in range(3)], axis=0
        ),
        r, precision=lax.Precision.HIGHEST, preferred_element_type=F32,
    )

    col_move = (iota((STRIP, 1), 0) - HALF).astype(F32) * (2.0 / WIDTH)
    for visit in range(V):
        const, by_row, by_col = (
            kernels[(visit * 3 + c) * STRIP : (visit * 3 + c + 1) * STRIP] for c in range(3)
        )
        const = jnp.where(is_level, const - col_move * by_col, by_col)
        by_row = jnp.where(is_level, by_row, 0.0)
        for u in range(TAPS):
            x = jnp.broadcast_to(const[u : u + 1], (8, BAND))
            x = pltpu.roll(x, 0, 1, stride=1, stride_axis=0)
            x = jnp.concatenate([x, pltpu.roll(x, 8, 1)], axis=0)
            y = jnp.broadcast_to(by_row[u : u + 1, :LANES], (8, LANES))
            y = pltpu.roll(y, 0, 1, stride=1, stride_axis=0)
            y = jnp.concatenate([y, pltpu.roll(y, 8, 1)], axis=0)
            at = slice(u * STRIP, (u + 1) * STRIP)
            level_out[visit, 0, at] = x[:, :LANES]
            level_out[visit, 1, at] = y
            high = x.astype(BF16).astype(F32)
            slope_out[visit, at] = jnp.where(low_lanes, x - high, high)[:, LANES:].astype(BF16)

        a = jnp.sum(jnp.where(ccd_lane, affine[visit], 0.0), axis=2, keepdims=True)
        out_row = iota((BLOCK, LANES), 0)
        local = out_row % ROWS
        in_row = iota((BLOCK, LANES), 1)
        row = (place[1] + out_row).astype(F32)
        shift = a[0, 0:1] + a[0, 1:2] * (row - (HEIGHT - 1) / 2.0) / HEIGHT
        step = in_row - local - WARP
        band_row = out_row + step
        keep = jnp.abs(step) <= WARP
        keep = keep & ((band_row >= 0) | (place[2] > 0)) & ((band_row < BLOCK) | (place[3] > 0))
        weights = jnp.where(keep, lanczos(shift - step.astype(F32)), 0.0)
        high = weights.astype(BF16).astype(F32)
        zero = jnp.zeros_like(weights)
        wide = jnp.concatenate([high, zero], axis=1)
        low = jnp.concatenate([weights - high, zero], axis=1)
        wide = wide + pltpu.roll(wide, MATCH, 1) + pltpu.roll(low, 2 * MATCH, 1)
        rows_out[visit] = wide.astype(BF16)

        lanes = iota((8, WIDTH), 1)
        offset = iota((8, WIDTH), 0) - WARP
        block = lanes // LANES
        carry = (block + offset + LANE_BLOCKS) // LANE_BLOCKS - 1
        from_lane = lanes % LANES - carry
        col = (from_lane * LANE_BLOCKS + block).astype(F32)
        col_shift = a[1, 0:1] + a[1, 1:2] * (col - (WIDTH - 1) / 2.0) / WIDTH
        within = (from_lane >= 0) & (from_lane < LANES) & (offset <= WARP)
        cols_out[visit] = jnp.where(within, lanczos(col_shift - offset.astype(F32)), 0.0)


def prepare(place, taps, psf, affine):
    ccds = affine.shape[1]
    return pl.pallas_call(
        prepare_kernel,
        grid_spec=pltpu.PrefetchScalarGridSpec(
            num_scalar_prefetch=1,
            grid=(1,),
            in_specs=[pl.BlockSpec(memory_space=pl.ANY)] * 3,
            out_specs=[
                pl.BlockSpec((V, 2, TAPS * STRIP, LANES), lambda i, place: (0, 0, 0, 0)),
                pl.BlockSpec((V, TAPS * STRIP, BAND - LANES), lambda i, place: (0, 0, 0)),
                pl.BlockSpec((V, BLOCK, 256), lambda i, place: (0, 0, 0)),
                pl.BlockSpec((V, 8, WIDTH), lambda i, place: (0, 0, 0)),
            ],
            scratch_shapes=[
                pltpu.VMEM((NBASIS, 2, TAPS), F32),
                pltpu.VMEM((1, 3, V, NBASIS), F32),
                pltpu.VMEM((V, 2, 2, ccds), F32),
                pltpu.SemaphoreType.DMA((3,)),
            ],
        ),
        out_shape=[
            jax.ShapeDtypeStruct((V, 2, TAPS * STRIP, LANES), F32),
            jax.ShapeDtypeStruct((V, TAPS * STRIP, BAND - LANES), BF16),
            jax.ShapeDtypeStruct((V, BLOCK, 256), BF16),
            jax.ShapeDtypeStruct((V, 8, WIDTH), F32),
        ],
        cost_estimate=pl.CostEstimate(flops=1 << 30, bytes_accessed=1 << 20, transcendentals=0),
        name="prepare",
    )(place, taps.transpose(1, 0, 2), psf.transpose(1, 3, 0, 2), affine.transpose(0, 2, 3, 1))


def lane_block(x, v):
    return x[:, v * LANES : (v + 1) * LANES]


def match(columns_of, level, slope, top_row):
    lane = iota((1, LANES), 1)
    low_lanes = (lane // STEP) % 3 == 2
    strip_row = (iota((TAPS * STRIP, 1), 0) % STRIP).astype(F32)

    def strip(k):
        match_row = (top_row + (k * STRIP - WARP)).astype(F32) + strip_row
        row_pos = (2.0 * match_row + 1.0) / HEIGHT - 1.0
        x = level[0] + row_pos * level[1]
        x = jnp.where(low_lanes, x - x.astype(BF16).astype(F32), x)
        matrix = jnp.concatenate([x.astype(BF16), slope], axis=1)
        taps = jnp.dot(matrix, columns_of(k), preferred_element_type=F32)
        out_blocks = []
        for v in range(LANE_BLOCKS):
            total = None
            for q in range(-(HALF // LANE_BLOCKS) - 1, HALF // LANE_BLOCKS + 2):
                part = None
                for u in range(TAPS):
                    if (v + u - HALF) // LANE_BLOCKS != q:
                        continue
                    w = (v + u - HALF) % LANE_BLOCKS
                    piece = lane_block(taps[u * STRIP : (u + 1) * STRIP], w)
                    part = piece if part is None else part + piece
                if part is None:
                    continue
                if q:
                    part = pltpu.roll(part, -q % LANES, 1)
                    part = jnp.where((lane + q >= 0) & (lane + q < LANES), part, 0.0)
                total = part if total is None else total + part
            out_blocks.append(total)
        return jnp.concatenate(out_blocks, axis=1)

    return strip


def warp_kernel(
    place, patch, slot, owner, weight, level, slope, row_weights, col_weights, sort_in, unsort_in,
    image, above, below, out,
    terms, ready, seen, label, label_ready, sort, unsort, sem, label_sem, sort_sem,
):
    step = pl.program_id(0)
    steps = pl.num_programs(0)
    top_row = place[1]
    tall = BLOCK + 2 * RIM
    sort_copy = pltpu.make_async_copy(sort_in, sort, sort_sem.at[0])
    unsort_copy = pltpu.make_async_copy(unsort_in, unsort, sort_sem.at[1])

    @pl.when(step == 0)
    def _():
        sort_copy.start()
        unsort_copy.start()
        terms[:, :, tall:] = jnp.zeros((TOGETHER, 4, TALL - tall, WIDTH), BF16)
        label[...] = jnp.zeros_like(label)

        def clear(p, _):
            seen[p] = 0
            return 0

        lax.fori_loop(0, owner.shape[0], clear, 0)
        sort_copy.wait()

    col_pos = (2.0 * column_at(iota((1, WIDTH), 1)).astype(F32) + 1.0) / WIDTH - 1.0
    for i in range(TOGETHER):
        raw = jnp.concatenate(
            [
                jnp.where(place[2] > 0, above[i], 0.0),
                image[i],
                jnp.where(place[3] > 0, below[i], 0.0),
            ],
            axis=0,
        )
        raw_high = raw.astype(BF16)
        raw_low = (raw - raw_high.astype(F32)).astype(BF16)
        sorted_terms = jnp.dot(
            jnp.concatenate([raw_high, raw_low], axis=0), sort[...], preferred_element_type=F32
        )
        high, low = sorted_terms[:tall], sorted_terms[tall:]
        tilted = (high + low) * col_pos
        tilted_high = tilted.astype(BF16)
        terms[i, 0, :tall] = high.astype(BF16)
        terms[i, 1, :tall] = low.astype(BF16)
        terms[i, 2, :tall] = tilted_high
        terms[i, 3, :tall] = (tilted - tilted_high.astype(F32)).astype(BF16)

    filler = jnp.zeros((BAND - GROUPS * STEP, WIDTH), BF16)

    def columns_of(i):
        def at(k):
            rows = slice(k * STRIP, k * STRIP + STEP)
            return jnp.concatenate([terms[i, h, rows] for h in (0, 1, 0, 2, 3, 2)] + [filler], axis=0)

        return at

    makers = [match(columns_of(i), level[i], slope[i], top_row) for i in range(TOGETHER)]
    strips = [[] for _ in makers]
    for k in range(STRIPS):
        for i, maker in enumerate(makers):
            strips[i].append(maker(k))

    empty = jnp.zeros((256 - 3 * MATCH, WIDTH), F32)
    warped = []
    for i in range(TOGETHER):
        matched = jnp.concatenate(strips[i], axis=0)
        high = matched.astype(BF16).astype(F32)
        low = matched - high
        halves = []
        for h in range(HALVES):
            rows = slice(h * ROWS, h * ROWS + MATCH)
            columns = jnp.concatenate([high[rows], low[rows], high[rows], empty], axis=0)
            halves.append(
                jnp.dot(
                    row_weights[i, h * ROWS : (h + 1) * ROWS], columns.astype(BF16),
                    preferred_element_type=F32,
                )
            )
        warped.append(jnp.concatenate(halves, axis=0))

    @pl.when(step == 0)
    def _():
        unsort_copy.wait()

    results = []
    for i in range(TOGETHER):
        col = col_weights[i]
        out_blocks = []
        for v in range(LANE_BLOCKS):
            total = None
            for q in (-1, 0, 1):
                part = None
                for s in range(2 * WARP + 1):
                    if (v + s - WARP) // LANE_BLOCKS != q:
                        continue
                    w = (v + s - WARP) % LANE_BLOCKS
                    piece = lane_block(col[s : s + 1], v) * lane_block(warped[i], w)
                    part = piece if part is None else part + piece
                if part is None:
                    continue
                if q:
                    part = pltpu.roll(part, -q % LANES, 1)
                total = part if total is None else total + part
            out_blocks.append(total.astype(BF16))
        results.append(
            jnp.dot(
                jnp.concatenate(out_blocks, axis=1), unsort[...], preferred_element_type=F32
            ).astype(BF16)
        )

    lane = iota((1, LANES), 1)
    ccd = iota(weight.shape, 1) == place[0]
    weights = jnp.sum(jnp.where(ccd, weight[...].astype(F32), 0.0), axis=1, keepdims=True)
    visits = iota((V, 1), 0)
    for i in range(TOGETHER):
        visit = step * TOGETHER + i
        own = jnp.sum(jnp.where(visits == visit, weights, 0.0), axis=0, keepdims=True)
        for j in range(BLKC):
            block = visit * BLKC + j
            ready[block] = results[i][:, j * BLOCK : (j + 1) * BLOCK]
            p = patch[0, block]
            rank = seen[p]
            seen[p] = rank + 1
            to = out.at[owner[p], pl.ds(pl.multiple_of(rank * BLOCK, BLOCK), BLOCK)]
            pltpu.make_async_copy(ready.at[block], to, sem.at[block]).start()
            row = label[pl.ds(owner[p], 1), :]
            row = jnp.where(lane == rank * 2, own, row)
            label[pl.ds(owner[p], 1), :] = jnp.where(
                lane == rank * 2 + 1, slot[0, block].astype(F32), row
            )

    @pl.when(step == steps - 1)
    def _():
        devices = label.shape[0]
        label_ready[...] = jnp.broadcast_to(
            label[...].reshape(devices, 1, LANES), (devices, LABEL, LANES)
        ).astype(BF16)
        copy = pltpu.make_async_copy(label_ready, out.at[:, pl.ds(CAP * BLOCK, LABEL)], label_sem)
        copy.start()
        copy.wait()
        for block in range(V * BLKC):
            pltpu.make_async_copy(ready.at[block], out.at[0, pl.ds(0, BLOCK)], sem.at[block]).wait()


def warp(place, patch, slot, owner, weight, ready, images, above, below, devices):
    smem = pl.BlockSpec(memory_space=pltpu.SMEM)
    hbm = pl.BlockSpec(memory_space=pl.ANY)
    sort = deinterleave()
    n = TOGETHER
    return pl.pallas_call(
        warp_kernel,
        grid_spec=pltpu.PrefetchScalarGridSpec(
            num_scalar_prefetch=1,
            grid=(V // n,),
            in_specs=[
                smem,
                smem,
                smem,
                pl.BlockSpec(weight.shape, lambda v, place: (0, 0)),
                pl.BlockSpec((n, 2, TAPS * STRIP, LANES), lambda v, place: (v, 0, 0, 0)),
                pl.BlockSpec((n, TAPS * STRIP, BAND - LANES), lambda v, place: (v, 0, 0)),
                pl.BlockSpec((n, BLOCK, 256), lambda v, place: (v, 0, 0)),
                pl.BlockSpec((n, 8, WIDTH), lambda v, place: (v, 0, 0)),
                hbm,
                hbm,
                pl.BlockSpec((n, BLOCK, WIDTH), lambda v, place: (v, 0, 0)),
                pl.BlockSpec((n, RIM, WIDTH), lambda v, place: (v, 0, 0)),
                pl.BlockSpec((n, RIM, WIDTH), lambda v, place: (v, 0, 0)),
            ],
            out_specs=hbm,
            scratch_shapes=[
                pltpu.VMEM((n, 4, TALL, WIDTH), BF16),
                pltpu.VMEM((V * BLKC, BLOCK, BLOCK), BF16),
                pltpu.SMEM((owner.shape[0],), jnp.int32),
                pltpu.VMEM((devices, LANES), F32),
                pltpu.VMEM((devices, LABEL, LANES), BF16),
                pltpu.VMEM((WIDTH, WIDTH), BF16),
                pltpu.VMEM((WIDTH, WIDTH), BF16),
                pltpu.SemaphoreType.DMA((V * BLKC,)),
                pltpu.SemaphoreType.DMA(()),
                pltpu.SemaphoreType.DMA((2,)),
            ],
        ),
        out_shape=jax.ShapeDtypeStruct((devices, CAP * BLOCK + LABEL, BLOCK), BF16),
        compiler_params=pltpu.CompilerParams(vmem_limit_bytes=60 << 20),
        cost_estimate=pl.CostEstimate(
            flops=V * 2 * STRIPS * TAPS * STRIP * BAND * WIDTH,
            bytes_accessed=V * (BLOCK * WIDTH * 6),
            transcendentals=0,
        ),
        name="match_warp",
    )(
        place, patch, slot, owner, weight, *ready,
        jnp.asarray(sort, BF16), jnp.asarray(sort.T, BF16), images, above, below,
    )


def coadd_kernel(got, out, total, table, numbers, sums, sem, out_sem):
    devices = got.shape[0]
    table[...] = got[:, CAP * BLOCK : CAP * BLOCK + LABEL].astype(F32)[:, 0]
    copy = pltpu.make_async_copy(table, numbers, sem)
    copy.start()
    total[...] = jnp.zeros_like(total)
    for c in range(CELLS):
        sums[c] = 0.0
    copy.wait()

    def add(source, _):
        for rank in range(CAP):
            weight = numbers[source, rank * 2]

            @pl.when(weight > 0.0)
            def _(rank=rank, weight=weight):
                c = numbers[source, rank * 2 + 1].astype(jnp.int32)
                sums[c] += weight
                rows = slice(rank * BLOCK, (rank + 1) * BLOCK)
                total[c] += weight * got[source, rows].astype(F32)

        return 0

    lax.fori_loop(0, devices, add, 0, unroll=4)
    copies = []
    for c in range(CELLS):
        inverse = 1.0 / jnp.maximum(jnp.full((1, BLOCK), sums[c], F32), 1.0)
        total[c] = total[c] * inverse
        rows = slice(c // PSIDE * BLOCK, (c // PSIDE + 1) * BLOCK)
        lanes = slice(c % PSIDE * BLOCK, (c % PSIDE + 1) * BLOCK)
        copies.append(pltpu.make_async_copy(total.at[c], out.at[0, rows, lanes], out_sem.at[c]))
        copies[-1].start()
    for copy in copies:
        copy.wait()


def coadd(got):
    devices = got.shape[0]
    return pl.pallas_call(
        coadd_kernel,
        in_specs=[pl.BlockSpec(memory_space=pltpu.VMEM)],
        out_specs=pl.BlockSpec(memory_space=pl.ANY),
        out_shape=jax.ShapeDtypeStruct((1, PSIDE * BLOCK, PSIDE * BLOCK), F32),
        scratch_shapes=[
            pltpu.VMEM((CELLS, BLOCK, BLOCK), F32),
            pltpu.VMEM((devices, LANES), F32),
            pltpu.SMEM((devices, LANES), F32),
            pltpu.SMEM((CELLS,), F32),
            pltpu.SemaphoreType.DMA(()),
            pltpu.SemaphoreType.DMA((CELLS,)),
        ],
        compiler_params=pltpu.CompilerParams(vmem_limit_bytes=32 << 20),
        name="coadd",
    )(got)


def shards(
    images, basis_taps, psf_coef, affine, visit_weight, block_patch, block_slot, patch_owner
):
    band = lax.axis_index("ccd")
    devices = lax.axis_size("ccd")
    shifted = band + SPLIT // 2
    quarter = shifted % SPLIT
    place = jnp.stack(
        [
            shifted // SPLIT,
            quarter * BLOCK,
            ((quarter > 0) & (band > 0)).astype(jnp.int32),
            ((quarter < SPLIT - 1) & (band < devices - 1)).astype(jnp.int32),
            band,
        ]
    ).astype(jnp.int32)
    down = [(i, i + 1) for i in range(devices - 1)]
    up = [(i + 1, i) for i in range(devices - 1)]
    above = lax.ppermute(images[:, BLOCK - RIM :], "ccd", down)
    below = lax.ppermute(images[:, :RIM], "ccd", up)
    patch = block_patch[:, :, 0]
    ready = prepare(place, basis_taps, psf_coef, affine)
    sent = warp(
        place, patch, block_slot, patch_owner, visit_weight, ready, images, above, below, devices
    )
    got = lax.all_to_all(sent, "ccd", split_axis=0, concat_axis=0, tiled=True)
    return coadd(got)


def solution(mesh):
    placed = (
        P(None, ("group", "ccd"), None),
        P(),
        P(None, "group", None, None),
        P(None, "group", None, None),
        P(None, "group"),
        P(("group", "ccd"), None, None),
        P(("group", "ccd"), None),
        P("group"),
    )
    return jax.shard_map(
        shards,
        mesh=mesh,
        in_specs=placed,
        out_specs=P(("group", "ccd"), None, None),
        check_vma=False,
    )
```

time: 58.3 us -> 58 us (level)
  Pallas kernels: 13 us -> 14.5 us
  local copies, waits for them, and re-layouts: 3.33 us -> 2.18 us
  other arithmetic: 0.69 us -> 0 us
    pallas_call x1, Pallas kernels: 2 us -> 3.89 us  [prepare(): pl.pallas_call(prepare_kernel, grid_spec=pltpu.PrefetchScalarGridSpec(num...]
    unnamed x18 -> x4, local copies, waits for them, and re-layouts: 2.18 us -> 0.63 us
    convert_element_type x2 -> x0, other arithmetic: 0.69 us -> none  [the longest x1 0.68 us: shards(): weight = visit_weight.astype(F32)]
    another operation x1, local copies, waits for them, and re-layouts: 0.08 us -> 0.68 us  [shards(): jnp.stack([shifted // SPLIT, quarter * BLOCK, ((quarter > 0) & (band > 0)...]
  transfers between devices with their start and end apart: 2 -> 2, of which waited for: 0 -> 0; matrix products, arithmetic and copies ran while one was open for 1% -> 1% of each run, Pallas kernels for 3% -> 7%
where the time goes in v4:
time: 58 us; the launch traced here: 57.6 us
  blocking collectives  36.5 us (63%)
  Pallas kernels  14.5 us (25%)
  starting transfers between devices  4.33 us (7%)
  local copies, waits for them, and re-layouts  2.18 us (4%)
    all_to_all x1, blocking collectives, shards(): got = lax.all_to_all(sent, 'ccd', split_axis=0, concat_axis=0, tiled=True)  36.5 us
    pallas_call x1, Pallas kernels, warp(): pl.pallas_call(warp_kernel, grid_spec=pltpu.PrefetchScalarGridSpec(num_sc...  8.37 us
    pallas_call x1, Pallas kernels, prepare(): pl.pallas_call(prepare_kernel, grid_spec=pltpu.PrefetchScalarGridSpec(num...  3.89 us
    ppermute x1, starting transfers between devices, shards(): above = lax.ppermute(images[:, BLOCK - RIM:], 'ccd', down)  3.03 us
    pallas_call x1, Pallas kernels, coadd(): pl.pallas_call(coadd_kernel, in_specs=[pl.BlockSpec(memory_space=pltpu.VM...  2.28 us
    ppermute x1, starting transfers between devices, shards(): below = lax.ppermute(images[:, :RIM], 'ccd', up)  1.29 us
  transfers between devices with their start and end apart: 2, of which 0 were waited for; matrix products, arithmetic and copies ran while one was open for 1% of the time, Pallas kernels for 7%

profile of v4, /device:TPU:0, one launch (start us, length us, event | category | flops | bytes accessed | tf_op | source)
XLA Modules:
  0.0 57.6 jit_solution(13718772815377253633)
XLA Ops:
  0.0 0.9 %fusion = (f32[4,8,512]{2,1,0:T(8,128)S(1)}, f32[4,8,512]{2,1,0:T(8,128)S(1)}) fusion(f32[4,128,512]{2,1,0:T(8,128)} %image.1), kind=kLoop, calls=%fused_computation | loop fusion | bytes 262144 | tf_op jit(solution)/shard_map/slice | solution.py:508
  0.9 1.3 %collective-permute-start.1 = (f32[4,8,512]{2,1,0:T(8,128)S(1)}, f32[4,8,512]{2,1,0:T(8,128)S(1)}, u32[]{:S(2)}, u32[]{:S(2)}) collective-permute-start(f32[4,8,512]{2,1,0:T(8,128)S(1)} %get-tuple-element.13), channel_id=1, source_target_pairs={{1,0},{2,1},{3,2},{4,3},{5,4},{6,5},{7,6},{8,7},{9,8},{10,9},{11,1... | collective-permute-start | bytes 196616 | tf_op jit(solution)/shard_map/ppermute | solution.py:508
  2.2 3.0 %collective-permute-start = (f32[4,8,512]{2,1,0:T(8,128)S(1)}, f32[4,8,512]{2,1,0:T(8,128)S(1)}, u32[]{:S(2)}, u32[]{:S(2)}) collective-permute-start(f32[4,8,512]{2,1,0:T(8,128)S(1)} %get-tuple-element.14), channel_id=1, source_target_pairs={{0,1},{1,2},{2,3},{3,4},{4,5},{5,6},{6,7},{7,8},{8,9},{9,10},{10,1... | collective-permute-start | bytes 196616 | tf_op jit(solution)/shard_map/ppermute | solution.py:507
  5.2 0.7 %stack.31.place = s32[5]{0:T(128)} concatenate(s32[1]{0:T(128)} %bitcast, s32[1]{0:T(128)} %bitcast.1, s32[1]{0:T(128)} %bitcast.2, s32[1]{0:T(128)} %bitcast.3, s32[1]{0:T(128)} %bitcast.4), dimensions={0} | concatenate | bytes 40 | tf_op jit(solution)/shard_map/stack | solution.py:496
  5.9 3.9 %prepare.1 = (f32[4,2,176,128]{3,2,1,0:T(8,128)}, bf16[4,176,128]{2,1,0:T(8,128)(2,1)}, bf16[4,128,256]{2,1,0:T(8,128)(2,1)}, f32[4,8,512]{2,1,0:T(8,128)}) custom-call(s32[5]{0:T(128)} %stack.31.place, f32[9,2,11]{2,1,0:T(2,128)} %bitcast.10, f32[5,3,4,9]{3,2,1,0:T(4,128)} %bitcast.9, f32[4,2,2,5]{3,2,1,0:T(2,128)} %bitcast.11), custom_call_target="tpu_custom_call" | custom-call | flops 1073741824 | bytes 1048576 | tf_op jit(solution)/shard_map/prepare/pallas_call | solution.py:165
  9.8 0.0 collective-permute-done.1.below
  9.8 0.0 copy-start
  9.8 0.0 collective-permute-done.above
  9.9 0.0 copy-start.1
  9.9 0.6 %copy-done = f32[4,8,512]{2,1,0:T(8,128)} copy-done((f32[4,8,512]{2,1,0:T(8,128)}, f32[4,8,512]{2,1,0:T(8,128)S(1)}, u32[]{:S(2)}) %copy-start) | copy-done | bytes 65560
  10.5 0.0 copy-done.1
  10.5 8.4 %match_warp.1 = bf16[16,272,128]{2,1,0:T(8,128)(2,1)} custom-call(s32[5]{0:T(128)} %stack.31.place, s32[1,16]{1,0:T(1,128)} %bitcast.12, s32[1,16]{1,0:T(1,128)} %slot.1, s32[16]{0:T(128)} %owner.1, bf16[4,5]{1,0:T(4,128)(2,1)} %weight.1, f32[4,2,176,128]{3,2,1,0:T(8,128)} %get-tuple-element.9.level, bf16[4,176,128]{2,1,0:T(8,128)(2,1)} %get-tuple-element.10.slope, ...), custom_call_target="tpu_custom_call" | custom-call | flops 1660944384 | bytes 1572864 | tf_op jit(solution)/shard_map/match_warp/pallas_call | solution.py:385
  18.9 36.5 %all_to_all.5.got = bf16[16,272,128]{2,1,0:T(8,128)(2,1)S(1)} all-to-all(bf16[16,272,128]{2,1,0:T(8,128)(2,1)} %match_warp.1), channel_id=1, replica_groups=mesh['group'=2,'ccd'=16] {'ccd'}, dimensions={0} | all-to-all | bytes 2228224 | tf_op jit(solution)/shard_map/all_to_all | solution.py:514
  55.4 2.3 %coadd.1 = f32[1,512,512]{2,1,0:T(8,128)} custom-call(bf16[16,272,128]{2,1,0:T(8,128)(2,1)S(1)} %all_to_all.5.got), custom_call_target="tpu_custom_call" | custom-call | tf_op jit(solution)/shard_map/coadd/pallas_call | solution.py:471
Async XLA Ops:
  0.9 8.9 %collective-permute-start.1 = (f32[4,8,512]{2,1,0:T(8,128)S(1)}, f32[4,8,512]{2,1,0:T(8,128)S(1)}, u32[]{:S(2)}, u32[]{:S(2)}) collective-permute-start(f32[4,8,512]{2,1,0:T(8,128)S(1)} %get-tuple-element.13), channel_id=1, source_target_pairs={{1,0},{2,1},{3,2},{4,3},{5,4},{6,5},{7,6},{8,7},{9,8},{10,9},{11,1... | collective-permute-start | bytes 196616 | tf_op jit(solution)/shard_map/ppermute | solution.py:508
  2.2 7.7 %collective-permute-start = (f32[4,8,512]{2,1,0:T(8,128)S(1)}, f32[4,8,512]{2,1,0:T(8,128)S(1)}, u32[]{:S(2)}, u32[]{:S(2)}) collective-permute-start(f32[4,8,512]{2,1,0:T(8,128)S(1)} %get-tuple-element.14), channel_id=1, source_target_pairs={{0,1},{1,2},{2,3},{3,4},{4,5},{5,6},{6,7},{7,8},{8,9},{9,10},{10,1... | collective-permute-start | bytes 196616 | tf_op jit(solution)/shard_map/ppermute | solution.py:507
  9.8 0.6 %copy-start = (f32[4,8,512]{2,1,0:T(8,128)}, f32[4,8,512]{2,1,0:T(8,128)S(1)}, u32[]{:S(2)}) copy-start(f32[4,8,512]{2,1,0:T(8,128)S(1)} %collective-permute-done.1.below) | copy-start | bytes 196612
  9.9 0.6 %copy-start.1 = (f32[4,8,512]{2,1,0:T(8,128)}, f32[4,8,512]{2,1,0:T(8,128)S(1)}, u32[]{:S(2)}) copy-start(f32[4,8,512]{2,1,0:T(8,128)S(1)} %collective-permute-done.above) | copy-start | bytes 196612

commit v5 on v2

v5 whole, which is shorter than its diff:
```python
import jax
import jax.numpy as jnp
import numpy as np
from jax import lax
from jax.experimental import pallas as pl
from jax.experimental.pallas import tpu as pltpu
from jax.sharding import PartitionSpec as P

V = 4
BLOCK = 128
BLKC = 4
SPLIT = 4
TAPS = 11
NBASIS = 9
PSIDE = 4
CELLS = PSIDE * PSIDE
CAP = 2

HALF = TAPS // 2
WARP = 3
RIM = HALF + WARP
HEIGHT = SPLIT * BLOCK
WIDTH = BLKC * BLOCK
LANES = 128
LANE_BLOCKS = WIDTH // LANES
STRIP = 16
STEP = 32
STRIPS = -(-(BLOCK + 2 * WARP) // STRIP)
GROUPS = 6
BAND = 256
TALL = (STRIPS - 1) * STRIP + STEP
HALVES = 2
ROWS = BLOCK // HALVES
WINDOW = ROWS + STRIP
LABEL = 16
F32 = jnp.float32
BF16 = jnp.bfloat16


def sin_pi(t):
    whole = jnp.round(t)
    f = t - whole
    odd = whole - 2.0 * jnp.floor(0.5 * whole)
    f2 = f * f
    out = 0.0
    for c in (
        0.00046630280576761, -0.0073704309457144, 0.0821458866111282,
        -0.599264529320792, 2.55016403987734, -5.16771278004997, 3.14159265358979,
    ):
        out = out * f2 + c
    return f * out * (1.0 - 2.0 * odd)


def lanczos(t):
    zero = t == 0.0
    safe = jnp.where(zero, 1.0, t)
    pt = jnp.pi * safe
    value = 3.0 * sin_pi(safe) * sin_pi(safe / 3.0) / (pt * pt)
    return jnp.where(jnp.abs(t) < 3.0, jnp.where(zero, 1.0, value), 0.0)


def iota(shape, dim):
    return lax.broadcasted_iota(jnp.int32, shape, dim)


def deinterleave():
    order = np.arange(WIDTH).reshape(LANES, LANE_BLOCKS).T.reshape(-1)
    return (np.arange(WIDTH)[:, None] == order[None, :]).astype(np.float32)


def column_at(lane):
    return lane % LANES * LANE_BLOCKS + lane // LANES


def lane_block(x, v):
    return x[:, v * LANES : (v + 1) * LANES]


def dot_exact(a, b, dims):
    return lax.dot_general(
        a, b, (dims, ((), ())), precision=lax.Precision.HIGHEST, preferred_element_type=F32
    )


def staircase(x, first):
    return jnp.concatenate(
        [
            pltpu.roll(x[g : g + 8], first + g, 1, stride=1, stride_axis=0)
            for g in range(0, x.shape[0], 8)
        ],
        axis=0,
    )


def lane_sum(terms_of, lane, count, weigh):
    blocks = []
    for v in range(LANE_BLOCKS):
        total = None
        half = count // 2
        for q in range(-(-half // LANE_BLOCKS) * -1, (half + LANE_BLOCKS - 1) // LANE_BLOCKS + 1):
            part = None
            for u in range(count):
                if (v + u - half) // LANE_BLOCKS != q:
                    continue
                piece = terms_of(u, v, (v + u - half) % LANE_BLOCKS)
                part = piece if part is None else part + piece
            if part is None:
                continue
            if q:
                part = pltpu.roll(part, -q % LANES, 1)
                if not weigh:
                    part = jnp.where((lane + q >= 0) & (lane + q < LANES), part, 0.0)
            total = part if total is None else total + part
        blocks.append(total)
    return blocks


def warp_kernel(
    patch, slot, owner, weight, taps, psf, affine, sort_in, unsort_in, image, above, below, out,
    row_taps, turned_taps, high_level, step_level, slope, terms, matched_terms,
    ready, seen, label, label_ready, sort, unsort, sem, label_sem, sort_sem,
):
    visit = pl.program_id(0)
    visits = pl.num_programs(0)
    band = lax.axis_index("ccd")
    devices = label.shape[0]
    ccd = (band + SPLIT // 2) // SPLIT
    quarter = (band + SPLIT // 2) % SPLIT
    top_row = quarter * BLOCK
    has_above = (quarter > 0) & (band > 0)
    has_below = (quarter < SPLIT - 1) & (band < devices - 1)
    tall = BLOCK + 2 * RIM
    sort_copy = pltpu.make_async_copy(sort_in, sort, sort_sem.at[0])
    unsort_copy = pltpu.make_async_copy(unsort_in, unsort, sort_sem.at[1])
    band_lane = iota((1, BAND), 1)
    seg = band_lane // STEP
    lane = iota((1, LANES), 1)

    @pl.when(visit == 0)
    def _():
        sort_copy.start()
        unsort_copy.start()
        tap = band_lane - seg * STEP
        onehot = (tap == iota((TAPS, BAND), 0)) & (seg < GROUPS)
        row_taps[...] = dot_exact(taps[:, 0], onehot.astype(F32), ((1,), (0,)))
        eye = (iota((TAPS, STRIP), 0) == iota((TAPS, STRIP), 1)).astype(F32)
        turned_taps[...] = dot_exact(eye, taps[:, 1], ((0,), (1,)))
        terms[:, tall:] = jnp.zeros((4, TALL - tall, WIDTH), BF16)
        label[...] = jnp.zeros_like(label)

        def clear(p, _):
            seen[p] = 0
            return 0

        lax.fori_loop(0, owner.shape[0], clear, 0)
        sort_copy.wait()

    col_pos = (2.0 * column_at(iota((1, WIDTH), 1)).astype(F32) + 1.0) / WIDTH - 1.0
    raw = jnp.concatenate(
        [jnp.where(has_above, above[0], 0.0), image[0], jnp.where(has_below, below[0], 0.0)],
        axis=0,
    )
    raw_high = raw.astype(BF16)
    raw_low = (raw - raw_high.astype(F32)).astype(BF16)
    sorted_terms = jnp.dot(
        jnp.concatenate([raw_high, raw_low], axis=0), sort[...], preferred_element_type=F32
    )
    high, low = sorted_terms[:tall], sorted_terms[tall:]
    tilted = (high + low) * col_pos
    tilted_high = tilted.astype(BF16)
    terms[0, :tall] = high.astype(BF16)
    terms[1, :tall] = low.astype(BF16)
    terms[2, :tall] = tilted_high
    terms[3, :tall] = (tilted - tilted_high.astype(F32)).astype(BF16)

    lhs = jnp.concatenate(
        [turned_taps[...] * psf[ccd, c, pl.ds(visit, 1), :] for c in range(3)], axis=0
    )
    kernels = dot_exact(lhs, row_taps[...], ((1,), (0,)))
    const, by_row, by_col = (kernels[c * STRIP : (c + 1) * STRIP] for c in range(3))
    is_level = seg < 3
    middle = STRIPS // 2
    per_strip = 2.0 * STRIP / HEIGHT
    middle_row = (top_row + (middle * STRIP - WARP)).astype(F32)
    middle_pos = (2.0 * middle_row + 1.0) / HEIGHT - 1.0
    col_move = (iota((STRIP, 1), 0) - HALF).astype(F32) * (2.0 / WIDTH)
    by_row = jnp.where(is_level, by_row, 0.0)
    const = jnp.where(is_level, const + middle_pos * by_row - col_move * by_col, by_col)
    reach = per_strip * (STRIPS - middle)
    largest = jnp.max(jnp.abs(const) + reach * jnp.abs(by_row), axis=(0, 1), keepdims=True)
    unit = jnp.maximum(largest, 1e-30) * (1.0 / 200.0)
    const = const / unit
    by_row = (by_row * per_strip) / unit
    low_lanes = (lane // STEP) % 3 == 2
    low_band = seg % 3 == 2
    row_part = iota((STRIP, 1), 0).astype(F32) * (1.0 / STRIP)
    for u in range(TAPS):
        at = slice(u * STRIP, (u + 1) * STRIP)
        x = staircase(jnp.broadcast_to(const[u : u + 1], (STRIP, BAND)), 0)
        y = staircase(jnp.broadcast_to(by_row[u : u + 1, :LANES], (STRIP, LANES)), 0)
        tail = x[:, LANES:]
        high = tail.astype(BF16).astype(F32)
        slope[at] = jnp.where(low_band[:, LANES:], tail - high, high).astype(BF16)
        x = x[:, :LANES] + row_part * y
        high = jnp.where(lane < 3 * STEP, jnp.round(x), x.astype(BF16).astype(F32))
        high_level[at] = jnp.where(low_lanes, x - high, high)
        high = jnp.round(y)
        step_level[at] = jnp.where(low_lanes, y - high, high)

    filler = jnp.zeros((BAND - GROUPS * STEP, WIDTH), BF16)
    for k in range(STRIPS):
        level = high_level[...]
        if k != middle:
            level = level + float(k - middle) * step_level[...]
        matrix = jnp.concatenate([level.astype(BF16), slope[...]], axis=1)
        rows = slice(k * STRIP, k * STRIP + STEP)
        columns = jnp.concatenate([terms[h, rows] for h in (0, 1, 0, 2, 3, 2)] + [filler], axis=0)
        results = jnp.dot(matrix, columns, preferred_element_type=F32)
        blocks = lane_sum(
            lambda u, v, w: lane_block(results[u * STRIP : (u + 1) * STRIP], w), lane, TAPS, False
        )
        matched = jnp.concatenate(blocks, axis=1)
        high = matched.astype(BF16)
        at = slice(k * STRIP, (k + 1) * STRIP)
        matched_terms[0, at] = high
        matched_terms[1, at] = (matched - high.astype(F32)).astype(BF16)

    a = jnp.sum(
        jnp.where(iota((1, 1, affine.shape[3]), 2) == ccd, affine[visit], 0.0),
        axis=2, keepdims=True,
    )
    offset = iota((8, LANES), 0) - WARP
    row = (top_row + lane).astype(F32)
    shift = a[0, 0:1] + a[0, 1:2] * (row - (HEIGHT - 1) / 2.0) / HEIGHT
    band_row = lane + offset
    keep = (offset <= WARP) & ((band_row >= 0) | has_above) & ((band_row < BLOCK) | has_below)
    weights = jnp.where(keep, lanczos(shift - offset.astype(F32)), 0.0) * unit
    weights = jnp.concatenate([weights, jnp.zeros((LANES - 8, LANES), F32)], axis=0).T
    empty = jnp.zeros((LANES - WINDOW, WIDTH), BF16)
    halves = []
    for h in range(HALVES):
        matrix = staircase(weights[h * ROWS : (h + 1) * ROWS], 0)
        high = matrix.astype(BF16)
        low = (matrix - high.astype(F32)).astype(BF16)
        rows = slice(h * ROWS, h * ROWS + WINDOW)
        first = jnp.concatenate([matched_terms[0, rows], empty], axis=0)
        second = jnp.concatenate([matched_terms[1, rows], empty], axis=0)
        both = jnp.dot(
            jnp.concatenate([high, high], axis=1), jnp.concatenate([first, second], axis=0),
            preferred_element_type=F32,
        )
        halves.append(both + jnp.dot(low, first, preferred_element_type=F32))
    warped = jnp.concatenate(halves, axis=0)

    lanes = iota((8, WIDTH), 1)
    step = iota((8, WIDTH), 0) - WARP
    block = lanes // LANES
    carry = (block + step + LANE_BLOCKS) // LANE_BLOCKS - 1
    from_lane = lanes % LANES - carry
    col = (from_lane * LANE_BLOCKS + block).astype(F32)
    col_shift = a[1, 0:1] + a[1, 1:2] * (col - (WIDTH - 1) / 2.0) / WIDTH
    within = (from_lane >= 0) & (from_lane < LANES) & (step <= WARP)
    cols = jnp.where(within, lanczos(col_shift - step.astype(F32)), 0.0)
    blocks = lane_sum(
        lambda s, v, w: lane_block(cols[s : s + 1], v) * lane_block(warped, w),
        lane, 2 * WARP + 1, True,
    )

    @pl.when(visit == 0)
    def _():
        unsort_copy.wait()

    result = jnp.dot(
        jnp.concatenate(blocks, axis=1).astype(BF16), unsort[...], preferred_element_type=F32
    ).astype(BF16)

    own = jnp.where(iota(weight.shape, 1) == ccd, weight[...].astype(F32), 0.0)
    own = jnp.where(iota(weight.shape, 0) == visit, own, 0.0)
    own = jnp.sum(own, axis=(0, 1), keepdims=True)
    for j in range(BLKC):
        block = visit * BLKC + j
        ready[block] = result[:, j * BLOCK : (j + 1) * BLOCK]
        p = patch[0, block]
        rank = seen[p]
        seen[p] = rank + 1
        to = out.at[owner[p], pl.ds(pl.multiple_of(rank * BLOCK, BLOCK), BLOCK)]
        pltpu.make_async_copy(ready.at[block], to, sem.at[block]).start()
        line = label[pl.ds(owner[p], 1), :]
        line = jnp.where(lane == rank * 2, own, line)
        label[pl.ds(owner[p], 1), :] = jnp.where(
            lane == rank * 2 + 1, slot[0, block].astype(F32), line
        )

    @pl.when(visit == visits - 1)
    def _():
        label_ready[...] = jnp.broadcast_to(
            label[...].reshape(devices, 1, LANES), (devices, LABEL, LANES)
        ).astype(BF16)
        copy = pltpu.make_async_copy(label_ready, out.at[:, pl.ds(CAP * BLOCK, LABEL)], label_sem)
        copy.start()
        copy.wait()
        for block in range(V * BLKC):
            pltpu.make_async_copy(ready.at[block], out.at[0, pl.ds(0, BLOCK)], sem.at[block]).wait()


def warp(patch, slot, owner, weight, taps, psf, affine, images, above, below, devices):
    smem = pl.BlockSpec(memory_space=pltpu.SMEM)
    hbm = pl.BlockSpec(memory_space=pl.ANY)
    sort = deinterleave()
    taps = taps.transpose(1, 0, 2)
    psf = psf.transpose(1, 3, 0, 2)
    affine = affine.transpose(0, 2, 3, 1)

    def whole(x):
        return pl.BlockSpec(x.shape, lambda v: (0,) * x.ndim)

    def by_visit(x):
        return pl.BlockSpec((1,) + x.shape[1:], lambda v: (v, 0, 0))

    return pl.pallas_call(
        warp_kernel,
        grid=(V,),
        in_specs=[smem, smem, smem, whole(weight), whole(taps), whole(psf), whole(affine)]
        + [hbm, hbm, by_visit(images), by_visit(above), by_visit(below)],
        out_specs=hbm,
        scratch_shapes=[
            pltpu.VMEM((NBASIS, BAND), F32),
            pltpu.VMEM((STRIP, NBASIS), F32),
            pltpu.VMEM((TAPS * STRIP, LANES), F32),
            pltpu.VMEM((TAPS * STRIP, LANES), F32),
            pltpu.VMEM((TAPS * STRIP, BAND - LANES), BF16),
            pltpu.VMEM((4, TALL, WIDTH), BF16),
            pltpu.VMEM((2, STRIPS * STRIP, WIDTH), BF16),
            pltpu.VMEM((V * BLKC, BLOCK, BLOCK), BF16),
            pltpu.SMEM((owner.shape[0],), jnp.int32),
            pltpu.VMEM((devices, LANES), F32),
            pltpu.VMEM((devices, LABEL, LANES), BF16),
            pltpu.VMEM((WIDTH, WIDTH), BF16),
            pltpu.VMEM((WIDTH, WIDTH), BF16),
            pltpu.SemaphoreType.DMA((V * BLKC,)),
            pltpu.SemaphoreType.DMA(()),
            pltpu.SemaphoreType.DMA((2,)),
        ],
        out_shape=jax.ShapeDtypeStruct((devices, CAP * BLOCK + LABEL, BLOCK), BF16),
        compiler_params=pltpu.CompilerParams(vmem_limit_bytes=32 << 20),
        cost_estimate=pl.CostEstimate(
            flops=V * 2 * STRIPS * TAPS * STRIP * BAND * WIDTH,
            bytes_accessed=V * (BLOCK * WIDTH * 6),
            transcendentals=0,
        ),
        name="match_warp",
    )(
        patch, slot, owner, weight, taps, psf, affine,
        jnp.asarray(sort, BF16), jnp.asarray(sort.T, BF16), images, above, below,
    )


def coadd_kernel(got, out, total, table, numbers, sums, sem, out_sem):
    devices = got.shape[0]
    table[...] = got[:, CAP * BLOCK : CAP * BLOCK + LABEL].astype(F32)[:, 0]
    copy = pltpu.make_async_copy(table, numbers, sem)
    copy.start()
    total[...] = jnp.zeros_like(total)
    for c in range(CELLS):
        sums[c] = 0.0
    copy.wait()

    def add(source, _):
        for rank in range(CAP):
            weight = numbers[source, rank * 2]

            @pl.when(weight > 0.0)
            def _(rank=rank, weight=weight):
                c = numbers[source, rank * 2 + 1].astype(jnp.int32)
                sums[c] += weight
                rows = slice(rank * BLOCK, (rank + 1) * BLOCK)
                total[c] += weight * got[source, rows].astype(F32)

        return 0

    lax.fori_loop(0, devices, add, 0, unroll=4)
    copies = []
    for c in range(CELLS):
        inverse = 1.0 / jnp.maximum(jnp.full((1, BLOCK), sums[c], F32), 1.0)
        total[c] = total[c] * inverse
        rows = slice(c // PSIDE * BLOCK, (c // PSIDE + 1) * BLOCK)
        lanes = slice(c % PSIDE * BLOCK, (c % PSIDE + 1) * BLOCK)
        copies.append(pltpu.make_async_copy(total.at[c], out.at[0, rows, lanes], out_sem.at[c]))
        copies[-1].start()
    for copy in copies:
        copy.wait()


def coadd(got):
    devices = got.shape[0]
    return pl.pallas_call(
        coadd_kernel,
        in_specs=[pl.BlockSpec(memory_space=pltpu.VMEM)],
        out_specs=pl.BlockSpec(memory_space=pl.ANY),
        out_shape=jax.ShapeDtypeStruct((1, PSIDE * BLOCK, PSIDE * BLOCK), F32),
        scratch_shapes=[
            pltpu.VMEM((CELLS, BLOCK, BLOCK), F32),
            pltpu.VMEM((devices, LANES), F32),
            pltpu.SMEM((devices, LANES), F32),
            pltpu.SMEM((CELLS,), F32),
            pltpu.SemaphoreType.DMA(()),
            pltpu.SemaphoreType.DMA((CELLS,)),
        ],
        compiler_params=pltpu.CompilerParams(vmem_limit_bytes=32 << 20),
        name="coadd",
    )(got)


def shards(
    images, basis_taps, psf_coef, affine, visit_weight, block_patch, block_slot, patch_owner
):
    devices = lax.axis_size("ccd")
    down = [(i, i + 1) for i in range(devices - 1)]
    up = [(i + 1, i) for i in range(devices - 1)]
    above = lax.ppermute(images[:, BLOCK - RIM :], "ccd", down)
    below = lax.ppermute(images[:, :RIM], "ccd", up)
    patch = block_patch[:, :, 0]
    sent = warp(
        patch, block_slot, patch_owner, visit_weight, basis_taps, psf_coef, affine,
        images, above, below, devices,
    )
    got = lax.all_to_all(sent, "ccd", split_axis=0, concat_axis=0, tiled=True)
    return coadd(got)


def solution(mesh):
    placed = (
        P(None, ("group", "ccd"), None),
        P(),
        P(None, "group", None, None),
        P(None, "group", None, None),
        P(None, "group"),
        P(("group", "ccd"), None, None),
        P(("group", "ccd"), None),
        P("group"),
    )
    return jax.shard_map(
        shards,
        mesh=mesh,
        in_specs=placed,
        out_specs=P(("group", "ccd"), None, None),
        check_vma=False,
    )
```

time: 58.3 us -> 65.2 us (1.12)
  local copies, waits for them, and re-layouts: 3.33 us -> 8.98 us
  blocking collectives: 36.3 us -> 38.8 us
  Pallas kernels: 13 us -> 11.6 us
  waiting for transfers between devices: 0.01 us -> 0.87 us
  other arithmetic: 0.69 us -> 0 us
    unnamed x18 -> x20, local copies, waits for them, and re-layouts: 2.18 us -> 8.1 us
    all_to_all x1, blocking collectives: 36.3 us -> 38.8 us  [shards(): got = lax.all_to_all(sent, 'ccd', split_axis=0, concat_axis=0, tiled=True)]
    pallas_call x3 -> x2, Pallas kernels: 13 us -> 11.6 us  [the longest x1 9.34 us: warp(): pl.pallas_call(warp_kernel, grid=(V,), in_specs=[smem, smem, smem, whole(...]
    ppermute x1, waiting for transfers between devices: 0.01 us -> 0.87 us  [shards(): above = lax.ppermute(images[:, BLOCK - RIM:], 'ccd', down)]
    convert_element_type x2 -> x0, other arithmetic: 0.69 us -> none  [the longest x1 0.68 us: shards(): weight = visit_weight.astype(F32)]
  transfers between devices with their start and end apart: 2 -> 2, of which waited for: 0 -> 1; matrix products, arithmetic and copies ran while one was open for 1% -> 0% of each run, Pallas kernels for 3% -> 0%
where the time goes in v5:
time: 65.2 us; the launch traced here: 64.6 us
  blocking collectives  38.8 us (60%)
  Pallas kernels  11.6 us (18%)
  local copies, waits for them, and re-layouts  8.98 us (14%)
  starting transfers between devices  4.33 us (7%)
  waiting for transfers between devices  0.87 us (1%)
    all_to_all x1, blocking collectives, shards(): got = lax.all_to_all(sent, 'ccd', split_axis=0, concat_axis=0, tiled=True)  38.8 us
    pallas_call x1, Pallas kernels, warp(): pl.pallas_call(warp_kernel, grid=(V,), in_specs=[smem, smem, smem, whole(...  9.34 us
    unnamed x20, local copies, waits for them, and re-layouts  8.1 us
    ppermute x1, starting transfers between devices, shards(): above = lax.ppermute(images[:, BLOCK - RIM:], 'ccd', down)  3.03 us
    pallas_call x1, Pallas kernels, coadd(): pl.pallas_call(coadd_kernel, in_specs=[pl.BlockSpec(memory_space=pltpu.VM...  2.27 us
  transfers between devices with their start and end apart: 2, of which 1 were waited for; matrix products, arithmetic and copies ran while one was open for 0% of the time, Pallas kernels for 0%

profile of v5, /device:TPU:0, one launch (start us, length us, event | category | flops | bytes accessed | tf_op | source)
XLA Modules:
  0.0 64.6 jit_solution(9311073664498452290)
XLA Ops:
  0.0 0.9 %fusion = (f32[4,8,512]{2,1,0:T(8,128)S(1)}, f32[4,8,512]{2,1,0:T(8,128)S(1)}) fusion(f32[4,128,512]{2,1,0:T(8,128)} %image.1), kind=kLoop, calls=%fused_computation | loop fusion | bytes 262144 | tf_op jit(solution)/shard_map/slice | solution.py:421
  0.9 1.3 %collective-permute-start.1 = (f32[4,8,512]{2,1,0:T(8,128)S(1)}, f32[4,8,512]{2,1,0:T(8,128)S(1)}, u32[]{:S(2)}, u32[]{:S(2)}) collective-permute-start(f32[4,8,512]{2,1,0:T(8,128)S(1)} %get-tuple-element.5), channel_id=1, source_target_pairs={{1,0},{2,1},{3,2},{4,3},{5,4},{6,5},{7,6},{8,7},{9,8},{10,9},{11,1... | collective-permute-start | bytes 196616 | tf_op jit(solution)/shard_map/ppermute | solution.py:421
  2.2 3.0 %collective-permute-start = (f32[4,8,512]{2,1,0:T(8,128)S(1)}, f32[4,8,512]{2,1,0:T(8,128)S(1)}, u32[]{:S(2)}, u32[]{:S(2)}) collective-permute-start(f32[4,8,512]{2,1,0:T(8,128)S(1)} %get-tuple-element.6), channel_id=1, source_target_pairs={{0,1},{1,2},{2,3},{3,4},{4,5},{5,6},{6,7},{7,8},{8,9},{9,10},{10,1... | collective-permute-start | bytes 196616 | tf_op jit(solution)/shard_map/ppermute | solution.py:420
  5.2 0.0 collective-permute-done.1.below
  5.2 0.9 %collective-permute-done.above = f32[4,8,512]{2,1,0:T(8,128)S(1)} collective-permute-done((f32[4,8,512]{2,1,0:T(8,128)S(1)}, f32[4,8,512]{2,1,0:T(8,128)S(1)}, u32[]{:S(2)}, u32[]{:S(2)}) %collective-permute-start) | collective-permute-done | bytes 65568 | tf_op jit(solution)/shard_map/ppermute | solution.py:420
  6.1 0.0 copy-start
  6.1 1.2 %copy-done = f32[4,128,512]{2,1,0:T(8,128)S(1)} copy-done((f32[4,128,512]{2,1,0:T(8,128)S(1)}, f32[4,128,512]{2,1,0:T(8,128)}, u32[]{:S(2)}) %copy-start) | copy-done | bytes 1048600
  7.3 0.0 copy-start.1
  7.3 0.8 %copy-done.1 = f32[4,5,9,3]{2,0,3,1:T(4,128)S(1)} copy-done((f32[4,5,9,3]{2,0,3,1:T(4,128)S(1)}, f32[4,5,9,3]{2,0,3,1:T(4,128)}, u32[]{:S(2)}) %copy-start.1) | copy-done | bytes 2184
  8.1 0.0 copy-start.2
  8.1 0.7 %copy-done.2 = f32[2,9,11]{2,0,1:T(2,128)S(1)} copy-done((f32[2,9,11]{2,0,1:T(2,128)S(1)}, f32[2,9,11]{2,0,1:T(2,128)}, u32[]{:S(2)}) %copy-start.2) | copy-done | bytes 816
  8.8 0.0 copy-start.3
  8.8 0.7 %copy-done.3 = f32[4,5,2,2]{1,3,2,0:T(2,128)S(1)} copy-done((f32[4,5,2,2]{1,3,2,0:T(2,128)S(1)}, f32[4,5,2,2]{1,3,2,0:T(2,128)}, u32[]{:S(2)}) %copy-start.3) | copy-done | bytes 344
  9.5 0.0 copy-start.4
  9.5 0.7 %copy-done.4 = bf16[4,5]{1,0:T(4,128)(2,1)S(1)} copy-done((bf16[4,5]{1,0:T(4,128)(2,1)S(1)}, bf16[4,5]{1,0:T(4,128)(2,1)}, u32[]{:S(2)}) %copy-start.4) | copy-done | bytes 64
  10.2 0.0 copy-start.5
  10.2 0.7 %copy-done.5 = s32[1,16,1]{1,2,0:T(1,128)S(1)} copy-done((s32[1,16,1]{1,2,0:T(1,128)S(1)}, s32[1,16,1]{1,2,0:T(1,128)}, u32[]{:S(2)}) %copy-start.5) | copy-done | bytes 88
  10.8 0.0 copy-start.6
  10.8 0.7 %copy-done.6 = s32[1,16]{1,0:T(1,128)S(1)} copy-done((s32[1,16]{1,0:T(1,128)S(1)}, s32[1,16]{1,0:T(1,128)}, u32[]{:S(2)}) %copy-start.6) | copy-done | bytes 88
  11.5 0.0 copy-start.7
  11.5 0.7 %copy-done.7 = s32[16]{0:T(128)S(1)} copy-done((s32[16]{0:T(128)S(1)}, s32[16]{0:T(128)}, u32[]{:S(2)}) %copy-start.7) | copy-done | bytes 88
  12.1 0.0 copy-start.8
  12.1 1.0 %copy-done.8 = bf16[512,512]{1,0:T(8,128)(2,1)S(1)} copy-done((bf16[512,512]{1,0:T(8,128)(2,1)S(1)}, bf16[512,512]{1,0:T(8,128)(2,1)}, u32[]{:S(2)}) %copy-start.8) | copy-done | bytes 524312
  13.2 0.0 copy-start.9
  13.2 1.0 %copy-done.9 = bf16[512,512]{1,0:T(8,128)(2,1)S(1)} copy-done((bf16[512,512]{1,0:T(8,128)(2,1)S(1)}, bf16[512,512]{1,0:T(8,128)(2,1)}, u32[]{:S(2)}) %copy-start.9) | copy-done | bytes 524312
  14.2 9.3 %match_warp.1 = bf16[16,272,128]{2,1,0:T(8,128)(2,1)S(1)} custom-call(s32[1,16]{1,0:T(1,128)S(1)} %bitcast.7, s32[1,16]{1,0:T(1,128)S(1)} %copy-done.6, s32[16]{0:T(128)S(1)} %copy-done.7, bf16[4,5]{1,0:T(4,128)(2,1)S(1)} %copy-done.4, f32[9,2,11]{2,1,0:T(2,128)S(1)} %bitcast.5, f32[5,3,4,9]{3,2,1,0:T(4,128)S(1)} %bitcast.4, f32[4,2,2,5]{3,2,1,0:T(2,128)S(1)} %bitcast.6, ...), custom_call_target="tpu_custom_call" | custom-call | flops 1660944384 | bytes 1572864 | tf_op jit(solution)/shard_map/match_warp/pallas_call | solution.py:320
  23.6 38.8 %all_to_all.5.got = bf16[16,272,128]{2,1,0:T(8,128)(2,1)S(1)} all-to-all(bf16[16,272,128]{2,1,0:T(8,128)(2,1)S(1)} %match_warp.1), channel_id=1, replica_groups=mesh['group'=2,'ccd'=16] {'ccd'}, dimensions={0} | all-to-all | bytes 2228224 | tf_op jit(solution)/shard_map/all_to_all | solution.py:427
  62.3 2.3 %coadd.1 = f32[1,512,512]{2,1,0:T(8,128)} custom-call(bf16[16,272,128]{2,1,0:T(8,128)(2,1)S(1)} %all_to_all.5.got), custom_call_target="tpu_custom_call" | custom-call | tf_op jit(solution)/shard_map/coadd/pallas_call | solution.py:396
Async XLA Ops:
  0.9 4.3 %collective-permute-start.1 = (f32[4,8,512]{2,1,0:T(8,128)S(1)}, f32[4,8,512]{2,1,0:T(8,128)S(1)}, u32[]{:S(2)}, u32[]{:S(2)}) collective-permute-start(f32[4,8,512]{2,1,0:T(8,128)S(1)} %get-tuple-element.5), channel_id=1, source_target_pairs={{1,0},{2,1},{3,2},{4,3},{5,4},{6,5},{7,6},{8,7},{9,8},{10,9},{11,1... | collective-permute-start | bytes 196616 | tf_op jit(solution)/shard_map/ppermute | solution.py:421
  2.2 3.9 %collective-permute-start = (f32[4,8,512]{2,1,0:T(8,128)S(1)}, f32[4,8,512]{2,1,0:T(8,128)S(1)}, u32[]{:S(2)}, u32[]{:S(2)}) collective-permute-start(f32[4,8,512]{2,1,0:T(8,128)S(1)} %get-tuple-element.6), channel_id=1, source_target_pairs={{0,1},{1,2},{2,3},{3,4},{4,5},{5,6},{6,7},{7,8},{8,9},{9,10},{10,1... | collective-permute-start | bytes 196616 | tf_op jit(solution)/shard_map/ppermute | solution.py:420
  6.1 1.2 %copy-start = (f32[4,128,512]{2,1,0:T(8,128)S(1)}, f32[4,128,512]{2,1,0:T(8,128)}, u32[]{:S(2)}) copy-start(f32[4,128,512]{2,1,0:T(8,128)} %image.1) | copy-start | bytes 3145732
  7.3 0.8 %copy-start.1 = (f32[4,5,9,3]{2,0,3,1:T(4,128)S(1)}, f32[4,5,9,3]{2,0,3,1:T(4,128)}, u32[]{:S(2)}) copy-start(f32[4,5,9,3]{2,0,3,1:T(4,128)} %param.12) | copy-start | bytes 6484
  8.1 0.7 %copy-start.2 = (f32[2,9,11]{2,0,1:T(2,128)S(1)}, f32[2,9,11]{2,0,1:T(2,128)}, u32[]{:S(2)}) copy-start(f32[2,9,11]{2,0,1:T(2,128)} %param.11) | copy-start | bytes 2380
  8.8 0.7 %copy-start.3 = (f32[4,5,2,2]{1,3,2,0:T(2,128)S(1)}, f32[4,5,2,2]{1,3,2,0:T(2,128)}, u32[]{:S(2)}) copy-start(f32[4,5,2,2]{1,3,2,0:T(2,128)} %param.13) | copy-start | bytes 964
  9.5 0.7 %copy-start.4 = (bf16[4,5]{1,0:T(4,128)(2,1)S(1)}, bf16[4,5]{1,0:T(4,128)(2,1)}, u32[]{:S(2)}) copy-start(bf16[4,5]{1,0:T(4,128)(2,1)} %weight.1) | copy-start | bytes 124
  10.2 0.7 %copy-start.5 = (s32[1,16,1]{1,2,0:T(1,128)S(1)}, s32[1,16,1]{1,2,0:T(1,128)}, u32[]{:S(2)}) copy-start(s32[1,16,1]{1,2,0:T(1,128)} %param.15) | copy-start | bytes 196
  10.8 0.7 %copy-start.6 = (s32[1,16]{1,0:T(1,128)S(1)}, s32[1,16]{1,0:T(1,128)}, u32[]{:S(2)}) copy-start(s32[1,16]{1,0:T(1,128)} %slot.1) | copy-start | bytes 196
  11.5 0.7 %copy-start.7 = (s32[16]{0:T(128)S(1)}, s32[16]{0:T(128)}, u32[]{:S(2)}) copy-start(s32[16]{0:T(128)} %owner.1) | copy-start | bytes 196
  12.1 1.0 %copy-start.8 = (bf16[512,512]{1,0:T(8,128)(2,1)S(1)}, bf16[512,512]{1,0:T(8,128)(2,1)}, u32[]{:S(2)}) copy-start(bf16[512,512]{1,0:T(8,128)(2,1)} %constant.5.clone.unsort_in) | copy-start | bytes 1572868
  13.2 1.0 %copy-start.9 = (bf16[512,512]{1,0:T(8,128)(2,1)S(1)}, bf16[512,512]{1,0:T(8,128)(2,1)}, u32[]{:S(2)}) copy-start(bf16[512,512]{1,0:T(8,128)(2,1)} %constant.4.clone.sort_in) | copy-start | bytes 1572868

commit v6 on v5

--- a/solution.py
+++ b/solution.py
@@ -1,3 +1,5 @@
+import functools
+
 import jax
 import jax.numpy as jnp
 import numpy as np
@@ -26,6 +28,7 @@
 STRIP = 16
 STEP = 32
 STRIPS = -(-(BLOCK + 2 * WARP) // STRIP)
+MIDDLE = STRIPS // 2
 GROUPS = 6
 BAND = 256
 TALL = (STRIPS - 1) * STRIP + STEP
@@ -115,36 +118,123 @@
     return blocks
 
 
+def whereabouts(devices):
+    band = lax.axis_index("ccd")
+    quarter = (band + SPLIT // 2) % SPLIT
+    has_above = (quarter > 0) & (band > 0)
+    has_below = (quarter < SPLIT - 1) & (band < devices - 1)
+    return (band + SPLIT // 2) // SPLIT, quarter * BLOCK, has_above, has_below
+
+
+def prepare_kernel(devices, taps, psf, affine, high_level, step_level, slope, rows_high, rows_low, cols_out):
+    ccd, top_row, has_above, has_below = whereabouts(devices)
+    band_lane = iota((1, BAND), 1)
+    seg = band_lane // STEP
+    lane = iota((1, LANES), 1)
+    tap = band_lane - seg * STEP
+    onehot = (tap == iota((TAPS, BAND), 0)) & (seg < GROUPS)
+    row_taps = dot_exact(taps[:, 0], onehot.astype(F32), ((1,), (0,)))
+    eye = (iota((TAPS, STRIP), 0) == iota((TAPS, STRIP), 1)).astype(F32)
+    turned_taps = dot_exact(eye, taps[:, 1], ((0,), (1,)))
+    for visit in range(V):
+        lhs = jnp.concatenate(
+            [turned_taps * psf[ccd, c, visit : visit + 1, :] for c in range(3)], axis=0
+        )
+        kernels = dot_exact(lhs, row_taps, ((1,), (0,)))
+        const, by_row, by_col = (kernels[c * STRIP : (c + 1) * STRIP] for c in range(3))
+        is_level = seg < 3
+        per_strip = 2.0 * STRIP / HEIGHT
+        middle_row = (top_row + (MIDDLE * STRIP - WARP)).astype(F32)
+        middle_pos = (2.0 * middle_row + 1.0) / HEIGHT - 1.0
+        col_move = (iota((STRIP, 1), 0) - HALF).astype(F32) * (2.0 / WIDTH)
+        by_row = jnp.where(is_level, by_row, 0.0)
+        const = jnp.where(is_level, const + middle_pos * by_row - col_move * by_col, by_col)
+        reach = per_strip * (STRIPS - MIDDLE)
+        largest = jnp.max(jnp.abs(const) + reach * jnp.abs(by_row), axis=(0, 1), keepdims=True)
+        unit = jnp.maximum(largest, 1e-30) * (1.0 / 200.0)
+        const = const / unit
+        by_row = (by_row * per_strip) / unit
+        low_lanes = (lane // STEP) % 3 == 2
+        low_band = seg % 3 == 2
+        row_part = iota((STRIP, 1), 0).astype(F32) * (1.0 / STRIP)
+        for u in range(TAPS):
+            at = slice(u * STRIP, (u + 1) * STRIP)
+            x = staircase(jnp.broadcast_to(const[u : u + 1], (STRIP, BAND)), 0)
+            y = staircase(jnp.broadcast_to(by_row[u : u + 1, :LANES], (STRIP, LANES)), 0)
+            tail = x[:, LANES:]
+            high = tail.astype(BF16).astype(F32)
+            slope[visit, at] = jnp.where(low_band[:, LANES:], tail - high, high).astype(BF16)
+            x = x[:, :LANES] + row_part * y
+            high = jnp.where(lane < 3 * STEP, jnp.round(x), x.astype(BF16).astype(F32))
+            high_level[visit, at] = jnp.where(low_lanes, x - high, high)
+            high = jnp.round(y)
+            step_level[visit, at] = jnp.where(low_lanes, y - high, high)
+
+        a = jnp.sum(
+            jnp.where(iota((1, 1, affine.shape[3]), 2) == ccd, affine[visit], 0.0),
+            axis=2, keepdims=True,
+        )
+        offset = iota((8, LANES), 0) - WARP
+        row = (top_row + lane).astype(F32)
+        shift = a[0, 0:1] + a[0, 1:2] * (row - (HEIGHT - 1) / 2.0) / HEIGHT
+        band_row = lane + offset
+        keep = (offset <= WARP) & ((band_row >= 0) | has_above) & ((band_row < BLOCK) | has_below)
+        weights = jnp.where(keep, lanczos(shift - offset.astype(F32)), 0.0) * unit
+        weights = jnp.concatenate([weights, jnp.zeros((LANES - 8, LANES), F32)], axis=0).T
+        for h in range(HALVES):
+            at = slice(h * ROWS, (h + 1) * ROWS)
+            matrix = staircase(weights[at], 0)
+            high = matrix.astype(BF16)
+            rows_high[visit, at] = high
+            rows_low[visit, at] = (matrix - high.astype(F32)).astype(BF16)
+
+        lanes = iota((8, WIDTH), 1)
+        step = iota((8, WIDTH), 0) - WARP
+        block = lanes // LANES
+        carry = (block + step + LANE_BLOCKS) // LANE_BLOCKS - 1
+        from_lane = lanes % LANES - carry
+        col = (from_lane * LANE_BLOCKS + block).astype(F32)
+        col_shift = a[1, 0:1] + a[1, 1:2] * (col - (WIDTH - 1) / 2.0) / WIDTH
+        within = (from_lane >= 0) & (from_lane < LANES) & (step <= WARP)
+        cols_out[visit] = jnp.where(within, lanczos(col_shift - step.astype(F32)), 0.0)
+
+
+def prepare(taps, psf, affine, devices):
+    shapes = [
+        ((V, TAPS * STRIP, LANES), F32),
+        ((V, TAPS * STRIP, LANES), F32),
+        ((V, TAPS * STRIP, BAND - LANES), BF16),
+        ((V, BLOCK, LANES), BF16),
+        ((V, BLOCK, LANES), BF16),
+        ((V, 8, WIDTH), F32),
+    ]
+    args = [taps.transpose(1, 0, 2), psf.transpose(1, 3, 0, 2), affine.transpose(0, 2, 3, 1)]
+    return pl.pallas_call(
+        functools.partial(prepare_kernel, devices),
+        grid=(1,),
+        in_specs=[pl.BlockSpec(x.shape, lambda i, n=x.ndim: (0,) * n) for x in args],
+        out_specs=[pl.BlockSpec(shape, lambda i: (0, 0, 0)) for shape, _ in shapes],
+        out_shape=[jax.ShapeDtypeStruct(shape, kind) for shape, kind in shapes],
+        compiler_params=pltpu.CompilerParams(vmem_limit_bytes=32 << 20),
+        cost_estimate=pl.CostEstimate(flops=1 << 30, bytes_accessed=1 << 20, transcendentals=0),
+        name="prepare",
+    )(*args)
+
+
 def warp_kernel(
-    patch, slot, owner, weight, taps, psf, affine, sort_in, unsort_in, image, above, below, out,
-    row_taps, turned_taps, high_level, step_level, slope, terms, matched_terms,
-    ready, seen, label, label_ready, sort, unsort, sem, label_sem, sort_sem,
+    patch, slot, owner, weight, high_level, step_level, slope, rows_high, rows_low, col_weights,
+    sort, unsort, image, above, below, out,
+    terms, matched_terms, ready, seen, label, label_ready, sem, label_sem,
 ):
     visit = pl.program_id(0)
     visits = pl.num_programs(0)
-    band = lax.axis_index("ccd")
     devices = label.shape[0]
-    ccd = (band + SPLIT // 2) // SPLIT
-    quarter = (band + SPLIT // 2) % SPLIT
-    top_row = quarter * BLOCK
-    has_above = (quarter > 0) & (band > 0)
-    has_below = (quarter < SPLIT - 1) & (band < devices - 1)
+    ccd, _, has_above, has_below = whereabouts(devices)
     tall = BLOCK + 2 * RIM
-    sort_copy = pltpu.make_async_copy(sort_in, sort, sort_sem.at[0])
-    unsort_copy = pltpu.make_async_copy(unsort_in, unsort, sort_sem.at[1])
-    band_lane = iota((1, BAND), 1)
-    seg = band_lane // STEP
     lane = iota((1, LANES), 1)
 
     @pl.when(visit == 0)
     def _():
-        sort_copy.start()
-        unsort_copy.start()
-        tap = band_lane - seg * STEP
-        onehot = (tap == iota((TAPS, BAND), 0)) & (seg < GROUPS)
-        row_taps[...] = dot_exact(taps[:, 0], onehot.astype(F32), ((1,), (0,)))
-        eye = (iota((TAPS, STRIP), 0) == iota((TAPS, STRIP), 1)).astype(F32)
-        turned_taps[...] = dot_exact(eye, taps[:, 1], ((0,), (1,)))
         terms[:, tall:] = jnp.zeros((4, TALL - tall, WIDTH), BF16)
         label[...] = jnp.zeros_like(label)
 
@@ -153,7 +243,6 @@
             return 0
 
         lax.fori_loop(0, owner.shape[0], clear, 0)
-        sort_copy.wait()
 
     col_pos = (2.0 * column_at(iota((1, WIDTH), 1)).astype(F32) + 1.0) / WIDTH - 1.0
     raw = jnp.concatenate(
@@ -173,46 +262,12 @@
     terms[2, :tall] = tilted_high
     terms[3, :tall] = (tilted - tilted_high.astype(F32)).astype(BF16)
 
-    lhs = jnp.concatenate(
-        [turned_taps[...] * psf[ccd, c, pl.ds(visit, 1), :] for c in range(3)], axis=0
-    )
-    kernels = dot_exact(lhs, row_taps[...], ((1,), (0,)))
-    const, by_row, by_col = (kernels[c * STRIP : (c + 1) * STRIP] for c in range(3))
-    is_level = seg < 3
-    middle = STRIPS // 2
-    per_strip = 2.0 * STRIP / HEIGHT
-    middle_row = (top_row + (middle * STRIP - WARP)).astype(F32)
-    middle_pos = (2.0 * middle_row + 1.0) / HEIGHT - 1.0
-    col_move = (iota((STRIP, 1), 0) - HALF).astype(F32) * (2.0 / WIDTH)
-    by_row = jnp.where(is_level, by_row, 0.0)
-    const = jnp.where(is_level, const + middle_pos * by_row - col_move * by_col, by_col)
-    reach = per_strip * (STRIPS - middle)
-    largest = jnp.max(jnp.abs(const) + reach * jnp.abs(by_row), axis=(0, 1), keepdims=True)
-    unit = jnp.maximum(largest, 1e-30) * (1.0 / 200.0)
-    const = const / unit
-    by_row = (by_row * per_strip) / unit
-    low_lanes = (lane // STEP) % 3 == 2
-    low_band = seg % 3 == 2
-    row_part = iota((STRIP, 1), 0).astype(F32) * (1.0 / STRIP)
-    for u in range(TAPS):
-        at = slice(u * STRIP, (u + 1) * STRIP)
-        x = staircase(jnp.broadcast_to(const[u : u + 1], (STRIP, BAND)), 0)
-        y = staircase(jnp.broadcast_to(by_row[u : u + 1, :LANES], (STRIP, LANES)), 0)
-        tail = x[:, LANES:]
-        high = tail.astype(BF16).astype(F32)
-        slope[at] = jnp.where(low_band[:, LANES:], tail - high, high).astype(BF16)
-        x = x[:, :LANES] + row_part * y
-        high = jnp.where(lane < 3 * STEP, jnp.round(x), x.astype(BF16).astype(F32))
-        high_level[at] = jnp.where(low_lanes, x - high, high)
-        high = jnp.round(y)
-        step_level[at] = jnp.where(low_lanes, y - high, high)
-
     filler = jnp.zeros((BAND - GROUPS * STEP, WIDTH), BF16)
     for k in range(STRIPS):
-        level = high_level[...]
-        if k != middle:
-            level = level + float(k - middle) * step_level[...]
-        matrix = jnp.concatenate([level.astype(BF16), slope[...]], axis=1)
+        level = high_level[0]
+        if k != MIDDLE:
+            level = level + float(k - MIDDLE) * step_level[0]
+        matrix = jnp.concatenate([level.astype(BF16), slope[0]], axis=1)
         rows = slice(k * STRIP, k * STRIP + STEP)
         columns = jnp.concatenate([terms[h, rows] for h in (0, 1, 0, 2, 3, 2)] + [filler], axis=0)
         results = jnp.dot(matrix, columns, preferred_element_type=F32)
@@ -225,23 +280,11 @@
         matched_terms[0, at] = high
         matched_terms[1, at] = (matched - high.astype(F32)).astype(BF16)
 
-    a = jnp.sum(
-        jnp.where(iota((1, 1, affine.shape[3]), 2) == ccd, affine[visit], 0.0),
-        axis=2, keepdims=True,
-    )
-    offset = iota((8, LANES), 0) - WARP
-    row = (top_row + lane).astype(F32)
-    shift = a[0, 0:1] + a[0, 1:2] * (row - (HEIGHT - 1) / 2.0) / HEIGHT
-    band_row = lane + offset
-    keep = (offset <= WARP) & ((band_row >= 0) | has_above) & ((band_row < BLOCK) | has_below)
-    weights = jnp.where(keep, lanczos(shift - offset.astype(F32)), 0.0) * unit
-    weights = jnp.concatenate([weights, jnp.zeros((LANES - 8, LANES), F32)], axis=0).T
     empty = jnp.zeros((LANES - WINDOW, WIDTH), BF16)
     halves = []
     for h in range(HALVES):
-        matrix = staircase(weights[h * ROWS : (h + 1) * ROWS], 0)
-        high = matrix.astype(BF16)
-        low = (matrix - high.astype(F32)).astype(BF16)
+        high = rows_high[0, h * ROWS : (h + 1) * ROWS]
+        low = rows_low[0, h * ROWS : (h + 1) * ROWS]
         rows = slice(h * ROWS, h * ROWS + WINDOW)
         first = jnp.concatenate([matched_terms[0, rows], empty], axis=0)
         second = jnp.concatenate([matched_terms[1, rows], empty], axis=0)
@@ -252,23 +295,11 @@
         halves.append(both + jnp.dot(low, first, preferred_element_type=F32))
     warped = jnp.concatenate(halves, axis=0)
 
-    lanes = iota((8, WIDTH), 1)
-    step = iota((8, WIDTH), 0) - WARP
-    block = lanes // LANES
-    carry = (block + step + LANE_BLOCKS) // LANE_BLOCKS - 1
-    from_lane = lanes % LANES - carry
-    col = (from_lane * LANE_BLOCKS + block).astype(F32)
-    col_shift = a[1, 0:1] + a[1, 1:2] * (col - (WIDTH - 1) / 2.0) / WIDTH
-    within = (from_lane >= 0) & (from_lane < LANES) & (step <= WARP)
-    cols = jnp.where(within, lanczos(col_shift - step.astype(F32)), 0.0)
+    cols = col_weights[0]
     blocks = lane_sum(
         lambda s, v, w: lane_block(cols[s : s + 1], v) * lane_block(warped, w),
         lane, 2 * WARP + 1, True,
     )
-
-    @pl.when(visit == 0)
-    def _():
-        unsort_copy.wait()
 
     result = jnp.dot(
         jnp.concatenate(blocks, axis=1).astype(BF16), unsort[...], preferred_element_type=F32
@@ -303,13 +334,11 @@
             pltpu.make_async_copy(ready.at[block], out.at[0, pl.ds(0, BLOCK)], sem.at[block]).wait()
 
 
-def warp(patch, slot, owner, weight, taps, psf, affine, images, above, below, devices):
+def warp(patch, slot, owner, weight, ready, images, above, below, devices):
     smem = pl.BlockSpec(memory_space=pltpu.SMEM)
     hbm = pl.BlockSpec(memory_space=pl.ANY)
     sort = deinterleave()
-    taps = taps.transpose(1, 0, 2)
-    psf = psf.transpose(1, 3, 0, 2)
-    affine = affine.transpose(0, 2, 3, 1)
+    constants = [jnp.asarray(sort, BF16), jnp.asarray(sort.T, BF16)]
 
     def whole(x):
         return pl.BlockSpec(x.shape, lambda v: (0,) * x.ndim)
@@ -320,26 +349,20 @@
     return pl.pallas_call(
         warp_kernel,
         grid=(V,),
-        in_specs=[smem, smem, smem, whole(weight), whole(taps), whole(psf), whole(affine)]
-        + [hbm, hbm, by_visit(images), by_visit(above), by_visit(below)],
+        in_specs=[smem, smem, smem, whole(weight)]
+        + [by_visit(x) for x in ready]
+        + [whole(x) for x in constants]
+        + [by_visit(x) for x in (images, above, below)],
         out_specs=hbm,
         scratch_shapes=[
-            pltpu.VMEM((NBASIS, BAND), F32),
-            pltpu.VMEM((STRIP, NBASIS), F32),
-            pltpu.VMEM((TAPS * STRIP, LANES), F32),
-            pltpu.VMEM((TAPS * STRIP, LANES), F32),
-            pltpu.VMEM((TAPS * STRIP, BAND - LANES), BF16),
             pltpu.VMEM((4, TALL, WIDTH), BF16),
             pltpu.VMEM((2, STRIPS * STRIP, WIDTH), BF16),
             pltpu.VMEM((V * BLKC, BLOCK, BLOCK), BF16),
             pltpu.SMEM((owner.shape[0],), jnp.int32),
             pltpu.VMEM((devices, LANES), F32),
             pltpu.VMEM((devices, LABEL, LANES), BF16),
-            pltpu.VMEM((WIDTH, WIDTH), BF16),
-            pltpu.VMEM((WIDTH, WIDTH), BF16),
             pltpu.SemaphoreType.DMA((V * BLKC,)),
             pltpu.SemaphoreType.DMA(()),
-            pltpu.SemaphoreType.DMA((2,)),
         ],
         out_shape=jax.ShapeDtypeStruct((devices, CAP * BLOCK + LABEL, BLOCK), BF16),
         compiler_params=pltpu.CompilerParams(vmem_limit_bytes=32 << 20),
@@ -349,10 +372,7 @@
             transcendentals=0,
         ),
         name="match_warp",
-    )(
-        patch, slot, owner, weight, taps, psf, affine,
-        jnp.asarray(sort, BF16), jnp.asarray(sort.T, BF16), images, above, below,
-    )
+    )(patch, slot, owner, weight, *ready, *constants, images, above, below)
 
 
 def coadd_kernel(got, out, total, table, numbers, sums, sem, out_sem):
@@ -420,9 +440,9 @@
     above = lax.ppermute(images[:, BLOCK - RIM :], "ccd", down)
     below = lax.ppermute(images[:, :RIM], "ccd", up)
     patch = block_patch[:, :, 0]
+    ready = prepare(basis_taps, psf_coef, affine, devices)
     sent = warp(
-        patch, block_slot, patch_owner, visit_weight, basis_taps, psf_coef, affine,
-        images, above, below, devices,
+        patch, block_slot, patch_owner, visit_weight, ready, images, above, below, devices
     )
     got = lax.all_to_all(sent, "ccd", split_axis=0, concat_axis=0, tiled=True)
     return coadd(got)

time: 65.2 us -> 55.4 us (0.85)
  local copies, waits for them, and re-layouts: 8.98 us -> 3.43 us
  blocking collectives: 38.8 us -> 36.3 us
  waiting for transfers between devices: 0.87 us -> 0.01 us
  Pallas kernels: 11.6 us -> 10.9 us
    unnamed x20, local copies, waits for them, and re-layouts: 8.1 us -> 2.55 us
    all_to_all x1, blocking collectives: 38.8 us -> 36.3 us  [shards(): got = lax.all_to_all(sent, 'ccd', split_axis=0, concat_axis=0, tiled=True)]
    pallas_call x1, Pallas kernels: 9.34 us -> 7.4 us  [warp(): pl.pallas_call(warp_kernel, grid=(V,), in_specs=[smem, smem, smem, whole(...]
    pallas_call x0 -> x1, Pallas kernels: none -> 1.11 us  [prepare(): pl.pallas_call(functools.partial(prepare_kernel, devices), grid=(1,), in_...]
    ppermute x1, waiting for transfers between devices: 0.87 us -> 0.01 us  [shards(): above = lax.ppermute(images[:, BLOCK - RIM:], 'ccd', down)]
  transfers between devices with their start and end apart: 2 -> 2, of which waited for: 1 -> 0; matrix products, arithmetic and copies ran while one was open for 0% -> 0% of each run, Pallas kernels for 0% -> 2%
where the time goes in v6:
time: 55.4 us; the launch traced here: 55.1 us
  blocking collectives  36.3 us (66%)
  Pallas kernels  10.9 us (20%)
  starting transfers between devices  4.33 us (8%)
  local copies, waits for them, and re-layouts  3.43 us (6%)
    all_to_all x1, blocking collectives, shards(): got = lax.all_to_all(sent, 'ccd', split_axis=0, concat_axis=0, tiled=True)  36.3 us
    pallas_call x1, Pallas kernels, warp(): pl.pallas_call(warp_kernel, grid=(V,), in_specs=[smem, smem, smem, whole(...  7.4 us
    ppermute x1, starting transfers between devices, shards(): above = lax.ppermute(images[:, BLOCK - RIM:], 'ccd', down)  3.03 us
    unnamed x20, local copies, waits for them, and re-layouts  2.55 us
    pallas_call x1, Pallas kernels, coadd(): pl.pallas_call(coadd_kernel, in_specs=[pl.BlockSpec(memory_space=pltpu.VM...  2.44 us
    ppermute x1, starting transfers between devices, shards(): below = lax.ppermute(images[:, :RIM], 'ccd', up)  1.29 us
    pallas_call x1, Pallas kernels, prepare(): pl.pallas_call(functools.partial(prepare_kernel, devices), grid=(1,), in_...  1.11 us
  transfers between devices with their start and end apart: 2, of which 0 were waited for; matrix products, arithmetic and copies ran while one was open for 0% of the time, Pallas kernels for 2%

profile of v6, /device:TPU:0, one launch (start us, length us, event | category | flops | bytes accessed | tf_op | source)
XLA Modules:
  0.0 55.1 jit_solution(8172405336367377650)
XLA Ops:
  0.0 0.9 %fusion = (f32[4,8,512]{2,1,0:T(8,128)S(1)}, f32[4,8,512]{2,1,0:T(8,128)S(1)}) fusion(f32[4,128,512]{2,1,0:T(8,128)} %image.1), kind=kLoop, calls=%fused_computation | loop fusion | bytes 262144 | tf_op jit(solution)/shard_map/slice | solution.py:441
  0.9 1.3 %collective-permute-start.1 = (f32[4,8,512]{2,1,0:T(8,128)S(1)}, f32[4,8,512]{2,1,0:T(8,128)S(1)}, u32[]{:S(2)}, u32[]{:S(2)}) collective-permute-start(f32[4,8,512]{2,1,0:T(8,128)S(1)} %get-tuple-element.17), channel_id=1, source_target_pairs={{1,0},{2,1},{3,2},{4,3},{5,4},{6,5},{7,6},{8,7},{9,8},{10,9},{11,1... | collective-permute-start | bytes 196616 | tf_op jit(solution)/shard_map/ppermute | solution.py:441
  2.2 3.0 %collective-permute-start = (f32[4,8,512]{2,1,0:T(8,128)S(1)}, f32[4,8,512]{2,1,0:T(8,128)S(1)}, u32[]{:S(2)}, u32[]{:S(2)}) collective-permute-start(f32[4,8,512]{2,1,0:T(8,128)S(1)} %get-tuple-element.18), channel_id=1, source_target_pairs={{0,1},{1,2},{2,3},{3,4},{4,5},{5,6},{6,7},{7,8},{8,9},{9,10},{10,1... | collective-permute-start | bytes 196616 | tf_op jit(solution)/shard_map/ppermute | solution.py:440
  5.2 0.0 copy-start.1
  5.2 0.7 %copy-done.1 = f32[4,5,9,3]{2,0,3,1:T(4,128)S(1)} copy-done((f32[4,5,9,3]{2,0,3,1:T(4,128)S(1)}, f32[4,5,9,3]{2,0,3,1:T(4,128)}, u32[]{:S(2)}) %copy-start.1) | copy-done | bytes 2184
  6.0 0.0 copy-start.2
  6.0 0.7 %copy-done.2 = f32[2,9,11]{2,0,1:T(2,128)S(1)} copy-done((f32[2,9,11]{2,0,1:T(2,128)S(1)}, f32[2,9,11]{2,0,1:T(2,128)}, u32[]{:S(2)}) %copy-start.2) | copy-done | bytes 816
  6.7 0.0 copy-start.3
  6.7 0.7 %copy-done.3 = f32[4,5,2,2]{1,3,2,0:T(2,128)S(1)} copy-done((f32[4,5,2,2]{1,3,2,0:T(2,128)S(1)}, f32[4,5,2,2]{1,3,2,0:T(2,128)}, u32[]{:S(2)}) %copy-start.3) | copy-done | bytes 344
  7.4 0.0 copy-start
  7.4 0.0 copy-start.4
  7.4 0.0 copy-start.5
  7.4 0.0 copy-start.6
  7.4 0.0 copy-start.7
  7.4 0.0 copy-start.8
  7.4 0.0 copy-start.9
  7.4 1.1 %prepare.1 = (f32[4,176,128]{2,1,0:T(8,128)S(1)}, f32[4,176,128]{2,1,0:T(8,128)S(1)}, bf16[4,176,128]{2,1,0:T(8,128)(2,1)S(1)}, bf16[4,128,128]{2,1,0:T(8,128)(2...) custom-call(f32[9,2,11]{2,1,0:T(2,128)S(1)} %bitcast.5, f32[5,3,4,9]{3,2,1,0:T(4,128)S(1)} %bitcast.4, ...), custom_call_target="tpu_custom_call" | custom-call | flops 1073741824 | bytes 1048576 | tf_op jit(solution)/shard_map/prepare/pallas_call | solution.py:212
  8.5 0.0 collective-permute-done.1.below
  8.6 0.0 collective-permute-done.above
  8.6 0.0 copy-done
  8.6 0.0 copy-done.4
  8.6 0.0 copy-done.5
  8.6 0.0 copy-done.6
  8.6 0.0 copy-done.7
  8.6 0.2 copy-done.8
  8.8 0.2 copy-done.9
  9.0 7.4 %match_warp.1 = bf16[16,272,128]{2,1,0:T(8,128)(2,1)S(1)} custom-call(s32[1,16]{1,0:T(1,128)S(1)} %bitcast.7, s32[1,16]{1,0:T(1,128)S(1)} %copy-done.6, s32[16]{0:T(128)S(1)} %copy-done.7, bf16[4,5]{1,0:T(4,128)(2,1)S(1)} %copy-done.4, f32[4,176,128]{2,1,0:T(8,128)S(1)} %get-tuple-element.11.high_level, f32[4,176,128]{2,1,0:T(8,128)S(1)} %get-tuple-element.12.step_level, ...), custom_call_target="tpu_custom_call" | custom-call | flops 1660944384 | bytes 1572864 | tf_op jit(solution)/shard_map/match_warp/pallas_call | solution.py:349
  16.4 36.3 %all_to_all.5.got = bf16[16,272,128]{2,1,0:T(8,128)(2,1)S(1)} all-to-all(bf16[16,272,128]{2,1,0:T(8,128)(2,1)S(1)} %match_warp.1), channel_id=1, replica_groups=mesh['group'=2,'ccd'=16] {'ccd'}, dimensions={0} | all-to-all | bytes 2228224 | tf_op jit(solution)/shard_map/all_to_all | solution.py:447
  52.7 2.4 %coadd.1 = f32[1,512,512]{2,1,0:T(8,128)} custom-call(bf16[16,272,128]{2,1,0:T(8,128)(2,1)S(1)} %all_to_all.5.got), custom_call_target="tpu_custom_call" | custom-call | tf_op jit(solution)/shard_map/coadd/pallas_call | solution.py:416
Async XLA Ops:
  0.9 7.7 %collective-permute-start.1 = (f32[4,8,512]{2,1,0:T(8,128)S(1)}, f32[4,8,512]{2,1,0:T(8,128)S(1)}, u32[]{:S(2)}, u32[]{:S(2)}) collective-permute-start(f32[4,8,512]{2,1,0:T(8,128)S(1)} %get-tuple-element.17), channel_id=1, source_target_pairs={{1,0},{2,1},{3,2},{4,3},{5,4},{6,5},{7,6},{8,7},{9,8},{10,9},{11,1... | collective-permute-start | bytes 196616 | tf_op jit(solution)/shard_map/ppermute | solution.py:441
  2.2 6.4 %collective-permute-start = (f32[4,8,512]{2,1,0:T(8,128)S(1)}, f32[4,8,512]{2,1,0:T(8,128)S(1)}, u32[]{:S(2)}, u32[]{:S(2)}) collective-permute-start(f32[4,8,512]{2,1,0:T(8,128)S(1)} %get-tuple-element.18), channel_id=1, source_target_pairs={{0,1},{1,2},{2,3},{3,4},{4,5},{5,6},{6,7},{7,8},{8,9},{9,10},{10,1... | collective-permute-start | bytes 196616 | tf_op jit(solution)/shard_map/ppermute | solution.py:440
  5.2 0.8 %copy-start.1 = (f32[4,5,9,3]{2,0,3,1:T(4,128)S(1)}, f32[4,5,9,3]{2,0,3,1:T(4,128)}, u32[]{:S(2)}) copy-start(f32[4,5,9,3]{2,0,3,1:T(4,128)} %param.12) | copy-start | bytes 6484
  6.0 0.7 %copy-start.2 = (f32[2,9,11]{2,0,1:T(2,128)S(1)}, f32[2,9,11]{2,0,1:T(2,128)}, u32[]{:S(2)}) copy-start(f32[2,9,11]{2,0,1:T(2,128)} %param.11) | copy-start | bytes 2380
  6.7 0.7 %copy-start.3 = (f32[4,5,2,2]{1,3,2,0:T(2,128)S(1)}, f32[4,5,2,2]{1,3,2,0:T(2,128)}, u32[]{:S(2)}) copy-start(f32[4,5,2,2]{1,3,2,0:T(2,128)} %param.13) | copy-start | bytes 964
  7.4 1.2 %copy-start = (f32[4,128,512]{2,1,0:T(8,128)S(1)}, f32[4,128,512]{2,1,0:T(8,128)}, u32[]{:S(2)}) copy-start(f32[4,128,512]{2,1,0:T(8,128)} %image.1) | copy-start | bytes 3145732
  7.4 1.2 %copy-start.4 = (bf16[4,5]{1,0:T(4,128)(2,1)S(1)}, bf16[4,5]{1,0:T(4,128)(2,1)}, u32[]{:S(2)}) copy-start(bf16[4,5]{1,0:T(4,128)(2,1)} %weight.1) | copy-start | bytes 124
  7.4 1.2 %copy-start.5 = (s32[1,16,1]{1,2,0:T(1,128)S(1)}, s32[1,16,1]{1,2,0:T(1,128)}, u32[]{:S(2)}) copy-start(s32[1,16,1]{1,2,0:T(1,128)} %param.15) | copy-start | bytes 196
  7.4 1.2 %copy-start.6 = (s32[1,16]{1,0:T(1,128)S(1)}, s32[1,16]{1,0:T(1,128)}, u32[]{:S(2)}) copy-start(s32[1,16]{1,0:T(1,128)} %slot.1) | copy-start | bytes 196
  7.4 1.2 %copy-start.7 = (s32[16]{0:T(128)S(1)}, s32[16]{0:T(128)}, u32[]{:S(2)}) copy-start(s32[16]{0:T(128)} %owner.1) | copy-start | bytes 196
  7.4 1.4 %copy-start.8 = (bf16[512,512]{1,0:T(8,128)(2,1)S(1)}, bf16[512,512]{1,0:T(8,128)(2,1)}, u32[]{:S(2)}) copy-start(bf16[512,512]{1,0:T(8,128)(2,1)} %constant.5.clone.unsort) | copy-start | bytes 1572868
  7.4 1.5 %copy-start.9 = (bf16[512,512]{1,0:T(8,128)(2,1)S(1)}, bf16[512,512]{1,0:T(8,128)(2,1)}, u32[]{:S(2)}) copy-start(bf16[512,512]{1,0:T(8,128)(2,1)} %constant.4.clone.sort) | copy-start | bytes 1572868

commit v7 on v6

--- a/solution.py
+++ b/solution.py
@@ -33,6 +33,7 @@
 BAND = 256
 TALL = (STRIPS - 1) * STRIP + STEP
 HALVES = 2
+TOGETHER = 2
 ROWS = BLOCK // HALVES
 WINDOW = ROWS + STRIP
 LABEL = 16
@@ -224,18 +225,19 @@
 def warp_kernel(
     patch, slot, owner, weight, high_level, step_level, slope, rows_high, rows_low, col_weights,
     sort, unsort, image, above, below, out,
-    terms, matched_terms, ready, seen, label, label_ready, sem, label_sem,
+    terms, matched_terms, ready, place_of, seen, label, label_ready, sem, label_sem,
 ):
-    visit = pl.program_id(0)
-    visits = pl.num_programs(0)
+    grid_step = pl.program_id(0)
+    grid_steps = pl.num_programs(0)
     devices = label.shape[0]
     ccd, _, has_above, has_below = whereabouts(devices)
     tall = BLOCK + 2 * RIM
     lane = iota((1, LANES), 1)
-
-    @pl.when(visit == 0)
+    label_copy = pltpu.make_async_copy(label_ready, out.at[:, pl.ds(CAP * BLOCK, LABEL)], label_sem)
+
+    @pl.when(grid_step == 0)
     def _():
-        terms[:, tall:] = jnp.zeros((4, TALL - tall, WIDTH), BF16)
+        terms[:, :, tall:] = jnp.zeros((TOGETHER, 4, TALL - tall, WIDTH), BF16)
         label[...] = jnp.zeros_like(label)
 
         def clear(p, _):
@@ -243,93 +245,102 @@
             return 0
 
         lax.fori_loop(0, owner.shape[0], clear, 0)
-
-    col_pos = (2.0 * column_at(iota((1, WIDTH), 1)).astype(F32) + 1.0) / WIDTH - 1.0
-    raw = jnp.concatenate(
-        [jnp.where(has_above, above[0], 0.0), image[0], jnp.where(has_below, below[0], 0.0)],
-        axis=0,
-    )
-    raw_high = raw.astype(BF16)
-    raw_low = (raw - raw_high.astype(F32)).astype(BF16)
-    sorted_terms = jnp.dot(
-        jnp.concatenate([raw_high, raw_low], axis=0), sort[...], preferred_element_type=F32
-    )
-    high, low = sorted_terms[:tall], sorted_terms[tall:]
-    tilted = (high + low) * col_pos
-    tilted_high = tilted.astype(BF16)
-    terms[0, :tall] = high.astype(BF16)
-    terms[1, :tall] = low.astype(BF16)
-    terms[2, :tall] = tilted_high
-    terms[3, :tall] = (tilted - tilted_high.astype(F32)).astype(BF16)
-
-    filler = jnp.zeros((BAND - GROUPS * STEP, WIDTH), BF16)
-    for k in range(STRIPS):
-        level = high_level[0]
-        if k != MIDDLE:
-            level = level + float(k - MIDDLE) * step_level[0]
-        matrix = jnp.concatenate([level.astype(BF16), slope[0]], axis=1)
-        rows = slice(k * STRIP, k * STRIP + STEP)
-        columns = jnp.concatenate([terms[h, rows] for h in (0, 1, 0, 2, 3, 2)] + [filler], axis=0)
-        results = jnp.dot(matrix, columns, preferred_element_type=F32)
-        blocks = lane_sum(
-            lambda u, v, w: lane_block(results[u * STRIP : (u + 1) * STRIP], w), lane, TAPS, False
-        )
-        matched = jnp.concatenate(blocks, axis=1)
-        high = matched.astype(BF16)
-        at = slice(k * STRIP, (k + 1) * STRIP)
-        matched_terms[0, at] = high
-        matched_terms[1, at] = (matched - high.astype(F32)).astype(BF16)
-
-    empty = jnp.zeros((LANES - WINDOW, WIDTH), BF16)
-    halves = []
-    for h in range(HALVES):
-        high = rows_high[0, h * ROWS : (h + 1) * ROWS]
-        low = rows_low[0, h * ROWS : (h + 1) * ROWS]
-        rows = slice(h * ROWS, h * ROWS + WINDOW)
-        first = jnp.concatenate([matched_terms[0, rows], empty], axis=0)
-        second = jnp.concatenate([matched_terms[1, rows], empty], axis=0)
-        both = jnp.dot(
-            jnp.concatenate([high, high], axis=1), jnp.concatenate([first, second], axis=0),
-            preferred_element_type=F32,
-        )
-        halves.append(both + jnp.dot(low, first, preferred_element_type=F32))
-    warped = jnp.concatenate(halves, axis=0)
-
-    cols = col_weights[0]
-    blocks = lane_sum(
-        lambda s, v, w: lane_block(cols[s : s + 1], v) * lane_block(warped, w),
-        lane, 2 * WARP + 1, True,
-    )
-
-    result = jnp.dot(
-        jnp.concatenate(blocks, axis=1).astype(BF16), unsort[...], preferred_element_type=F32
-    ).astype(BF16)
-
-    own = jnp.where(iota(weight.shape, 1) == ccd, weight[...].astype(F32), 0.0)
-    own = jnp.where(iota(weight.shape, 0) == visit, own, 0.0)
-    own = jnp.sum(own, axis=(0, 1), keepdims=True)
-    for j in range(BLKC):
-        block = visit * BLKC + j
-        ready[block] = result[:, j * BLOCK : (j + 1) * BLOCK]
-        p = patch[0, block]
-        rank = seen[p]
-        seen[p] = rank + 1
-        to = out.at[owner[p], pl.ds(pl.multiple_of(rank * BLOCK, BLOCK), BLOCK)]
-        pltpu.make_async_copy(ready.at[block], to, sem.at[block]).start()
-        line = label[pl.ds(owner[p], 1), :]
-        line = jnp.where(lane == rank * 2, own, line)
-        label[pl.ds(owner[p], 1), :] = jnp.where(
-            lane == rank * 2 + 1, slot[0, block].astype(F32), line
-        )
-
-    @pl.when(visit == visits - 1)
-    def _():
+        own = jnp.where(iota(weight.shape, 1) == ccd, weight[...].astype(F32), 0.0)
+        own = jnp.sum(own, axis=1, keepdims=True)
+        for block in range(V * BLKC):
+            p = patch[0, block]
+            to = owner[p]
+            rank = seen[p]
+            seen[p] = rank + 1
+            place_of[block] = to * CAP + rank
+            line = label[pl.ds(to, 1), :]
+            line = jnp.where(lane == rank * 2, own[block // BLKC : block // BLKC + 1], line)
+            line = jnp.where(lane == rank * 2 + 1, slot[0, block].astype(F32), line)
+            label[pl.ds(to, 1), :] = line
         label_ready[...] = jnp.broadcast_to(
             label[...].reshape(devices, 1, LANES), (devices, LABEL, LANES)
         ).astype(BF16)
-        copy = pltpu.make_async_copy(label_ready, out.at[:, pl.ds(CAP * BLOCK, LABEL)], label_sem)
-        copy.start()
-        copy.wait()
+        label_copy.start()
+
+    col_pos = (2.0 * column_at(iota((1, WIDTH), 1)).astype(F32) + 1.0) / WIDTH - 1.0
+    for i in range(TOGETHER):
+        raw = jnp.concatenate(
+            [jnp.where(has_above, above[i], 0.0), image[i], jnp.where(has_below, below[i], 0.0)],
+            axis=0,
+        )
+        raw_high = raw.astype(BF16)
+        raw_low = (raw - raw_high.astype(F32)).astype(BF16)
+        sorted_terms = jnp.dot(
+            jnp.concatenate([raw_high, raw_low], axis=0), sort[...], preferred_element_type=F32
+        )
+        high, low = sorted_terms[:tall], sorted_terms[tall:]
+        tilted = (high + low) * col_pos
+        tilted_high = tilted.astype(BF16)
+        terms[i, 0, :tall] = high.astype(BF16)
+        terms[i, 1, :tall] = low.astype(BF16)
+        terms[i, 2, :tall] = tilted_high
+        terms[i, 3, :tall] = (tilted - tilted_high.astype(F32)).astype(BF16)
+
+    filler = jnp.zeros((BAND - GROUPS * STEP, WIDTH), BF16)
+    for k in range(STRIPS):
+        for i in range(TOGETHER):
+            level = high_level[i]
+            if k != MIDDLE:
+                level = level + float(k - MIDDLE) * step_level[i]
+            matrix = jnp.concatenate([level.astype(BF16), slope[i]], axis=1)
+            rows = slice(k * STRIP, k * STRIP + STEP)
+            columns = jnp.concatenate(
+                [terms[i, h, rows] for h in (0, 1, 0, 2, 3, 2)] + [filler], axis=0
+            )
+            results = jnp.dot(matrix, columns, preferred_element_type=F32)
+            blocks = lane_sum(
+                lambda u, v, w: lane_block(results[u * STRIP : (u + 1) * STRIP], w),
+                lane, TAPS, False,
+            )
+            matched = jnp.concatenate(blocks, axis=1)
+            high = matched.astype(BF16)
+            at = slice(k * STRIP, (k + 1) * STRIP)
+            matched_terms[i, 0, at] = high
+            matched_terms[i, 1, at] = (matched - high.astype(F32)).astype(BF16)
+
+    empty = jnp.zeros((LANES - WINDOW, WIDTH), BF16)
+    warped = []
+    for i in range(TOGETHER):
+        halves = []
+        for h in range(HALVES):
+            high = rows_high[i, h * ROWS : (h + 1) * ROWS]
+            low = rows_low[i, h * ROWS : (h + 1) * ROWS]
+            rows = slice(h * ROWS, h * ROWS + WINDOW)
+            first = jnp.concatenate([matched_terms[i, 0, rows], empty], axis=0)
+            second = jnp.concatenate([matched_terms[i, 1, rows], empty], axis=0)
+            both = jnp.dot(
+                jnp.concatenate([high, high], axis=1), jnp.concatenate([first, second], axis=0),
+                preferred_element_type=F32,
+            )
+            halves.append(both + jnp.dot(low, first, preferred_element_type=F32))
+        warped.append(jnp.concatenate(halves, axis=0))
+
+    for i in range(TOGETHER):
+        cols = col_weights[i]
+        blocks = lane_sum(
+            lambda s, v, w: lane_block(cols[s : s + 1], v) * lane_block(warped[i], w),
+            lane, 2 * WARP + 1, True,
+        )
+        result = jnp.dot(
+            jnp.concatenate(blocks, axis=1).astype(BF16), unsort[...], preferred_element_type=F32
+        ).astype(BF16)
+        for j in range(BLKC):
+            block = (grid_step * TOGETHER + i) * BLKC + j
+            ready[block] = result[:, j * BLOCK : (j + 1) * BLOCK]
+            to = place_of[block]
+            row = pl.multiple_of(to % CAP * BLOCK, BLOCK)
+            pltpu.make_async_copy(
+                ready.at[block], out.at[to // CAP, pl.ds(row, BLOCK)], sem.at[block]
+            ).start()
+
+    @pl.when(grid_step == grid_steps - 1)
+    def _():
+        label_copy.wait()
         for block in range(V * BLKC):
             pltpu.make_async_copy(ready.at[block], out.at[0, pl.ds(0, BLOCK)], sem.at[block]).wait()
 
@@ -344,20 +355,21 @@
         return pl.BlockSpec(x.shape, lambda v: (0,) * x.ndim)
 
     def by_visit(x):
-        return pl.BlockSpec((1,) + x.shape[1:], lambda v: (v, 0, 0))
+        return pl.BlockSpec((TOGETHER,) + x.shape[1:], lambda v: (v, 0, 0))
 
     return pl.pallas_call(
         warp_kernel,
-        grid=(V,),
+        grid=(V // TOGETHER,),
         in_specs=[smem, smem, smem, whole(weight)]
         + [by_visit(x) for x in ready]
         + [whole(x) for x in constants]
         + [by_visit(x) for x in (images, above, below)],
         out_specs=hbm,
         scratch_shapes=[
-            pltpu.VMEM((4, TALL, WIDTH), BF16),
-            pltpu.VMEM((2, STRIPS * STRIP, WIDTH), BF16),
+            pltpu.VMEM((TOGETHER, 4, TALL, WIDTH), BF16),
+            pltpu.VMEM((TOGETHER, 2, STRIPS * STRIP, WIDTH), BF16),
             pltpu.VMEM((V * BLKC, BLOCK, BLOCK), BF16),
+            pltpu.SMEM((V * BLKC,), jnp.int32),
             pltpu.SMEM((owner.shape[0],), jnp.int32),
             pltpu.VMEM((devices, LANES), F32),
             pltpu.VMEM((devices, LABEL, LANES), BF16),
@@ -375,30 +387,23 @@
     )(patch, slot, owner, weight, *ready, *constants, images, above, below)
 
 
-def coadd_kernel(got, out, total, table, numbers, sums, sem, out_sem):
+def coadd_kernel(got, out, total, sums, out_sem):
     devices = got.shape[0]
-    table[...] = got[:, CAP * BLOCK : CAP * BLOCK + LABEL].astype(F32)[:, 0]
-    copy = pltpu.make_async_copy(table, numbers, sem)
-    copy.start()
+    labels = got[:, CAP * BLOCK : CAP * BLOCK + LABEL].astype(F32)[:, 0]
     total[...] = jnp.zeros_like(total)
     for c in range(CELLS):
         sums[c] = 0.0
-    copy.wait()
-
-    def add(source, _):
+    for source in range(devices):
         for rank in range(CAP):
-            weight = numbers[source, rank * 2]
+            weight = labels[source, rank * 2]
 
             @pl.when(weight > 0.0)
-            def _(rank=rank, weight=weight):
-                c = numbers[source, rank * 2 + 1].astype(jnp.int32)
+            def _(source=source, rank=rank, weight=weight):
+                c = labels[source, rank * 2 + 1].astype(jnp.int32)
                 sums[c] += weight
                 rows = slice(rank * BLOCK, (rank + 1) * BLOCK)
                 total[c] += weight * got[source, rows].astype(F32)
 
-        return 0
-
-    lax.fori_loop(0, devices, add, 0, unroll=4)
     copies = []
     for c in range(CELLS):
         inverse = 1.0 / jnp.maximum(jnp.full((1, BLOCK), sums[c], F32), 1.0)
@@ -412,7 +417,6 @@
 
 
 def coadd(got):
-    devices = got.shape[0]
     return pl.pallas_call(
         coadd_kernel,
         in_specs=[pl.BlockSpec(memory_space=pltpu.VMEM)],
@@ -420,10 +424,7 @@
         out_shape=jax.ShapeDtypeStruct((1, PSIDE * BLOCK, PSIDE * BLOCK), F32),
         scratch_shapes=[
             pltpu.VMEM((CELLS, BLOCK, BLOCK), F32),
-            pltpu.VMEM((devices, LANES), F32),
-            pltpu.SMEM((devices, LANES), F32),
             pltpu.SMEM((CELLS,), F32),
-            pltpu.SemaphoreType.DMA(()),
             pltpu.SemaphoreType.DMA((CELLS,)),
         ],
         compiler_params=pltpu.CompilerParams(vmem_limit_bytes=32 << 20),

time: 55.4 us -> 57.9 us (1.045); the launches traced: 55.1 us -> 57 us
  Pallas kernels: 10.9 us -> 12.9 us
    pallas_call x1, Pallas kernels: 2.44 us -> 5.19 us  [coadd(): pl.pallas_call(coadd_kernel, in_specs=[pl.BlockSpec(memory_space=pltpu.VM...]
    pallas_call x1, Pallas kernels: 7.4 us -> 6.56 us  [warp(): pl.pallas_call(warp_kernel, grid=(V // TOGETHER,), in_specs=[smem, smem,...]
where the time goes in v7:
time: 57.9 us; the launch traced here: 57 us
  blocking collectives  36.3 us (63%)
  Pallas kernels  12.9 us (22%)
  starting transfers between devices  4.33 us (7%)
  local copies, waits for them, and re-layouts  3.43 us (6%)
    all_to_all x1, blocking collectives, shards(): got = lax.all_to_all(sent, 'ccd', split_axis=0, concat_axis=0, tiled=True)  36.3 us
    pallas_call x1, Pallas kernels, warp(): pl.pallas_call(warp_kernel, grid=(V // TOGETHER,), in_specs=[smem, smem,...  6.56 us
    pallas_call x1, Pallas kernels, coadd(): pl.pallas_call(coadd_kernel, in_specs=[pl.BlockSpec(memory_space=pltpu.VM...  5.19 us
    ppermute x1, starting transfers between devices, shards(): above = lax.ppermute(images[:, BLOCK - RIM:], 'ccd', down)  3.03 us
    unnamed x20, local copies, waits for them, and re-layouts  2.55 us
    ppermute x1, starting transfers between devices, shards(): below = lax.ppermute(images[:, :RIM], 'ccd', up)  1.29 us
  transfers between devices with their start and end apart: 2, of which 0 were waited for; matrix products, arithmetic and copies ran while one was open for 0% of the time, Pallas kernels for 2%

profile of v7, /device:TPU:0, one launch (start us, length us, event | category | flops | bytes accessed | tf_op | source)
XLA Modules:
  0.0 57.0 jit_solution(16508986329560981785)
XLA Ops:
  0.0 0.9 %fusion = (f32[4,8,512]{2,1,0:T(8,128)S(1)}, f32[4,8,512]{2,1,0:T(8,128)S(1)}) fusion(f32[4,128,512]{2,1,0:T(8,128)} %image.1), kind=kLoop, calls=%fused_computation | loop fusion | bytes 262144 | tf_op jit(solution)/shard_map/slice | solution.py:442
  0.9 1.3 %collective-permute-start.1 = (f32[4,8,512]{2,1,0:T(8,128)S(1)}, f32[4,8,512]{2,1,0:T(8,128)S(1)}, u32[]{:S(2)}, u32[]{:S(2)}) collective-permute-start(f32[4,8,512]{2,1,0:T(8,128)S(1)} %get-tuple-element.17), channel_id=1, source_target_pairs={{1,0},{2,1},{3,2},{4,3},{5,4},{6,5},{7,6},{8,7},{9,8},{10,9},{11,1... | collective-permute-start | bytes 196616 | tf_op jit(solution)/shard_map/ppermute | solution.py:442
  2.2 3.0 %collective-permute-start = (f32[4,8,512]{2,1,0:T(8,128)S(1)}, f32[4,8,512]{2,1,0:T(8,128)S(1)}, u32[]{:S(2)}, u32[]{:S(2)}) collective-permute-start(f32[4,8,512]{2,1,0:T(8,128)S(1)} %get-tuple-element.18), channel_id=1, source_target_pairs={{0,1},{1,2},{2,3},{3,4},{4,5},{5,6},{6,7},{7,8},{8,9},{9,10},{10,1... | collective-permute-start | bytes 196616 | tf_op jit(solution)/shard_map/ppermute | solution.py:441
  5.2 0.0 copy-start.1
  5.2 0.7 %copy-done.1 = f32[4,5,9,3]{2,0,3,1:T(4,128)S(1)} copy-done((f32[4,5,9,3]{2,0,3,1:T(4,128)S(1)}, f32[4,5,9,3]{2,0,3,1:T(4,128)}, u32[]{:S(2)}) %copy-start.1) | copy-done | bytes 2184
  6.0 0.0 copy-start.2
  6.0 0.7 %copy-done.2 = f32[2,9,11]{2,0,1:T(2,128)S(1)} copy-done((f32[2,9,11]{2,0,1:T(2,128)S(1)}, f32[2,9,11]{2,0,1:T(2,128)}, u32[]{:S(2)}) %copy-start.2) | copy-done | bytes 816
  6.7 0.0 copy-start.3
  6.7 0.7 %copy-done.3 = f32[4,5,2,2]{1,3,2,0:T(2,128)S(1)} copy-done((f32[4,5,2,2]{1,3,2,0:T(2,128)S(1)}, f32[4,5,2,2]{1,3,2,0:T(2,128)}, u32[]{:S(2)}) %copy-start.3) | copy-done | bytes 344
  7.4 0.0 copy-start
  7.4 0.0 copy-start.4
  7.4 0.0 copy-start.5
  7.4 0.0 copy-start.6
  7.4 0.0 copy-start.7
  7.4 0.0 copy-start.8
  7.4 0.0 copy-start.9
  7.4 1.1 %prepare.1 = (f32[4,176,128]{2,1,0:T(8,128)S(1)}, f32[4,176,128]{2,1,0:T(8,128)S(1)}, bf16[4,176,128]{2,1,0:T(8,128)(2,1)S(1)}, bf16[4,128,128]{2,1,0:T(8,128)(2...) custom-call(f32[9,2,11]{2,1,0:T(2,128)S(1)} %bitcast.5, f32[5,3,4,9]{3,2,1,0:T(4,128)S(1)} %bitcast.4, ...), custom_call_target="tpu_custom_call" | custom-call | flops 1073741824 | bytes 1048576 | tf_op jit(solution)/shard_map/prepare/pallas_call | solution.py:213
  8.5 0.0 collective-permute-done.1.below
  8.6 0.0 collective-permute-done.above
  8.6 0.0 copy-done
  8.6 0.0 copy-done.4
  8.6 0.0 copy-done.5
  8.6 0.0 copy-done.6
  8.6 0.0 copy-done.7
  8.6 0.2 copy-done.8
  8.8 0.2 copy-done.9
  9.0 6.6 %match_warp.1 = bf16[16,272,128]{2,1,0:T(8,128)(2,1)S(1)} custom-call(s32[1,16]{1,0:T(1,128)S(1)} %bitcast.7, s32[1,16]{1,0:T(1,128)S(1)} %copy-done.6, s32[16]{0:T(128)S(1)} %copy-done.7, bf16[4,5]{1,0:T(4,128)(2,1)S(1)} %copy-done.4, f32[4,176,128]{2,1,0:T(8,128)S(1)} %get-tuple-element.11.high_level, f32[4,176,128]{2,1,0:T(8,128)S(1)} %get-tuple-element.12.step_level, ...), custom_call_target="tpu_custom_call" | custom-call | flops 1660944384 | bytes 1572864 | tf_op jit(solution)/shard_map/match_warp/pallas_call | solution.py:360
  15.5 36.3 %all_to_all.5.got = bf16[16,272,128]{2,1,0:T(8,128)(2,1)S(1)} all-to-all(bf16[16,272,128]{2,1,0:T(8,128)(2,1)S(1)} %match_warp.1), channel_id=1, replica_groups=mesh['group'=2,'ccd'=16] {'ccd'}, dimensions={0} | all-to-all | bytes 2228224 | tf_op jit(solution)/shard_map/all_to_all | solution.py:448
  51.8 5.2 %coadd.1 = f32[1,512,512]{2,1,0:T(8,128)} custom-call(bf16[16,272,128]{2,1,0:T(8,128)(2,1)S(1)} %all_to_all.5.got), custom_call_target="tpu_custom_call" | custom-call | tf_op jit(solution)/shard_map/coadd/pallas_call | solution.py:420
Async XLA Ops:
  0.9 7.7 %collective-permute-start.1 = (f32[4,8,512]{2,1,0:T(8,128)S(1)}, f32[4,8,512]{2,1,0:T(8,128)S(1)}, u32[]{:S(2)}, u32[]{:S(2)}) collective-permute-start(f32[4,8,512]{2,1,0:T(8,128)S(1)} %get-tuple-element.17), channel_id=1, source_target_pairs={{1,0},{2,1},{3,2},{4,3},{5,4},{6,5},{7,6},{8,7},{9,8},{10,9},{11,1... | collective-permute-start | bytes 196616 | tf_op jit(solution)/shard_map/ppermute | solution.py:442
  2.2 6.4 %collective-permute-start = (f32[4,8,512]{2,1,0:T(8,128)S(1)}, f32[4,8,512]{2,1,0:T(8,128)S(1)}, u32[]{:S(2)}, u32[]{:S(2)}) collective-permute-start(f32[4,8,512]{2,1,0:T(8,128)S(1)} %get-tuple-element.18), channel_id=1, source_target_pairs={{0,1},{1,2},{2,3},{3,4},{4,5},{5,6},{6,7},{7,8},{8,9},{9,10},{10,1... | collective-permute-start | bytes 196616 | tf_op jit(solution)/shard_map/ppermute | solution.py:441
  5.2 0.8 %copy-start.1 = (f32[4,5,9,3]{2,0,3,1:T(4,128)S(1)}, f32[4,5,9,3]{2,0,3,1:T(4,128)}, u32[]{:S(2)}) copy-start(f32[4,5,9,3]{2,0,3,1:T(4,128)} %param.12) | copy-start | bytes 6484
  6.0 0.7 %copy-start.2 = (f32[2,9,11]{2,0,1:T(2,128)S(1)}, f32[2,9,11]{2,0,1:T(2,128)}, u32[]{:S(2)}) copy-start(f32[2,9,11]{2,0,1:T(2,128)} %param.11) | copy-start | bytes 2380
  6.7 0.7 %copy-start.3 = (f32[4,5,2,2]{1,3,2,0:T(2,128)S(1)}, f32[4,5,2,2]{1,3,2,0:T(2,128)}, u32[]{:S(2)}) copy-start(f32[4,5,2,2]{1,3,2,0:T(2,128)} %param.13) | copy-start | bytes 964
  7.4 1.2 %copy-start = (f32[4,128,512]{2,1,0:T(8,128)S(1)}, f32[4,128,512]{2,1,0:T(8,128)}, u32[]{:S(2)}) copy-start(f32[4,128,512]{2,1,0:T(8,128)} %image.1) | copy-start | bytes 3145732
  7.4 1.2 %copy-start.4 = (bf16[4,5]{1,0:T(4,128)(2,1)S(1)}, bf16[4,5]{1,0:T(4,128)(2,1)}, u32[]{:S(2)}) copy-start(bf16[4,5]{1,0:T(4,128)(2,1)} %weight.1) | copy-start | bytes 124
  7.4 1.2 %copy-start.5 = (s32[1,16,1]{1,2,0:T(1,128)S(1)}, s32[1,16,1]{1,2,0:T(1,128)}, u32[]{:S(2)}) copy-start(s32[1,16,1]{1,2,0:T(1,128)} %param.15) | copy-start | bytes 196
  7.4 1.2 %copy-start.6 = (s32[1,16]{1,0:T(1,128)S(1)}, s32[1,16]{1,0:T(1,128)}, u32[]{:S(2)}) copy-start(s32[1,16]{1,0:T(1,128)} %slot.1) | copy-start | bytes 196
  7.4 1.2 %copy-start.7 = (s32[16]{0:T(128)S(1)}, s32[16]{0:T(128)}, u32[]{:S(2)}) copy-start(s32[16]{0:T(128)} %owner.1) | copy-start | bytes 196
  7.4 1.4 %copy-start.8 = (bf16[512,512]{1,0:T(8,128)(2,1)S(1)}, bf16[512,512]{1,0:T(8,128)(2,1)}, u32[]{:S(2)}) copy-start(bf16[512,512]{1,0:T(8,128)(2,1)} %constant.5.clone.unsort) | copy-start | bytes 1572868
  7.4 1.5 %copy-start.9 = (bf16[512,512]{1,0:T(8,128)(2,1)S(1)}, bf16[512,512]{1,0:T(8,128)(2,1)}, u32[]{:S(2)}) copy-start(bf16[512,512]{1,0:T(8,128)(2,1)} %constant.4.clone.sort) | copy-start | bytes 1572868

commit v8 on v7

--- a/solution.py
+++ b/solution.py
@@ -33,7 +33,7 @@
 BAND = 256
 TALL = (STRIPS - 1) * STRIP + STEP
 HALVES = 2
-TOGETHER = 2
+PIECES = 3
 ROWS = BLOCK // HALVES
 WINDOW = ROWS + STRIP
 LABEL = 16
@@ -225,156 +225,166 @@
 def warp_kernel(
     patch, slot, owner, weight, high_level, step_level, slope, rows_high, rows_low, col_weights,
     sort, unsort, image, above, below, out,
-    terms, matched_terms, ready, place_of, seen, label, label_ready, sem, label_sem,
+    terms, matched_terms, ready, place_of, seen, nothing, label, label_ready, sem, label_sem, clear_sem,
 ):
-    grid_step = pl.program_id(0)
-    grid_steps = pl.num_programs(0)
     devices = label.shape[0]
     ccd, _, has_above, has_below = whereabouts(devices)
     tall = BLOCK + 2 * RIM
     lane = iota((1, LANES), 1)
+
+    nothing[...] = jnp.zeros_like(nothing)
+    clears = [
+        pltpu.make_async_copy(nothing, out.at[d, pl.ds(0, CAP * BLOCK)], clear_sem.at[d])
+        for d in range(devices)
+    ]
+    for copy in clears:
+        copy.start()
+    label[...] = jnp.zeros_like(label)
+
+    def forget(p, _):
+        seen[p] = 0
+        return 0
+
+    lax.fori_loop(0, owner.shape[0], forget, 0)
+    own = jnp.where(iota(weight.shape, 1) == ccd, weight[...].astype(F32), 0.0)
+    own = jnp.sum(own, axis=1, keepdims=True)
+    for block in range(V * BLKC):
+        p = patch[0, block]
+        to = owner[p]
+        rank = seen[p]
+        seen[p] = rank + 1
+        place_of[block] = to * CAP + rank
+        line = label[pl.ds(to, 1), :]
+        line = jnp.where(lane == rank * 2, own[block // BLKC : block // BLKC + 1], line)
+        line = jnp.where(lane == rank * 2 + 1, slot[0, block].astype(F32), line)
+        label[pl.ds(to, 1), :] = line
+    label_ready[...] = jnp.broadcast_to(
+        label[...].reshape(devices, 1, LANES), (devices, LABEL, LANES)
+    ).astype(BF16)
     label_copy = pltpu.make_async_copy(label_ready, out.at[:, pl.ds(CAP * BLOCK, LABEL)], label_sem)
-
-    @pl.when(grid_step == 0)
-    def _():
-        terms[:, :, tall:] = jnp.zeros((TOGETHER, 4, TALL - tall, WIDTH), BF16)
-        label[...] = jnp.zeros_like(label)
-
-        def clear(p, _):
-            seen[p] = 0
-            return 0
-
-        lax.fori_loop(0, owner.shape[0], clear, 0)
-        own = jnp.where(iota(weight.shape, 1) == ccd, weight[...].astype(F32), 0.0)
-        own = jnp.sum(own, axis=1, keepdims=True)
-        for block in range(V * BLKC):
-            p = patch[0, block]
-            to = owner[p]
-            rank = seen[p]
-            seen[p] = rank + 1
-            place_of[block] = to * CAP + rank
-            line = label[pl.ds(to, 1), :]
-            line = jnp.where(lane == rank * 2, own[block // BLKC : block // BLKC + 1], line)
-            line = jnp.where(lane == rank * 2 + 1, slot[0, block].astype(F32), line)
-            label[pl.ds(to, 1), :] = line
-        label_ready[...] = jnp.broadcast_to(
-            label[...].reshape(devices, 1, LANES), (devices, LABEL, LANES)
-        ).astype(BF16)
-        label_copy.start()
-
+    label_copy.start()
+
+    terms[:, :, tall:] = jnp.zeros((V, 4, TALL - tall, WIDTH), BF16)
     col_pos = (2.0 * column_at(iota((1, WIDTH), 1)).astype(F32) + 1.0) / WIDTH - 1.0
-    for i in range(TOGETHER):
-        raw = jnp.concatenate(
-            [jnp.where(has_above, above[i], 0.0), image[i], jnp.where(has_below, below[i], 0.0)],
-            axis=0,
-        )
+    filler = jnp.zeros((BAND - GROUPS * STEP, WIDTH), BF16)
+    empty = jnp.zeros((LANES - WINDOW, WIDTH), BF16)
+
+    def sort_rows(i, piece):
+        size = tall // PIECES
+        low_row, high_row = piece * size - RIM, (piece + 1) * size - RIM
+        raw = [image[i, max(low_row, 0) : min(high_row, BLOCK)]]
+        if low_row < 0:
+            raw = [jnp.where(has_above, above[i], 0.0)] + raw
+        if high_row > BLOCK:
+            raw = raw + [jnp.where(has_below, below[i], 0.0)]
+        raw = jnp.concatenate(raw, axis=0)
         raw_high = raw.astype(BF16)
         raw_low = (raw - raw_high.astype(F32)).astype(BF16)
-        sorted_terms = jnp.dot(
+        both = jnp.dot(
             jnp.concatenate([raw_high, raw_low], axis=0), sort[...], preferred_element_type=F32
         )
-        high, low = sorted_terms[:tall], sorted_terms[tall:]
+        high, low = both[:size], both[size:]
         tilted = (high + low) * col_pos
         tilted_high = tilted.astype(BF16)
-        terms[i, 0, :tall] = high.astype(BF16)
-        terms[i, 1, :tall] = low.astype(BF16)
-        terms[i, 2, :tall] = tilted_high
-        terms[i, 3, :tall] = (tilted - tilted_high.astype(F32)).astype(BF16)
-
-    filler = jnp.zeros((BAND - GROUPS * STEP, WIDTH), BF16)
-    for k in range(STRIPS):
-        for i in range(TOGETHER):
-            level = high_level[i]
-            if k != MIDDLE:
-                level = level + float(k - MIDDLE) * step_level[i]
-            matrix = jnp.concatenate([level.astype(BF16), slope[i]], axis=1)
-            rows = slice(k * STRIP, k * STRIP + STEP)
-            columns = jnp.concatenate(
-                [terms[i, h, rows] for h in (0, 1, 0, 2, 3, 2)] + [filler], axis=0
-            )
-            results = jnp.dot(matrix, columns, preferred_element_type=F32)
-            blocks = lane_sum(
-                lambda u, v, w: lane_block(results[u * STRIP : (u + 1) * STRIP], w),
-                lane, TAPS, False,
-            )
-            matched = jnp.concatenate(blocks, axis=1)
-            high = matched.astype(BF16)
-            at = slice(k * STRIP, (k + 1) * STRIP)
-            matched_terms[i, 0, at] = high
-            matched_terms[i, 1, at] = (matched - high.astype(F32)).astype(BF16)
-
-    empty = jnp.zeros((LANES - WINDOW, WIDTH), BF16)
-    warped = []
-    for i in range(TOGETHER):
-        halves = []
-        for h in range(HALVES):
-            high = rows_high[i, h * ROWS : (h + 1) * ROWS]
-            low = rows_low[i, h * ROWS : (h + 1) * ROWS]
-            rows = slice(h * ROWS, h * ROWS + WINDOW)
-            first = jnp.concatenate([matched_terms[i, 0, rows], empty], axis=0)
-            second = jnp.concatenate([matched_terms[i, 1, rows], empty], axis=0)
-            both = jnp.dot(
-                jnp.concatenate([high, high], axis=1), jnp.concatenate([first, second], axis=0),
-                preferred_element_type=F32,
-            )
-            halves.append(both + jnp.dot(low, first, preferred_element_type=F32))
-        warped.append(jnp.concatenate(halves, axis=0))
-
-    for i in range(TOGETHER):
+        at = slice(piece * size, (piece + 1) * size)
+        terms[i, 0, at] = high.astype(BF16)
+        terms[i, 1, at] = low.astype(BF16)
+        terms[i, 2, at] = tilted_high
+        terms[i, 3, at] = (tilted - tilted_high.astype(F32)).astype(BF16)
+
+    def match_strip(i, k):
+        level = high_level[i]
+        if k != MIDDLE:
+            level = level + float(k - MIDDLE) * step_level[i]
+        matrix = jnp.concatenate([level.astype(BF16), slope[i]], axis=1)
+        rows = slice(k * STRIP, k * STRIP + STEP)
+        columns = jnp.concatenate([terms[i, h, rows] for h in (0, 1, 0, 2, 3, 2)] + [filler], axis=0)
+        results = jnp.dot(matrix, columns, preferred_element_type=F32)
+        blocks = lane_sum(
+            lambda u, v, w: lane_block(results[u * STRIP : (u + 1) * STRIP], w), lane, TAPS, False
+        )
+        matched = jnp.concatenate(blocks, axis=1)
+        high = matched.astype(BF16)
+        at = slice(k * STRIP, (k + 1) * STRIP)
+        matched_terms[i, 0, at] = high
+        matched_terms[i, 1, at] = (matched - high.astype(F32)).astype(BF16)
+
+    def warp_half(i, h):
+        high = rows_high[i, h * ROWS : (h + 1) * ROWS]
+        low = rows_low[i, h * ROWS : (h + 1) * ROWS]
+        rows = slice(h * ROWS, h * ROWS + WINDOW)
+        first = jnp.concatenate([matched_terms[i, 0, rows], empty], axis=0)
+        second = jnp.concatenate([matched_terms[i, 1, rows], empty], axis=0)
+        warped = jnp.dot(
+            jnp.concatenate([high, high], axis=1), jnp.concatenate([first, second], axis=0),
+            preferred_element_type=F32,
+        )
+        warped = warped + jnp.dot(low, first, preferred_element_type=F32)
         cols = col_weights[i]
         blocks = lane_sum(
-            lambda s, v, w: lane_block(cols[s : s + 1], v) * lane_block(warped[i], w),
+            lambda s, v, w: lane_block(cols[s : s + 1], v) * lane_block(warped, w),
             lane, 2 * WARP + 1, True,
         )
         result = jnp.dot(
             jnp.concatenate(blocks, axis=1).astype(BF16), unsort[...], preferred_element_type=F32
         ).astype(BF16)
         for j in range(BLKC):
-            block = (grid_step * TOGETHER + i) * BLKC + j
-            ready[block] = result[:, j * BLOCK : (j + 1) * BLOCK]
+            ready[i * BLKC + j, h * ROWS : (h + 1) * ROWS] = lane_block(result, j)
+
+    def send(i):
+        if i == 0:
+            for copy in clears:
+                copy.wait()
+        for block in range(i * BLKC, (i + 1) * BLKC):
             to = place_of[block]
             row = pl.multiple_of(to % CAP * BLOCK, BLOCK)
             pltpu.make_async_copy(
                 ready.at[block], out.at[to // CAP, pl.ds(row, BLOCK)], sem.at[block]
             ).start()
 
-    @pl.when(grid_step == grid_steps - 1)
-    def _():
-        label_copy.wait()
-        for block in range(V * BLKC):
-            pltpu.make_async_copy(ready.at[block], out.at[0, pl.ds(0, BLOCK)], sem.at[block]).wait()
+    for piece in range(PIECES):
+        sort_rows(0, piece)
+    for i in range(V):
+        between = {}
+        if i > 0:
+            between[1] = functools.partial(warp_half, i - 1, 0)
+            between[3] = functools.partial(warp_half, i - 1, 1)
+            between[4] = functools.partial(send, i - 1)
+        if i < V - 1:
+            for piece in range(PIECES):
+                between[STRIPS - PIECES + piece] = functools.partial(sort_rows, i + 1, piece)
+        for k in range(STRIPS):
+            match_strip(i, k)
+            if k in between:
+                between[k]()
+    for h in range(HALVES):
+        warp_half(V - 1, h)
+    send(V - 1)
+    label_copy.wait()
+    for block in range(V * BLKC):
+        pltpu.make_async_copy(ready.at[block], out.at[0, pl.ds(0, BLOCK)], sem.at[block]).wait()
 
 
 def warp(patch, slot, owner, weight, ready, images, above, below, devices):
     smem = pl.BlockSpec(memory_space=pltpu.SMEM)
-    hbm = pl.BlockSpec(memory_space=pl.ANY)
+    vmem = pl.BlockSpec(memory_space=pltpu.VMEM)
     sort = deinterleave()
-    constants = [jnp.asarray(sort, BF16), jnp.asarray(sort.T, BF16)]
-
-    def whole(x):
-        return pl.BlockSpec(x.shape, lambda v: (0,) * x.ndim)
-
-    def by_visit(x):
-        return pl.BlockSpec((TOGETHER,) + x.shape[1:], lambda v: (v, 0, 0))
-
     return pl.pallas_call(
         warp_kernel,
-        grid=(V // TOGETHER,),
-        in_specs=[smem, smem, smem, whole(weight)]
-        + [by_visit(x) for x in ready]
-        + [whole(x) for x in constants]
-        + [by_visit(x) for x in (images, above, below)],
-        out_specs=hbm,
+        in_specs=[smem] * 3 + [vmem] * 12,
+        out_specs=pl.BlockSpec(memory_space=pl.ANY),
         scratch_shapes=[
-            pltpu.VMEM((TOGETHER, 4, TALL, WIDTH), BF16),
-            pltpu.VMEM((TOGETHER, 2, STRIPS * STRIP, WIDTH), BF16),
+            pltpu.VMEM((V, 4, TALL, WIDTH), BF16),
+            pltpu.VMEM((V, 2, STRIPS * STRIP, WIDTH), BF16),
             pltpu.VMEM((V * BLKC, BLOCK, BLOCK), BF16),
             pltpu.SMEM((V * BLKC,), jnp.int32),
             pltpu.SMEM((owner.shape[0],), jnp.int32),
+            pltpu.VMEM((CAP * BLOCK, BLOCK), BF16),
             pltpu.VMEM((devices, LANES), F32),
             pltpu.VMEM((devices, LABEL, LANES), BF16),
             pltpu.SemaphoreType.DMA((V * BLKC,)),
             pltpu.SemaphoreType.DMA(()),
+            pltpu.SemaphoreType.DMA((devices,)),
         ],
         out_shape=jax.ShapeDtypeStruct((devices, CAP * BLOCK + LABEL, BLOCK), BF16),
         compiler_params=pltpu.CompilerParams(vmem_limit_bytes=32 << 20),
@@ -384,34 +394,67 @@
             transcendentals=0,
         ),
         name="match_warp",
-    )(patch, slot, owner, weight, *ready, *constants, images, above, below)
-
-
-def coadd_kernel(got, out, total, sums, out_sem):
+    )(
+        patch, slot, owner, weight, *ready,
+        jnp.asarray(sort, BF16), jnp.asarray(sort.T, BF16), images, above, below,
+    )
+
+
+def coadd_kernel(got, out, total, out_sem):
     devices = got.shape[0]
-    labels = got[:, CAP * BLOCK : CAP * BLOCK + LABEL].astype(F32)[:, 0]
-    total[...] = jnp.zeros_like(total)
-    for c in range(CELLS):
-        sums[c] = 0.0
-    for source in range(devices):
-        for rank in range(CAP):
-            weight = labels[source, rank * 2]
-
-            @pl.when(weight > 0.0)
-            def _(source=source, rank=rank, weight=weight):
-                c = labels[source, rank * 2 + 1].astype(jnp.int32)
-                sums[c] += weight
-                rows = slice(rank * BLOCK, (rank + 1) * BLOCK)
-                total[c] += weight * got[source, rows].astype(F32)
-
+    wide = devices * CAP * STRIP
+    labels = got[:, CAP * BLOCK : CAP * BLOCK + LABEL][:, 0]
+    lane = iota((1, wide), 1)
+    rank = lane // STRIP % CAP
+    source = lane // (STRIP * CAP)
+
+    def spread(entry):
+        onehot = (iota((LANES, wide), 0) == rank * 2 + entry).astype(F32).astype(BF16)
+        every = jnp.dot(labels, onehot, preferred_element_type=F32)
+        return jnp.sum(
+            jnp.where(iota((devices, wide), 0) == source, every, 0.0), axis=0, keepdims=True
+        )
+
+    weights, cells = spread(0), spread(1)
+    row = iota((CELLS * STRIP, 1), 0)
+    mine = (cells == (row // STRIP).astype(F32)) & (lane % STRIP == row % STRIP)
+    matrix = jnp.where(mine, weights, 0.0)
+    sums = jnp.sum(matrix, axis=1, keepdims=True)
+    inverse = 1.0 / jnp.maximum(sums, 1.0)
+    matrix = matrix.astype(BF16)
     copies = []
-    for c in range(CELLS):
-        inverse = 1.0 / jnp.maximum(jnp.full((1, BLOCK), sums[c], F32), 1.0)
-        total[c] = total[c] * inverse
-        rows = slice(c // PSIDE * BLOCK, (c // PSIDE + 1) * BLOCK)
-        lanes = slice(c % PSIDE * BLOCK, (c % PSIDE + 1) * BLOCK)
-        copies.append(pltpu.make_async_copy(total.at[c], out.at[0, rows, lanes], out_sem.at[c]))
-        copies[-1].start()
+    for pair in range(BLOCK // STRIP // 2):
+        columns = jnp.concatenate(
+            [
+                jnp.concatenate(
+                    [
+                        got[s, r * BLOCK + k * STRIP : r * BLOCK + (k + 1) * STRIP]
+                        for s in range(devices)
+                        for r in range(CAP)
+                    ],
+                    axis=0,
+                )
+                for k in (2 * pair, 2 * pair + 1)
+            ],
+            axis=1,
+        )
+        result = jnp.dot(matrix, columns, preferred_element_type=F32) * inverse
+        for c in range(CELLS):
+            part = result[c * STRIP : (c + 1) * STRIP]
+            lanes = slice(c % PSIDE * BLOCK, (c % PSIDE + 1) * BLOCK)
+            for n in range(2):
+                first = (2 * pair + n) * STRIP
+                total[c // PSIDE, first : first + STRIP, lanes] = lane_block(part, n)
+        size = 2 * STRIP
+        for line in range(PSIDE):
+            copies.append(
+                pltpu.make_async_copy(
+                    total.at[line, pl.ds(pair * size, size)],
+                    out.at[0, pl.ds(line * BLOCK + pair * size, size)],
+                    out_sem.at[pair, line],
+                )
+            )
+            copies[-1].start()
     for copy in copies:
         copy.wait()
 
@@ -423,9 +466,8 @@
         out_specs=pl.BlockSpec(memory_space=pl.ANY),
         out_shape=jax.ShapeDtypeStruct((1, PSIDE * BLOCK, PSIDE * BLOCK), F32),
         scratch_shapes=[
-            pltpu.VMEM((CELLS, BLOCK, BLOCK), F32),
-            pltpu.SMEM((CELLS,), F32),
-            pltpu.SemaphoreType.DMA((CELLS,)),
+            pltpu.VMEM((PSIDE, BLOCK, WIDTH), F32),
+            pltpu.SemaphoreType.DMA((BLOCK // STRIP // 2, PSIDE)),
         ],
         compiler_params=pltpu.CompilerParams(vmem_limit_bytes=32 << 20),
         name="coadd",

time: 57.9 us -> 56.6 us (0.978)
  Pallas kernels: 12.9 us -> 12 us
    pallas_call x1, Pallas kernels: 5.19 us -> 1.6 us  [coadd(): pl.pallas_call(coadd_kernel, in_specs=[pl.BlockSpec(memory_space=pltpu.VM...]
    pallas_call x1, Pallas kernels: 6.56 us -> 9.3 us  [warp(): pl.pallas_call(warp_kernel, in_specs=[smem] * 3 + [vmem] * 12, out_specs=...]
where the time goes in v8:
time: 56.6 us; the launch traced here: 56.2 us
  blocking collectives  36.3 us (64%)
  Pallas kernels  12 us (21%)
  starting transfers between devices  4.33 us (8%)
  local copies, waits for them, and re-layouts  3.43 us (6%)
    all_to_all x1, blocking collectives, shards(): got = lax.all_to_all(sent, 'ccd', split_axis=0, concat_axis=0, tiled=True)  36.3 us
    pallas_call x1, Pallas kernels, warp(): pl.pallas_call(warp_kernel, in_specs=[smem] * 3 + [vmem] * 12, out_specs=...  9.3 us
    ppermute x1, starting transfers between devices, shards(): above = lax.ppermute(images[:, BLOCK - RIM:], 'ccd', down)  3.03 us
    unnamed x20, local copies, waits for them, and re-layouts  2.55 us
    pallas_call x1, Pallas kernels, coadd(): pl.pallas_call(coadd_kernel, in_specs=[pl.BlockSpec(memory_space=pltpu.VM...  1.6 us
    ppermute x1, starting transfers between devices, shards(): below = lax.ppermute(images[:, :RIM], 'ccd', up)  1.29 us
  transfers between devices with their start and end apart: 2, of which 0 were waited for; matrix products, arithmetic and copies ran while one was open for 0% of the time, Pallas kernels for 2%

profile of v8, /device:TPU:0, one launch (start us, length us, event | category | flops | bytes accessed | tf_op | source)
XLA Modules:
  0.0 56.2 jit_solution(6006426863471693862)
XLA Ops:
  0.0 0.9 %fusion = (f32[4,8,512]{2,1,0:T(8,128)S(1)}, f32[4,8,512]{2,1,0:T(8,128)S(1)}) fusion(f32[4,128,512]{2,1,0:T(8,128)} %image.1), kind=kLoop, calls=%fused_computation | loop fusion | bytes 262144 | tf_op jit(solution)/shard_map/slice | solution.py:484
  0.9 1.3 %collective-permute-start.1 = (f32[4,8,512]{2,1,0:T(8,128)S(1)}, f32[4,8,512]{2,1,0:T(8,128)S(1)}, u32[]{:S(2)}, u32[]{:S(2)}) collective-permute-start(f32[4,8,512]{2,1,0:T(8,128)S(1)} %get-tuple-element.17), channel_id=1, source_target_pairs={{1,0},{2,1},{3,2},{4,3},{5,4},{6,5},{7,6},{8,7},{9,8},{10,9},{11,1... | collective-permute-start | bytes 196616 | tf_op jit(solution)/shard_map/ppermute | solution.py:484
  2.2 3.0 %collective-permute-start = (f32[4,8,512]{2,1,0:T(8,128)S(1)}, f32[4,8,512]{2,1,0:T(8,128)S(1)}, u32[]{:S(2)}, u32[]{:S(2)}) collective-permute-start(f32[4,8,512]{2,1,0:T(8,128)S(1)} %get-tuple-element.18), channel_id=1, source_target_pairs={{0,1},{1,2},{2,3},{3,4},{4,5},{5,6},{6,7},{7,8},{8,9},{9,10},{10,1... | collective-permute-start | bytes 196616 | tf_op jit(solution)/shard_map/ppermute | solution.py:483
  5.2 0.0 copy-start.1
  5.2 0.7 %copy-done.1 = f32[4,5,9,3]{2,0,3,1:T(4,128)S(1)} copy-done((f32[4,5,9,3]{2,0,3,1:T(4,128)S(1)}, f32[4,5,9,3]{2,0,3,1:T(4,128)}, u32[]{:S(2)}) %copy-start.1) | copy-done | bytes 2184
  6.0 0.0 copy-start.2
  6.0 0.7 %copy-done.2 = f32[2,9,11]{2,0,1:T(2,128)S(1)} copy-done((f32[2,9,11]{2,0,1:T(2,128)S(1)}, f32[2,9,11]{2,0,1:T(2,128)}, u32[]{:S(2)}) %copy-start.2) | copy-done | bytes 816
  6.7 0.0 copy-start.3
  6.7 0.7 %copy-done.3 = f32[4,5,2,2]{1,3,2,0:T(2,128)S(1)} copy-done((f32[4,5,2,2]{1,3,2,0:T(2,128)S(1)}, f32[4,5,2,2]{1,3,2,0:T(2,128)}, u32[]{:S(2)}) %copy-start.3) | copy-done | bytes 344
  7.4 0.0 copy-start
  7.4 0.0 copy-start.4
  7.4 0.0 copy-start.5
  7.4 0.0 copy-start.6
  7.4 0.0 copy-start.7
  7.4 0.0 copy-start.8
  7.4 0.0 copy-start.9
  7.4 1.1 %prepare.1 = (f32[4,176,128]{2,1,0:T(8,128)S(1)}, f32[4,176,128]{2,1,0:T(8,128)S(1)}, bf16[4,176,128]{2,1,0:T(8,128)(2,1)S(1)}, bf16[4,128,128]{2,1,0:T(8,128)(2...) custom-call(f32[9,2,11]{2,1,0:T(2,128)S(1)} %bitcast.5, f32[5,3,4,9]{3,2,1,0:T(4,128)S(1)} %bitcast.4, ...), custom_call_target="tpu_custom_call" | custom-call | flops 1073741824 | bytes 1048576 | tf_op jit(solution)/shard_map/prepare/pallas_call | solution.py:213
  8.5 0.0 collective-permute-done.1.below
  8.6 0.0 collective-permute-done.above
  8.6 0.0 copy-done
  8.6 0.0 copy-done.4
  8.6 0.0 copy-done.5
  8.6 0.0 copy-done.6
  8.6 0.0 copy-done.7
  8.6 0.2 copy-done.8
  8.8 0.2 copy-done.9
  9.0 9.3 %match_warp.1 = bf16[16,272,128]{2,1,0:T(8,128)(2,1)S(1)} custom-call(s32[1,16]{1,0:T(1,128)S(1)} %bitcast.7, s32[1,16]{1,0:T(1,128)S(1)} %copy-done.6, s32[16]{0:T(128)S(1)} %copy-done.7, bf16[4,5]{1,0:T(4,128)(2,1)S(1)} %copy-done.4, f32[4,176,128]{2,1,0:T(8,128)S(1)} %get-tuple-element.11.high_level, f32[4,176,128]{2,1,0:T(8,128)S(1)} %get-tuple-element.12.step_level, ...), custom_call_target="tpu_custom_call" | custom-call | flops 1660944384 | bytes 1572864 | tf_op jit(solution)/shard_map/match_warp/pallas_call | solution.py:372
  18.3 36.3 %all_to_all.5.got = bf16[16,272,128]{2,1,0:T(8,128)(2,1)S(1)} all-to-all(bf16[16,272,128]{2,1,0:T(8,128)(2,1)S(1)} %match_warp.1), channel_id=1, replica_groups=mesh['group'=2,'ccd'=16] {'ccd'}, dimensions={0} | all-to-all | bytes 2228224 | tf_op jit(solution)/shard_map/all_to_all | solution.py:490
  54.6 1.6 %coadd.1 = f32[1,512,512]{2,1,0:T(8,128)} custom-call(bf16[16,272,128]{2,1,0:T(8,128)(2,1)S(1)} %all_to_all.5.got), custom_call_target="tpu_custom_call" | custom-call | tf_op jit(solution)/shard_map/coadd/pallas_call | solution.py:463
Async XLA Ops:
  0.9 7.7 %collective-permute-start.1 = (f32[4,8,512]{2,1,0:T(8,128)S(1)}, f32[4,8,512]{2,1,0:T(8,128)S(1)}, u32[]{:S(2)}, u32[]{:S(2)}) collective-permute-start(f32[4,8,512]{2,1,0:T(8,128)S(1)} %get-tuple-element.17), channel_id=1, source_target_pairs={{1,0},{2,1},{3,2},{4,3},{5,4},{6,5},{7,6},{8,7},{9,8},{10,9},{11,1... | collective-permute-start | bytes 196616 | tf_op jit(solution)/shard_map/ppermute | solution.py:484
  2.2 6.4 %collective-permute-start = (f32[4,8,512]{2,1,0:T(8,128)S(1)}, f32[4,8,512]{2,1,0:T(8,128)S(1)}, u32[]{:S(2)}, u32[]{:S(2)}) collective-permute-start(f32[4,8,512]{2,1,0:T(8,128)S(1)} %get-tuple-element.18), channel_id=1, source_target_pairs={{0,1},{1,2},{2,3},{3,4},{4,5},{5,6},{6,7},{7,8},{8,9},{9,10},{10,1... | collective-permute-start | bytes 196616 | tf_op jit(solution)/shard_map/ppermute | solution.py:483
  5.2 0.8 %copy-start.1 = (f32[4,5,9,3]{2,0,3,1:T(4,128)S(1)}, f32[4,5,9,3]{2,0,3,1:T(4,128)}, u32[]{:S(2)}) copy-start(f32[4,5,9,3]{2,0,3,1:T(4,128)} %param.12) | copy-start | bytes 6484
  6.0 0.7 %copy-start.2 = (f32[2,9,11]{2,0,1:T(2,128)S(1)}, f32[2,9,11]{2,0,1:T(2,128)}, u32[]{:S(2)}) copy-start(f32[2,9,11]{2,0,1:T(2,128)} %param.11) | copy-start | bytes 2380
  6.7 0.7 %copy-start.3 = (f32[4,5,2,2]{1,3,2,0:T(2,128)S(1)}, f32[4,5,2,2]{1,3,2,0:T(2,128)}, u32[]{:S(2)}) copy-start(f32[4,5,2,2]{1,3,2,0:T(2,128)} %param.13) | copy-start | bytes 964
  7.4 1.2 %copy-start = (f32[4,128,512]{2,1,0:T(8,128)S(1)}, f32[4,128,512]{2,1,0:T(8,128)}, u32[]{:S(2)}) copy-start(f32[4,128,512]{2,1,0:T(8,128)} %image.1) | copy-start | bytes 3145732
  7.4 1.2 %copy-start.4 = (bf16[4,5]{1,0:T(4,128)(2,1)S(1)}, bf16[4,5]{1,0:T(4,128)(2,1)}, u32[]{:S(2)}) copy-start(bf16[4,5]{1,0:T(4,128)(2,1)} %weight.1) | copy-start | bytes 124
  7.4 1.2 %copy-start.5 = (s32[1,16,1]{1,2,0:T(1,128)S(1)}, s32[1,16,1]{1,2,0:T(1,128)}, u32[]{:S(2)}) copy-start(s32[1,16,1]{1,2,0:T(1,128)} %param.15) | copy-start | bytes 196
  7.4 1.2 %copy-start.6 = (s32[1,16]{1,0:T(1,128)S(1)}, s32[1,16]{1,0:T(1,128)}, u32[]{:S(2)}) copy-start(s32[1,16]{1,0:T(1,128)} %slot.1) | copy-start | bytes 196
  7.4 1.2 %copy-start.7 = (s32[16]{0:T(128)S(1)}, s32[16]{0:T(128)}, u32[]{:S(2)}) copy-start(s32[16]{0:T(128)} %owner.1) | copy-start | bytes 196
  7.4 1.4 %copy-start.8 = (bf16[512,512]{1,0:T(8,128)(2,1)S(1)}, bf16[512,512]{1,0:T(8,128)(2,1)}, u32[]{:S(2)}) copy-start(bf16[512,512]{1,0:T(8,128)(2,1)} %constant.5.clone.unsort) | copy-start | bytes 1572868
  7.4 1.5 %copy-start.9 = (bf16[512,512]{1,0:T(8,128)(2,1)S(1)}, bf16[512,512]{1,0:T(8,128)(2,1)}, u32[]{:S(2)}) copy-start(bf16[512,512]{1,0:T(8,128)(2,1)} %constant.4.clone.sort) | copy-start | bytes 1572868

commit v9 on v8

--- a/solution.py
+++ b/solution.py
@@ -33,6 +33,7 @@
 BAND = 256
 TALL = (STRIPS - 1) * STRIP + STEP
 HALVES = 2
+TOGETHER = 2
 PIECES = 3
 ROWS = BLOCK // HALVES
 WINDOW = ROWS + STRIP
@@ -225,7 +226,7 @@
 def warp_kernel(
     patch, slot, owner, weight, high_level, step_level, slope, rows_high, rows_low, col_weights,
     sort, unsort, image, above, below, out,
-    terms, matched_terms, ready, place_of, seen, nothing, label, label_ready, sem, label_sem, clear_sem,
+    raw, terms, matched_terms, ready, place_of, seen, nothing, label, label_ready, sem, label_sem, clear_sem,
 ):
     devices = label.shape[0]
     ccd, _, has_above, has_below = whereabouts(devices)
@@ -264,102 +265,105 @@
     label_copy = pltpu.make_async_copy(label_ready, out.at[:, pl.ds(CAP * BLOCK, LABEL)], label_sem)
     label_copy.start()
 
-    terms[:, :, tall:] = jnp.zeros((V, 4, TALL - tall, WIDTH), BF16)
+    terms[:, :, tall:] = jnp.zeros((TOGETHER, 4, TALL - tall, WIDTH), BF16)
     col_pos = (2.0 * column_at(iota((1, WIDTH), 1)).astype(F32) + 1.0) / WIDTH - 1.0
     filler = jnp.zeros((BAND - GROUPS * STEP, WIDTH), BF16)
     empty = jnp.zeros((LANES - WINDOW, WIDTH), BF16)
-
-    def sort_rows(i, piece):
-        size = tall // PIECES
-        low_row, high_row = piece * size - RIM, (piece + 1) * size - RIM
-        raw = [image[i, max(low_row, 0) : min(high_row, BLOCK)]]
-        if low_row < 0:
-            raw = [jnp.where(has_above, above[i], 0.0)] + raw
-        if high_row > BLOCK:
-            raw = raw + [jnp.where(has_below, below[i], 0.0)]
-        raw = jnp.concatenate(raw, axis=0)
-        raw_high = raw.astype(BF16)
-        raw_low = (raw - raw_high.astype(F32)).astype(BF16)
-        both = jnp.dot(
-            jnp.concatenate([raw_high, raw_low], axis=0), sort[...], preferred_element_type=F32
-        )
-        high, low = both[:size], both[size:]
-        tilted = (high + low) * col_pos
-        tilted_high = tilted.astype(BF16)
-        at = slice(piece * size, (piece + 1) * size)
-        terms[i, 0, at] = high.astype(BF16)
-        terms[i, 1, at] = low.astype(BF16)
-        terms[i, 2, at] = tilted_high
-        terms[i, 3, at] = (tilted - tilted_high.astype(F32)).astype(BF16)
-
-    def match_strip(i, k):
-        level = high_level[i]
-        if k != MIDDLE:
-            level = level + float(k - MIDDLE) * step_level[i]
-        matrix = jnp.concatenate([level.astype(BF16), slope[i]], axis=1)
-        rows = slice(k * STRIP, k * STRIP + STEP)
-        columns = jnp.concatenate([terms[i, h, rows] for h in (0, 1, 0, 2, 3, 2)] + [filler], axis=0)
-        results = jnp.dot(matrix, columns, preferred_element_type=F32)
-        blocks = lane_sum(
-            lambda u, v, w: lane_block(results[u * STRIP : (u + 1) * STRIP], w), lane, TAPS, False
-        )
-        matched = jnp.concatenate(blocks, axis=1)
-        high = matched.astype(BF16)
-        at = slice(k * STRIP, (k + 1) * STRIP)
-        matched_terms[i, 0, at] = high
-        matched_terms[i, 1, at] = (matched - high.astype(F32)).astype(BF16)
-
-    def warp_half(i, h):
-        high = rows_high[i, h * ROWS : (h + 1) * ROWS]
-        low = rows_low[i, h * ROWS : (h + 1) * ROWS]
-        rows = slice(h * ROWS, h * ROWS + WINDOW)
-        first = jnp.concatenate([matched_terms[i, 0, rows], empty], axis=0)
-        second = jnp.concatenate([matched_terms[i, 1, rows], empty], axis=0)
-        warped = jnp.dot(
-            jnp.concatenate([high, high], axis=1), jnp.concatenate([first, second], axis=0),
-            preferred_element_type=F32,
-        )
-        warped = warped + jnp.dot(low, first, preferred_element_type=F32)
-        cols = col_weights[i]
-        blocks = lane_sum(
-            lambda s, v, w: lane_block(cols[s : s + 1], v) * lane_block(warped, w),
-            lane, 2 * WARP + 1, True,
-        )
-        result = jnp.dot(
-            jnp.concatenate(blocks, axis=1).astype(BF16), unsort[...], preferred_element_type=F32
-        ).astype(BF16)
-        for j in range(BLKC):
-            ready[i * BLKC + j, h * ROWS : (h + 1) * ROWS] = lane_block(result, j)
-
-    def send(i):
-        if i == 0:
-            for copy in clears:
-                copy.wait()
-        for block in range(i * BLKC, (i + 1) * BLKC):
-            to = place_of[block]
-            row = pl.multiple_of(to % CAP * BLOCK, BLOCK)
-            pltpu.make_async_copy(
-                ready.at[block], out.at[to // CAP, pl.ds(row, BLOCK)], sem.at[block]
-            ).start()
-
-    for piece in range(PIECES):
-        sort_rows(0, piece)
-    for i in range(V):
-        between = {}
-        if i > 0:
-            between[1] = functools.partial(warp_half, i - 1, 0)
-            between[3] = functools.partial(warp_half, i - 1, 1)
-            between[4] = functools.partial(send, i - 1)
-        if i < V - 1:
-            for piece in range(PIECES):
-                between[STRIPS - PIECES + piece] = functools.partial(sort_rows, i + 1, piece)
-        for k in range(STRIPS):
-            match_strip(i, k)
-            if k in between:
-                between[k]()
-    for h in range(HALVES):
-        warp_half(V - 1, h)
-    send(V - 1)
+    for copy in clears:
+        copy.wait()
+
+    def some_visits(turn, _):
+        visits = [turn * TOGETHER + i for i in range(TOGETHER)]
+        for i, visit in enumerate(visits):
+            raw[i, :RIM] = jnp.where(has_above, above[visit], 0.0)
+            raw[i, RIM : RIM + BLOCK] = image[visit]
+            raw[i, RIM + BLOCK :] = jnp.where(has_below, below[visit], 0.0)
+
+        def sort_rows(piece, _):
+            size = tall // PIECES
+            at = pl.ds(pl.multiple_of(piece * size, STRIP), size)
+            for i in range(TOGETHER):
+                rows = raw[i, at]
+                rows_high = rows.astype(BF16)
+                rows_low = (rows - rows_high.astype(F32)).astype(BF16)
+                both = jnp.dot(
+                    jnp.concatenate([rows_high, rows_low], axis=0), sort[...],
+                    preferred_element_type=F32,
+                )
+                high, low = both[:size], both[size:]
+                tilted = (high + low) * col_pos
+                tilted_high = tilted.astype(BF16)
+                terms[i, 0, at] = high.astype(BF16)
+                terms[i, 1, at] = low.astype(BF16)
+                terms[i, 2, at] = tilted_high
+                terms[i, 3, at] = (tilted - tilted_high.astype(F32)).astype(BF16)
+            return 0
+
+        lax.fori_loop(0, PIECES, sort_rows, 0)
+
+        def match_strip(k, _):
+            first = pl.multiple_of(k * STRIP, STRIP)
+            away = (k - MIDDLE).astype(F32)
+            for i, visit in enumerate(visits):
+                level = high_level[visit] + away * step_level[visit]
+                matrix = jnp.concatenate([level.astype(BF16), slope[visit]], axis=1)
+                columns = jnp.concatenate(
+                    [terms[i, h, pl.ds(first, STEP)] for h in (0, 1, 0, 2, 3, 2)] + [filler], axis=0
+                )
+                results = jnp.dot(matrix, columns, preferred_element_type=F32)
+                blocks = lane_sum(
+                    lambda u, v, w: lane_block(results[u * STRIP : (u + 1) * STRIP], w),
+                    lane, TAPS, False,
+                )
+                matched = jnp.concatenate(blocks, axis=1)
+                high = matched.astype(BF16)
+                at = pl.ds(first, STRIP)
+                matched_terms[i, 0, at] = high
+                matched_terms[i, 1, at] = (matched - high.astype(F32)).astype(BF16)
+            return 0
+
+        lax.fori_loop(0, STRIPS, match_strip, 0)
+
+        def warp_half(h, _):
+            first_row = pl.multiple_of(h * ROWS, ROWS)
+            at = pl.ds(first_row, ROWS)
+            rows = pl.ds(first_row, WINDOW)
+            for i, visit in enumerate(visits):
+                high = rows_high[visit, at]
+                low = rows_low[visit, at]
+                first = jnp.concatenate([matched_terms[i, 0, rows], empty], axis=0)
+                second = jnp.concatenate([matched_terms[i, 1, rows], empty], axis=0)
+                warped = jnp.dot(
+                    jnp.concatenate([high, high], axis=1),
+                    jnp.concatenate([first, second], axis=0),
+                    preferred_element_type=F32,
+                )
+                warped = warped + jnp.dot(low, first, preferred_element_type=F32)
+                cols = col_weights[visit]
+                blocks = lane_sum(
+                    lambda s, v, w: lane_block(cols[s : s + 1], v) * lane_block(warped, w),
+                    lane, 2 * WARP + 1, True,
+                )
+                result = jnp.dot(
+                    jnp.concatenate(blocks, axis=1).astype(BF16), unsort[...],
+                    preferred_element_type=F32,
+                ).astype(BF16)
+                for j in range(BLKC):
+                    ready[visit * BLKC + j, at] = lane_block(result, j)
+            return 0
+
+        lax.fori_loop(0, HALVES, warp_half, 0)
+        for visit in visits:
+            for j in range(BLKC):
+                block = visit * BLKC + j
+                to = place_of[block]
+                row = pl.multiple_of(to % CAP * BLOCK, BLOCK)
+                pltpu.make_async_copy(
+                    ready.at[block], out.at[to // CAP, pl.ds(row, BLOCK)], sem.at[block]
+                ).start()
+        return 0
+
+    lax.fori_loop(0, V // TOGETHER, some_visits, 0)
     label_copy.wait()
     for block in range(V * BLKC):
         pltpu.make_async_copy(ready.at[block], out.at[0, pl.ds(0, BLOCK)], sem.at[block]).wait()
@@ -374,8 +378,9 @@
         in_specs=[smem] * 3 + [vmem] * 12,
         out_specs=pl.BlockSpec(memory_space=pl.ANY),
         scratch_shapes=[
-            pltpu.VMEM((V, 4, TALL, WIDTH), BF16),
-            pltpu.VMEM((V, 2, STRIPS * STRIP, WIDTH), BF16),
+            pltpu.VMEM((TOGETHER, BLOCK + 2 * RIM, WIDTH), F32),
+            pltpu.VMEM((TOGETHER, 4, TALL, WIDTH), BF16),
+            pltpu.VMEM((TOGETHER, 2, STRIPS * STRIP, WIDTH), BF16),
             pltpu.VMEM((V * BLKC, BLOCK, BLOCK), BF16),
             pltpu.SMEM((V * BLKC,), jnp.int32),
             pltpu.SMEM((owner.shape[0],), jnp.int32),

time: 56.6 us -> 61.4 us (1.085)
  Pallas kernels: 12 us -> 16.9 us
    pallas_call x1, Pallas kernels: 9.3 us -> 14.2 us  [warp(): pl.pallas_call(warp_kernel, in_specs=[smem] * 3 + [vmem] * 12, out_specs=...]
where the time goes in v9:
time: 61.4 us; the launch traced here: 61 us
  blocking collectives  36.3 us (59%)
  Pallas kernels  16.9 us (28%)
  starting transfers between devices  4.33 us (7%)
  local copies, waits for them, and re-layouts  3.43 us (6%)
    all_to_all x1, blocking collectives, shards(): got = lax.all_to_all(sent, 'ccd', split_axis=0, concat_axis=0, tiled=True)  36.3 us
    pallas_call x1, Pallas kernels, warp(): pl.pallas_call(warp_kernel, in_specs=[smem] * 3 + [vmem] * 12, out_specs=...  14.2 us
    ppermute x1, starting transfers between devices, shards(): above = lax.ppermute(images[:, BLOCK - RIM:], 'ccd', down)  3.03 us
    unnamed x20, local copies, waits for them, and re-layouts  2.55 us
    pallas_call x1, Pallas kernels, coadd(): pl.pallas_call(coadd_kernel, in_specs=[pl.BlockSpec(memory_space=pltpu.VM...  1.59 us
    ppermute x1, starting transfers between devices, shards(): below = lax.ppermute(images[:, :RIM], 'ccd', up)  1.29 us
  transfers between devices with their start and end apart: 2, of which 0 were waited for; matrix products, arithmetic and copies ran while one was open for 0% of the time, Pallas kernels for 2%

profile of v9, /device:TPU:0, one launch (start us, length us, event | category | flops | bytes accessed | tf_op | source)
XLA Modules:
  0.0 61.0 jit_solution(10945408579305596674)
XLA Ops:
  0.0 0.9 %fusion = (f32[4,8,512]{2,1,0:T(8,128)S(1)}, f32[4,8,512]{2,1,0:T(8,128)S(1)}) fusion(f32[4,128,512]{2,1,0:T(8,128)} %image.1), kind=kLoop, calls=%fused_computation | loop fusion | bytes 262144 | tf_op jit(solution)/shard_map/slice | solution.py:489
  0.9 1.3 %collective-permute-start.1 = (f32[4,8,512]{2,1,0:T(8,128)S(1)}, f32[4,8,512]{2,1,0:T(8,128)S(1)}, u32[]{:S(2)}, u32[]{:S(2)}) collective-permute-start(f32[4,8,512]{2,1,0:T(8,128)S(1)} %get-tuple-element.17), channel_id=1, source_target_pairs={{1,0},{2,1},{3,2},{4,3},{5,4},{6,5},{7,6},{8,7},{9,8},{10,9},{11,1... | collective-permute-start | bytes 196616 | tf_op jit(solution)/shard_map/ppermute | solution.py:489
  2.2 3.0 %collective-permute-start = (f32[4,8,512]{2,1,0:T(8,128)S(1)}, f32[4,8,512]{2,1,0:T(8,128)S(1)}, u32[]{:S(2)}, u32[]{:S(2)}) collective-permute-start(f32[4,8,512]{2,1,0:T(8,128)S(1)} %get-tuple-element.18), channel_id=1, source_target_pairs={{0,1},{1,2},{2,3},{3,4},{4,5},{5,6},{6,7},{7,8},{8,9},{9,10},{10,1... | collective-permute-start | bytes 196616 | tf_op jit(solution)/shard_map/ppermute | solution.py:488
  5.2 0.0 copy-start.1
  5.2 0.7 %copy-done.1 = f32[4,5,9,3]{2,0,3,1:T(4,128)S(1)} copy-done((f32[4,5,9,3]{2,0,3,1:T(4,128)S(1)}, f32[4,5,9,3]{2,0,3,1:T(4,128)}, u32[]{:S(2)}) %copy-start.1) | copy-done | bytes 2184
  6.0 0.0 copy-start.2
  6.0 0.7 %copy-done.2 = f32[2,9,11]{2,0,1:T(2,128)S(1)} copy-done((f32[2,9,11]{2,0,1:T(2,128)S(1)}, f32[2,9,11]{2,0,1:T(2,128)}, u32[]{:S(2)}) %copy-start.2) | copy-done | bytes 816
  6.7 0.0 copy-start.3
  6.7 0.7 %copy-done.3 = f32[4,5,2,2]{1,3,2,0:T(2,128)S(1)} copy-done((f32[4,5,2,2]{1,3,2,0:T(2,128)S(1)}, f32[4,5,2,2]{1,3,2,0:T(2,128)}, u32[]{:S(2)}) %copy-start.3) | copy-done | bytes 344
  7.4 0.0 copy-start
  7.4 0.0 copy-start.4
  7.4 0.0 copy-start.5
  7.4 0.0 copy-start.6
  7.4 0.0 copy-start.7
  7.4 0.0 copy-start.8
  7.4 0.0 copy-start.9
  7.4 1.1 %prepare.1 = (f32[4,176,128]{2,1,0:T(8,128)S(1)}, f32[4,176,128]{2,1,0:T(8,128)S(1)}, bf16[4,176,128]{2,1,0:T(8,128)(2,1)S(1)}, bf16[4,128,128]{2,1,0:T(8,128)(2...) custom-call(f32[9,2,11]{2,1,0:T(2,128)S(1)} %bitcast.5, f32[5,3,4,9]{3,2,1,0:T(4,128)S(1)} %bitcast.4, ...), custom_call_target="tpu_custom_call" | custom-call | flops 1073741824 | bytes 1048576 | tf_op jit(solution)/shard_map/prepare/pallas_call | solution.py:214
  8.5 0.0 collective-permute-done.1.below
  8.6 0.0 collective-permute-done.above
  8.6 0.0 copy-done
  8.6 0.0 copy-done.4
  8.6 0.0 copy-done.5
  8.6 0.0 copy-done.6
  8.6 0.0 copy-done.7
  8.6 0.2 copy-done.8
  8.8 0.2 copy-done.9
  9.0 14.2 %match_warp.1 = bf16[16,272,128]{2,1,0:T(8,128)(2,1)S(1)} custom-call(s32[1,16]{1,0:T(1,128)S(1)} %bitcast.7, s32[1,16]{1,0:T(1,128)S(1)} %copy-done.6, s32[16]{0:T(128)S(1)} %copy-done.7, bf16[4,5]{1,0:T(4,128)(2,1)S(1)} %copy-done.4, f32[4,176,128]{2,1,0:T(8,128)S(1)} %get-tuple-element.11.high_level, f32[4,176,128]{2,1,0:T(8,128)S(1)} %get-tuple-element.12.step_level, ...), custom_call_target="tpu_custom_call" | custom-call | flops 1660944384 | bytes 1572864 | tf_op jit(solution)/shard_map/match_warp/pallas_call | solution.py:376
  23.1 36.3 %all_to_all.5.got = bf16[16,272,128]{2,1,0:T(8,128)(2,1)S(1)} all-to-all(bf16[16,272,128]{2,1,0:T(8,128)(2,1)S(1)} %match_warp.1), channel_id=1, replica_groups=mesh['group'=2,'ccd'=16] {'ccd'}, dimensions={0} | all-to-all | bytes 2228224 | tf_op jit(solution)/shard_map/all_to_all | solution.py:495
  59.4 1.6 %coadd.1 = f32[1,512,512]{2,1,0:T(8,128)} custom-call(bf16[16,272,128]{2,1,0:T(8,128)(2,1)S(1)} %all_to_all.5.got), custom_call_target="tpu_custom_call" | custom-call | tf_op jit(solution)/shard_map/coadd/pallas_call | solution.py:468
Async XLA Ops:
  0.9 7.7 %collective-permute-start.1 = (f32[4,8,512]{2,1,0:T(8,128)S(1)}, f32[4,8,512]{2,1,0:T(8,128)S(1)}, u32[]{:S(2)}, u32[]{:S(2)}) collective-permute-start(f32[4,8,512]{2,1,0:T(8,128)S(1)} %get-tuple-element.17), channel_id=1, source_target_pairs={{1,0},{2,1},{3,2},{4,3},{5,4},{6,5},{7,6},{8,7},{9,8},{10,9},{11,1... | collective-permute-start | bytes 196616 | tf_op jit(solution)/shard_map/ppermute | solution.py:489
  2.2 6.4 %collective-permute-start = (f32[4,8,512]{2,1,0:T(8,128)S(1)}, f32[4,8,512]{2,1,0:T(8,128)S(1)}, u32[]{:S(2)}, u32[]{:S(2)}) collective-permute-start(f32[4,8,512]{2,1,0:T(8,128)S(1)} %get-tuple-element.18), channel_id=1, source_target_pairs={{0,1},{1,2},{2,3},{3,4},{4,5},{5,6},{6,7},{7,8},{8,9},{9,10},{10,1... | collective-permute-start | bytes 196616 | tf_op jit(solution)/shard_map/ppermute | solution.py:488
  5.2 0.8 %copy-start.1 = (f32[4,5,9,3]{2,0,3,1:T(4,128)S(1)}, f32[4,5,9,3]{2,0,3,1:T(4,128)}, u32[]{:S(2)}) copy-start(f32[4,5,9,3]{2,0,3,1:T(4,128)} %param.12) | copy-start | bytes 6484
  6.0 0.7 %copy-start.2 = (f32[2,9,11]{2,0,1:T(2,128)S(1)}, f32[2,9,11]{2,0,1:T(2,128)}, u32[]{:S(2)}) copy-start(f32[2,9,11]{2,0,1:T(2,128)} %param.11) | copy-start | bytes 2380
  6.7 0.7 %copy-start.3 = (f32[4,5,2,2]{1,3,2,0:T(2,128)S(1)}, f32[4,5,2,2]{1,3,2,0:T(2,128)}, u32[]{:S(2)}) copy-start(f32[4,5,2,2]{1,3,2,0:T(2,128)} %param.13) | copy-start | bytes 964
  7.4 1.2 %copy-start = (f32[4,128,512]{2,1,0:T(8,128)S(1)}, f32[4,128,512]{2,1,0:T(8,128)}, u32[]{:S(2)}) copy-start(f32[4,128,512]{2,1,0:T(8,128)} %image.1) | copy-start | bytes 3145732
  7.4 1.2 %copy-start.4 = (bf16[4,5]{1,0:T(4,128)(2,1)S(1)}, bf16[4,5]{1,0:T(4,128)(2,1)}, u32[]{:S(2)}) copy-start(bf16[4,5]{1,0:T(4,128)(2,1)} %weight.1) | copy-start | bytes 124
  7.4 1.2 %copy-start.5 = (s32[1,16,1]{1,2,0:T(1,128)S(1)}, s32[1,16,1]{1,2,0:T(1,128)}, u32[]{:S(2)}) copy-start(s32[1,16,1]{1,2,0:T(1,128)} %param.15) | copy-start | bytes 196
  7.4 1.2 %copy-start.6 = (s32[1,16]{1,0:T(1,128)S(1)}, s32[1,16]{1,0:T(1,128)}, u32[]{:S(2)}) copy-start(s32[1,16]{1,0:T(1,128)} %slot.1) | copy-start | bytes 196
  7.4 1.2 %copy-start.7 = (s32[16]{0:T(128)S(1)}, s32[16]{0:T(128)}, u32[]{:S(2)}) copy-start(s32[16]{0:T(128)} %owner.1) | copy-start | bytes 196
  7.4 1.4 %copy-start.8 = (bf16[512,512]{1,0:T(8,128)(2,1)S(1)}, bf16[512,512]{1,0:T(8,128)(2,1)}, u32[]{:S(2)}) copy-start(bf16[512,512]{1,0:T(8,128)(2,1)} %constant.5.clone.unsort) | copy-start | bytes 1572868
  7.4 1.5 %copy-start.9 = (bf16[512,512]{1,0:T(8,128)(2,1)S(1)}, bf16[512,512]{1,0:T(8,128)(2,1)}, u32[]{:S(2)}) copy-start(bf16[512,512]{1,0:T(8,128)(2,1)} %constant.4.clone.sort) | copy-start | bytes 1572868

commit v10 on v7

--- a/solution.py
+++ b/solution.py
@@ -127,7 +127,17 @@
     return (band + SPLIT // 2) // SPLIT, quarter * BLOCK, has_above, has_below
 
 
-def prepare_kernel(devices, taps, psf, affine, high_level, step_level, slope, rows_high, rows_low, cols_out):
+def prepare_kernel(
+    devices, taps, psf, affine,
+    high_level, step_level, slope, rows_high, rows_low, cols_out, empty_out,
+    nothing, sems,
+):
+    nothing[...] = jnp.zeros_like(nothing)
+    clears = [
+        pltpu.make_async_copy(nothing, empty_out.at[d], sems.at[d]) for d in range(devices)
+    ]
+    for copy in clears:
+        copy.start()
     ccd, top_row, has_above, has_below = whereabouts(devices)
     band_lane = iota((1, BAND), 1)
     seg = band_lane // STEP
@@ -198,6 +208,8 @@
         col_shift = a[1, 0:1] + a[1, 1:2] * (col - (WIDTH - 1) / 2.0) / WIDTH
         within = (from_lane >= 0) & (from_lane < LANES) & (step <= WARP)
         cols_out[visit] = jnp.where(within, lanczos(col_shift - step.astype(F32)), 0.0)
+    for copy in clears:
+        copy.wait()
 
 
 def prepare(taps, psf, affine, devices):
@@ -209,13 +221,16 @@
         ((V, BLOCK, LANES), BF16),
         ((V, 8, WIDTH), F32),
     ]
+    places = (devices, CAP * BLOCK + LABEL, BLOCK)
     args = [taps.transpose(1, 0, 2), psf.transpose(1, 3, 0, 2), affine.transpose(0, 2, 3, 1)]
     return pl.pallas_call(
         functools.partial(prepare_kernel, devices),
         grid=(1,),
         in_specs=[pl.BlockSpec(x.shape, lambda i, n=x.ndim: (0,) * n) for x in args],
-        out_specs=[pl.BlockSpec(shape, lambda i: (0, 0, 0)) for shape, _ in shapes],
-        out_shape=[jax.ShapeDtypeStruct(shape, kind) for shape, kind in shapes],
+        out_specs=[pl.BlockSpec(shape, lambda i: (0, 0, 0)) for shape, _ in shapes]
+        + [pl.BlockSpec(memory_space=pl.ANY)],
+        out_shape=[jax.ShapeDtypeStruct(shape, kind) for shape, kind in shapes + [(places, BF16)]],
+        scratch_shapes=[pltpu.VMEM(places[1:], BF16), pltpu.SemaphoreType.DMA((devices,))],
         compiler_params=pltpu.CompilerParams(vmem_limit_bytes=32 << 20),
         cost_estimate=pl.CostEstimate(flops=1 << 30, bytes_accessed=1 << 20, transcendentals=0),
         name="prepare",
@@ -224,7 +239,7 @@
 
 def warp_kernel(
     patch, slot, owner, weight, high_level, step_level, slope, rows_high, rows_low, col_weights,
-    sort, unsort, image, above, below, out,
+    sort, unsort, image, above, below, _, out,
     terms, matched_terms, ready, place_of, seen, label, label_ready, sem, label_sem,
 ):
     grid_step = pl.program_id(0)
@@ -350,6 +365,8 @@
     hbm = pl.BlockSpec(memory_space=pl.ANY)
     sort = deinterleave()
     constants = [jnp.asarray(sort, BF16), jnp.asarray(sort.T, BF16)]
+    *ready, places = ready
+    args = [patch, slot, owner, weight, *ready, *constants, images, above, below, places]
 
     def whole(x):
         return pl.BlockSpec(x.shape, lambda v: (0,) * x.ndim)
@@ -363,7 +380,8 @@
         in_specs=[smem, smem, smem, whole(weight)]
         + [by_visit(x) for x in ready]
         + [whole(x) for x in constants]
-        + [by_visit(x) for x in (images, above, below)],
+        + [by_visit(x) for x in (images, above, below)]
+        + [hbm],
         out_specs=hbm,
         scratch_shapes=[
             pltpu.VMEM((TOGETHER, 4, TALL, WIDTH), BF16),
@@ -376,7 +394,8 @@
             pltpu.SemaphoreType.DMA((V * BLKC,)),
             pltpu.SemaphoreType.DMA(()),
         ],
-        out_shape=jax.ShapeDtypeStruct((devices, CAP * BLOCK + LABEL, BLOCK), BF16),
+        out_shape=jax.ShapeDtypeStruct(places.shape, BF16),
+        input_output_aliases={len(args) - 1: 0},
         compiler_params=pltpu.CompilerParams(vmem_limit_bytes=32 << 20),
         cost_estimate=pl.CostEstimate(
             flops=V * 2 * STRIPS * TAPS * STRIP * BAND * WIDTH,
@@ -384,34 +403,64 @@
             transcendentals=0,
         ),
         name="match_warp",
-    )(patch, slot, owner, weight, *ready, *constants, images, above, below)
-
-
-def coadd_kernel(got, out, total, sums, out_sem):
+    )(*args)
+
+
+def coadd_kernel(got, out, total, out_sem):
     devices = got.shape[0]
-    labels = got[:, CAP * BLOCK : CAP * BLOCK + LABEL].astype(F32)[:, 0]
-    total[...] = jnp.zeros_like(total)
-    for c in range(CELLS):
-        sums[c] = 0.0
-    for source in range(devices):
-        for rank in range(CAP):
-            weight = labels[source, rank * 2]
-
-            @pl.when(weight > 0.0)
-            def _(source=source, rank=rank, weight=weight):
-                c = labels[source, rank * 2 + 1].astype(jnp.int32)
-                sums[c] += weight
-                rows = slice(rank * BLOCK, (rank + 1) * BLOCK)
-                total[c] += weight * got[source, rows].astype(F32)
-
+    wide = devices * CAP * STRIP
+    labels = got[:, CAP * BLOCK : CAP * BLOCK + LABEL][:, 0]
+    lane = iota((1, wide), 1)
+    rank = lane // STRIP % CAP
+    source = lane // (STRIP * CAP)
+
+    def spread(entry):
+        onehot = (iota((LANES, wide), 0) == rank * 2 + entry).astype(F32).astype(BF16)
+        every = jnp.dot(labels, onehot, preferred_element_type=F32)
+        return jnp.sum(
+            jnp.where(iota((devices, wide), 0) == source, every, 0.0), axis=0, keepdims=True
+        )
+
+    weights, cells = spread(0), spread(1)
+    row = iota((CELLS * STRIP, 1), 0)
+    mine = (cells == (row // STRIP).astype(F32)) & (lane % STRIP == row % STRIP)
+    matrix = jnp.where(mine, weights, 0.0)
+    sums = jnp.sum(matrix, axis=1, keepdims=True)
+    inverse = 1.0 / jnp.maximum(sums, 1.0)
+    matrix = matrix.astype(BF16)
     copies = []
-    for c in range(CELLS):
-        inverse = 1.0 / jnp.maximum(jnp.full((1, BLOCK), sums[c], F32), 1.0)
-        total[c] = total[c] * inverse
-        rows = slice(c // PSIDE * BLOCK, (c // PSIDE + 1) * BLOCK)
-        lanes = slice(c % PSIDE * BLOCK, (c % PSIDE + 1) * BLOCK)
-        copies.append(pltpu.make_async_copy(total.at[c], out.at[0, rows, lanes], out_sem.at[c]))
-        copies[-1].start()
+    for pair in range(BLOCK // STRIP // 2):
+        columns = jnp.concatenate(
+            [
+                jnp.concatenate(
+                    [
+                        got[s, r * BLOCK + k * STRIP : r * BLOCK + (k + 1) * STRIP]
+                        for s in range(devices)
+                        for r in range(CAP)
+                    ],
+                    axis=0,
+                )
+                for k in (2 * pair, 2 * pair + 1)
+            ],
+            axis=1,
+        )
+        result = jnp.dot(matrix, columns, preferred_element_type=F32) * inverse
+        for c in range(CELLS):
+            part = result[c * STRIP : (c + 1) * STRIP]
+            lanes = slice(c % PSIDE * BLOCK, (c % PSIDE + 1) * BLOCK)
+            for n in range(2):
+                first = (2 * pair + n) * STRIP
+                total[c // PSIDE, first : first + STRIP, lanes] = lane_block(part, n)
+        size = 2 * STRIP
+        for line in range(PSIDE):
+            copies.append(
+                pltpu.make_async_copy(
+                    total.at[line, pl.ds(pair * size, size)],
+                    out.at[0, pl.ds(line * BLOCK + pair * size, size)],
+                    out_sem.at[pair, line],
+                )
+            )
+            copies[-1].start()
     for copy in copies:
         copy.wait()
 
@@ -423,9 +472,8 @@
         out_specs=pl.BlockSpec(memory_space=pl.ANY),
         out_shape=jax.ShapeDtypeStruct((1, PSIDE * BLOCK, PSIDE * BLOCK), F32),
         scratch_shapes=[
-            pltpu.VMEM((CELLS, BLOCK, BLOCK), F32),
-            pltpu.SMEM((CELLS,), F32),
-            pltpu.SemaphoreType.DMA((CELLS,)),
+            pltpu.VMEM((PSIDE, BLOCK, WIDTH), F32),
+            pltpu.SemaphoreType.DMA((BLOCK // STRIP // 2, PSIDE)),
         ],
         compiler_params=pltpu.CompilerParams(vmem_limit_bytes=32 << 20),
         name="coadd",

time: 57.9 us -> 55.1 us (0.952)
  Pallas kernels: 12.9 us -> 10.9 us
    pallas_call x1, Pallas kernels: 5.19 us -> 1.6 us  [coadd(): pl.pallas_call(coadd_kernel, in_specs=[pl.BlockSpec(memory_space=pltpu.VM...]
    pallas_call x1, Pallas kernels: 1.11 us -> 2.73 us  [prepare(): pl.pallas_call(functools.partial(prepare_kernel, devices), grid=(1,), in_...]
  transfers between devices with their start and end apart: 2 -> 2, of which waited for: 0 -> 0; matrix products, arithmetic and copies ran while one was open for 0% -> 0% of each run, Pallas kernels for 2% -> 5%
where the time goes in v10:
time: 55.1 us; the launch traced here: 54.8 us
  blocking collectives  36.3 us (66%)
  Pallas kernels  10.9 us (20%)
  starting transfers between devices  4.33 us (8%)
  local copies, waits for them, and re-layouts  3.06 us (6%)
    all_to_all x1, blocking collectives, shards(): got = lax.all_to_all(sent, 'ccd', split_axis=0, concat_axis=0, tiled=True)  36.3 us
    pallas_call x1, Pallas kernels, warp(): pl.pallas_call(warp_kernel, grid=(V // TOGETHER,), in_specs=[smem, smem,...  6.61 us
    ppermute x1, starting transfers between devices, shards(): above = lax.ppermute(images[:, BLOCK - RIM:], 'ccd', down)  3.03 us
    pallas_call x1, Pallas kernels, prepare(): pl.pallas_call(functools.partial(prepare_kernel, devices), grid=(1,), in_...  2.73 us
    unnamed x20, local copies, waits for them, and re-layouts  2.18 us
    pallas_call x1, Pallas kernels, coadd(): pl.pallas_call(coadd_kernel, in_specs=[pl.BlockSpec(memory_space=pltpu.VM...  1.6 us
    ppermute x1, starting transfers between devices, shards(): below = lax.ppermute(images[:, :RIM], 'ccd', up)  1.29 us
  transfers between devices with their start and end apart: 2, of which 0 were waited for; matrix products, arithmetic and copies ran while one was open for 0% of the time, Pallas kernels for 5%

profile of v10, /device:TPU:0, one launch (start us, length us, event | category | flops | bytes accessed | tf_op | source)
XLA Modules:
  0.0 54.8 jit_solution(17358961296924880022)
XLA Ops:
  0.0 0.9 %fusion = (f32[4,8,512]{2,1,0:T(8,128)S(1)}, f32[4,8,512]{2,1,0:T(8,128)S(1)}) fusion(f32[4,128,512]{2,1,0:T(8,128)} %image.1), kind=kLoop, calls=%fused_computation | loop fusion | bytes 262144 | tf_op jit(solution)/shard_map/slice | solution.py:490
  0.9 1.3 %collective-permute-start.1 = (f32[4,8,512]{2,1,0:T(8,128)S(1)}, f32[4,8,512]{2,1,0:T(8,128)S(1)}, u32[]{:S(2)}, u32[]{:S(2)}) collective-permute-start(f32[4,8,512]{2,1,0:T(8,128)S(1)} %get-tuple-element.19), channel_id=1, source_target_pairs={{1,0},{2,1},{3,2},{4,3},{5,4},{6,5},{7,6},{8,7},{9,8},{10,9},{11,1... | collective-permute-start | bytes 196616 | tf_op jit(solution)/shard_map/ppermute | solution.py:490
  2.2 3.0 %collective-permute-start = (f32[4,8,512]{2,1,0:T(8,128)S(1)}, f32[4,8,512]{2,1,0:T(8,128)S(1)}, u32[]{:S(2)}, u32[]{:S(2)}) collective-permute-start(f32[4,8,512]{2,1,0:T(8,128)S(1)} %get-tuple-element.20), channel_id=1, source_target_pairs={{0,1},{1,2},{2,3},{3,4},{4,5},{5,6},{6,7},{7,8},{8,9},{9,10},{10,1... | collective-permute-start | bytes 196616 | tf_op jit(solution)/shard_map/ppermute | solution.py:489
  5.2 0.0 copy-start.1
  5.2 0.7 %copy-done.1 = f32[4,5,9,3]{2,0,3,1:T(4,128)S(1)} copy-done((f32[4,5,9,3]{2,0,3,1:T(4,128)S(1)}, f32[4,5,9,3]{2,0,3,1:T(4,128)}, u32[]{:S(2)}) %copy-start.1) | copy-done | bytes 2184
  6.0 0.0 copy-start.2
  6.0 0.7 %copy-done.2 = f32[2,9,11]{2,0,1:T(2,128)S(1)} copy-done((f32[2,9,11]{2,0,1:T(2,128)S(1)}, f32[2,9,11]{2,0,1:T(2,128)}, u32[]{:S(2)}) %copy-start.2) | copy-done | bytes 816
  6.7 0.0 copy-start.3
  6.7 0.7 %copy-done.3 = f32[4,5,2,2]{1,3,2,0:T(2,128)S(1)} copy-done((f32[4,5,2,2]{1,3,2,0:T(2,128)S(1)}, f32[4,5,2,2]{1,3,2,0:T(2,128)}, u32[]{:S(2)}) %copy-start.3) | copy-done | bytes 344
  7.4 0.0 copy-start
  7.4 0.0 copy-start.4
  7.4 0.0 copy-start.5
  7.4 0.0 copy-start.6
  7.4 0.0 copy-start.7
  7.4 0.0 copy-start.8
  7.4 0.0 copy-start.9
  7.4 2.7 %prepare.1 = (f32[4,176,128]{2,1,0:T(8,128)S(1)}, f32[4,176,128]{2,1,0:T(8,128)S(1)}, bf16[4,176,128]{2,1,0:T(8,128)(2,1)S(1)}, bf16[4,128,128]{2,1,0:T(8,128)(2...) custom-call(f32[9,2,11]{2,1,0:T(2,128)S(1)} %bitcast.5, ...), custom_call_target="tpu_custom_call" | custom-call | flops 1073741824 | bytes 1048576 | tf_op jit(solution)/shard_map/prepare/pallas_call | solution.py:226
  10.2 0.0 collective-permute-done.1.below
  10.2 0.0 collective-permute-done.above
  10.2 0.0 copy-done
  10.2 0.0 copy-done.4
  10.2 0.0 copy-done.5
  10.2 0.0 copy-done.6
  10.2 0.0 copy-done.7
  10.2 0.0 copy-done.8
  10.2 0.0 copy-done.9
  10.3 6.6 %match_warp.1 = bf16[16,272,128]{2,1,0:T(8,128)(2,1)S(1)} custom-call(s32[1,16]{1,0:T(1,128)S(1)} %bitcast.7, s32[1,16]{1,0:T(1,128)S(1)} %copy-done.6, s32[16]{0:T(128)S(1)} %copy-done.7, bf16[4,5]{1,0:T(4,128)(2,1)S(1)} %copy-done.4, f32[4,176,128]{2,1,0:T(8,128)S(1)} %get-tuple-element.12.high_level, ...), custom_call_target="tpu_custom_call", output_to_operand_aliasing={{}: (15, {})} | custom-call | flops 1660944384 | bytes 1572864 | tf_op jit(solution)/shard_map/match_warp/pallas_call | solution.py:377
  16.9 36.3 %all_to_all.5.got = bf16[16,272,128]{2,1,0:T(8,128)(2,1)S(1)} all-to-all(bf16[16,272,128]{2,1,0:T(8,128)(2,1)S(1)} %match_warp.1), channel_id=1, replica_groups=mesh['group'=2,'ccd'=16] {'ccd'}, dimensions={0} | all-to-all | bytes 2228224 | tf_op jit(solution)/shard_map/all_to_all | solution.py:496
  53.2 1.6 %coadd.1 = f32[1,512,512]{2,1,0:T(8,128)} custom-call(bf16[16,272,128]{2,1,0:T(8,128)(2,1)S(1)} %all_to_all.5.got), custom_call_target="tpu_custom_call" | custom-call | tf_op jit(solution)/shard_map/coadd/pallas_call | solution.py:469
Async XLA Ops:
  0.9 9.3 %collective-permute-start.1 = (f32[4,8,512]{2,1,0:T(8,128)S(1)}, f32[4,8,512]{2,1,0:T(8,128)S(1)}, u32[]{:S(2)}, u32[]{:S(2)}) collective-permute-start(f32[4,8,512]{2,1,0:T(8,128)S(1)} %get-tuple-element.19), channel_id=1, source_target_pairs={{1,0},{2,1},{3,2},{4,3},{5,4},{6,5},{7,6},{8,7},{9,8},{10,9},{11,1... | collective-permute-start | bytes 196616 | tf_op jit(solution)/shard_map/ppermute | solution.py:490
  2.2 8.0 %collective-permute-start = (f32[4,8,512]{2,1,0:T(8,128)S(1)}, f32[4,8,512]{2,1,0:T(8,128)S(1)}, u32[]{:S(2)}, u32[]{:S(2)}) collective-permute-start(f32[4,8,512]{2,1,0:T(8,128)S(1)} %get-tuple-element.20), channel_id=1, source_target_pairs={{0,1},{1,2},{2,3},{3,4},{4,5},{5,6},{6,7},{7,8},{8,9},{9,10},{10,1... | collective-permute-start | bytes 196616 | tf_op jit(solution)/shard_map/ppermute | solution.py:489
  5.2 0.8 %copy-start.1 = (f32[4,5,9,3]{2,0,3,1:T(4,128)S(1)}, f32[4,5,9,3]{2,0,3,1:T(4,128)}, u32[]{:S(2)}) copy-start(f32[4,5,9,3]{2,0,3,1:T(4,128)} %param.12) | copy-start | bytes 6484
  6.0 0.7 %copy-start.2 = (f32[2,9,11]{2,0,1:T(2,128)S(1)}, f32[2,9,11]{2,0,1:T(2,128)}, u32[]{:S(2)}) copy-start(f32[2,9,11]{2,0,1:T(2,128)} %param.11) | copy-start | bytes 2380
  6.7 0.7 %copy-start.3 = (f32[4,5,2,2]{1,3,2,0:T(2,128)S(1)}, f32[4,5,2,2]{1,3,2,0:T(2,128)}, u32[]{:S(2)}) copy-start(f32[4,5,2,2]{1,3,2,0:T(2,128)} %param.13) | copy-start | bytes 964
  7.4 2.8 %copy-start = (f32[4,128,512]{2,1,0:T(8,128)S(1)}, f32[4,128,512]{2,1,0:T(8,128)}, u32[]{:S(2)}) copy-start(f32[4,128,512]{2,1,0:T(8,128)} %image.1) | copy-start | bytes 3145732
  7.4 2.8 %copy-start.4 = (bf16[4,5]{1,0:T(4,128)(2,1)S(1)}, bf16[4,5]{1,0:T(4,128)(2,1)}, u32[]{:S(2)}) copy-start(bf16[4,5]{1,0:T(4,128)(2,1)} %weight.1) | copy-start | bytes 124
  7.4 2.8 %copy-start.5 = (s32[1,16,1]{1,2,0:T(1,128)S(1)}, s32[1,16,1]{1,2,0:T(1,128)}, u32[]{:S(2)}) copy-start(s32[1,16,1]{1,2,0:T(1,128)} %param.15) | copy-start | bytes 196
  7.4 2.8 %copy-start.6 = (s32[1,16]{1,0:T(1,128)S(1)}, s32[1,16]{1,0:T(1,128)}, u32[]{:S(2)}) copy-start(s32[1,16]{1,0:T(1,128)} %slot.1) | copy-start | bytes 196
  7.4 2.8 %copy-start.7 = (s32[16]{0:T(128)S(1)}, s32[16]{0:T(128)}, u32[]{:S(2)}) copy-start(s32[16]{0:T(128)} %owner.1) | copy-start | bytes 196
  7.4 2.8 %copy-start.8 = (bf16[512,512]{1,0:T(8,128)(2,1)S(1)}, bf16[512,512]{1,0:T(8,128)(2,1)}, u32[]{:S(2)}) copy-start(bf16[512,512]{1,0:T(8,128)(2,1)} %constant.5.clone.unsort) | copy-start | bytes 1572868
  7.4 2.8 %copy-start.9 = (bf16[512,512]{1,0:T(8,128)(2,1)S(1)}, bf16[512,512]{1,0:T(8,128)(2,1)}, u32[]{:S(2)}) copy-start(bf16[512,512]{1,0:T(8,128)(2,1)} %constant.4.clone.sort) | copy-start | bytes 1572868

commit v11 on v10

--- a/solution.py
+++ b/solution.py
@@ -127,18 +127,36 @@
     return (band + SPLIT // 2) // SPLIT, quarter * BLOCK, has_above, has_below
 
 
+def lanczos_kernel(devices, affine, rows_out, cols_out):
+    ccd, top_row, has_above, has_below = whereabouts(devices)
+    lane = iota((1, LANES), 1)
+    for visit in range(V):
+        a = jnp.sum(
+            jnp.where(iota((1, 1, affine.shape[3]), 2) == ccd, affine[visit], 0.0),
+            axis=2, keepdims=True,
+        )
+        offset = iota((8, LANES), 0) - WARP
+        row = (top_row + lane).astype(F32)
+        shift = a[0, 0:1] + a[0, 1:2] * (row - (HEIGHT - 1) / 2.0) / HEIGHT
+        band_row = lane + offset
+        keep = (offset <= WARP) & ((band_row >= 0) | has_above) & ((band_row < BLOCK) | has_below)
+        weights = jnp.where(keep, lanczos(shift - offset.astype(F32)), 0.0)
+        rows_out[visit] = jnp.concatenate([weights, jnp.zeros((LANES - 8, LANES), F32)], axis=0).T
+        lanes = iota((8, WIDTH), 1)
+        step = iota((8, WIDTH), 0) - WARP
+        block = lanes // LANES
+        carry = (block + step + LANE_BLOCKS) // LANE_BLOCKS - 1
+        from_lane = lanes % LANES - carry
+        col = (from_lane * LANE_BLOCKS + block).astype(F32)
+        col_shift = a[1, 0:1] + a[1, 1:2] * (col - (WIDTH - 1) / 2.0) / WIDTH
+        within = (from_lane >= 0) & (from_lane < LANES) & (step <= WARP)
+        cols_out[visit] = jnp.where(within, lanczos(col_shift - step.astype(F32)), 0.0)
+
+
 def prepare_kernel(
-    devices, taps, psf, affine,
-    high_level, step_level, slope, rows_high, rows_low, cols_out, empty_out,
-    nothing, sems,
+    devices, taps, psf, row_weights, high_level, step_level, slope, rows_high, rows_low
 ):
-    nothing[...] = jnp.zeros_like(nothing)
-    clears = [
-        pltpu.make_async_copy(nothing, empty_out.at[d], sems.at[d]) for d in range(devices)
-    ]
-    for copy in clears:
-        copy.start()
-    ccd, top_row, has_above, has_below = whereabouts(devices)
+    ccd, top_row, _, _ = whereabouts(devices)
     band_lane = iota((1, BAND), 1)
     seg = band_lane // STEP
     lane = iota((1, LANES), 1)
@@ -181,65 +199,50 @@
             high = jnp.round(y)
             step_level[visit, at] = jnp.where(low_lanes, y - high, high)
 
-        a = jnp.sum(
-            jnp.where(iota((1, 1, affine.shape[3]), 2) == ccd, affine[visit], 0.0),
-            axis=2, keepdims=True,
-        )
-        offset = iota((8, LANES), 0) - WARP
-        row = (top_row + lane).astype(F32)
-        shift = a[0, 0:1] + a[0, 1:2] * (row - (HEIGHT - 1) / 2.0) / HEIGHT
-        band_row = lane + offset
-        keep = (offset <= WARP) & ((band_row >= 0) | has_above) & ((band_row < BLOCK) | has_below)
-        weights = jnp.where(keep, lanczos(shift - offset.astype(F32)), 0.0) * unit
-        weights = jnp.concatenate([weights, jnp.zeros((LANES - 8, LANES), F32)], axis=0).T
         for h in range(HALVES):
             at = slice(h * ROWS, (h + 1) * ROWS)
-            matrix = staircase(weights[at], 0)
+            matrix = staircase(row_weights[visit, at] * unit, 0)
             high = matrix.astype(BF16)
             rows_high[visit, at] = high
             rows_low[visit, at] = (matrix - high.astype(F32)).astype(BF16)
 
-        lanes = iota((8, WIDTH), 1)
-        step = iota((8, WIDTH), 0) - WARP
-        block = lanes // LANES
-        carry = (block + step + LANE_BLOCKS) // LANE_BLOCKS - 1
-        from_lane = lanes % LANES - carry
-        col = (from_lane * LANE_BLOCKS + block).astype(F32)
-        col_shift = a[1, 0:1] + a[1, 1:2] * (col - (WIDTH - 1) / 2.0) / WIDTH
-        within = (from_lane >= 0) & (from_lane < LANES) & (step <= WARP)
-        cols_out[visit] = jnp.where(within, lanczos(col_shift - step.astype(F32)), 0.0)
-    for copy in clears:
-        copy.wait()
-
-
-def prepare(taps, psf, affine, devices):
-    shapes = [
-        ((V, TAPS * STRIP, LANES), F32),
-        ((V, TAPS * STRIP, LANES), F32),
-        ((V, TAPS * STRIP, BAND - LANES), BF16),
-        ((V, BLOCK, LANES), BF16),
-        ((V, BLOCK, LANES), BF16),
-        ((V, 8, WIDTH), F32),
-    ]
-    places = (devices, CAP * BLOCK + LABEL, BLOCK)
-    args = [taps.transpose(1, 0, 2), psf.transpose(1, 3, 0, 2), affine.transpose(0, 2, 3, 1)]
+
+def small_kernel(body, name, args, shapes):
     return pl.pallas_call(
-        functools.partial(prepare_kernel, devices),
+        body,
         grid=(1,),
         in_specs=[pl.BlockSpec(x.shape, lambda i, n=x.ndim: (0,) * n) for x in args],
-        out_specs=[pl.BlockSpec(shape, lambda i: (0, 0, 0)) for shape, _ in shapes]
-        + [pl.BlockSpec(memory_space=pl.ANY)],
-        out_shape=[jax.ShapeDtypeStruct(shape, kind) for shape, kind in shapes + [(places, BF16)]],
-        scratch_shapes=[pltpu.VMEM(places[1:], BF16), pltpu.SemaphoreType.DMA((devices,))],
+        out_specs=[pl.BlockSpec(shape, lambda i: (0, 0, 0)) for shape, _ in shapes],
+        out_shape=[jax.ShapeDtypeStruct(shape, kind) for shape, kind in shapes],
         compiler_params=pltpu.CompilerParams(vmem_limit_bytes=32 << 20),
         cost_estimate=pl.CostEstimate(flops=1 << 30, bytes_accessed=1 << 20, transcendentals=0),
-        name="prepare",
+        name=name,
     )(*args)
+
+
+def prepare(taps, psf, affine, devices):
+    row_weights, col_weights = small_kernel(
+        functools.partial(lanczos_kernel, devices), "lanczos_weights",
+        [affine.transpose(0, 2, 3, 1)],
+        [((V, BLOCK, LANES), F32), ((V, 8, WIDTH), F32)],
+    )
+    matrices = small_kernel(
+        functools.partial(prepare_kernel, devices), "matrices",
+        [taps.transpose(1, 0, 2), psf.transpose(1, 3, 0, 2), row_weights],
+        [
+            ((V, TAPS * STRIP, LANES), F32),
+            ((V, TAPS * STRIP, LANES), F32),
+            ((V, TAPS * STRIP, BAND - LANES), BF16),
+            ((V, BLOCK, LANES), BF16),
+            ((V, BLOCK, LANES), BF16),
+        ],
+    )
+    return [*matrices, col_weights]
 
 
 def warp_kernel(
     patch, slot, owner, weight, high_level, step_level, slope, rows_high, rows_low, col_weights,
-    sort, unsort, image, above, below, _, out,
+    sort, unsort, image, above, below, out,
     terms, matched_terms, ready, place_of, seen, label, label_ready, sem, label_sem,
 ):
     grid_step = pl.program_id(0)
@@ -365,8 +368,6 @@
     hbm = pl.BlockSpec(memory_space=pl.ANY)
     sort = deinterleave()
     constants = [jnp.asarray(sort, BF16), jnp.asarray(sort.T, BF16)]
-    *ready, places = ready
-    args = [patch, slot, owner, weight, *ready, *constants, images, above, below, places]
 
     def whole(x):
         return pl.BlockSpec(x.shape, lambda v: (0,) * x.ndim)
@@ -380,8 +381,7 @@
         in_specs=[smem, smem, smem, whole(weight)]
         + [by_visit(x) for x in ready]
         + [whole(x) for x in constants]
-        + [by_visit(x) for x in (images, above, below)]
-        + [hbm],
+        + [by_visit(x) for x in (images, above, below)],
         out_specs=hbm,
         scratch_shapes=[
             pltpu.VMEM((TOGETHER, 4, TALL, WIDTH), BF16),
@@ -394,8 +394,7 @@
             pltpu.SemaphoreType.DMA((V * BLKC,)),
             pltpu.SemaphoreType.DMA(()),
         ],
-        out_shape=jax.ShapeDtypeStruct(places.shape, BF16),
-        input_output_aliases={len(args) - 1: 0},
+        out_shape=jax.ShapeDtypeStruct((devices, CAP * BLOCK + LABEL, BLOCK), BF16),
         compiler_params=pltpu.CompilerParams(vmem_limit_bytes=32 << 20),
         cost_estimate=pl.CostEstimate(
             flops=V * 2 * STRIPS * TAPS * STRIP * BAND * WIDTH,
@@ -403,7 +402,7 @@
             transcendentals=0,
         ),
         name="match_warp",
-    )(*args)
+    )(patch, slot, owner, weight, *ready, *constants, images, above, below)
 
 
 def coadd_kernel(got, out, total, out_sem):
@@ -428,17 +427,22 @@
     sums = jnp.sum(matrix, axis=1, keepdims=True)
     inverse = 1.0 / jnp.maximum(sums, 1.0)
     matrix = matrix.astype(BF16)
+    taken = {}
+    for r in range(CAP):
+        column = jnp.broadcast_to(labels[:, 2 * r : 2 * r + 1].astype(F32), (devices, LANES))
+        for s in range(devices):
+            taken[s, r] = jnp.broadcast_to(column[s : s + 1], (STRIP, LANES)).astype(BF16) > 0
+
+    def tile(s, r, k):
+        first = r * BLOCK + k * STRIP
+        return jnp.where(taken[s, r], got[s, first : first + STRIP], jnp.zeros((), BF16))
+
     copies = []
     for pair in range(BLOCK // STRIP // 2):
         columns = jnp.concatenate(
             [
                 jnp.concatenate(
-                    [
-                        got[s, r * BLOCK + k * STRIP : r * BLOCK + (k + 1) * STRIP]
-                        for s in range(devices)
-                        for r in range(CAP)
-                    ],
-                    axis=0,
+                    [tile(s, r, k) for s in range(devices) for r in range(CAP)], axis=0
                 )
                 for k in (2 * pair, 2 * pair + 1)
             ],

time: 55.1 us -> 53.5 us (0.971)
  Pallas kernels: 10.9 us -> 9.48 us
  local copies, waits for them, and re-layouts: 3.06 us -> 2.49 us
    pallas_call x1 -> x2, Pallas kernels: 2.73 us -> 1.35 us  [small_kernel(): pl.pallas_call(body, grid=(1,), in_specs=[pl.BlockSpec(x.shape, lambda i,...]
    unnamed x20, local copies, waits for them, and re-layouts: 2.18 us -> 1.61 us
  transfers between devices with their start and end apart: 2 -> 2, of which waited for: 0 -> 0; matrix products, arithmetic and copies ran while one was open for 0% -> 0% of each run, Pallas kernels for 5% -> 3%
where the time goes in v11:
time: 53.5 us; the launch traced here: 53.1 us
  blocking collectives  36.7 us (69%)
  Pallas kernels  9.48 us (18%)
  starting transfers between devices  4.33 us (8%)
  local copies, waits for them, and re-layouts  2.49 us (5%)
    all_to_all x1, blocking collectives, shards(): got = lax.all_to_all(sent, 'ccd', split_axis=0, concat_axis=0, tiled=True)  36.7 us
    pallas_call x1, Pallas kernels, warp(): pl.pallas_call(warp_kernel, grid=(V // TOGETHER,), in_specs=[smem, smem,...  6.45 us
    ppermute x1, starting transfers between devices, shards(): above = lax.ppermute(images[:, BLOCK - RIM:], 'ccd', down)  3.03 us
    pallas_call x1, Pallas kernels, coadd(): pl.pallas_call(coadd_kernel, in_specs=[pl.BlockSpec(memory_space=pltpu.VM...  1.67 us
    unnamed x20, local copies, waits for them, and re-layouts  1.61 us
    pallas_call x2, Pallas kernels, small_kernel(): pl.pallas_call(body, grid=(1,), in_specs=[pl.BlockSpec(x.shape, lambda i,...  1.35 us
    ppermute x1, starting transfers between devices, shards(): below = lax.ppermute(images[:, :RIM], 'ccd', up)  1.29 us
  transfers between devices with their start and end apart: 2, of which 0 were waited for; matrix products, arithmetic and copies ran while one was open for 0% of the time, Pallas kernels for 3%

profile of v11, /device:TPU:0, one launch (start us, length us, event | category | flops | bytes accessed | tf_op | source)
XLA Modules:
  0.0 53.1 jit_solution(9486323345883494381)
XLA Ops:
  0.0 0.9 %fusion = (f32[4,8,512]{2,1,0:T(8,128)S(1)}, f32[4,8,512]{2,1,0:T(8,128)S(1)}) fusion(f32[4,128,512]{2,1,0:T(8,128)} %image.1), kind=kLoop, calls=%fused_computation | loop fusion | bytes 262144 | tf_op jit(solution)/shard_map/slice | solution.py:494
  0.9 1.3 %collective-permute-start.1 = (f32[4,8,512]{2,1,0:T(8,128)S(1)}, f32[4,8,512]{2,1,0:T(8,128)S(1)}, u32[]{:S(2)}, u32[]{:S(2)}) collective-permute-start(f32[4,8,512]{2,1,0:T(8,128)S(1)} %get-tuple-element.19), channel_id=1, source_target_pairs={{1,0},{2,1},{3,2},{4,3},{5,4},{6,5},{7,6},{8,7},{9,8},{10,9},{11,1... | collective-permute-start | bytes 196616 | tf_op jit(solution)/shard_map/ppermute | solution.py:494
  2.2 3.0 %collective-permute-start = (f32[4,8,512]{2,1,0:T(8,128)S(1)}, f32[4,8,512]{2,1,0:T(8,128)S(1)}, u32[]{:S(2)}, u32[]{:S(2)}) collective-permute-start(f32[4,8,512]{2,1,0:T(8,128)S(1)} %get-tuple-element.20), channel_id=1, source_target_pairs={{0,1},{1,2},{2,3},{3,4},{4,5},{5,6},{6,7},{7,8},{8,9},{9,10},{10,1... | collective-permute-start | bytes 196616 | tf_op jit(solution)/shard_map/ppermute | solution.py:493
  5.2 0.0 copy-start.3
  5.2 0.7 %copy-done.3 = f32[4,5,2,2]{1,3,2,0:T(2,128)S(1)} copy-done((f32[4,5,2,2]{1,3,2,0:T(2,128)S(1)}, f32[4,5,2,2]{1,3,2,0:T(2,128)}, u32[]{:S(2)}) %copy-start.3) | copy-done | bytes 344
  5.9 0.0 copy-start.1
  5.9 0.0 copy-start.2
  5.9 0.4 lanczos_weights.1
  6.3 0.4 copy-done.1
  6.7 0.0 copy-done.2
  6.7 0.0 copy-start
  6.7 0.0 copy-start.4
  6.7 0.0 copy-start.5
  6.7 0.0 copy-start.6
  6.7 0.0 copy-start.7
  6.7 0.0 copy-start.8
  6.7 0.0 copy-start.9
  6.7 1.0 %matrices.1 = (f32[4,176,128]{2,1,0:T(8,128)S(1)}, f32[4,176,128]{2,1,0:T(8,128)S(1)}, bf16[4,176,128]{2,1,0:T(8,128)(2,1)S(1)}, bf16[4,128,128]{2,1,0:T(8,128)(2,1)S(1)}, bf16[4,128,128]{2,1,0:T(8,128)(2,1)S(1)}) custom-call(f32[9,2,11]{2,1,0:T(2,128)S(1)} %bitcast.5, f32[5,3,4,9]{3,2,1,0:T(4,128)S(1)} %bitcast.4, ...), custom_call_target="tpu_custom_call" | custom-call | flops 1073741824 | bytes 1048576 | tf_op jit(solution)/shard_map/matrices/pallas_call | solution.py:211
  7.7 0.0 collective-permute-done.1.below
  7.7 0.0 collective-permute-done.above
  7.7 0.2 copy-done
  7.9 0.0 copy-done.4
  7.9 0.0 copy-done.5
  7.9 0.0 copy-done.6
  7.9 0.0 copy-done.7
  7.9 0.2 copy-done.8
  8.1 0.2 copy-done.9
  8.3 6.5 %match_warp.1 = bf16[16,272,128]{2,1,0:T(8,128)(2,1)S(1)} custom-call(s32[1,16]{1,0:T(1,128)S(1)} %bitcast.7, s32[1,16]{1,0:T(1,128)S(1)} %copy-done.6, s32[16]{0:T(128)S(1)} %copy-done.7, bf16[4,5]{1,0:T(4,128)(2,1)S(1)} %copy-done.4, f32[4,176,128]{2,1,0:T(8,128)S(1)} %get-tuple-element.13.high_level, f32[4,176,128]{2,1,0:T(8,128)S(1)} %get-tuple-element.14.step_level, ...), custom_call_target="tpu_custom_call" | custom-call | flops 1660944384 | bytes 1572864 | tf_op jit(solution)/shard_map/match_warp/pallas_call | solution.py:378
  14.7 36.7 %all_to_all.5.got = bf16[16,272,128]{2,1,0:T(8,128)(2,1)S(1)} all-to-all(bf16[16,272,128]{2,1,0:T(8,128)(2,1)S(1)} %match_warp.1), channel_id=1, replica_groups=mesh['group'=2,'ccd'=16] {'ccd'}, dimensions={0} | all-to-all | bytes 2228224 | tf_op jit(solution)/shard_map/all_to_all | solution.py:500
  51.4 1.7 %coadd.1 = f32[1,512,512]{2,1,0:T(8,128)} custom-call(bf16[16,272,128]{2,1,0:T(8,128)(2,1)S(1)} %all_to_all.5.got), custom_call_target="tpu_custom_call" | custom-call | tf_op jit(solution)/shard_map/coadd/pallas_call | solution.py:473
Async XLA Ops:
  0.9 6.8 %collective-permute-start.1 = (f32[4,8,512]{2,1,0:T(8,128)S(1)}, f32[4,8,512]{2,1,0:T(8,128)S(1)}, u32[]{:S(2)}, u32[]{:S(2)}) collective-permute-start(f32[4,8,512]{2,1,0:T(8,128)S(1)} %get-tuple-element.19), channel_id=1, source_target_pairs={{1,0},{2,1},{3,2},{4,3},{5,4},{6,5},{7,6},{8,7},{9,8},{10,9},{11,1... | collective-permute-start | bytes 196616 | tf_op jit(solution)/shard_map/ppermute | solution.py:494
  2.2 5.6 %collective-permute-start = (f32[4,8,512]{2,1,0:T(8,128)S(1)}, f32[4,8,512]{2,1,0:T(8,128)S(1)}, u32[]{:S(2)}, u32[]{:S(2)}) collective-permute-start(f32[4,8,512]{2,1,0:T(8,128)S(1)} %get-tuple-element.20), channel_id=1, source_target_pairs={{0,1},{1,2},{2,3},{3,4},{4,5},{5,6},{6,7},{7,8},{8,9},{9,10},{10,1... | collective-permute-start | bytes 196616 | tf_op jit(solution)/shard_map/ppermute | solution.py:493
  5.2 0.7 %copy-start.3 = (f32[4,5,2,2]{1,3,2,0:T(2,128)S(1)}, f32[4,5,2,2]{1,3,2,0:T(2,128)}, u32[]{:S(2)}) copy-start(f32[4,5,2,2]{1,3,2,0:T(2,128)} %param.13) | copy-start | bytes 964
  5.9 0.8 %copy-start.1 = (f32[4,5,9,3]{2,0,3,1:T(4,128)S(1)}, f32[4,5,9,3]{2,0,3,1:T(4,128)}, u32[]{:S(2)}) copy-start(f32[4,5,9,3]{2,0,3,1:T(4,128)} %param.12) | copy-start | bytes 6484
  5.9 0.8 %copy-start.2 = (f32[2,9,11]{2,0,1:T(2,128)S(1)}, f32[2,9,11]{2,0,1:T(2,128)}, u32[]{:S(2)}) copy-start(f32[2,9,11]{2,0,1:T(2,128)} %param.11) | copy-start | bytes 2380
  6.7 1.2 %copy-start = (f32[4,128,512]{2,1,0:T(8,128)S(1)}, f32[4,128,512]{2,1,0:T(8,128)}, u32[]{:S(2)}) copy-start(f32[4,128,512]{2,1,0:T(8,128)} %image.1) | copy-start | bytes 3145732
  6.7 1.2 %copy-start.4 = (bf16[4,5]{1,0:T(4,128)(2,1)S(1)}, bf16[4,5]{1,0:T(4,128)(2,1)}, u32[]{:S(2)}) copy-start(bf16[4,5]{1,0:T(4,128)(2,1)} %weight.1) | copy-start | bytes 124
  6.7 1.2 %copy-start.5 = (s32[1,16,1]{1,2,0:T(1,128)S(1)}, s32[1,16,1]{1,2,0:T(1,128)}, u32[]{:S(2)}) copy-start(s32[1,16,1]{1,2,0:T(1,128)} %param.15) | copy-start | bytes 196
  6.7 1.2 %copy-start.6 = (s32[1,16]{1,0:T(1,128)S(1)}, s32[1,16]{1,0:T(1,128)}, u32[]{:S(2)}) copy-start(s32[1,16]{1,0:T(1,128)} %slot.1) | copy-start | bytes 196
  6.7 1.2 %copy-start.7 = (s32[16]{0:T(128)S(1)}, s32[16]{0:T(128)}, u32[]{:S(2)}) copy-start(s32[16]{0:T(128)} %owner.1) | copy-start | bytes 196
  6.7 1.4 %copy-start.8 = (bf16[512,512]{1,0:T(8,128)(2,1)S(1)}, bf16[512,512]{1,0:T(8,128)(2,1)}, u32[]{:S(2)}) copy-start(bf16[512,512]{1,0:T(8,128)(2,1)} %constant.5.clone.unsort) | copy-start | bytes 1572868
  6.7 1.5 %copy-start.9 = (bf16[512,512]{1,0:T(8,128)(2,1)S(1)}, bf16[512,512]{1,0:T(8,128)(2,1)}, u32[]{:S(2)}) copy-start(bf16[512,512]{1,0:T(8,128)(2,1)} %constant.4.clone.sort) | copy-start | bytes 1572868

commit v12 on v11

--- a/solution.py
+++ b/solution.py
@@ -243,156 +243,131 @@
 def warp_kernel(
     patch, slot, owner, weight, high_level, step_level, slope, rows_high, rows_low, col_weights,
     sort, unsort, image, above, below, out,
-    terms, matched_terms, ready, place_of, seen, label, label_ready, sem, label_sem,
+    terms, matched_terms, place_of, seen, label,
 ):
-    grid_step = pl.program_id(0)
-    grid_steps = pl.num_programs(0)
     devices = label.shape[0]
     ccd, _, has_above, has_below = whereabouts(devices)
     tall = BLOCK + 2 * RIM
     lane = iota((1, LANES), 1)
-    label_copy = pltpu.make_async_copy(label_ready, out.at[:, pl.ds(CAP * BLOCK, LABEL)], label_sem)
-
-    @pl.when(grid_step == 0)
-    def _():
-        terms[:, :, tall:] = jnp.zeros((TOGETHER, 4, TALL - tall, WIDTH), BF16)
-        label[...] = jnp.zeros_like(label)
-
-        def clear(p, _):
-            seen[p] = 0
-            return 0
-
-        lax.fori_loop(0, owner.shape[0], clear, 0)
-        own = jnp.where(iota(weight.shape, 1) == ccd, weight[...].astype(F32), 0.0)
-        own = jnp.sum(own, axis=1, keepdims=True)
-        for block in range(V * BLKC):
-            p = patch[0, block]
-            to = owner[p]
-            rank = seen[p]
-            seen[p] = rank + 1
-            place_of[block] = to * CAP + rank
-            line = label[pl.ds(to, 1), :]
-            line = jnp.where(lane == rank * 2, own[block // BLKC : block // BLKC + 1], line)
-            line = jnp.where(lane == rank * 2 + 1, slot[0, block].astype(F32), line)
-            label[pl.ds(to, 1), :] = line
-        label_ready[...] = jnp.broadcast_to(
-            label[...].reshape(devices, 1, LANES), (devices, LABEL, LANES)
-        ).astype(BF16)
-        label_copy.start()
-
-    col_pos = (2.0 * column_at(iota((1, WIDTH), 1)).astype(F32) + 1.0) / WIDTH - 1.0
-    for i in range(TOGETHER):
-        raw = jnp.concatenate(
-            [jnp.where(has_above, above[i], 0.0), image[i], jnp.where(has_below, below[i], 0.0)],
-            axis=0,
-        )
-        raw_high = raw.astype(BF16)
-        raw_low = (raw - raw_high.astype(F32)).astype(BF16)
-        sorted_terms = jnp.dot(
-            jnp.concatenate([raw_high, raw_low], axis=0), sort[...], preferred_element_type=F32
-        )
-        high, low = sorted_terms[:tall], sorted_terms[tall:]
-        tilted = (high + low) * col_pos
-        tilted_high = tilted.astype(BF16)
-        terms[i, 0, :tall] = high.astype(BF16)
-        terms[i, 1, :tall] = low.astype(BF16)
-        terms[i, 2, :tall] = tilted_high
-        terms[i, 3, :tall] = (tilted - tilted_high.astype(F32)).astype(BF16)
-
-    filler = jnp.zeros((BAND - GROUPS * STEP, WIDTH), BF16)
-    for k in range(STRIPS):
+    terms[:, :, tall:] = jnp.zeros((TOGETHER, 4, TALL - tall, WIDTH), BF16)
+    label[...] = jnp.zeros_like(label)
+
+    def clear(p, _):
+        seen[p] = 0
+        return 0
+
+    lax.fori_loop(0, owner.shape[0], clear, 0)
+    own = jnp.where(iota(weight.shape, 1) == ccd, weight[...].astype(F32), 0.0)
+    own = jnp.sum(own, axis=1, keepdims=True)
+    for block in range(V * BLKC):
+        p = patch[0, block]
+        to = owner[p]
+        rank = seen[p]
+        seen[p] = rank + 1
+        place_of[block] = to * CAP + rank
+        line = label[pl.ds(to, 1), :]
+        line = jnp.where(lane == rank * 2, own[block // BLKC : block // BLKC + 1], line)
+        line = jnp.where(lane == rank * 2 + 1, slot[0, block].astype(F32), line)
+        label[pl.ds(to, 1), :] = line
+    out[:, CAP * BLOCK :] = jnp.broadcast_to(
+        label[...].reshape(devices, 1, LANES), (devices, LABEL, LANES)
+    ).astype(BF16)
+
+    def some_visits(turn, _):
+        col_pos = (2.0 * column_at(iota((1, WIDTH), 1)).astype(F32) + 1.0) / WIDTH - 1.0
         for i in range(TOGETHER):
-            level = high_level[i]
-            if k != MIDDLE:
-                level = level + float(k - MIDDLE) * step_level[i]
-            matrix = jnp.concatenate([level.astype(BF16), slope[i]], axis=1)
-            rows = slice(k * STRIP, k * STRIP + STEP)
-            columns = jnp.concatenate(
-                [terms[i, h, rows] for h in (0, 1, 0, 2, 3, 2)] + [filler], axis=0
+            raw = jnp.concatenate(
+                [jnp.where(has_above, above[turn * TOGETHER + i], 0.0), image[turn * TOGETHER + i], jnp.where(has_below, below[turn * TOGETHER + i], 0.0)],
+                axis=0,
             )
-            results = jnp.dot(matrix, columns, preferred_element_type=F32)
+            raw_high = raw.astype(BF16)
+            raw_low = (raw - raw_high.astype(F32)).astype(BF16)
+            sorted_terms = jnp.dot(
+                jnp.concatenate([raw_high, raw_low], axis=0), sort[...], preferred_element_type=F32
+            )
+            high, low = sorted_terms[:tall], sorted_terms[tall:]
+            tilted = (high + low) * col_pos
+            tilted_high = tilted.astype(BF16)
+            terms[i, 0, :tall] = high.astype(BF16)
+            terms[i, 1, :tall] = low.astype(BF16)
+            terms[i, 2, :tall] = tilted_high
+            terms[i, 3, :tall] = (tilted - tilted_high.astype(F32)).astype(BF16)
+
+        filler = jnp.zeros((BAND - GROUPS * STEP, WIDTH), BF16)
+        for k in range(STRIPS):
+            for i in range(TOGETHER):
+                level = high_level[turn * TOGETHER + i]
+                if k != MIDDLE:
+                    level = level + float(k - MIDDLE) * step_level[turn * TOGETHER + i]
+                matrix = jnp.concatenate([level.astype(BF16), slope[turn * TOGETHER + i]], axis=1)
+                rows = slice(k * STRIP, k * STRIP + STEP)
+                columns = jnp.concatenate(
+                    [terms[i, h, rows] for h in (0, 1, 0, 2, 3, 2)] + [filler], axis=0
+                )
+                results = jnp.dot(matrix, columns, preferred_element_type=F32)
+                blocks = lane_sum(
+                    lambda u, v, w: lane_block(results[u * STRIP : (u + 1) * STRIP], w),
+                    lane, TAPS, False,
+                )
+                matched = jnp.concatenate(blocks, axis=1)
+                high = matched.astype(BF16)
+                at = slice(k * STRIP, (k + 1) * STRIP)
+                matched_terms[i, 0, at] = high
+                matched_terms[i, 1, at] = (matched - high.astype(F32)).astype(BF16)
+
+        empty = jnp.zeros((LANES - WINDOW, WIDTH), BF16)
+        warped = []
+        for i in range(TOGETHER):
+            halves = []
+            for h in range(HALVES):
+                high = rows_high[turn * TOGETHER + i, h * ROWS : (h + 1) * ROWS]
+                low = rows_low[turn * TOGETHER + i, h * ROWS : (h + 1) * ROWS]
+                rows = slice(h * ROWS, h * ROWS + WINDOW)
+                first = jnp.concatenate([matched_terms[i, 0, rows], empty], axis=0)
+                second = jnp.concatenate([matched_terms[i, 1, rows], empty], axis=0)
+                both = jnp.dot(
+                    jnp.concatenate([high, high], axis=1), jnp.concatenate([first, second], axis=0),
+                    preferred_element_type=F32,
+                )
+                halves.append(both + jnp.dot(low, first, preferred_element_type=F32))
+            warped.append(jnp.concatenate(halves, axis=0))
+
+        for i in range(TOGETHER):
+            cols = col_weights[turn * TOGETHER + i]
             blocks = lane_sum(
-                lambda u, v, w: lane_block(results[u * STRIP : (u + 1) * STRIP], w),
-                lane, TAPS, False,
+                lambda s, v, w: lane_block(cols[s : s + 1], v) * lane_block(warped[i], w),
+                lane, 2 * WARP + 1, True,
             )
-            matched = jnp.concatenate(blocks, axis=1)
-            high = matched.astype(BF16)
-            at = slice(k * STRIP, (k + 1) * STRIP)
-            matched_terms[i, 0, at] = high
-            matched_terms[i, 1, at] = (matched - high.astype(F32)).astype(BF16)
-
-    empty = jnp.zeros((LANES - WINDOW, WIDTH), BF16)
-    warped = []
-    for i in range(TOGETHER):
-        halves = []
-        for h in range(HALVES):
-            high = rows_high[i, h * ROWS : (h + 1) * ROWS]
-            low = rows_low[i, h * ROWS : (h + 1) * ROWS]
-            rows = slice(h * ROWS, h * ROWS + WINDOW)
-            first = jnp.concatenate([matched_terms[i, 0, rows], empty], axis=0)
-            second = jnp.concatenate([matched_terms[i, 1, rows], empty], axis=0)
-            both = jnp.dot(
-                jnp.concatenate([high, high], axis=1), jnp.concatenate([first, second], axis=0),
-                preferred_element_type=F32,
-            )
-            halves.append(both + jnp.dot(low, first, preferred_element_type=F32))
-        warped.append(jnp.concatenate(halves, axis=0))
-
-    for i in range(TOGETHER):
-        cols = col_weights[i]
-        blocks = lane_sum(
-            lambda s, v, w: lane_block(cols[s : s + 1], v) * lane_block(warped[i], w),
-            lane, 2 * WARP + 1, True,
-        )
-        result = jnp.dot(
-            jnp.concatenate(blocks, axis=1).astype(BF16), unsort[...], preferred_element_type=F32
-        ).astype(BF16)
-        for j in range(BLKC):
-            block = (grid_step * TOGETHER + i) * BLKC + j
-            ready[block] = result[:, j * BLOCK : (j + 1) * BLOCK]
-            to = place_of[block]
-            row = pl.multiple_of(to % CAP * BLOCK, BLOCK)
-            pltpu.make_async_copy(
-                ready.at[block], out.at[to // CAP, pl.ds(row, BLOCK)], sem.at[block]
-            ).start()
-
-    @pl.when(grid_step == grid_steps - 1)
-    def _():
-        label_copy.wait()
-        for block in range(V * BLKC):
-            pltpu.make_async_copy(ready.at[block], out.at[0, pl.ds(0, BLOCK)], sem.at[block]).wait()
+            result = jnp.dot(
+                jnp.concatenate(blocks, axis=1).astype(BF16), unsort[...], preferred_element_type=F32
+            ).astype(BF16)
+            for j in range(BLKC):
+                to = place_of[(turn * TOGETHER + i) * BLKC + j]
+                rows = pl.ds(pl.multiple_of(to % CAP * BLOCK, BLOCK), BLOCK)
+                out[to // CAP, rows] = lane_block(result, j)
+        return 0
+
+    lax.fori_loop(0, V // TOGETHER, some_visits, 0)
 
 
 def warp(patch, slot, owner, weight, ready, images, above, below, devices):
     smem = pl.BlockSpec(memory_space=pltpu.SMEM)
-    hbm = pl.BlockSpec(memory_space=pl.ANY)
+    vmem = pl.BlockSpec(memory_space=pltpu.VMEM)
     sort = deinterleave()
-    constants = [jnp.asarray(sort, BF16), jnp.asarray(sort.T, BF16)]
-
-    def whole(x):
-        return pl.BlockSpec(x.shape, lambda v: (0,) * x.ndim)
-
-    def by_visit(x):
-        return pl.BlockSpec((TOGETHER,) + x.shape[1:], lambda v: (v, 0, 0))
-
+    args = [
+        patch, slot, owner, weight, *ready,
+        jnp.asarray(sort, BF16), jnp.asarray(sort.T, BF16), images, above, below,
+    ]
     return pl.pallas_call(
         warp_kernel,
-        grid=(V // TOGETHER,),
-        in_specs=[smem, smem, smem, whole(weight)]
-        + [by_visit(x) for x in ready]
-        + [whole(x) for x in constants]
-        + [by_visit(x) for x in (images, above, below)],
-        out_specs=hbm,
+        in_specs=[smem] * 3 + [vmem] * (len(args) - 3),
+        out_specs=vmem,
         scratch_shapes=[
             pltpu.VMEM((TOGETHER, 4, TALL, WIDTH), BF16),
             pltpu.VMEM((TOGETHER, 2, STRIPS * STRIP, WIDTH), BF16),
-            pltpu.VMEM((V * BLKC, BLOCK, BLOCK), BF16),
             pltpu.SMEM((V * BLKC,), jnp.int32),
             pltpu.SMEM((owner.shape[0],), jnp.int32),
             pltpu.VMEM((devices, LANES), F32),
-            pltpu.VMEM((devices, LABEL, LANES), BF16),
-            pltpu.SemaphoreType.DMA((V * BLKC,)),
-            pltpu.SemaphoreType.DMA(()),
         ],
         out_shape=jax.ShapeDtypeStruct((devices, CAP * BLOCK + LABEL, BLOCK), BF16),
         compiler_params=pltpu.CompilerParams(vmem_limit_bytes=32 << 20),
@@ -402,7 +377,7 @@
             transcendentals=0,
         ),
         name="match_warp",
-    )(patch, slot, owner, weight, *ready, *constants, images, above, below)
+    )(*args)
 
 
 def coadd_kernel(got, out, total, out_sem):

time: 53.5 us -> 52 us (0.972)
  Pallas kernels: 9.48 us -> 8.03 us
    pallas_call x1, Pallas kernels: 6.45 us -> 5 us  [warp(): pl.pallas_call(warp_kernel, in_specs=[smem] * 3 + [vmem] * (len(args) - 3...]
where the time goes in v12:
time: 52 us; the launch traced here: 51.6 us
  blocking collectives  36.7 us (71%)
  Pallas kernels  8.03 us (15%)
  starting transfers between devices  4.33 us (8%)
  local copies, waits for them, and re-layouts  2.49 us (5%)
    all_to_all x1, blocking collectives, shards(): got = lax.all_to_all(sent, 'ccd', split_axis=0, concat_axis=0, tiled=True)  36.7 us
    pallas_call x1, Pallas kernels, warp(): pl.pallas_call(warp_kernel, in_specs=[smem] * 3 + [vmem] * (len(args) - 3...  5 us
    ppermute x1, starting transfers between devices, shards(): above = lax.ppermute(images[:, BLOCK - RIM:], 'ccd', down)  3.03 us
    pallas_call x1, Pallas kernels, coadd(): pl.pallas_call(coadd_kernel, in_specs=[pl.BlockSpec(memory_space=pltpu.VM...  1.67 us
    unnamed x20, local copies, waits for them, and re-layouts  1.61 us
    pallas_call x2, Pallas kernels, small_kernel(): pl.pallas_call(body, grid=(1,), in_specs=[pl.BlockSpec(x.shape, lambda i,...  1.35 us
    ppermute x1, starting transfers between devices, shards(): below = lax.ppermute(images[:, :RIM], 'ccd', up)  1.29 us
  transfers between devices with their start and end apart: 2, of which 0 were waited for; matrix products, arithmetic and copies ran while one was open for 0% of the time, Pallas kernels for 3%

profile of v12, /device:TPU:0, one launch (start us, length us, event | category | flops | bytes accessed | tf_op | source)
XLA Modules:
  0.0 51.6 jit_solution(964983368333812848)
XLA Ops:
  0.0 0.9 %fusion = (f32[4,8,512]{2,1,0:T(8,128)S(1)}, f32[4,8,512]{2,1,0:T(8,128)S(1)}) fusion(f32[4,128,512]{2,1,0:T(8,128)} %image.1), kind=kLoop, calls=%fused_computation | loop fusion | bytes 262144 | tf_op jit(solution)/shard_map/slice | solution.py:469
  0.9 1.3 %collective-permute-start.1 = (f32[4,8,512]{2,1,0:T(8,128)S(1)}, f32[4,8,512]{2,1,0:T(8,128)S(1)}, u32[]{:S(2)}, u32[]{:S(2)}) collective-permute-start(f32[4,8,512]{2,1,0:T(8,128)S(1)} %get-tuple-element.19), channel_id=1, source_target_pairs={{1,0},{2,1},{3,2},{4,3},{5,4},{6,5},{7,6},{8,7},{9,8},{10,9},{11,1... | collective-permute-start | bytes 196616 | tf_op jit(solution)/shard_map/ppermute | solution.py:469
  2.2 3.0 %collective-permute-start = (f32[4,8,512]{2,1,0:T(8,128)S(1)}, f32[4,8,512]{2,1,0:T(8,128)S(1)}, u32[]{:S(2)}, u32[]{:S(2)}) collective-permute-start(f32[4,8,512]{2,1,0:T(8,128)S(1)} %get-tuple-element.20), channel_id=1, source_target_pairs={{0,1},{1,2},{2,3},{3,4},{4,5},{5,6},{6,7},{7,8},{8,9},{9,10},{10,1... | collective-permute-start | bytes 196616 | tf_op jit(solution)/shard_map/ppermute | solution.py:468
  5.2 0.0 copy-start.3
  5.2 0.7 %copy-done.3 = f32[4,5,2,2]{1,3,2,0:T(2,128)S(1)} copy-done((f32[4,5,2,2]{1,3,2,0:T(2,128)S(1)}, f32[4,5,2,2]{1,3,2,0:T(2,128)}, u32[]{:S(2)}) %copy-start.3) | copy-done | bytes 344
  5.9 0.0 copy-start.1
  5.9 0.0 copy-start.2
  5.9 0.4 lanczos_weights.1
  6.3 0.4 copy-done.1
  6.7 0.0 copy-done.2
  6.7 0.0 copy-start
  6.7 0.0 copy-start.4
  6.7 0.0 copy-start.5
  6.7 0.0 copy-start.6
  6.7 0.0 copy-start.7
  6.7 0.0 copy-start.8
  6.7 0.0 copy-start.9
  6.7 1.0 %matrices.1 = (f32[4,176,128]{2,1,0:T(8,128)S(1)}, f32[4,176,128]{2,1,0:T(8,128)S(1)}, bf16[4,176,128]{2,1,0:T(8,128)(2,1)S(1)}, bf16[4,128,128]{2,1,0:T(8,128)(2,1)S(1)}, bf16[4,128,128]{2,1,0:T(8,128)(2,1)S(1)}) custom-call(f32[9,2,11]{2,1,0:T(2,128)S(1)} %bitcast.5, f32[5,3,4,9]{3,2,1,0:T(4,128)S(1)} %bitcast.4, ...), custom_call_target="tpu_custom_call" | custom-call | flops 1073741824 | bytes 1048576 | tf_op jit(solution)/shard_map/matrices/pallas_call | solution.py:211
  7.7 0.0 collective-permute-done.1.below
  7.7 0.0 collective-permute-done.above
  7.7 0.2 copy-done
  7.9 0.0 copy-done.4
  7.9 0.0 copy-done.5
  7.9 0.0 copy-done.6
  7.9 0.0 copy-done.7
  7.9 0.2 copy-done.8
  8.1 0.2 copy-done.9
  8.3 5.0 %match_warp.1 = bf16[16,272,128]{2,1,0:T(8,128)(2,1)S(1)} custom-call(s32[1,16]{1,0:T(1,128)S(1)} %bitcast.7, s32[1,16]{1,0:T(1,128)S(1)} %copy-done.6, s32[16]{0:T(128)S(1)} %copy-done.7, bf16[4,5]{1,0:T(4,128)(2,1)S(1)} %copy-done.4, f32[4,176,128]{2,1,0:T(8,128)S(1)} %get-tuple-element.13.high_level, f32[4,176,128]{2,1,0:T(8,128)S(1)} %get-tuple-element.14.step_level, ...), custom_call_target="tpu_custom_call" | custom-call | flops 1660944384 | bytes 1572864 | tf_op jit(solution)/shard_map/match_warp/pallas_call | solution.py:361
  13.3 36.7 %all_to_all.5.got = bf16[16,272,128]{2,1,0:T(8,128)(2,1)S(1)} all-to-all(bf16[16,272,128]{2,1,0:T(8,128)(2,1)S(1)} %match_warp.1), channel_id=1, replica_groups=mesh['group'=2,'ccd'=16] {'ccd'}, dimensions={0} | all-to-all | bytes 2228224 | tf_op jit(solution)/shard_map/all_to_all | solution.py:475
  50.0 1.7 %coadd.1 = f32[1,512,512]{2,1,0:T(8,128)} custom-call(bf16[16,272,128]{2,1,0:T(8,128)(2,1)S(1)} %all_to_all.5.got), custom_call_target="tpu_custom_call" | custom-call | tf_op jit(solution)/shard_map/coadd/pallas_call | solution.py:448
Async XLA Ops:
  0.9 6.8 %collective-permute-start.1 = (f32[4,8,512]{2,1,0:T(8,128)S(1)}, f32[4,8,512]{2,1,0:T(8,128)S(1)}, u32[]{:S(2)}, u32[]{:S(2)}) collective-permute-start(f32[4,8,512]{2,1,0:T(8,128)S(1)} %get-tuple-element.19), channel_id=1, source_target_pairs={{1,0},{2,1},{3,2},{4,3},{5,4},{6,5},{7,6},{8,7},{9,8},{10,9},{11,1... | collective-permute-start | bytes 196616 | tf_op jit(solution)/shard_map/ppermute | solution.py:469
  2.2 5.6 %collective-permute-start = (f32[4,8,512]{2,1,0:T(8,128)S(1)}, f32[4,8,512]{2,1,0:T(8,128)S(1)}, u32[]{:S(2)}, u32[]{:S(2)}) collective-permute-start(f32[4,8,512]{2,1,0:T(8,128)S(1)} %get-tuple-element.20), channel_id=1, source_target_pairs={{0,1},{1,2},{2,3},{3,4},{4,5},{5,6},{6,7},{7,8},{8,9},{9,10},{10,1... | collective-permute-start | bytes 196616 | tf_op jit(solution)/shard_map/ppermute | solution.py:468
  5.2 0.7 %copy-start.3 = (f32[4,5,2,2]{1,3,2,0:T(2,128)S(1)}, f32[4,5,2,2]{1,3,2,0:T(2,128)}, u32[]{:S(2)}) copy-start(f32[4,5,2,2]{1,3,2,0:T(2,128)} %param.13) | copy-start | bytes 964
  5.9 0.8 %copy-start.1 = (f32[4,5,9,3]{2,0,3,1:T(4,128)S(1)}, f32[4,5,9,3]{2,0,3,1:T(4,128)}, u32[]{:S(2)}) copy-start(f32[4,5,9,3]{2,0,3,1:T(4,128)} %param.12) | copy-start | bytes 6484
  5.9 0.8 %copy-start.2 = (f32[2,9,11]{2,0,1:T(2,128)S(1)}, f32[2,9,11]{2,0,1:T(2,128)}, u32[]{:S(2)}) copy-start(f32[2,9,11]{2,0,1:T(2,128)} %param.11) | copy-start | bytes 2380
  6.7 1.2 %copy-start = (f32[4,128,512]{2,1,0:T(8,128)S(1)}, f32[4,128,512]{2,1,0:T(8,128)}, u32[]{:S(2)}) copy-start(f32[4,128,512]{2,1,0:T(8,128)} %image.1) | copy-start | bytes 3145732
  6.7 1.2 %copy-start.4 = (bf16[4,5]{1,0:T(4,128)(2,1)S(1)}, bf16[4,5]{1,0:T(4,128)(2,1)}, u32[]{:S(2)}) copy-start(bf16[4,5]{1,0:T(4,128)(2,1)} %weight.1) | copy-start | bytes 124
  6.7 1.2 %copy-start.5 = (s32[1,16,1]{1,2,0:T(1,128)S(1)}, s32[1,16,1]{1,2,0:T(1,128)}, u32[]{:S(2)}) copy-start(s32[1,16,1]{1,2,0:T(1,128)} %param.15) | copy-start | bytes 196
  6.7 1.2 %copy-start.6 = (s32[1,16]{1,0:T(1,128)S(1)}, s32[1,16]{1,0:T(1,128)}, u32[]{:S(2)}) copy-start(s32[1,16]{1,0:T(1,128)} %slot.1) | copy-start | bytes 196
  6.7 1.2 %copy-start.7 = (s32[16]{0:T(128)S(1)}, s32[16]{0:T(128)}, u32[]{:S(2)}) copy-start(s32[16]{0:T(128)} %owner.1) | copy-start | bytes 196
  6.7 1.4 %copy-start.8 = (bf16[512,512]{1,0:T(8,128)(2,1)S(1)}, bf16[512,512]{1,0:T(8,128)(2,1)}, u32[]{:S(2)}) copy-start(bf16[512,512]{1,0:T(8,128)(2,1)} %constant.5.clone.unsort) | copy-start | bytes 1572868
  6.7 1.5 %copy-start.9 = (bf16[512,512]{1,0:T(8,128)(2,1)S(1)}, bf16[512,512]{1,0:T(8,128)(2,1)}, u32[]{:S(2)}) copy-start(bf16[512,512]{1,0:T(8,128)(2,1)} %constant.4.clone.sort) | copy-start | bytes 1572868

commit v13 on v12

--- a/solution.py
+++ b/solution.py
@@ -1,4 +1,5 @@
 import functools
+import itertools
 
 import jax
 import jax.numpy as jnp
@@ -21,6 +22,7 @@
 HALF = TAPS // 2
 WARP = 3
 RIM = HALF + WARP
+HEAD = 16
 HEIGHT = SPLIT * BLOCK
 WIDTH = BLKC * BLOCK
 LANES = 128
@@ -31,11 +33,14 @@
 MIDDLE = STRIPS // 2
 GROUPS = 6
 BAND = 256
-TALL = (STRIPS - 1) * STRIP + STEP
+OWN_STRIPS = STRIPS - 1
+NEXT_STRIPS = 2
+NEXT_FIRST = (STRIPS - NEXT_STRIPS) * STRIP
 HALVES = 2
 TOGETHER = 2
 ROWS = BLOCK // HALVES
 WINDOW = ROWS + STRIP
+BODY = BLOCK - HEAD
 LABEL = 16
 F32 = jnp.float32
 BF16 = jnp.bfloat16
@@ -121,42 +126,49 @@
 
 def whereabouts(devices):
     band = lax.axis_index("ccd")
+    after = lax.rem(band + 1, devices)
     quarter = (band + SPLIT // 2) % SPLIT
-    has_above = (quarter > 0) & (band > 0)
-    has_below = (quarter < SPLIT - 1) & (band < devices - 1)
-    return (band + SPLIT // 2) // SPLIT, quarter * BLOCK, has_above, has_below
+    own = ((band + SPLIT // 2) // SPLIT, quarter * BLOCK + HEAD)
+    following = (
+        (after + SPLIT // 2) // SPLIT,
+        (after + SPLIT // 2) % SPLIT * BLOCK - BODY,
+    )
+    return (own, following), (quarter < SPLIT - 1) & (band < devices - 1)
 
 
 def lanczos_kernel(devices, affine, rows_out, cols_out):
-    ccd, top_row, has_above, has_below = whereabouts(devices)
+    bands, same = whereabouts(devices)
     lane = iota((1, LANES), 1)
+    lanes = iota((8, WIDTH), 1)
+    step = iota((8, WIDTH), 0) - WARP
+    block = lanes // LANES
+    carry = (block + step + LANE_BLOCKS) // LANE_BLOCKS - 1
+    from_lane = lanes % LANES - carry
+    col = (from_lane * LANE_BLOCKS + block).astype(F32)
+    within = (from_lane >= 0) & (from_lane < LANES) & (step <= WARP)
+    offset = iota((8, LANES), 0) - WARP
+    crosses = (lane + offset >= BODY) != (lane >= BODY)
+    keep = (offset <= WARP) & (same | jnp.logical_not(crosses))
     for visit in range(V):
-        a = jnp.sum(
-            jnp.where(iota((1, 1, affine.shape[3]), 2) == ccd, affine[visit], 0.0),
-            axis=2, keepdims=True,
-        )
-        offset = iota((8, LANES), 0) - WARP
-        row = (top_row + lane).astype(F32)
-        shift = a[0, 0:1] + a[0, 1:2] * (row - (HEIGHT - 1) / 2.0) / HEIGHT
-        band_row = lane + offset
-        keep = (offset <= WARP) & ((band_row >= 0) | has_above) & ((band_row < BLOCK) | has_below)
+        shifts = []
+        for n, (ccd, top_row) in enumerate(bands):
+            a = jnp.sum(
+                jnp.where(iota((1, 1, affine.shape[3]), 2) == ccd, affine[visit], 0.0),
+                axis=2, keepdims=True,
+            )
+            row = (top_row + lane).astype(F32)
+            shifts.append(a[0, 0:1] + a[0, 1:2] * (row - (HEIGHT - 1) / 2.0) / HEIGHT)
+            col_shift = a[1, 0:1] + a[1, 1:2] * (col - (WIDTH - 1) / 2.0) / WIDTH
+            cols_out[n * V + visit] = jnp.where(within, lanczos(col_shift - step.astype(F32)), 0.0)
+        shift = jnp.where(lane < BODY, shifts[0], shifts[1])
         weights = jnp.where(keep, lanczos(shift - offset.astype(F32)), 0.0)
         rows_out[visit] = jnp.concatenate([weights, jnp.zeros((LANES - 8, LANES), F32)], axis=0).T
-        lanes = iota((8, WIDTH), 1)
-        step = iota((8, WIDTH), 0) - WARP
-        block = lanes // LANES
-        carry = (block + step + LANE_BLOCKS) // LANE_BLOCKS - 1
-        from_lane = lanes % LANES - carry
-        col = (from_lane * LANE_BLOCKS + block).astype(F32)
-        col_shift = a[1, 0:1] + a[1, 1:2] * (col - (WIDTH - 1) / 2.0) / WIDTH
-        within = (from_lane >= 0) & (from_lane < LANES) & (step <= WARP)
-        cols_out[visit] = jnp.where(within, lanczos(col_shift - step.astype(F32)), 0.0)
 
 
 def prepare_kernel(
     devices, taps, psf, row_weights, high_level, step_level, slope, rows_high, rows_low
 ):
-    ccd, top_row, _, _ = whereabouts(devices)
+    bands, _ = whereabouts(devices)
     band_lane = iota((1, BAND), 1)
     seg = band_lane // STEP
     lane = iota((1, LANES), 1)
@@ -165,7 +177,9 @@
     row_taps = dot_exact(taps[:, 0], onehot.astype(F32), ((1,), (0,)))
     eye = (iota((TAPS, STRIP), 0) == iota((TAPS, STRIP), 1)).astype(F32)
     turned_taps = dot_exact(eye, taps[:, 1], ((0,), (1,)))
-    for visit in range(V):
+    units = []
+    for n, visit in itertools.product(range(2), range(V)):
+        ccd, top_row = bands[n]
         lhs = jnp.concatenate(
             [turned_taps * psf[ccd, c, visit : visit + 1, :] for c in range(3)], axis=0
         )
@@ -181,6 +195,7 @@
         reach = per_strip * (STRIPS - MIDDLE)
         largest = jnp.max(jnp.abs(const) + reach * jnp.abs(by_row), axis=(0, 1), keepdims=True)
         unit = jnp.maximum(largest, 1e-30) * (1.0 / 200.0)
+        units.append(unit)
         const = const / unit
         by_row = (by_row * per_strip) / unit
         low_lanes = (lane // STEP) % 3 == 2
@@ -192,19 +207,26 @@
             y = staircase(jnp.broadcast_to(by_row[u : u + 1, :LANES], (STRIP, LANES)), 0)
             tail = x[:, LANES:]
             high = tail.astype(BF16).astype(F32)
-            slope[visit, at] = jnp.where(low_band[:, LANES:], tail - high, high).astype(BF16)
+            slope[n * V + visit, at] = jnp.where(low_band[:, LANES:], tail - high, high).astype(BF16)
             x = x[:, :LANES] + row_part * y
             high = jnp.where(lane < 3 * STEP, jnp.round(x), x.astype(BF16).astype(F32))
-            high_level[visit, at] = jnp.where(low_lanes, x - high, high)
+            high_level[n * V + visit, at] = jnp.where(low_lanes, x - high, high)
             high = jnp.round(y)
-            step_level[visit, at] = jnp.where(low_lanes, y - high, high)
-
-        for h in range(HALVES):
-            at = slice(h * ROWS, (h + 1) * ROWS)
-            matrix = staircase(row_weights[visit, at] * unit, 0)
-            high = matrix.astype(BF16)
-            rows_high[visit, at] = high
-            rows_low[visit, at] = (matrix - high.astype(F32)).astype(BF16)
+            step_level[n * V + visit, at] = jnp.where(low_lanes, y - high, high)
+
+    for visit in range(V):
+        weights = row_weights[visit]
+        matrix = jnp.concatenate(
+            [
+                staircase(weights[:ROWS] * units[visit], 0),
+                staircase(weights[ROWS:BODY] * units[visit], 0),
+                staircase(weights[BODY:] * units[V + visit], ROWS),
+            ],
+            axis=0,
+        )
+        high = matrix.astype(BF16)
+        rows_high[visit] = high
+        rows_low[visit] = (matrix - high.astype(F32)).astype(BF16)
 
 
 def small_kernel(body, name, args, shapes):
@@ -224,15 +246,15 @@
     row_weights, col_weights = small_kernel(
         functools.partial(lanczos_kernel, devices), "lanczos_weights",
         [affine.transpose(0, 2, 3, 1)],
-        [((V, BLOCK, LANES), F32), ((V, 8, WIDTH), F32)],
+        [((V, BLOCK, LANES), F32), ((2 * V, 8, WIDTH), F32)],
     )
     matrices = small_kernel(
         functools.partial(prepare_kernel, devices), "matrices",
         [taps.transpose(1, 0, 2), psf.transpose(1, 3, 0, 2), row_weights],
         [
-            ((V, TAPS * STRIP, LANES), F32),
-            ((V, TAPS * STRIP, LANES), F32),
-            ((V, TAPS * STRIP, BAND - LANES), BF16),
+            ((2 * V, TAPS * STRIP, LANES), F32),
+            ((2 * V, TAPS * STRIP, LANES), F32),
+            ((2 * V, TAPS * STRIP, BAND - LANES), BF16),
             ((V, BLOCK, LANES), BF16),
             ((V, BLOCK, LANES), BF16),
         ],
@@ -242,28 +264,37 @@
 
 def warp_kernel(
     patch, slot, owner, weight, high_level, step_level, slope, rows_high, rows_low, col_weights,
-    sort, unsort, image, above, below, out,
-    terms, matched_terms, place_of, seen, label,
+    sort, unsort, image, below, out,
+    terms, next_terms, matched_terms, next_matched, next_names, place_of, seen, label, name_sem,
 ):
     devices = label.shape[0]
-    ccd, _, has_above, has_below = whereabouts(devices)
-    tall = BLOCK + 2 * RIM
+    blocks_here = V * BLKC
+    ((ccd, _), _), same = whereabouts(devices)
+    names_copy = pltpu.make_async_copy(
+        below.at[0, pl.ds(HEAD + RIM, 8), pl.ds(0, LANES)], next_names, name_sem
+    )
+    names_copy.start()
     lane = iota((1, LANES), 1)
-    terms[:, :, tall:] = jnp.zeros((TOGETHER, 4, TALL - tall, WIDTH), BF16)
+    next_terms[:, :, STEP:] = jnp.zeros((TOGETHER, 4, STRIP, WIDTH), BF16)
     label[...] = jnp.zeros_like(label)
 
-    def clear(p, _):
-        seen[p] = 0
-        return 0
-
-    lax.fori_loop(0, owner.shape[0], clear, 0)
+    def forget():
+        def clear(p, _):
+            seen[p] = 0
+            return 0
+
+        lax.fori_loop(0, owner.shape[0], clear, 0)
+
+    def take(p):
+        rank = seen[p]
+        seen[p] = rank + 1
+        return owner[p], rank
+
+    forget()
     own = jnp.where(iota(weight.shape, 1) == ccd, weight[...].astype(F32), 0.0)
     own = jnp.sum(own, axis=1, keepdims=True)
-    for block in range(V * BLKC):
-        p = patch[0, block]
-        to = owner[p]
-        rank = seen[p]
-        seen[p] = rank + 1
+    for block in range(blocks_here):
+        to, rank = take(patch[0, block])
         place_of[block] = to * CAP + rank
         line = label[pl.ds(to, 1), :]
         line = jnp.where(lane == rank * 2, own[block // BLKC : block // BLKC + 1], line)
@@ -272,14 +303,26 @@
     out[:, CAP * BLOCK :] = jnp.broadcast_to(
         label[...].reshape(devices, 1, LANES), (devices, LABEL, LANES)
     ).astype(BF16)
+    forget()
+    names_copy.wait()
+    for block in range(blocks_here):
+        to, rank = take(next_names[0, block].astype(jnp.int32))
+        place_of[blocks_here + block] = to * CAP + rank
+
+    seam_row = iota((STEP, 1), 0) < STEP - HEAD - RIM
+    both = jnp.where(same, 1.0, 0.0)
+    own_sees = jnp.where(seam_row, 1.0, both)
+    next_sees = jnp.where(seam_row, both, 1.0)
+    col_pos = (2.0 * column_at(iota((1, WIDTH), 1)).astype(F32) + 1.0) / WIDTH - 1.0
+    filler = jnp.zeros((BAND - GROUPS * STEP, WIDTH), BF16)
+    tall = BLOCK + 2 * RIM
+    seam = tall - STEP
 
     def some_visits(turn, _):
-        col_pos = (2.0 * column_at(iota((1, WIDTH), 1)).astype(F32) + 1.0) / WIDTH - 1.0
-        for i in range(TOGETHER):
-            raw = jnp.concatenate(
-                [jnp.where(has_above, above[turn * TOGETHER + i], 0.0), image[turn * TOGETHER + i], jnp.where(has_below, below[turn * TOGETHER + i], 0.0)],
-                axis=0,
-            )
+        visits = [turn * TOGETHER + i for i in range(TOGETHER)]
+
+        for i, visit in enumerate(visits):
+            raw = jnp.concatenate([image[visit, RIM:], below[visit, : HEAD + RIM]], axis=0)
             raw_high = raw.astype(BF16)
             raw_low = (raw - raw_high.astype(F32)).astype(BF16)
             sorted_terms = jnp.dot(
@@ -287,87 +330,117 @@
             )
             high, low = sorted_terms[:tall], sorted_terms[tall:]
             tilted = (high + low) * col_pos
-            tilted_high = tilted.astype(BF16)
-            terms[i, 0, :tall] = high.astype(BF16)
-            terms[i, 1, :tall] = low.astype(BF16)
-            terms[i, 2, :tall] = tilted_high
-            terms[i, 3, :tall] = (tilted - tilted_high.astype(F32)).astype(BF16)
-
-        filler = jnp.zeros((BAND - GROUPS * STEP, WIDTH), BF16)
-        for k in range(STRIPS):
-            for i in range(TOGETHER):
-                level = high_level[turn * TOGETHER + i]
-                if k != MIDDLE:
-                    level = level + float(k - MIDDLE) * step_level[turn * TOGETHER + i]
-                matrix = jnp.concatenate([level.astype(BF16), slope[turn * TOGETHER + i]], axis=1)
-                rows = slice(k * STRIP, k * STRIP + STEP)
-                columns = jnp.concatenate(
-                    [terms[i, h, rows] for h in (0, 1, 0, 2, 3, 2)] + [filler], axis=0
+            tilted_high = tilted.astype(BF16).astype(F32)
+            for h, value in enumerate((high, low, tilted_high, tilted - tilted_high)):
+                terms[i, h, :seam] = value[:seam].astype(BF16)
+                terms[i, h, seam:] = (value[seam:] * own_sees).astype(BF16)
+                next_terms[i, h, :STEP] = (value[seam:] * next_sees).astype(BF16)
+
+        def strip(matrices, source, rows, k):
+            level = high_level[matrices]
+            if k != MIDDLE:
+                level = level + float(k - MIDDLE) * step_level[matrices]
+            matrix = jnp.concatenate([level.astype(BF16), slope[matrices]], axis=1)
+            columns = jnp.concatenate(
+                [source[h, rows] for h in (0, 1, 0, 2, 3, 2)] + [filler], axis=0
+            )
+            results = jnp.dot(matrix, columns, preferred_element_type=F32)
+            blocks = lane_sum(
+                lambda u, v, w: lane_block(results[u * STRIP : (u + 1) * STRIP], w),
+                lane, TAPS, False,
+            )
+            matched = jnp.concatenate(blocks, axis=1)
+            high = matched.astype(BF16)
+            return high, (matched - high.astype(F32)).astype(BF16)
+
+        for k in range(OWN_STRIPS):
+            for i, visit in enumerate(visits):
+                at = slice(k * STRIP, (k + 1) * STRIP)
+                matched_terms[i, 0, at], matched_terms[i, 1, at] = strip(
+                    visit, terms.at[i], slice(k * STRIP, k * STRIP + STEP), k
                 )
-                results = jnp.dot(matrix, columns, preferred_element_type=F32)
-                blocks = lane_sum(
-                    lambda u, v, w: lane_block(results[u * STRIP : (u + 1) * STRIP], w),
-                    lane, TAPS, False,
+        for k in range(NEXT_STRIPS):
+            for i, visit in enumerate(visits):
+                at = slice(k * STRIP, (k + 1) * STRIP)
+                next_matched[i, 0, at], next_matched[i, 1, at] = strip(
+                    V + visit, next_terms.at[i], slice(k * STRIP, k * STRIP + STEP),
+                    STRIPS - NEXT_STRIPS + k,
                 )
-                matched = jnp.concatenate(blocks, axis=1)
-                high = matched.astype(BF16)
-                at = slice(k * STRIP, (k + 1) * STRIP)
-                matched_terms[i, 0, at] = high
-                matched_terms[i, 1, at] = (matched - high.astype(F32)).astype(BF16)
-
-        empty = jnp.zeros((LANES - WINDOW, WIDTH), BF16)
+
         warped = []
-        for i in range(TOGETHER):
+        for i, visit in enumerate(visits):
             halves = []
             for h in range(HALVES):
-                high = rows_high[turn * TOGETHER + i, h * ROWS : (h + 1) * ROWS]
-                low = rows_low[turn * TOGETHER + i, h * ROWS : (h + 1) * ROWS]
-                rows = slice(h * ROWS, h * ROWS + WINDOW)
-                first = jnp.concatenate([matched_terms[i, 0, rows], empty], axis=0)
-                second = jnp.concatenate([matched_terms[i, 1, rows], empty], axis=0)
-                both = jnp.dot(
-                    jnp.concatenate([high, high], axis=1), jnp.concatenate([first, second], axis=0),
+                at = slice(h * ROWS, (h + 1) * ROWS)
+                high, low = rows_high[visit, at], rows_low[visit, at]
+
+                def under(term):
+                    if h == 0:
+                        parts = [matched_terms[i, term, :WINDOW]]
+                    else:
+                        parts = [matched_terms[i, term, ROWS:], next_matched[i, term]]
+                    left = LANES - sum([x.shape[0] for x in parts])
+                    return jnp.concatenate(parts + [jnp.zeros((left, WIDTH), BF16)], axis=0)
+
+                first = under(0)
+                total = jnp.dot(
+                    jnp.concatenate([high, high], axis=1),
+                    jnp.concatenate([first, under(1)], axis=0),
                     preferred_element_type=F32,
                 )
-                halves.append(both + jnp.dot(low, first, preferred_element_type=F32))
+                halves.append(total + jnp.dot(low, first, preferred_element_type=F32))
             warped.append(jnp.concatenate(halves, axis=0))
 
-        for i in range(TOGETHER):
-            cols = col_weights[turn * TOGETHER + i]
-            blocks = lane_sum(
-                lambda s, v, w: lane_block(cols[s : s + 1], v) * lane_block(warped[i], w),
-                lane, 2 * WARP + 1, True,
-            )
+        for i, visit in enumerate(visits):
+            parts = []
+            for rows, weights in (
+                (slice(0, BODY), col_weights[visit]),
+                (slice(BODY, BLOCK), col_weights[V + visit]),
+            ):
+                some = warped[i][rows]
+                blocks = lane_sum(
+                    lambda s, v, w: lane_block(weights[s : s + 1], v) * lane_block(some, w),
+                    lane, 2 * WARP + 1, True,
+                )
+                parts.append(jnp.concatenate(blocks, axis=1).astype(BF16))
             result = jnp.dot(
-                jnp.concatenate(blocks, axis=1).astype(BF16), unsort[...], preferred_element_type=F32
+                jnp.concatenate(parts, axis=0), unsort[...], preferred_element_type=F32
             ).astype(BF16)
             for j in range(BLKC):
-                to = place_of[(turn * TOGETHER + i) * BLKC + j]
-                rows = pl.ds(pl.multiple_of(to % CAP * BLOCK, BLOCK), BLOCK)
-                out[to // CAP, rows] = lane_block(result, j)
+                piece = lane_block(result, j)
+                to = place_of[visit * BLKC + j]
+                rows = pl.ds(pl.multiple_of(to % CAP * BODY, HEAD), BODY)
+                out[to // CAP, rows] = piece[:BODY]
+                to = place_of[blocks_here + visit * BLKC + j]
+                rows = pl.ds(pl.multiple_of(CAP * BODY + to % CAP * HEAD, HEAD), HEAD)
+                out[to // CAP, rows] = piece[BODY:]
         return 0
 
     lax.fori_loop(0, V // TOGETHER, some_visits, 0)
 
 
-def warp(patch, slot, owner, weight, ready, images, above, below, devices):
+def warp(patch, slot, owner, weight, ready, images, below, devices):
     smem = pl.BlockSpec(memory_space=pltpu.SMEM)
     vmem = pl.BlockSpec(memory_space=pltpu.VMEM)
     sort = deinterleave()
     args = [
         patch, slot, owner, weight, *ready,
-        jnp.asarray(sort, BF16), jnp.asarray(sort.T, BF16), images, above, below,
+        jnp.asarray(sort, BF16), jnp.asarray(sort.T, BF16), images, below,
     ]
     return pl.pallas_call(
         warp_kernel,
         in_specs=[smem] * 3 + [vmem] * (len(args) - 3),
         out_specs=vmem,
         scratch_shapes=[
-            pltpu.VMEM((TOGETHER, 4, TALL, WIDTH), BF16),
-            pltpu.VMEM((TOGETHER, 2, STRIPS * STRIP, WIDTH), BF16),
-            pltpu.SMEM((V * BLKC,), jnp.int32),
+            pltpu.VMEM((TOGETHER, 4, BLOCK + 2 * RIM, WIDTH), BF16),
+            pltpu.VMEM((TOGETHER, 4, STEP + STRIP, WIDTH), BF16),
+            pltpu.VMEM((TOGETHER, 2, OWN_STRIPS * STRIP, WIDTH), BF16),
+            pltpu.VMEM((TOGETHER, 2, NEXT_STRIPS * STRIP, WIDTH), BF16),
+            pltpu.SMEM((8, LANES), F32),
+            pltpu.SMEM((2 * V * BLKC,), jnp.int32),
             pltpu.SMEM((owner.shape[0],), jnp.int32),
             pltpu.VMEM((devices, LANES), F32),
+            pltpu.SemaphoreType.DMA(()),
         ],
         out_shape=jax.ShapeDtypeStruct((devices, CAP * BLOCK + LABEL, BLOCK), BF16),
         compiler_params=pltpu.CompilerParams(vmem_limit_bytes=32 << 20),
@@ -409,8 +482,10 @@
             taken[s, r] = jnp.broadcast_to(column[s : s + 1], (STRIP, LANES)).astype(BF16) > 0
 
     def tile(s, r, k):
-        first = r * BLOCK + k * STRIP
-        return jnp.where(taken[s, r], got[s, first : first + STRIP], jnp.zeros((), BF16))
+        device, first = s, r * BODY + k * STRIP - HEAD
+        if k == 0:
+            device, first = (s - 1) % devices, CAP * BODY + r * HEAD
+        return jnp.where(taken[s, r], got[device, first : first + STRIP], jnp.zeros((), BF16))
 
     copies = []
     for pair in range(BLOCK // STRIP // 2):
@@ -463,14 +538,16 @@
     images, basis_taps, psf_coef, affine, visit_weight, block_patch, block_slot, patch_owner
 ):
     devices = lax.axis_size("ccd")
-    down = [(i, i + 1) for i in range(devices - 1)]
-    up = [(i + 1, i) for i in range(devices - 1)]
-    above = lax.ppermute(images[:, BLOCK - RIM :], "ccd", down)
-    below = lax.ppermute(images[:, :RIM], "ccd", up)
     patch = block_patch[:, :, 0]
+    names = lax.pad(
+        patch.astype(F32)[:, None, :], jnp.zeros((), F32),
+        ((0, V - 1, 0), (0, 7, 0), (0, WIDTH - V * BLKC, 0)),
+    )
+    head = jnp.concatenate([images[:, : HEAD + RIM], names], axis=1)
+    below = lax.ppermute(head, "ccd", [((i + 1) % devices, i) for i in range(devices)])
     ready = prepare(basis_taps, psf_coef, affine, devices)
     sent = warp(
-        patch, block_slot, patch_owner, visit_weight, ready, images, above, below, devices
+        patch, block_slot, patch_owner, visit_weight, ready, images, below, devices
     )
     got = lax.all_to_all(sent, "ccd", split_axis=0, concat_axis=0, tiled=True)
     return coadd(got)

time: 52 us -> 52.9 us (1.017)
  blocking collectives: 36.7 us -> 34.3 us
  starting transfers between devices: 4.33 us -> 5.5 us
  Pallas kernels: 8.03 us -> 9.13 us
  waiting for transfers between devices: 0.01 us -> 1.01 us
  other arithmetic: 0 us -> 0.68 us
  local copies, waits for them, and re-layouts: 2.49 us -> 1.89 us
    all_to_all x1, blocking collectives: 36.7 us -> 34.3 us  [shards(): got = lax.all_to_all(sent, 'ccd', split_axis=0, concat_axis=0, tiled=True)]
    ppermute x2 -> x1, starting transfers between devices: 4.33 us -> 5.5 us  [shards(): lax.ppermute(head, 'ccd', [((i + 1) % devices, i) for i in range(devices)])]
    ppermute x2 -> x1, waiting for transfers between devices: 0.01 us -> 1.01 us  [shards(): lax.ppermute(head, 'ccd', [((i + 1) % devices, i) for i in range(devices)])]
    unnamed x20, local copies, waits for them, and re-layouts: 1.61 us -> 0.95 us
    convert_element_type x0 -> x1, other arithmetic: none -> 0.66 us  [shards(): patch.astype(F32)[:, None, :]]
    pallas_call x1, Pallas kernels: 5 us -> 5.56 us  [warp(): pl.pallas_call(warp_kernel, in_specs=[smem] * 3 + [vmem] * (len(args) - 3...]
    pallas_call x2, Pallas kernels: 1.35 us -> 1.9 us  [small_kernel(): pl.pallas_call(body, grid=(1,), in_specs=[pl.BlockSpec(x.shape, lambda i,...]
  transfers between devices with their start and end apart: 2 -> 1, of which waited for: 0 -> 1; matrix products, arithmetic and copies ran while one was open for 0% -> 0% of each run, Pallas kernels for 3% -> 4%
where the time goes in v13:
time: 52.9 us; the launch traced here: 52.6 us
  blocking collectives  34.3 us (65%)
  Pallas kernels  9.13 us (17%)
  starting transfers between devices  5.5 us (10%)
  local copies, waits for them, and re-layouts  1.89 us (4%)
  waiting for transfers between devices  1.01 us (2%)
  other arithmetic  0.68 us (1%)
    all_to_all x1, blocking collectives, shards(): got = lax.all_to_all(sent, 'ccd', split_axis=0, concat_axis=0, tiled=True)  34.3 us
    pallas_call x1, Pallas kernels, warp(): pl.pallas_call(warp_kernel, in_specs=[smem] * 3 + [vmem] * (len(args) - 3...  5.56 us
    ppermute x1, starting transfers between devices, shards(): lax.ppermute(head, 'ccd', [((i + 1) % devices, i) for i in range(devices)])  5.5 us
    pallas_call x2, Pallas kernels, small_kernel(): pl.pallas_call(body, grid=(1,), in_specs=[pl.BlockSpec(x.shape, lambda i,...  1.9 us
    pallas_call x1, Pallas kernels, coadd(): pl.pallas_call(coadd_kernel, in_specs=[pl.BlockSpec(memory_space=pltpu.VM...  1.67 us
  transfers between devices with their start and end apart: 1, of which 1 were waited for; matrix products, arithmetic and copies ran while one was open for 0% of the time, Pallas kernels for 4%

profile of v13, /device:TPU:0, one launch (start us, length us, event | category | flops | bytes accessed | tf_op | source)
XLA Modules:
  0.0 52.6 jit_solution(18305898468810935761)
XLA Ops:
  0.0 0.7 %convert_bitcast_fusion = f32[1,1,16]{2,1,0:T(1,128)S(1)} fusion(s32[1,16,1]{1,2,0:T(1,128)} %param.15), kind=kLoop, calls=%fused_computation.2 | loop fusion | flops 16 | bytes 128 | tf_op jit(solution)/shard_map/convert_element_type | solution.py:543
  0.7 0.9 %slice.3 = f32[4,24,512]{2,1,0:T(8,128)S(1)} slice(f32[4,128,512]{2,1,0:T(8,128)} %image.1), slice={[0:4], [0:24], [0:512]} | slice | bytes 393216 | tf_op jit(solution)/shard_map/slice | solution.py:546
  1.6 5.5 %collective-permute-start = (f32[4,32,512]{2,1,0:T(8,128)S(1)}, f32[4,32,512]{2,1,0:T(8,128)S(1)}, u32[]{:S(2)}, u32[]{:S(2)}) collective-permute-start(f32[4,32,512]{2,1,0:T(8,128)S(1)} %select_maximum_fusion), channel_id=1, source_target_pairs={{1,0},{2,1},{3,2},{4,3},{5,4},{6,5},{7,6},{8,7},{9,8},{10,9},{11,1... | collective-permute-start | bytes 786440 | tf_op jit(solution)/shard_map/ppermute | solution.py:547
  7.1 0.0 copy-start.3
  7.1 0.7 %copy-done.3 = f32[4,5,2,2]{1,3,2,0:T(2,128)S(1)} copy-done((f32[4,5,2,2]{1,3,2,0:T(2,128)S(1)}, f32[4,5,2,2]{1,3,2,0:T(2,128)}, u32[]{:S(2)}) %copy-start.3) | copy-done | bytes 344
  7.8 0.0 copy-start.1
  7.8 0.0 copy-start.2
  7.8 0.5 %lanczos_weights.1 = (f32[4,128,128]{2,1,0:T(8,128)S(1)}, f32[8,8,512]{2,1,0:T(8,128)S(1)}) custom-call(f32[4,2,2,5]{3,2,1,0:T(2,128)S(1)} %bitcast.8), custom_call_target="tpu_custom_call" | custom-call | flops 1073741824 | bytes 1048576 | tf_op jit(solution)/shard_map/lanczos_weights/pallas_call | solution.py:233
  8.4 0.2 copy-done.1
  8.6 0.0 copy-done.2
  8.6 0.0 copy-start
  8.6 0.0 copy-start.4
  8.6 0.0 copy-start.5
  8.6 0.0 copy-start.6
  8.6 0.0 copy-start.7
  8.6 0.0 copy-start.8
  8.6 0.0 copy-start.9
  8.6 1.4 %matrices.1 = (f32[8,176,128]{2,1,0:T(8,128)S(1)}, f32[8,176,128]{2,1,0:T(8,128)S(1)}, bf16[8,176,128]{2,1,0:T(8,128)(2,1)S(1)}, bf16[4,128,128]{2,1,0:T(8,128)(2,1)S(1)}, bf16[4,128,128]{2,1,0:T(8,128)(2,1)S(1)}) custom-call(f32[9,2,11]{2,1,0:T(2,128)S(1)} %bitcast.7, f32[5,3,4,9]{3,2,1,0:T(4,128)S(1)} %bitcast.6, ...), custom_call_target="tpu_custom_call" | custom-call | flops 1073741824 | bytes 1048576 | tf_op jit(solution)/shard_map/matrices/pallas_call | solution.py:233
  10.0 1.0 %collective-permute-done.below = f32[4,32,512]{2,1,0:T(8,128)S(1)} collective-permute-done((f32[4,32,512]{2,1,0:T(8,128)S(1)}, f32[4,32,512]{2,1,0:T(8,128)S(1)}, u32[]{:S(2)}, u32[]{:S(2)}) %collective-permute-start) | collective-permute-done | bytes 262176 | tf_op jit(solution)/shard_map/ppermute | solution.py:547
  11.0 0.0 copy-done
  11.0 0.0 copy-done.4
  11.0 0.0 copy-done.5
  11.0 0.0 copy-done.6
  11.0 0.0 copy-done.7
  11.0 0.0 copy-done.8
  11.0 0.0 copy-done.9
  11.1 5.6 %match_warp.1 = bf16[16,272,128]{2,1,0:T(8,128)(2,1)S(1)} custom-call(s32[1,16]{1,0:T(1,128)S(1)} %bitcast.9, s32[1,16]{1,0:T(1,128)S(1)} %copy-done.6, s32[16]{0:T(128)S(1)} %copy-done.7, bf16[4,5]{1,0:T(4,128)(2,1)S(1)} %copy-done.4, f32[8,176,128]{2,1,0:T(8,128)S(1)} %get-tuple-element.13.high_level, f32[8,176,128]{2,1,0:T(8,128)S(1)} %get-tuple-element.14.step_level, ...), custom_call_target="tpu_custom_call" | custom-call | flops 1660944384 | bytes 1572864 | tf_op jit(solution)/shard_map/match_warp/pallas_call | solution.py:430
  16.6 34.3 %all_to_all.5.got = bf16[16,272,128]{2,1,0:T(8,128)(2,1)S(1)} all-to-all(bf16[16,272,128]{2,1,0:T(8,128)(2,1)S(1)} %match_warp.1), channel_id=1, replica_groups=mesh['group'=2,'ccd'=16] {'ccd'}, dimensions={0} | all-to-all | bytes 2228224 | tf_op jit(solution)/shard_map/all_to_all | solution.py:552
  50.9 1.7 %coadd.1 = f32[1,512,512]{2,1,0:T(8,128)} custom-call(bf16[16,272,128]{2,1,0:T(8,128)(2,1)S(1)} %all_to_all.5.got), custom_call_target="tpu_custom_call" | custom-call | tf_op jit(solution)/shard_map/coadd/pallas_call | solution.py:523
  (1 shorter events, 0.0 us)
Async XLA Ops:
  1.6 9.4 %collective-permute-start = (f32[4,32,512]{2,1,0:T(8,128)S(1)}, f32[4,32,512]{2,1,0:T(8,128)S(1)}, u32[]{:S(2)}, u32[]{:S(2)}) collective-permute-start(f32[4,32,512]{2,1,0:T(8,128)S(1)} %select_maximum_fusion), channel_id=1, source_target_pairs={{1,0},{2,1},{3,2},{4,3},{5,4},{6,5},{7,6},{8,7},{9,8},{10,9},{11,1... | collective-permute-start | bytes 786440 | tf_op jit(solution)/shard_map/ppermute | solution.py:547
  7.1 0.7 %copy-start.3 = (f32[4,5,2,2]{1,3,2,0:T(2,128)S(1)}, f32[4,5,2,2]{1,3,2,0:T(2,128)}, u32[]{:S(2)}) copy-start(f32[4,5,2,2]{1,3,2,0:T(2,128)} %param.13) | copy-start | bytes 964
  7.8 0.8 %copy-start.1 = (f32[4,5,9,3]{2,0,3,1:T(4,128)S(1)}, f32[4,5,9,3]{2,0,3,1:T(4,128)}, u32[]{:S(2)}) copy-start(f32[4,5,9,3]{2,0,3,1:T(4,128)} %param.12) | copy-start | bytes 6484
  7.8 0.8 %copy-start.2 = (f32[2,9,11]{2,0,1:T(2,128)S(1)}, f32[2,9,11]{2,0,1:T(2,128)}, u32[]{:S(2)}) copy-start(f32[2,9,11]{2,0,1:T(2,128)} %param.11) | copy-start | bytes 2380
  8.6 2.4 %copy-start = (f32[4,128,512]{2,1,0:T(8,128)S(1)}, f32[4,128,512]{2,1,0:T(8,128)}, u32[]{:S(2)}) copy-start(f32[4,128,512]{2,1,0:T(8,128)} %image.1) | copy-start | bytes 3145732
  8.6 2.4 %copy-start.4 = (bf16[4,5]{1,0:T(4,128)(2,1)S(1)}, bf16[4,5]{1,0:T(4,128)(2,1)}, u32[]{:S(2)}) copy-start(bf16[4,5]{1,0:T(4,128)(2,1)} %weight.1) | copy-start | bytes 124
  8.6 2.4 %copy-start.5 = (s32[1,16,1]{1,2,0:T(1,128)S(1)}, s32[1,16,1]{1,2,0:T(1,128)}, u32[]{:S(2)}) copy-start(s32[1,16,1]{1,2,0:T(1,128)} %param.15) | copy-start | bytes 196
  8.6 2.4 %copy-start.6 = (s32[1,16]{1,0:T(1,128)S(1)}, s32[1,16]{1,0:T(1,128)}, u32[]{:S(2)}) copy-start(s32[1,16]{1,0:T(1,128)} %slot.1) | copy-start | bytes 196
  8.6 2.4 %copy-start.7 = (s32[16]{0:T(128)S(1)}, s32[16]{0:T(128)}, u32[]{:S(2)}) copy-start(s32[16]{0:T(128)} %owner.1) | copy-start | bytes 196
  8.6 2.4 %copy-start.8 = (bf16[512,512]{1,0:T(8,128)(2,1)S(1)}, bf16[512,512]{1,0:T(8,128)(2,1)}, u32[]{:S(2)}) copy-start(bf16[512,512]{1,0:T(8,128)(2,1)} %constant.7.clone.unsort) | copy-start | bytes 1572868
  8.6 2.4 %copy-start.9 = (bf16[512,512]{1,0:T(8,128)(2,1)S(1)}, bf16[512,512]{1,0:T(8,128)(2,1)}, u32[]{:S(2)}) copy-start(bf16[512,512]{1,0:T(8,128)(2,1)} %constant.6.clone.sort) | copy-start | bytes 1572868

commit v14 on v13

--- a/solution.py
+++ b/solution.py
@@ -33,6 +33,7 @@
 MIDDLE = STRIPS // 2
 GROUPS = 6
 BAND = 256
+FIRST_STRIPS = 6
 OWN_STRIPS = STRIPS - 1
 NEXT_STRIPS = 2
 NEXT_FIRST = (STRIPS - NEXT_STRIPS) * STRIP
@@ -41,6 +42,7 @@
 ROWS = BLOCK // HALVES
 WINDOW = ROWS + STRIP
 BODY = BLOCK - HEAD
+SEEN = -(-(FIRST_STRIPS * STRIP + TAPS - 1) // STRIP) * STRIP
 LABEL = 16
 F32 = jnp.float32
 BF16 = jnp.bfloat16
@@ -262,109 +264,139 @@
     return [*matrices, col_weights]
 
 
-def warp_kernel(
-    patch, slot, owner, weight, high_level, step_level, slope, rows_high, rows_low, col_weights,
-    sort, unsort, image, below, out,
-    terms, next_terms, matched_terms, next_matched, next_names, place_of, seen, label, name_sem,
+def sorted_rows(raw, sort):
+    col_pos = (2.0 * column_at(iota((1, WIDTH), 1)).astype(F32) + 1.0) / WIDTH - 1.0
+    count = raw.shape[0]
+    raw_high = raw.astype(BF16)
+    raw_low = (raw - raw_high.astype(F32)).astype(BF16)
+    both = jnp.dot(
+        jnp.concatenate([raw_high, raw_low], axis=0), sort, preferred_element_type=F32
+    )
+    high, low = both[:count], both[count:]
+    tilted = (high + low) * col_pos
+    tilted_high = tilted.astype(BF16).astype(F32)
+    return high, low, tilted_high, tilted - tilted_high
+
+
+def match_strip(level, step, slope, source, first, k):
+    lane = iota((1, LANES), 1)
+    if k != MIDDLE:
+        level = level + float(k - MIDDLE) * step
+    matrix = jnp.concatenate([level.astype(BF16), slope], axis=1)
+    filler = jnp.zeros((BAND - GROUPS * STEP, WIDTH), BF16)
+    rows = slice(first, first + STEP)
+    columns = jnp.concatenate([source[h, rows] for h in (0, 1, 0, 2, 3, 2)] + [filler], axis=0)
+    results = jnp.dot(matrix, columns, preferred_element_type=F32)
+    blocks = lane_sum(
+        lambda u, v, w: lane_block(results[u * STRIP : (u + 1) * STRIP], w), lane, TAPS, False
+    )
+    matched = jnp.concatenate(blocks, axis=1)
+    high = matched.astype(BF16)
+    return high, (matched - high.astype(F32)).astype(BF16)
+
+
+def forget(seen):
+    def clear(p, _):
+        seen[p] = 0
+        return 0
+
+    lax.fori_loop(0, seen.shape[0], clear, 0)
+
+
+def take(p, owner, seen):
+    rank = seen[p]
+    seen[p] = rank + 1
+    return owner[p], rank
+
+
+def match_kernel(
+    patch, slot, owner, weight, high_level, step_level, slope, sort, image,
+    place_of, label, matched_terms, terms, seen,
 ):
     devices = label.shape[0]
-    blocks_here = V * BLKC
-    ((ccd, _), _), same = whereabouts(devices)
-    names_copy = pltpu.make_async_copy(
-        below.at[0, pl.ds(HEAD + RIM, 8), pl.ds(0, LANES)], next_names, name_sem
-    )
-    names_copy.start()
+    ((ccd, _), _), _ = whereabouts(devices)
     lane = iota((1, LANES), 1)
-    next_terms[:, :, STEP:] = jnp.zeros((TOGETHER, 4, STRIP, WIDTH), BF16)
     label[...] = jnp.zeros_like(label)
-
-    def forget():
-        def clear(p, _):
-            seen[p] = 0
-            return 0
-
-        lax.fori_loop(0, owner.shape[0], clear, 0)
-
-    def take(p):
-        rank = seen[p]
-        seen[p] = rank + 1
-        return owner[p], rank
-
-    forget()
+    forget(seen)
     own = jnp.where(iota(weight.shape, 1) == ccd, weight[...].astype(F32), 0.0)
     own = jnp.sum(own, axis=1, keepdims=True)
-    for block in range(blocks_here):
-        to, rank = take(patch[0, block])
+    for block in range(V * BLKC):
+        to, rank = take(patch[0, block], owner, seen)
         place_of[block] = to * CAP + rank
         line = label[pl.ds(to, 1), :]
         line = jnp.where(lane == rank * 2, own[block // BLKC : block // BLKC + 1], line)
         line = jnp.where(lane == rank * 2 + 1, slot[0, block].astype(F32), line)
         label[pl.ds(to, 1), :] = line
+
+    def some_visits(turn, _):
+        visits = [turn * TOGETHER + i for i in range(TOGETHER)]
+        for i, visit in enumerate(visits):
+            for h, value in enumerate(sorted_rows(image[visit, RIM : RIM + SEEN], sort[...])):
+                terms[i, h] = value.astype(BF16)
+        for k in range(FIRST_STRIPS):
+            for i, visit in enumerate(visits):
+                at = slice(k * STRIP, (k + 1) * STRIP)
+                matched_terms[visit, 0, at], matched_terms[visit, 1, at] = match_strip(
+                    high_level[visit], step_level[visit], slope[visit],
+                    terms.at[i], k * STRIP, k,
+                )
+        return 0
+
+    lax.fori_loop(0, V // TOGETHER, some_visits, 0)
+
+
+def warp_kernel(
+    owner, place_of, label, high_level, step_level, slope, rows_high, rows_low, col_weights,
+    sort, unsort, image, below, matched_first, out,
+    terms, next_terms, matched_terms, next_matched, next_names, next_place, seen, name_sem,
+):
+    devices = label.shape[0]
+    _, same = whereabouts(devices)
+    names_copy = pltpu.make_async_copy(
+        below.at[pl.ds(V * (HEAD + RIM), 8), pl.ds(0, LANES)], next_names, name_sem
+    )
+    names_copy.start()
+    lane = iota((1, LANES), 1)
+    next_terms[:, :, STEP:] = jnp.zeros((TOGETHER, 4, STRIP, WIDTH), BF16)
     out[:, CAP * BLOCK :] = jnp.broadcast_to(
         label[...].reshape(devices, 1, LANES), (devices, LABEL, LANES)
     ).astype(BF16)
-    forget()
+    forget(seen)
     names_copy.wait()
-    for block in range(blocks_here):
-        to, rank = take(next_names[0, block].astype(jnp.int32))
-        place_of[blocks_here + block] = to * CAP + rank
-
+    for block in range(V * BLKC):
+        to, rank = take(next_names[0, block].astype(jnp.int32), owner, seen)
+        next_place[block] = to * CAP + rank
+
+    first_row = FIRST_STRIPS * STRIP
+    tall = BLOCK + 2 * RIM
+    seam = tall - STEP - first_row
     seam_row = iota((STEP, 1), 0) < STEP - HEAD - RIM
     both = jnp.where(same, 1.0, 0.0)
     own_sees = jnp.where(seam_row, 1.0, both)
     next_sees = jnp.where(seam_row, both, 1.0)
-    col_pos = (2.0 * column_at(iota((1, WIDTH), 1)).astype(F32) + 1.0) / WIDTH - 1.0
-    filler = jnp.zeros((BAND - GROUPS * STEP, WIDTH), BF16)
-    tall = BLOCK + 2 * RIM
-    seam = tall - STEP
 
     def some_visits(turn, _):
         visits = [turn * TOGETHER + i for i in range(TOGETHER)]
-
         for i, visit in enumerate(visits):
-            raw = jnp.concatenate([image[visit, RIM:], below[visit, : HEAD + RIM]], axis=0)
-            raw_high = raw.astype(BF16)
-            raw_low = (raw - raw_high.astype(F32)).astype(BF16)
-            sorted_terms = jnp.dot(
-                jnp.concatenate([raw_high, raw_low], axis=0), sort[...], preferred_element_type=F32
-            )
-            high, low = sorted_terms[:tall], sorted_terms[tall:]
-            tilted = (high + low) * col_pos
-            tilted_high = tilted.astype(BF16).astype(F32)
-            for h, value in enumerate((high, low, tilted_high, tilted - tilted_high)):
+            head = pl.ds(pl.multiple_of(visit * (HEAD + RIM), 8), HEAD + RIM)
+            raw = jnp.concatenate([image[visit, RIM + first_row :], below[head]], axis=0)
+            for h, value in enumerate(sorted_rows(raw, sort[...])):
                 terms[i, h, :seam] = value[:seam].astype(BF16)
                 terms[i, h, seam:] = (value[seam:] * own_sees).astype(BF16)
                 next_terms[i, h, :STEP] = (value[seam:] * next_sees).astype(BF16)
-
-        def strip(matrices, source, rows, k):
-            level = high_level[matrices]
-            if k != MIDDLE:
-                level = level + float(k - MIDDLE) * step_level[matrices]
-            matrix = jnp.concatenate([level.astype(BF16), slope[matrices]], axis=1)
-            columns = jnp.concatenate(
-                [source[h, rows] for h in (0, 1, 0, 2, 3, 2)] + [filler], axis=0
-            )
-            results = jnp.dot(matrix, columns, preferred_element_type=F32)
-            blocks = lane_sum(
-                lambda u, v, w: lane_block(results[u * STRIP : (u + 1) * STRIP], w),
-                lane, TAPS, False,
-            )
-            matched = jnp.concatenate(blocks, axis=1)
-            high = matched.astype(BF16)
-            return high, (matched - high.astype(F32)).astype(BF16)
-
-        for k in range(OWN_STRIPS):
+        for k in range(FIRST_STRIPS, OWN_STRIPS):
             for i, visit in enumerate(visits):
-                at = slice(k * STRIP, (k + 1) * STRIP)
-                matched_terms[i, 0, at], matched_terms[i, 1, at] = strip(
-                    visit, terms.at[i], slice(k * STRIP, k * STRIP + STEP), k
+                first = k * STRIP - first_row
+                at = slice(first, first + STRIP)
+                matched_terms[i, 0, at], matched_terms[i, 1, at] = match_strip(
+                    high_level[visit], step_level[visit], slope[visit], terms.at[i], first, k
                 )
         for k in range(NEXT_STRIPS):
             for i, visit in enumerate(visits):
                 at = slice(k * STRIP, (k + 1) * STRIP)
-                next_matched[i, 0, at], next_matched[i, 1, at] = strip(
-                    V + visit, next_terms.at[i], slice(k * STRIP, k * STRIP + STEP),
-                    STRIPS - NEXT_STRIPS + k,
+                next_matched[i, 0, at], next_matched[i, 1, at] = match_strip(
+                    high_level[V + visit], step_level[V + visit], slope[V + visit],
+                    next_terms.at[i], k * STRIP, STRIPS - NEXT_STRIPS + k,
                 )
 
         warped = []
@@ -376,9 +408,13 @@
 
                 def under(term):
                     if h == 0:
-                        parts = [matched_terms[i, term, :WINDOW]]
+                        parts = [matched_first[visit, term, :WINDOW]]
                     else:
-                        parts = [matched_terms[i, term, ROWS:], next_matched[i, term]]
+                        parts = [
+                            matched_first[visit, term, ROWS:],
+                            matched_terms[i, term],
+                            next_matched[i, term],
+                        ]
                     left = LANES - sum([x.shape[0] for x in parts])
                     return jnp.concatenate(parts + [jnp.zeros((left, WIDTH), BF16)], axis=0)
 
@@ -411,7 +447,7 @@
                 to = place_of[visit * BLKC + j]
                 rows = pl.ds(pl.multiple_of(to % CAP * BODY, HEAD), BODY)
                 out[to // CAP, rows] = piece[:BODY]
-                to = place_of[blocks_here + visit * BLKC + j]
+                to = next_place[visit * BLKC + j]
                 rows = pl.ds(pl.multiple_of(CAP * BODY + to % CAP * HEAD, HEAD), HEAD)
                 out[to // CAP, rows] = piece[BODY:]
         return 0
@@ -422,24 +458,47 @@
 def warp(patch, slot, owner, weight, ready, images, below, devices):
     smem = pl.BlockSpec(memory_space=pltpu.SMEM)
     vmem = pl.BlockSpec(memory_space=pltpu.VMEM)
-    sort = deinterleave()
+    order = deinterleave()
+    sort, unsort = jnp.asarray(order, BF16), jnp.asarray(order.T, BF16)
+    *matrices, rows_high, rows_low, col_weights = ready
+    args = [patch, slot, owner, weight, *matrices, sort, images]
+    place_of, label, matched = pl.pallas_call(
+        match_kernel,
+        in_specs=[smem] * 3 + [vmem] * (len(args) - 3),
+        out_specs=[smem, vmem, vmem],
+        out_shape=[
+            jax.ShapeDtypeStruct((V * BLKC,), jnp.int32),
+            jax.ShapeDtypeStruct((devices, LANES), F32),
+            jax.ShapeDtypeStruct((V, 2, FIRST_STRIPS * STRIP, WIDTH), BF16),
+        ],
+        scratch_shapes=[
+            pltpu.VMEM((TOGETHER, 4, SEEN, WIDTH), BF16),
+            pltpu.SMEM((owner.shape[0],), jnp.int32),
+        ],
+        compiler_params=pltpu.CompilerParams(vmem_limit_bytes=32 << 20),
+        cost_estimate=pl.CostEstimate(
+            flops=V * 2 * FIRST_STRIPS * TAPS * STRIP * BAND * WIDTH,
+            bytes_accessed=V * (BLOCK * WIDTH * 6),
+            transcendentals=0,
+        ),
+        name="match",
+    )(*args)
     args = [
-        patch, slot, owner, weight, *ready,
-        jnp.asarray(sort, BF16), jnp.asarray(sort.T, BF16), images, below,
+        owner, place_of, label, *matrices, rows_high, rows_low, col_weights,
+        sort, unsort, images, below, matched,
     ]
     return pl.pallas_call(
         warp_kernel,
-        in_specs=[smem] * 3 + [vmem] * (len(args) - 3),
+        in_specs=[smem] * 2 + [vmem] * (len(args) - 2),
         out_specs=vmem,
         scratch_shapes=[
-            pltpu.VMEM((TOGETHER, 4, BLOCK + 2 * RIM, WIDTH), BF16),
+            pltpu.VMEM((TOGETHER, 4, BLOCK + 2 * RIM - FIRST_STRIPS * STRIP, WIDTH), BF16),
             pltpu.VMEM((TOGETHER, 4, STEP + STRIP, WIDTH), BF16),
-            pltpu.VMEM((TOGETHER, 2, OWN_STRIPS * STRIP, WIDTH), BF16),
+            pltpu.VMEM((TOGETHER, 2, (OWN_STRIPS - FIRST_STRIPS) * STRIP, WIDTH), BF16),
             pltpu.VMEM((TOGETHER, 2, NEXT_STRIPS * STRIP, WIDTH), BF16),
             pltpu.SMEM((8, LANES), F32),
-            pltpu.SMEM((2 * V * BLKC,), jnp.int32),
+            pltpu.SMEM((V * BLKC,), jnp.int32),
             pltpu.SMEM((owner.shape[0],), jnp.int32),
-            pltpu.VMEM((devices, LANES), F32),
             pltpu.SemaphoreType.DMA(()),
         ],
         out_shape=jax.ShapeDtypeStruct((devices, CAP * BLOCK + LABEL, BLOCK), BF16),
@@ -449,7 +508,7 @@
             bytes_accessed=V * (BLOCK * WIDTH * 6),
             transcendentals=0,
         ),
-        name="match_warp",
+        name="warp",
     )(*args)
 
 
@@ -540,10 +599,9 @@
     devices = lax.axis_size("ccd")
     patch = block_patch[:, :, 0]
     names = lax.pad(
-        patch.astype(F32)[:, None, :], jnp.zeros((), F32),
-        ((0, V - 1, 0), (0, 7, 0), (0, WIDTH - V * BLKC, 0)),
-    )
-    head = jnp.concatenate([images[:, : HEAD + RIM], names], axis=1)
+        patch.astype(F32), jnp.zeros((), F32), ((0, 7, 0), (0, WIDTH - V * BLKC, 0))
+    )
+    head = jnp.concatenate([images[:, : HEAD + RIM].reshape(-1, WIDTH), names], axis=0)
     below = lax.ppermute(head, "ccd", [((i + 1) % devices, i) for i in range(devices)])
     ready = prepare(basis_taps, psf_coef, affine, devices)
     sent = warp(

time: 52.9 us -> 50.9 us (0.962)
  blocking collectives: 34.3 us -> 31.6 us
  Pallas kernels: 9.13 us -> 10.9 us
  waiting for transfers between devices: 1.01 us -> 0.01 us
    all_to_all x1, blocking collectives: 34.3 us -> 31.6 us  [shards(): got = lax.all_to_all(sent, 'ccd', split_axis=0, concat_axis=0, tiled=True)]
    pallas_call x1 -> x2, Pallas kernels: 5.56 us -> 7.31 us  [the longest x1 4.17 us: warp(): pl.pallas_call(warp_kernel, in_specs=[smem] * 2 + [vmem] * (len(args) - 2...]
    ppermute x1, waiting for transfers between devices: 1.01 us -> 0.01 us  [shards(): lax.ppermute(head, 'ccd', [((i + 1) % devices, i) for i in range(devices)])]
  transfers between devices with their start and end apart: 1 -> 1, of which waited for: 1 -> 0; matrix products, arithmetic and copies ran while one was open for 0% -> 0% of each run, Pallas kernels for 4% -> 10%
where the time goes in v14:
time: 50.9 us; the launch traced here: 50.6 us
  blocking collectives  31.6 us (62%)
  Pallas kernels  10.9 us (21%)
  starting transfers between devices  5.5 us (11%)
  local copies, waits for them, and re-layouts  1.89 us (4%)
  other arithmetic  0.67 us (1%)
    all_to_all x1, blocking collectives, shards(): got = lax.all_to_all(sent, 'ccd', split_axis=0, concat_axis=0, tiled=True)  31.6 us
    ppermute x1, starting transfers between devices, shards(): lax.ppermute(head, 'ccd', [((i + 1) % devices, i) for i in range(devices)])  5.5 us
    pallas_call x1, Pallas kernels, warp(): pl.pallas_call(warp_kernel, in_specs=[smem] * 2 + [vmem] * (len(args) - 2...  4.17 us
    pallas_call x1, Pallas kernels, warp(): pl.pallas_call(match_kernel, in_specs=[smem] * 3 + [vmem] * (len(args) -...  3.14 us
    pallas_call x2, Pallas kernels, small_kernel(): pl.pallas_call(body, grid=(1,), in_specs=[pl.BlockSpec(x.shape, lambda i,...  1.9 us
    pallas_call x1, Pallas kernels, coadd(): pl.pallas_call(coadd_kernel, in_specs=[pl.BlockSpec(memory_space=pltpu.VM...  1.68 us
  transfers between devices with their start and end apart: 1, of which 0 were waited for; matrix products, arithmetic and copies ran while one was open for 0% of the time, Pallas kernels for 10%

profile of v14, /device:TPU:0, one launch (start us, length us, event | category | flops | bytes accessed | tf_op | source)
XLA Modules:
  0.0 50.6 jit_solution(11638069987888295414)
XLA Ops:
  0.0 0.7 %bitcast_convert_fusion = f32[1,16]{1,0:T(1,128)S(1)} fusion(s32[1,16,1]{1,2,0:T(1,128)} %param.15), kind=kLoop, calls=%fused_computation.2 | loop fusion | flops 16 | bytes 128 | tf_op jit(solution)/shard_map/convert_element_type | solution.py:602
  0.7 0.9 %slice.3 = f32[4,24,512]{2,1,0:T(8,128)S(1)} slice(f32[4,128,512]{2,1,0:T(8,128)} %image.3), slice={[0:4], [0:24], [0:512]} | slice | bytes 393216 | tf_op jit(solution)/shard_map/slice | solution.py:604
  1.6 5.5 %collective-permute-start = (f32[104,512]{1,0:T(8,128)S(1)}, f32[104,512]{1,0:T(8,128)S(1)}, u32[]{:S(2)}, u32[]{:S(2)}) collective-permute-start(f32[104,512]{1,0:T(8,128)S(1)} %select_maximum_fusion), channel_id=1, source_target_pairs={{1,0},{2,1},{3,2},{4,3},{5,4},{6,5},{7,6},{8,7},{9,8},{10,9},{11,1... | collective-permute-start | bytes 638984 | tf_op jit(solution)/shard_map/ppermute | solution.py:605
  7.1 0.0 copy-start.6
  7.1 0.7 %copy-done.6 = f32[4,5,2,2]{1,3,2,0:T(2,128)S(1)} copy-done((f32[4,5,2,2]{1,3,2,0:T(2,128)S(1)}, f32[4,5,2,2]{1,3,2,0:T(2,128)}, u32[]{:S(2)}) %copy-start.6) | copy-done | bytes 344
  7.8 0.0 copy-start.4
  7.8 0.0 copy-start.5
  7.8 0.5 %lanczos_weights.1 = (f32[4,128,128]{2,1,0:T(8,128)S(1)}, f32[8,8,512]{2,1,0:T(8,128)S(1)}) custom-call(f32[4,2,2,5]{3,2,1,0:T(2,128)S(1)} %bitcast.8), custom_call_target="tpu_custom_call" | custom-call | flops 1073741824 | bytes 1048576 | tf_op jit(solution)/shard_map/lanczos_weights/pallas_call | solution.py:235
  8.4 0.2 copy-done.4
  8.6 0.0 copy-done.5
  8.6 0.0 copy-start
  8.6 0.0 copy-start.1
  8.6 0.0 copy-start.3
  8.6 0.0 copy-start.7
  8.6 0.0 copy-start.8
  8.6 0.0 copy-start.9
  8.6 1.4 %matrices.1 = (f32[8,176,128]{2,1,0:T(8,128)S(1)}, f32[8,176,128]{2,1,0:T(8,128)S(1)}, bf16[8,176,128]{2,1,0:T(8,128)(2,1)S(1)}, bf16[4,128,128]{2,1,0:T(8,128)(2,1)S(1)}, bf16[4,128,128]{2,1,0:T(8,128)(2,1)S(1)}) custom-call(f32[9,2,11]{2,1,0:T(2,128)S(1)} %bitcast.7, f32[5,3,4,9]{3,2,1,0:T(4,128)S(1)} %bitcast.6, ...), custom_call_target="tpu_custom_call" | custom-call | flops 1073741824 | bytes 1048576 | tf_op jit(solution)/shard_map/matrices/pallas_call | solution.py:235
  10.0 0.0 copy-done
  10.0 0.0 copy-done.1
  10.0 0.0 copy-done.3
  10.0 0.0 copy-done.7
  10.0 0.0 copy-done.8
  10.0 0.0 copy-done.9
  10.0 0.0 copy-start.2
  10.1 3.1 %match.1 = (s32[16]{0:T(128)S(1)}, f32[16,128]{1,0:T(8,128)S(1)}, bf16[4,2,96,512]{3,2,1,0:T(8,128)(2,1)S(1)}) custom-call(s32[1,16]{1,0:T(1,128)S(1)} %bitcast.9, s32[1,16]{1,0:T(1,128)S(1)} %copy-done.9, s32[16]{0:T(128)S(1)} %copy-done.3, bf16[4,5]{1,0:T(4,128)(2,1)S(1)} %copy-done.7, f32[8,176,128]{2,1,0:T(8,128)S(1)} %get-tuple-element.16.high_level, ...), custom_call_target="tpu_custom_call" | custom-call | flops 1107296256 | bytes 1572864 | tf_op jit(solution)/shard_map/match/pallas_call | solution.py:465
  13.2 0.0 collective-permute-done.below
  13.2 0.0 copy-done.2
  13.2 4.2 %warp.1 = bf16[16,272,128]{2,1,0:T(8,128)(2,1)S(1)} custom-call(s32[16]{0:T(128)S(1)} %copy-done.3, s32[16]{0:T(128)S(1)} %get-tuple-element.19.place_of, f32[16,128]{1,0:T(8,128)S(1)} %get-tuple-element.20.label, f32[8,176,128]{2,1,0:T(8,128)S(1)} %get-tuple-element.16.high_level, f32[8,176,128]{2,1,0:T(8,128)S(1)} %get-tuple-element.17.step_level, ...), custom_call_target="tpu_custom_call" | custom-call | flops 1660944384 | bytes 1572864 | tf_op jit(solution)/shard_map/warp/pallas_call | solution.py:490
  17.4 31.6 %all_to_all.5.got = bf16[16,272,128]{2,1,0:T(8,128)(2,1)S(1)} all-to-all(bf16[16,272,128]{2,1,0:T(8,128)(2,1)S(1)} %warp.1), channel_id=1, replica_groups=mesh['group'=2,'ccd'=16] {'ccd'}, dimensions={0} | all-to-all | bytes 2228224 | tf_op jit(solution)/shard_map/all_to_all | solution.py:610
  49.0 1.7 %coadd.1 = f32[1,512,512]{2,1,0:T(8,128)} custom-call(bf16[16,272,128]{2,1,0:T(8,128)(2,1)S(1)} %all_to_all.5.got), custom_call_target="tpu_custom_call" | custom-call | tf_op jit(solution)/shard_map/coadd/pallas_call | solution.py:582
  (1 shorter events, 0.0 us)
Async XLA Ops:
  1.6 11.6 %collective-permute-start = (f32[104,512]{1,0:T(8,128)S(1)}, f32[104,512]{1,0:T(8,128)S(1)}, u32[]{:S(2)}, u32[]{:S(2)}) collective-permute-start(f32[104,512]{1,0:T(8,128)S(1)} %select_maximum_fusion), channel_id=1, source_target_pairs={{1,0},{2,1},{3,2},{4,3},{5,4},{6,5},{7,6},{8,7},{9,8},{10,9},{11,1... | collective-permute-start | bytes 638984 | tf_op jit(solution)/shard_map/ppermute | solution.py:605
  7.1 0.7 %copy-start.6 = (f32[4,5,2,2]{1,3,2,0:T(2,128)S(1)}, f32[4,5,2,2]{1,3,2,0:T(2,128)}, u32[]{:S(2)}) copy-start(f32[4,5,2,2]{1,3,2,0:T(2,128)} %param.13) | copy-start | bytes 964
  7.8 0.8 %copy-start.4 = (f32[4,5,9,3]{2,0,3,1:T(4,128)S(1)}, f32[4,5,9,3]{2,0,3,1:T(4,128)}, u32[]{:S(2)}) copy-start(f32[4,5,9,3]{2,0,3,1:T(4,128)} %param.12) | copy-start | bytes 6484
  7.8 0.8 %copy-start.5 = (f32[2,9,11]{2,0,1:T(2,128)S(1)}, f32[2,9,11]{2,0,1:T(2,128)}, u32[]{:S(2)}) copy-start(f32[2,9,11]{2,0,1:T(2,128)} %param.11) | copy-start | bytes 2380
  8.6 1.4 %copy-start = (f32[4,128,512]{2,1,0:T(8,128)S(1)}, f32[4,128,512]{2,1,0:T(8,128)}, u32[]{:S(2)}) copy-start(f32[4,128,512]{2,1,0:T(8,128)} %image.3) | copy-start | bytes 3145732
  8.6 1.4 %copy-start.1 = (bf16[512,512]{1,0:T(8,128)(2,1)S(1)}, bf16[512,512]{1,0:T(8,128)(2,1)}, u32[]{:S(2)}) copy-start(bf16[512,512]{1,0:T(8,128)(2,1)} %constant.6.clone.sort) | copy-start | bytes 1572868
  8.6 1.4 %copy-start.3 = (s32[16]{0:T(128)S(1)}, s32[16]{0:T(128)}, u32[]{:S(2)}) copy-start(s32[16]{0:T(128)} %owner.3) | copy-start | bytes 196
  8.6 1.4 %copy-start.7 = (bf16[4,5]{1,0:T(4,128)(2,1)S(1)}, bf16[4,5]{1,0:T(4,128)(2,1)}, u32[]{:S(2)}) copy-start(bf16[4,5]{1,0:T(4,128)(2,1)} %weight.1) | copy-start | bytes 124
  8.6 1.4 %copy-start.8 = (s32[1,16,1]{1,2,0:T(1,128)S(1)}, s32[1,16,1]{1,2,0:T(1,128)}, u32[]{:S(2)}) copy-start(s32[1,16,1]{1,2,0:T(1,128)} %param.15) | copy-start | bytes 196
  8.6 1.4 %copy-start.9 = (s32[1,16]{1,0:T(1,128)S(1)}, s32[1,16]{1,0:T(1,128)}, u32[]{:S(2)}) copy-start(s32[1,16]{1,0:T(1,128)} %slot.1) | copy-start | bytes 196
  10.0 3.2 %copy-start.2 = (bf16[512,512]{1,0:T(8,128)(2,1)S(1)}, bf16[512,512]{1,0:T(8,128)(2,1)}, u32[]{:S(2)}) copy-start(bf16[512,512]{1,0:T(8,128)(2,1)} %constant.7.clone.unsort) | copy-start | bytes 1572868

commit v15 on v14

--- a/solution.py
+++ b/solution.py
@@ -232,11 +232,11 @@
 
 
 def small_kernel(body, name, args, shapes):
+    vmem = pl.BlockSpec(memory_space=pltpu.VMEM)
     return pl.pallas_call(
         body,
-        grid=(1,),
-        in_specs=[pl.BlockSpec(x.shape, lambda i, n=x.ndim: (0,) * n) for x in args],
-        out_specs=[pl.BlockSpec(shape, lambda i: (0, 0, 0)) for shape, _ in shapes],
+        in_specs=[vmem] * len(args),
+        out_specs=[vmem] * len(shapes),
         out_shape=[jax.ShapeDtypeStruct(shape, kind) for shape, kind in shapes],
         compiler_params=pltpu.CompilerParams(vmem_limit_bytes=32 << 20),
         cost_estimate=pl.CostEstimate(flops=1 << 30, bytes_accessed=1 << 20, transcendentals=0),
@@ -295,38 +295,46 @@
     return high, (matched - high.astype(F32)).astype(BF16)
 
 
-def forget(seen):
-    def clear(p, _):
-        seen[p] = 0
-        return 0
-
-    lax.fori_loop(0, seen.shape[0], clear, 0)
-
-
-def take(p, owner, seen):
-    rank = seen[p]
-    seen[p] = rank + 1
-    return owner[p], rank
+def upright(line):
+    count = line.shape[1]
+    square = (count, count)
+    return jnp.sum(
+        jnp.where(iota(square, 0) == iota(square, 1), jnp.broadcast_to(line, square), 0),
+        axis=1, keepdims=True,
+    )
+
+
+def route(patch, owner):
+    square = (patch.shape[1], patch.shape[1])
+    earlier = (iota(square, 0) < iota(square, 1)) & (upright(patch) == patch)
+    rank = jnp.sum(earlier.astype(jnp.int32), axis=0, keepdims=True)
+    named = iota((owner.shape[1], patch.shape[1]), 0) == patch
+    to = jnp.sum(jnp.where(named, upright(owner), 0), axis=0, keepdims=True)
+    return to, rank
 
 
 def match_kernel(
     patch, slot, owner, weight, high_level, step_level, slope, sort, image,
-    place_of, label, matched_terms, terms, seen,
+    places, label, matched_terms, terms,
 ):
-    devices = label.shape[0]
-    ((ccd, _), _), _ = whereabouts(devices)
-    lane = iota((1, LANES), 1)
-    label[...] = jnp.zeros_like(label)
-    forget(seen)
+    ((ccd, _), _), _ = whereabouts(label.shape[0])
+    to, rank = route(patch[...], owner[...])
+    places[...] = to * CAP + rank
+
     own = jnp.where(iota(weight.shape, 1) == ccd, weight[...].astype(F32), 0.0)
     own = jnp.sum(own, axis=1, keepdims=True)
-    for block in range(V * BLKC):
-        to, rank = take(patch[0, block], owner, seen)
-        place_of[block] = to * CAP + rank
-        line = label[pl.ds(to, 1), :]
-        line = jnp.where(lane == rank * 2, own[block // BLKC : block // BLKC + 1], line)
-        line = jnp.where(lane == rank * 2 + 1, slot[0, block].astype(F32), line)
-        label[pl.ds(to, 1), :] = line
+    each = (V, V * BLKC)
+    weights = jnp.sum(
+        jnp.where(iota(each, 1) // BLKC == iota(each, 0), own, 0.0), axis=0, keepdims=True
+    )
+    goes = iota((label.shape[0], V * BLKC), 0) == to
+    lane = iota(label.shape, 1)
+    lines = jnp.zeros(label.shape, F32)
+    for r in range(CAP):
+        for n, value in enumerate((weights, slot[...].astype(F32))):
+            column = jnp.sum(jnp.where(goes & (rank == r), value, 0.0), axis=1, keepdims=True)
+            lines = jnp.where(lane == 2 * r + n, column, lines)
+    label[...] = lines
 
     def some_visits(turn, _):
         visits = [turn * TOGETHER + i for i in range(TOGETHER)]
@@ -346,26 +354,23 @@
 
 
 def warp_kernel(
-    owner, place_of, label, high_level, step_level, slope, rows_high, rows_low, col_weights,
+    owner, places, label, high_level, step_level, slope, rows_high, rows_low, col_weights,
     sort, unsort, image, below, matched_first, out,
-    terms, next_terms, matched_terms, next_matched, next_names, next_place, seen, name_sem,
+    terms, next_terms, matched_terms, next_matched, both_places, place_of, place_sem,
 ):
     devices = label.shape[0]
     _, same = whereabouts(devices)
-    names_copy = pltpu.make_async_copy(
-        below.at[pl.ds(V * (HEAD + RIM), 8), pl.ds(0, LANES)], next_names, name_sem
-    )
-    names_copy.start()
+    next_patch = below[V * (HEAD + RIM) : V * (HEAD + RIM) + 1, : V * BLKC].astype(jnp.int32)
+    to, rank = route(next_patch, owner[...])
+    both_places[0:1, : V * BLKC] = places[...]
+    both_places[1:2, : V * BLKC] = to * CAP + rank
+    place_copy = pltpu.make_async_copy(both_places, place_of, place_sem)
+    place_copy.start()
     lane = iota((1, LANES), 1)
     next_terms[:, :, STEP:] = jnp.zeros((TOGETHER, 4, STRIP, WIDTH), BF16)
     out[:, CAP * BLOCK :] = jnp.broadcast_to(
         label[...].reshape(devices, 1, LANES), (devices, LABEL, LANES)
     ).astype(BF16)
-    forget(seen)
-    names_copy.wait()
-    for block in range(V * BLKC):
-        to, rank = take(next_names[0, block].astype(jnp.int32), owner, seen)
-        next_place[block] = to * CAP + rank
 
     first_row = FIRST_STRIPS * STRIP
     tall = BLOCK + 2 * RIM
@@ -427,6 +432,10 @@
                 halves.append(total + jnp.dot(low, first, preferred_element_type=F32))
             warped.append(jnp.concatenate(halves, axis=0))
 
+        @pl.when(turn == 0)
+        def _():
+            place_copy.wait()
+
         for i, visit in enumerate(visits):
             parts = []
             for rows, weights in (
@@ -444,10 +453,10 @@
             ).astype(BF16)
             for j in range(BLKC):
                 piece = lane_block(result, j)
-                to = place_of[visit * BLKC + j]
+                to = place_of[0, visit * BLKC + j]
                 rows = pl.ds(pl.multiple_of(to % CAP * BODY, HEAD), BODY)
                 out[to // CAP, rows] = piece[:BODY]
-                to = next_place[visit * BLKC + j]
+                to = place_of[1, visit * BLKC + j]
                 rows = pl.ds(pl.multiple_of(CAP * BODY + to % CAP * HEAD, HEAD), HEAD)
                 out[to // CAP, rows] = piece[BODY:]
         return 0
@@ -456,24 +465,23 @@
 
 
 def warp(patch, slot, owner, weight, ready, images, below, devices):
-    smem = pl.BlockSpec(memory_space=pltpu.SMEM)
     vmem = pl.BlockSpec(memory_space=pltpu.VMEM)
     order = deinterleave()
     sort, unsort = jnp.asarray(order, BF16), jnp.asarray(order.T, BF16)
     *matrices, rows_high, rows_low, col_weights = ready
+    owner = owner.reshape(1, -1)
     args = [patch, slot, owner, weight, *matrices, sort, images]
-    place_of, label, matched = pl.pallas_call(
+    places, label, matched = pl.pallas_call(
         match_kernel,
-        in_specs=[smem] * 3 + [vmem] * (len(args) - 3),
-        out_specs=[smem, vmem, vmem],
+        in_specs=[vmem] * len(args),
+        out_specs=[vmem, vmem, vmem],
         out_shape=[
-            jax.ShapeDtypeStruct((V * BLKC,), jnp.int32),
+            jax.ShapeDtypeStruct((1, V * BLKC), jnp.int32),
             jax.ShapeDtypeStruct((devices, LANES), F32),
             jax.ShapeDtypeStruct((V, 2, FIRST_STRIPS * STRIP, WIDTH), BF16),
         ],
         scratch_shapes=[
             pltpu.VMEM((TOGETHER, 4, SEEN, WIDTH), BF16),
-            pltpu.SMEM((owner.shape[0],), jnp.int32),
         ],
         compiler_params=pltpu.CompilerParams(vmem_limit_bytes=32 << 20),
         cost_estimate=pl.CostEstimate(
@@ -484,21 +492,20 @@
         name="match",
     )(*args)
     args = [
-        owner, place_of, label, *matrices, rows_high, rows_low, col_weights,
+        owner, places, label, *matrices, rows_high, rows_low, col_weights,
         sort, unsort, images, below, matched,
     ]
     return pl.pallas_call(
         warp_kernel,
-        in_specs=[smem] * 2 + [vmem] * (len(args) - 2),
+        in_specs=[vmem] * len(args),
         out_specs=vmem,
         scratch_shapes=[
             pltpu.VMEM((TOGETHER, 4, BLOCK + 2 * RIM - FIRST_STRIPS * STRIP, WIDTH), BF16),
             pltpu.VMEM((TOGETHER, 4, STEP + STRIP, WIDTH), BF16),
             pltpu.VMEM((TOGETHER, 2, (OWN_STRIPS - FIRST_STRIPS) * STRIP, WIDTH), BF16),
             pltpu.VMEM((TOGETHER, 2, NEXT_STRIPS * STRIP, WIDTH), BF16),
-            pltpu.SMEM((8, LANES), F32),
-            pltpu.SMEM((V * BLKC,), jnp.int32),
-            pltpu.SMEM((owner.shape[0],), jnp.int32),
+            pltpu.VMEM((8, LANES), jnp.int32),
+            pltpu.SMEM((8, LANES), jnp.int32),
             pltpu.SemaphoreType.DMA(()),
         ],
         out_shape=jax.ShapeDtypeStruct((devices, CAP * BLOCK + LABEL, BLOCK), BF16),
@@ -598,10 +605,11 @@
 ):
     devices = lax.axis_size("ccd")
     patch = block_patch[:, :, 0]
-    names = lax.pad(
-        patch.astype(F32), jnp.zeros((), F32), ((0, 7, 0), (0, WIDTH - V * BLKC, 0))
-    )
-    head = jnp.concatenate([images[:, : HEAD + RIM].reshape(-1, WIDTH), names], axis=0)
+    zero = jnp.zeros((), F32)
+    rows = V * (HEAD + RIM)
+    head = lax.pad(
+        images[:, : HEAD + RIM].reshape(rows, WIDTH), zero, ((0, 8, 0), (0, 0, 0))
+    ) + lax.pad(patch.astype(F32), zero, ((rows, 7, 0), (0, WIDTH - V * BLKC, 0)))
     below = lax.ppermute(head, "ccd", [((i + 1) % devices, i) for i in range(devices)])
     ready = prepare(basis_taps, psf_coef, affine, devices)
     sent = warp(

time: 50.9 us -> 50.1 us (0.984)
  Pallas kernels: 10.9 us -> 9.46 us
  blocking collectives: 31.6 us -> 32.2 us
    pallas_call x4, Pallas kernels: 9.21 us -> 7.78 us  [the longest x1 3.37 us: warp(): pl.pallas_call(warp_kernel, in_specs=[vmem] * len(args), out_specs=vmem,...]
    all_to_all x1, blocking collectives: 31.6 us -> 32.2 us  [shards(): got = lax.all_to_all(sent, 'ccd', split_axis=0, concat_axis=0, tiled=True)]
  transfers between devices with their start and end apart: 1 -> 1, of which waited for: 0 -> 0; matrix products, arithmetic and copies ran while one was open for 0% -> 0% of each run, Pallas kernels for 10% -> 9%
where the time goes in v15:
time: 50.1 us; the launch traced here: 49.9 us
  blocking collectives  32.2 us (64%)
  Pallas kernels  9.46 us (19%)
  starting transfers between devices  5.5 us (11%)
  local copies, waits for them, and re-layouts  1.89 us (4%)
  other arithmetic  0.67 us (1%)
    all_to_all x1, blocking collectives, shards(): got = lax.all_to_all(sent, 'ccd', split_axis=0, concat_axis=0, tiled=True)  32.2 us
    ppermute x1, starting transfers between devices, shards(): lax.ppermute(head, 'ccd', [((i + 1) % devices, i) for i in range(devices)])  5.5 us
    pallas_call x1, Pallas kernels, warp(): pl.pallas_call(warp_kernel, in_specs=[vmem] * len(args), out_specs=vmem,...  3.37 us
    pallas_call x1, Pallas kernels, warp(): pl.pallas_call(match_kernel, in_specs=[vmem] * len(args), out_specs=[vmem...  2.51 us
    pallas_call x2, Pallas kernels, small_kernel(): pl.pallas_call(body, in_specs=[vmem] * len(args), out_specs=[vmem] * len(...  1.9 us
    pallas_call x1, Pallas kernels, coadd(): pl.pallas_call(coadd_kernel, in_specs=[pl.BlockSpec(memory_space=pltpu.VM...  1.67 us
  transfers between devices with their start and end apart: 1, of which 0 were waited for; matrix products, arithmetic and copies ran while one was open for 0% of the time, Pallas kernels for 9%

profile of v15, /device:TPU:0, one launch (start us, length us, event | category | flops | bytes accessed | tf_op | source)
XLA Modules:
  0.0 49.9 jit_solution(2452053572514608419)
XLA Ops:
  0.0 0.7 %bitcast_convert_fusion = f32[1,16]{1,0:T(1,128)S(1)} fusion(s32[1,16,1]{1,2,0:T(1,128)} %param.15), kind=kLoop, calls=%fused_computation.1 | loop fusion | flops 16 | bytes 128 | tf_op jit(solution)/shard_map/convert_element_type | solution.py:612
  0.7 0.9 %slice.3 = f32[4,24,512]{2,1,0:T(8,128)S(1)} slice(f32[4,128,512]{2,1,0:T(8,128)} %image.3), slice={[0:4], [0:24], [0:512]} | slice | bytes 393216 | tf_op jit(solution)/shard_map/slice | solution.py:611
  1.6 5.5 %collective-permute-start = (f32[104,512]{1,0:T(8,128)S(1)}, f32[104,512]{1,0:T(8,128)S(1)}, u32[]{:S(2)}, u32[]{:S(2)}) collective-permute-start(f32[104,512]{1,0:T(8,128)S(1)} %pad_add_fusion), channel_id=1, source_target_pairs={{1,0},{2,1},{3,2},{4,3},{5,4},{6,5},{7,6},{8,7},{9,8},{10,9},{11,1... | collective-permute-start | bytes 638984 | tf_op jit(solution)/shard_map/ppermute | solution.py:613
  7.1 0.0 copy-start.6
  7.1 0.7 %copy-done.6 = f32[4,5,2,2]{1,3,2,0:T(2,128)S(1)} copy-done((f32[4,5,2,2]{1,3,2,0:T(2,128)S(1)}, f32[4,5,2,2]{1,3,2,0:T(2,128)}, u32[]{:S(2)}) %copy-start.6) | copy-done | bytes 344
  7.8 0.0 copy-start.4
  7.8 0.0 copy-start.5
  7.8 0.5 %lanczos_weights.1 = (f32[4,128,128]{2,1,0:T(8,128)S(1)}, f32[8,8,512]{2,1,0:T(8,128)S(1)}) custom-call(f32[4,2,2,5]{3,2,1,0:T(2,128)S(1)} %bitcast.11), custom_call_target="tpu_custom_call" | custom-call | flops 1073741824 | bytes 1048576 | tf_op jit(solution)/shard_map/lanczos_weights/pallas_call | solution.py:236
  8.4 0.2 copy-done.4
  8.6 0.0 copy-done.5
  8.6 0.0 copy-start
  8.6 0.0 copy-start.1
  8.6 0.0 copy-start.3
  8.6 0.0 copy-start.7
  8.6 0.0 copy-start.8
  8.6 0.0 copy-start.9
  8.6 1.4 %matrices.1 = (f32[8,176,128]{2,1,0:T(8,128)S(1)}, f32[8,176,128]{2,1,0:T(8,128)S(1)}, bf16[8,176,128]{2,1,0:T(8,128)(2,1)S(1)}, bf16[4,128,128]{2,1,0:T(8,128)(2,1)S(1)}, bf16[4,128,128]{2,1,0:T(8,128)(2,1)S(1)}) custom-call(f32[9,2,11]{2,1,0:T(2,128)S(1)} %bitcast.10, f32[5,3,4,9]{3,2,1,0:T(4,128)S(1)} %bitcast.9, ...), custom_call_target="tpu_custom_call" | custom-call | flops 1073741824 | bytes 1048576 | tf_op jit(solution)/shard_map/matrices/pallas_call | solution.py:236
  10.0 0.0 copy-done
  10.0 0.0 copy-done.1
  10.0 0.0 copy-done.3
  10.0 0.0 copy-done.7
  10.0 0.0 copy-done.8
  10.0 0.0 copy-done.9
  10.0 0.0 copy-start.2
  10.1 2.5 %match.1 = (s32[1,16]{1,0:T(1,128)S(1)}, f32[16,128]{1,0:T(8,128)S(1)}, bf16[4,2,96,512]{3,2,1,0:T(8,128)(2,1)S(1)}) custom-call(s32[1,16]{1,0:T(1,128)S(1)} %bitcast.12, s32[1,16]{1,0:T(1,128)S(1)} %copy-done.9, s32[1,16]{1,0:T(1,128)S(1)} %bitcast.7, bf16[4,5]{1,0:T(4,128)(2,1)S(1)} %copy-done.7, f32[8,176,128]{2,1,0:T(8,128)S(1)} %get-tuple-element.16.high_level, ...), custom_call_target="tpu_custom_call" | custom-call | flops 1107296256 | bytes 1572864 | tf_op jit(solution)/shard_map/match/pallas_call | solution.py:474
  12.6 0.0 collective-permute-done.below
  12.6 0.0 copy-done.2
  12.6 3.4 %warp.1 = bf16[16,272,128]{2,1,0:T(8,128)(2,1)S(1)} custom-call(s32[1,16]{1,0:T(1,128)S(1)} %bitcast.8, s32[1,16]{1,0:T(1,128)S(1)} %get-tuple-element.19.places, f32[16,128]{1,0:T(8,128)S(1)} %get-tuple-element.20.label, f32[8,176,128]{2,1,0:T(8,128)S(1)} %get-tuple-element.16.high_level, f32[8,176,128]{2,1,0:T(8,128)S(1)} %get-tuple-element.17.step_level, ...), custom_call_target="tpu_custom_call" | custom-call | flops 1660944384 | bytes 1572864 | tf_op jit(solution)/shard_map/warp/pallas_call | solution.py:498
  16.0 32.2 %all_to_all.5.got = bf16[16,272,128]{2,1,0:T(8,128)(2,1)S(1)} all-to-all(bf16[16,272,128]{2,1,0:T(8,128)(2,1)S(1)} %warp.1), channel_id=1, replica_groups=mesh['group'=2,'ccd'=16] {'ccd'}, dimensions={0} | all-to-all | bytes 2228224 | tf_op jit(solution)/shard_map/all_to_all | solution.py:618
  48.2 1.7 %coadd.1 = f32[1,512,512]{2,1,0:T(8,128)} custom-call(bf16[16,272,128]{2,1,0:T(8,128)(2,1)S(1)} %all_to_all.5.got), custom_call_target="tpu_custom_call" | custom-call | tf_op jit(solution)/shard_map/coadd/pallas_call | solution.py:589
  (1 shorter events, 0.0 us)
Async XLA Ops:
  1.6 11.0 %collective-permute-start = (f32[104,512]{1,0:T(8,128)S(1)}, f32[104,512]{1,0:T(8,128)S(1)}, u32[]{:S(2)}, u32[]{:S(2)}) collective-permute-start(f32[104,512]{1,0:T(8,128)S(1)} %pad_add_fusion), channel_id=1, source_target_pairs={{1,0},{2,1},{3,2},{4,3},{5,4},{6,5},{7,6},{8,7},{9,8},{10,9},{11,1... | collective-permute-start | bytes 638984 | tf_op jit(solution)/shard_map/ppermute | solution.py:613
  7.1 0.7 %copy-start.6 = (f32[4,5,2,2]{1,3,2,0:T(2,128)S(1)}, f32[4,5,2,2]{1,3,2,0:T(2,128)}, u32[]{:S(2)}) copy-start(f32[4,5,2,2]{1,3,2,0:T(2,128)} %param.13) | copy-start | bytes 964
  7.8 0.8 %copy-start.4 = (f32[4,5,9,3]{2,0,3,1:T(4,128)S(1)}, f32[4,5,9,3]{2,0,3,1:T(4,128)}, u32[]{:S(2)}) copy-start(f32[4,5,9,3]{2,0,3,1:T(4,128)} %param.12) | copy-start | bytes 6484
  7.8 0.8 %copy-start.5 = (f32[2,9,11]{2,0,1:T(2,128)S(1)}, f32[2,9,11]{2,0,1:T(2,128)}, u32[]{:S(2)}) copy-start(f32[2,9,11]{2,0,1:T(2,128)} %param.11) | copy-start | bytes 2380
  8.6 1.4 %copy-start = (f32[4,128,512]{2,1,0:T(8,128)S(1)}, f32[4,128,512]{2,1,0:T(8,128)}, u32[]{:S(2)}) copy-start(f32[4,128,512]{2,1,0:T(8,128)} %image.3) | copy-start | bytes 3145732
  8.6 1.4 %copy-start.1 = (bf16[512,512]{1,0:T(8,128)(2,1)S(1)}, bf16[512,512]{1,0:T(8,128)(2,1)}, u32[]{:S(2)}) copy-start(bf16[512,512]{1,0:T(8,128)(2,1)} %constant.6.clone.sort) | copy-start | bytes 1572868
  8.6 1.4 %copy-start.3 = (s32[16]{0:T(128)S(1)}, s32[16]{0:T(128)}, u32[]{:S(2)}) copy-start(s32[16]{0:T(128)} %param.17) | copy-start | bytes 196
  8.6 1.4 %copy-start.7 = (bf16[4,5]{1,0:T(4,128)(2,1)S(1)}, bf16[4,5]{1,0:T(4,128)(2,1)}, u32[]{:S(2)}) copy-start(bf16[4,5]{1,0:T(4,128)(2,1)} %weight.1) | copy-start | bytes 124
  8.6 1.4 %copy-start.8 = (s32[1,16,1]{1,2,0:T(1,128)S(1)}, s32[1,16,1]{1,2,0:T(1,128)}, u32[]{:S(2)}) copy-start(s32[1,16,1]{1,2,0:T(1,128)} %param.15) | copy-start | bytes 196
  8.6 1.4 %copy-start.9 = (s32[1,16]{1,0:T(1,128)S(1)}, s32[1,16]{1,0:T(1,128)}, u32[]{:S(2)}) copy-start(s32[1,16]{1,0:T(1,128)} %slot.1) | copy-start | bytes 196
  10.0 2.5 %copy-start.2 = (bf16[512,512]{1,0:T(8,128)(2,1)S(1)}, bf16[512,512]{1,0:T(8,128)(2,1)}, u32[]{:S(2)}) copy-start(bf16[512,512]{1,0:T(8,128)(2,1)} %constant.7.clone.unsort) | copy-start | bytes 1572868

commit v16 on v15

--- a/solution.py
+++ b/solution.py
@@ -22,7 +22,7 @@
 HALF = TAPS // 2
 WARP = 3
 RIM = HALF + WARP
-HEAD = 16
+TAIL = 16
 HEIGHT = SPLIT * BLOCK
 WIDTH = BLKC * BLOCK
 LANES = 128
@@ -33,16 +33,16 @@
 MIDDLE = STRIPS // 2
 GROUPS = 6
 BAND = 256
-FIRST_STRIPS = 6
-OWN_STRIPS = STRIPS - 1
-NEXT_STRIPS = 2
-NEXT_FIRST = (STRIPS - NEXT_STRIPS) * STRIP
+PAST_STRIPS = 2
+OWN_FIRST = 1
+FREE_FIRST = 2
 HALVES = 2
 TOGETHER = 2
 ROWS = BLOCK // HALVES
 WINDOW = ROWS + STRIP
-BODY = BLOCK - HEAD
-SEEN = -(-(FIRST_STRIPS * STRIP + TAPS - 1) // STRIP) * STRIP
+BODY = BLOCK - TAIL
+GOT = TAIL + RIM
+OPEN = (STRIPS - 1) * STRIP + STEP - FREE_FIRST * STRIP
 LABEL = 16
 F32 = jnp.float32
 BF16 = jnp.bfloat16
@@ -128,14 +128,54 @@
 
 def whereabouts(devices):
     band = lax.axis_index("ccd")
-    after = lax.rem(band + 1, devices)
+    past = lax.rem(band + devices - 1, devices)
     quarter = (band + SPLIT // 2) % SPLIT
-    own = ((band + SPLIT // 2) // SPLIT, quarter * BLOCK + HEAD)
-    following = (
-        (after + SPLIT // 2) // SPLIT,
-        (after + SPLIT // 2) % SPLIT * BLOCK - BODY,
-    )
-    return (own, following), (quarter < SPLIT - 1) & (band < devices - 1)
+    own = ((band + SPLIT // 2) // SPLIT, quarter * BLOCK - TAIL)
+    before = ((past + SPLIT // 2) // SPLIT, (past + SPLIT // 2) % SPLIT * BLOCK + BODY)
+    return (own, before), (quarter > 0) & (band > 0)
+
+
+def collect_kernel(images, patch, *refs):
+    count = (len(refs) - 3) // 2
+    small, head, copies_out, numbers, sems = (
+        refs[:count], refs[count], refs[count + 1 : 2 * count + 1], refs[-2], refs[-1]
+    )
+    copies = [
+        pltpu.make_async_copy(
+            images.at[v, pl.ds(BLOCK - GOT, GOT)], head.at[pl.ds(v * GOT, GOT)], sems.at[v]
+        )
+        for v in range(V)
+    ]
+    copies += [
+        pltpu.make_async_copy(a, b, sems.at[V + 1 + n])
+        for n, (a, b) in enumerate(zip(small, copies_out))
+    ]
+    names = pltpu.make_async_copy(patch, numbers, sems.at[V])
+    names.start()
+    for copy in copies:
+        copy.start()
+    head[V * GOT :] = jnp.zeros((8, WIDTH), F32)
+    names.wait()
+    head[V * GOT : V * GOT + 1, : V * BLKC] = numbers[...].astype(F32)
+    for copy in copies:
+        copy.wait()
+
+
+def collect(images, patch, small):
+    hbm = pl.BlockSpec(memory_space=pl.ANY)
+    vmem = pl.BlockSpec(memory_space=pltpu.VMEM)
+    return pl.pallas_call(
+        collect_kernel,
+        in_specs=[hbm] * (2 + len(small)),
+        out_specs=[vmem] * (1 + len(small)),
+        out_shape=[jax.ShapeDtypeStruct((V * GOT + 8, WIDTH), F32)]
+        + [jax.ShapeDtypeStruct(x.shape, x.dtype) for x in small],
+        scratch_shapes=[
+            pltpu.VMEM(patch.shape, jnp.int32),
+            pltpu.SemaphoreType.DMA((V + 1 + len(small),)),
+        ],
+        name="collect",
+    )(images, patch, *small)
 
 
 def lanczos_kernel(devices, affine, rows_out, cols_out):
@@ -149,7 +189,7 @@
     col = (from_lane * LANE_BLOCKS + block).astype(F32)
     within = (from_lane >= 0) & (from_lane < LANES) & (step <= WARP)
     offset = iota((8, LANES), 0) - WARP
-    crosses = (lane + offset >= BODY) != (lane >= BODY)
+    crosses = (lane + offset >= TAIL) != (lane >= TAIL)
     keep = (offset <= WARP) & (same | jnp.logical_not(crosses))
     for visit in range(V):
         shifts = []
@@ -162,7 +202,7 @@
             shifts.append(a[0, 0:1] + a[0, 1:2] * (row - (HEIGHT - 1) / 2.0) / HEIGHT)
             col_shift = a[1, 0:1] + a[1, 1:2] * (col - (WIDTH - 1) / 2.0) / WIDTH
             cols_out[n * V + visit] = jnp.where(within, lanczos(col_shift - step.astype(F32)), 0.0)
-        shift = jnp.where(lane < BODY, shifts[0], shifts[1])
+        shift = jnp.where(lane < TAIL, shifts[1], shifts[0])
         weights = jnp.where(keep, lanczos(shift - offset.astype(F32)), 0.0)
         rows_out[visit] = jnp.concatenate([weights, jnp.zeros((LANES - 8, LANES), F32)], axis=0).T
 
@@ -220,9 +260,9 @@
         weights = row_weights[visit]
         matrix = jnp.concatenate(
             [
-                staircase(weights[:ROWS] * units[visit], 0),
-                staircase(weights[ROWS:BODY] * units[visit], 0),
-                staircase(weights[BODY:] * units[V + visit], ROWS),
+                staircase(weights[:TAIL] * units[V + visit], 0),
+                staircase(weights[TAIL:ROWS] * units[visit], PAST_STRIPS * STRIP),
+                staircase(weights[ROWS:] * units[visit], 0),
             ],
             axis=0,
         )
@@ -247,12 +287,12 @@
 def prepare(taps, psf, affine, devices):
     row_weights, col_weights = small_kernel(
         functools.partial(lanczos_kernel, devices), "lanczos_weights",
-        [affine.transpose(0, 2, 3, 1)],
+        [affine],
         [((V, BLOCK, LANES), F32), ((2 * V, 8, WIDTH), F32)],
     )
     matrices = small_kernel(
         functools.partial(prepare_kernel, devices), "matrices",
-        [taps.transpose(1, 0, 2), psf.transpose(1, 3, 0, 2), row_weights],
+        [taps, psf, row_weights],
         [
             ((2 * V, TAPS * STRIP, LANES), F32),
             ((2 * V, TAPS * STRIP, LANES), F32),
@@ -336,17 +376,22 @@
             lines = jnp.where(lane == 2 * r + n, column, lines)
     label[...] = lines
 
+    open_row = FREE_FIRST * STRIP - GOT
+    seen = OPEN - STRIP
+    terms[:, :, seen:] = jnp.zeros((TOGETHER, 4, STRIP, WIDTH), BF16)
+
     def some_visits(turn, _):
         visits = [turn * TOGETHER + i for i in range(TOGETHER)]
         for i, visit in enumerate(visits):
-            for h, value in enumerate(sorted_rows(image[visit, RIM : RIM + SEEN], sort[...])):
-                terms[i, h] = value.astype(BF16)
-        for k in range(FIRST_STRIPS):
+            rows = sorted_rows(image[visit, open_row : open_row + seen], sort[...])
+            for h, value in enumerate(rows):
+                terms[i, h, :seen] = value.astype(BF16)
+        for k in range(FREE_FIRST, STRIPS):
+            first = (k - FREE_FIRST) * STRIP
             for i, visit in enumerate(visits):
-                at = slice(k * STRIP, (k + 1) * STRIP)
+                at = slice(first, first + STRIP)
                 matched_terms[visit, 0, at], matched_terms[visit, 1, at] = match_strip(
-                    high_level[visit], step_level[visit], slope[visit],
-                    terms.at[i], k * STRIP, k,
+                    high_level[visit], step_level[visit], slope[visit], terms.at[i], first, k
                 )
         return 0
 
@@ -355,53 +400,47 @@
 
 def warp_kernel(
     owner, places, label, high_level, step_level, slope, rows_high, rows_low, col_weights,
-    sort, unsort, image, below, matched_first, out,
-    terms, next_terms, matched_terms, next_matched, both_places, place_of, place_sem,
+    sort, unsort, image, above, matched_free, out,
+    own_terms, past_terms, own_matched, past_matched, both_places, place_of, place_sem,
 ):
     devices = label.shape[0]
     _, same = whereabouts(devices)
-    next_patch = below[V * (HEAD + RIM) : V * (HEAD + RIM) + 1, : V * BLKC].astype(jnp.int32)
-    to, rank = route(next_patch, owner[...])
+    past_patch = above[V * GOT : V * GOT + 1, : V * BLKC].astype(jnp.int32)
+    to, rank = route(past_patch, owner[...])
     both_places[0:1, : V * BLKC] = places[...]
     both_places[1:2, : V * BLKC] = to * CAP + rank
     place_copy = pltpu.make_async_copy(both_places, place_of, place_sem)
     place_copy.start()
     lane = iota((1, LANES), 1)
-    next_terms[:, :, STEP:] = jnp.zeros((TOGETHER, 4, STRIP, WIDTH), BF16)
     out[:, CAP * BLOCK :] = jnp.broadcast_to(
         label[...].reshape(devices, 1, LANES), (devices, LABEL, LANES)
     ).astype(BF16)
 
-    first_row = FIRST_STRIPS * STRIP
-    tall = BLOCK + 2 * RIM
-    seam = tall - STEP - first_row
-    seam_row = iota((STEP, 1), 0) < STEP - HEAD - RIM
+    seam = STRIP + STEP
+    foreign = iota((seam, 1), 0) < GOT
     both = jnp.where(same, 1.0, 0.0)
-    own_sees = jnp.where(seam_row, 1.0, both)
-    next_sees = jnp.where(seam_row, both, 1.0)
+    own_sees = jnp.where(foreign, both, 1.0)
+    past_sees = jnp.where(foreign, 1.0, both)
 
     def some_visits(turn, _):
         visits = [turn * TOGETHER + i for i in range(TOGETHER)]
         for i, visit in enumerate(visits):
-            head = pl.ds(pl.multiple_of(visit * (HEAD + RIM), 8), HEAD + RIM)
-            raw = jnp.concatenate([image[visit, RIM + first_row :], below[head]], axis=0)
+            tail = pl.ds(pl.multiple_of(visit * GOT, 8), GOT)
+            raw = jnp.concatenate([above[tail], image[visit, : seam - GOT]], axis=0)
             for h, value in enumerate(sorted_rows(raw, sort[...])):
-                terms[i, h, :seam] = value[:seam].astype(BF16)
-                terms[i, h, seam:] = (value[seam:] * own_sees).astype(BF16)
-                next_terms[i, h, :STEP] = (value[seam:] * next_sees).astype(BF16)
-        for k in range(FIRST_STRIPS, OWN_STRIPS):
-            for i, visit in enumerate(visits):
-                first = k * STRIP - first_row
-                at = slice(first, first + STRIP)
-                matched_terms[i, 0, at], matched_terms[i, 1, at] = match_strip(
-                    high_level[visit], step_level[visit], slope[visit], terms.at[i], first, k
-                )
-        for k in range(NEXT_STRIPS):
+                own_terms[i, h] = (value * own_sees).astype(BF16)
+                past_terms[i, h] = (value * past_sees).astype(BF16)
+        for i, visit in enumerate(visits):
+            own_matched[i, 0], own_matched[i, 1] = match_strip(
+                high_level[visit], step_level[visit], slope[visit],
+                own_terms.at[i], OWN_FIRST * STRIP, OWN_FIRST,
+            )
+        for k in range(PAST_STRIPS):
             for i, visit in enumerate(visits):
                 at = slice(k * STRIP, (k + 1) * STRIP)
-                next_matched[i, 0, at], next_matched[i, 1, at] = match_strip(
+                past_matched[i, 0, at], past_matched[i, 1, at] = match_strip(
                     high_level[V + visit], step_level[V + visit], slope[V + visit],
-                    next_terms.at[i], k * STRIP, STRIPS - NEXT_STRIPS + k,
+                    past_terms.at[i], k * STRIP, k,
                 )
 
         warped = []
@@ -410,16 +449,17 @@
             for h in range(HALVES):
                 at = slice(h * ROWS, (h + 1) * ROWS)
                 high, low = rows_high[visit, at], rows_low[visit, at]
+                free = FREE_FIRST * STRIP
 
                 def under(term):
                     if h == 0:
-                        parts = [matched_first[visit, term, :WINDOW]]
+                        parts = [
+                            past_matched[i, term],
+                            own_matched[i, term],
+                            matched_free[visit, term, : WINDOW - free],
+                        ]
                     else:
-                        parts = [
-                            matched_first[visit, term, ROWS:],
-                            matched_terms[i, term],
-                            next_matched[i, term],
-                        ]
+                        parts = [matched_free[visit, term, ROWS - free :]]
                     left = LANES - sum([x.shape[0] for x in parts])
                     return jnp.concatenate(parts + [jnp.zeros((left, WIDTH), BF16)], axis=0)
 
@@ -439,8 +479,8 @@
         for i, visit in enumerate(visits):
             parts = []
             for rows, weights in (
-                (slice(0, BODY), col_weights[visit]),
-                (slice(BODY, BLOCK), col_weights[V + visit]),
+                (slice(0, TAIL), col_weights[V + visit]),
+                (slice(TAIL, BLOCK), col_weights[visit]),
             ):
                 some = warped[i][rows]
                 blocks = lane_sum(
@@ -454,17 +494,17 @@
             for j in range(BLKC):
                 piece = lane_block(result, j)
                 to = place_of[0, visit * BLKC + j]
-                rows = pl.ds(pl.multiple_of(to % CAP * BODY, HEAD), BODY)
-                out[to // CAP, rows] = piece[:BODY]
+                rows = pl.ds(pl.multiple_of(to % CAP * BODY, TAIL), BODY)
+                out[to // CAP, rows] = piece[TAIL:]
                 to = place_of[1, visit * BLKC + j]
-                rows = pl.ds(pl.multiple_of(CAP * BODY + to % CAP * HEAD, HEAD), HEAD)
-                out[to // CAP, rows] = piece[BODY:]
+                rows = pl.ds(pl.multiple_of(CAP * BODY + to % CAP * TAIL, TAIL), TAIL)
+                out[to // CAP, rows] = piece[:TAIL]
         return 0
 
     lax.fori_loop(0, V // TOGETHER, some_visits, 0)
 
 
-def warp(patch, slot, owner, weight, ready, images, below, devices):
+def warp(patch, slot, owner, weight, ready, images, above, devices):
     vmem = pl.BlockSpec(memory_space=pltpu.VMEM)
     order = deinterleave()
     sort, unsort = jnp.asarray(order, BF16), jnp.asarray(order.T, BF16)
@@ -478,14 +518,14 @@
         out_shape=[
             jax.ShapeDtypeStruct((1, V * BLKC), jnp.int32),
             jax.ShapeDtypeStruct((devices, LANES), F32),
-            jax.ShapeDtypeStruct((V, 2, FIRST_STRIPS * STRIP, WIDTH), BF16),
+            jax.ShapeDtypeStruct((V, 2, (STRIPS - FREE_FIRST) * STRIP, WIDTH), BF16),
         ],
         scratch_shapes=[
-            pltpu.VMEM((TOGETHER, 4, SEEN, WIDTH), BF16),
+            pltpu.VMEM((TOGETHER, 4, OPEN, WIDTH), BF16),
         ],
         compiler_params=pltpu.CompilerParams(vmem_limit_bytes=32 << 20),
         cost_estimate=pl.CostEstimate(
-            flops=V * 2 * FIRST_STRIPS * TAPS * STRIP * BAND * WIDTH,
+            flops=V * 2 * (STRIPS - FREE_FIRST) * TAPS * STRIP * BAND * WIDTH,
             bytes_accessed=V * (BLOCK * WIDTH * 6),
             transcendentals=0,
         ),
@@ -493,17 +533,17 @@
     )(*args)
     args = [
         owner, places, label, *matrices, rows_high, rows_low, col_weights,
-        sort, unsort, images, below, matched,
+        sort, unsort, images, above, matched,
     ]
     return pl.pallas_call(
         warp_kernel,
         in_specs=[vmem] * len(args),
         out_specs=vmem,
         scratch_shapes=[
-            pltpu.VMEM((TOGETHER, 4, BLOCK + 2 * RIM - FIRST_STRIPS * STRIP, WIDTH), BF16),
-            pltpu.VMEM((TOGETHER, 4, STEP + STRIP, WIDTH), BF16),
-            pltpu.VMEM((TOGETHER, 2, (OWN_STRIPS - FIRST_STRIPS) * STRIP, WIDTH), BF16),
-            pltpu.VMEM((TOGETHER, 2, NEXT_STRIPS * STRIP, WIDTH), BF16),
+            pltpu.VMEM((TOGETHER, 4, STRIP + STEP, WIDTH), BF16),
+            pltpu.VMEM((TOGETHER, 4, STRIP + STEP, WIDTH), BF16),
+            pltpu.VMEM((TOGETHER, 2, STRIP, WIDTH), BF16),
+            pltpu.VMEM((TOGETHER, 2, PAST_STRIPS * STRIP, WIDTH), BF16),
             pltpu.VMEM((8, LANES), jnp.int32),
             pltpu.SMEM((8, LANES), jnp.int32),
             pltpu.SemaphoreType.DMA(()),
@@ -548,9 +588,9 @@
             taken[s, r] = jnp.broadcast_to(column[s : s + 1], (STRIP, LANES)).astype(BF16) > 0
 
     def tile(s, r, k):
-        device, first = s, r * BODY + k * STRIP - HEAD
-        if k == 0:
-            device, first = (s - 1) % devices, CAP * BODY + r * HEAD
+        device, first = s, r * BODY + k * STRIP
+        if first - r * BODY >= BODY:
+            device, first = (s + 1) % devices, CAP * BODY + r * TAIL
         return jnp.where(taken[s, r], got[device, first : first + STRIP], jnp.zeros((), BF16))
 
     copies = []
@@ -605,15 +645,14 @@
 ):
     devices = lax.axis_size("ccd")
     patch = block_patch[:, :, 0]
-    zero = jnp.zeros((), F32)
-    rows = V * (HEAD + RIM)
-    head = lax.pad(
-        images[:, : HEAD + RIM].reshape(rows, WIDTH), zero, ((0, 8, 0), (0, 0, 0))
-    ) + lax.pad(patch.astype(F32), zero, ((rows, 7, 0), (0, WIDTH - V * BLKC, 0)))
-    below = lax.ppermute(head, "ccd", [((i + 1) % devices, i) for i in range(devices)])
-    ready = prepare(basis_taps, psf_coef, affine, devices)
+    head, taps, psf, affine = collect(
+        images, patch,
+        [basis_taps.transpose(1, 0, 2), psf_coef.transpose(1, 3, 0, 2), affine.transpose(0, 2, 3, 1)],
+    )
+    above = lax.ppermute(head, "ccd", [(i, (i + 1) % devices) for i in range(devices)])
+    ready = prepare(taps, psf, affine, devices)
     sent = warp(
-        patch, block_slot, patch_owner, visit_weight, ready, images, below, devices
+        patch, block_slot, patch_owner, visit_weight, ready, images, above, devices
     )
     got = lax.all_to_all(sent, "ccd", split_axis=0, concat_axis=0, tiled=True)
     return coadd(got)

time: 50.1 us -> 48.7 us (0.972)
  starting transfers between devices: 5.5 us -> 0.5 us
  waiting for transfers between devices: 0.01 us -> 2.99 us
  Pallas kernels: 9.46 us -> 11.2 us
  local copies, waits for them, and re-layouts: 1.89 us -> 0.95 us
  other arithmetic: 0.67 us -> 0 us
    ppermute x1, starting transfers between devices: 5.5 us -> 0.5 us  [shards(): lax.ppermute(head, 'ccd', [(i, (i + 1) % devices) for i in range(devices)])]
    ppermute x1, waiting for transfers between devices: 0.01 us -> 2.99 us  [shards(): lax.ppermute(head, 'ccd', [(i, (i + 1) % devices) for i in range(devices)])]
    pallas_call x0 -> x1, Pallas kernels: none -> 1.65 us  [collect(): pl.pallas_call(collect_kernel, in_specs=[hbm] * (2 + len(small)), out_spe...]
    slice x1 -> x0, local copies, waits for them, and re-layouts: 0.94 us -> none  [shards(): images[:, :HEAD + RIM].reshape(rows, WIDTH)]
    convert_element_type x1 -> x0, other arithmetic: 0.66 us -> none  [shards(): patch.astype(F32)]
  transfers between devices with their start and end apart: 1 -> 1, of which waited for: 0 -> 1; matrix products, arithmetic and copies ran while one was open for 0% -> 0% of each run, Pallas kernels for 9% -> 10%
where the time goes in v16:
time: 48.7 us; the launch traced here: 48.3 us
  blocking collectives  32.6 us (67%)
  Pallas kernels  11.2 us (23%)
  waiting for transfers between devices  2.99 us (6%)
  local copies, waits for them, and re-layouts  0.95 us (2%)
  starting transfers between devices  0.5 us (1%)
    all_to_all x1, blocking collectives, shards(): got = lax.all_to_all(sent, 'ccd', split_axis=0, concat_axis=0, tiled=True)  32.6 us
    pallas_call x1, Pallas kernels, warp(): pl.pallas_call(warp_kernel, in_specs=[vmem] * len(args), out_specs=vmem,...  3.19 us
    ppermute x1, waiting for transfers between devices, shards(): lax.ppermute(head, 'ccd', [(i, (i + 1) % devices) for i in range(devices)])  2.99 us
    pallas_call x1, Pallas kernels, warp(): pl.pallas_call(match_kernel, in_specs=[vmem] * len(args), out_specs=[vmem...  2.79 us
    pallas_call x2, Pallas kernels, small_kernel(): pl.pallas_call(body, in_specs=[vmem] * len(args), out_specs=[vmem] * len(...  1.9 us
    pallas_call x1, Pallas kernels, coadd(): pl.pallas_call(coadd_kernel, in_specs=[pl.BlockSpec(memory_space=pltpu.VM...  1.67 us
    pallas_call x1, Pallas kernels, collect(): pl.pallas_call(collect_kernel, in_specs=[hbm] * (2 + len(small)), out_spe...  1.65 us
  transfers between devices with their start and end apart: 1, of which 1 were waited for; matrix products, arithmetic and copies ran while one was open for 0% of the time, Pallas kernels for 10%

profile of v16, /device:TPU:0, one launch (start us, length us, event | category | flops | bytes accessed | tf_op | source)
XLA Modules:
  0.0 48.3 jit_solution(10547571402589511813)
XLA Ops:
  0.0 1.6 %collect.1 = (f32[104,512]{1,0:T(8,128)}, f32[9,2,11]{2,1,0:T(2,128)}, f32[5,3,4,9]{3,2,1,0:T(4,128)}, f32[4,2,2,5]{3,2,1,0:T(2,128)}) custom-call(f32[4,128,512]{2,1,0:T(8,128)} %image.3, s32[1,16]{1,0:T(1,128)} %bitcast.5, f32[9,2,11]{2,1,0:T(2,128)} %bitcast.10, f32[5,3,4,9]{3,2,1,0:T(4,128)} %bitcast.9, f32[4,2,2,5]{3,2,1,0:T(2,128)} %bitcast.11), custom_call_target="tpu_custom_call" | custom-call | tf_op jit(solution)/shard_map/collect/pallas_call | solution.py:167
  1.7 0.5 %collective-permute-start = (f32[104,512]{1,0:T(8,128)}, f32[104,512]{1,0:T(8,128)S(1)}, u32[]{:S(2)}, u32[]{:S(2)}) collective-permute-start(f32[104,512]{1,0:T(8,128)} %get-tuple-element.31), channel_id=1, source_target_pairs={{0,1},{1,2},{2,3},{3,4},{4,5},{5,6},{6,7},{7,8},{8,9},{9,10},{10,1... | collective-permute-start | bytes 638984 | tf_op jit(solution)/shard_map/ppermute | solution.py:652
  2.2 0.0 copy-start.7
  2.2 0.7 %copy-done.7 = f32[4,2,2,5]{3,2,1,0:T(2,128)S(1)} copy-done((f32[4,2,2,5]{3,2,1,0:T(2,128)S(1)}, f32[4,2,2,5]{3,2,1,0:T(2,128)}, u32[]{:S(2)}) %copy-start.7) | copy-done | bytes 344
  2.9 0.0 copy-start.5
  2.9 0.0 copy-start.6
  2.9 0.5 %lanczos_weights.1 = (f32[4,128,128]{2,1,0:T(8,128)S(1)}, f32[8,8,512]{2,1,0:T(8,128)S(1)}) custom-call(f32[4,2,2,5]{3,2,1,0:T(2,128)S(1)} %copy-done.7), custom_call_target="tpu_custom_call" | custom-call | flops 1073741824 | bytes 1048576 | tf_op jit(solution)/shard_map/lanczos_weights/pallas_call | solution.py:276
  3.4 0.2 copy-done.5
  3.6 0.0 copy-done.6
  3.6 0.0 copy-start
  3.6 0.0 copy-start.1
  3.6 0.0 copy-start.3
  3.6 0.0 copy-start.4
  3.6 0.0 copy-start.8
  3.6 0.0 copy-start.9
  3.7 1.4 %matrices.1 = (f32[8,176,128]{2,1,0:T(8,128)S(1)}, f32[8,176,128]{2,1,0:T(8,128)S(1)}, bf16[8,176,128]{2,1,0:T(8,128)(2,1)S(1)}, bf16[4,128,128]{2,1,0:T(8,128)(2,1)S(1)}, bf16[4,128,128]{2,1,0:T(8,128)(2,1)S(1)}) custom-call(f32[9,2,11]{2,1,0:T(2,128)S(1)} %copy-done.6, f32[5,3,4,9]{3,2,1,0:T(4,128)S(1)} %copy-done.5, ...), custom_call_target="tpu_custom_call" | custom-call | flops 1073741824 | bytes 1048576 | tf_op jit(solution)/shard_map/matrices/pallas_call | solution.py:276
  5.0 0.0 copy-done
  5.0 0.0 copy-done.1
  5.0 0.0 copy-done.3
  5.1 0.0 copy-done.4
  5.1 0.0 copy-done.8
  5.1 0.0 copy-done.9
  5.1 0.0 copy-start.2
  5.1 2.8 %match.1 = (s32[1,16]{1,0:T(1,128)S(1)}, f32[16,128]{1,0:T(8,128)S(1)}, bf16[4,2,112,512]{3,2,1,0:T(8,128)(2,1)S(1)}) custom-call(s32[1,16]{1,0:T(1,128)S(1)} %bitcast.6, s32[1,16]{1,0:T(1,128)S(1)} %copy-done.9, s32[1,16]{1,0:T(1,128)S(1)} %bitcast.7, bf16[4,5]{1,0:T(4,128)(2,1)S(1)} %copy-done.8, f32[8,176,128]{2,1,0:T(8,128)S(1)} %get-tuple-element.23.high_level, ...), custom_call_target="tpu_custom_call" | custom-call | flops 1291845632 | bytes 1572864 | tf_op jit(solution)/shard_map/match/pallas_call | solution.py:514
  7.9 3.0 %collective-permute-done.above = f32[104,512]{1,0:T(8,128)S(1)} collective-permute-done((f32[104,512]{1,0:T(8,128)}, f32[104,512]{1,0:T(8,128)S(1)}, u32[]{:S(2)}, u32[]{:S(2)}) %collective-permute-start) | collective-permute-done | bytes 213024 | tf_op jit(solution)/shard_map/ppermute | solution.py:652
  10.9 0.0 copy-done.2
  10.9 3.2 %warp.1 = bf16[16,272,128]{2,1,0:T(8,128)(2,1)S(1)} custom-call(s32[1,16]{1,0:T(1,128)S(1)} %bitcast.8, s32[1,16]{1,0:T(1,128)S(1)} %get-tuple-element.26.places, f32[16,128]{1,0:T(8,128)S(1)} %get-tuple-element.27.label, f32[8,176,128]{2,1,0:T(8,128)S(1)} %get-tuple-element.23.high_level, f32[8,176,128]{2,1,0:T(8,128)S(1)} %get-tuple-element.24.step_level, ...), custom_call_target="tpu_custom_call" | custom-call | flops 1660944384 | bytes 1572864 | tf_op jit(solution)/shard_map/warp/pallas_call | solution.py:538
  14.1 32.6 %all_to_all.5.got = bf16[16,272,128]{2,1,0:T(8,128)(2,1)S(1)} all-to-all(bf16[16,272,128]{2,1,0:T(8,128)(2,1)S(1)} %warp.1), channel_id=1, replica_groups=mesh['group'=2,'ccd'=16] {'ccd'}, dimensions={0} | all-to-all | bytes 2228224 | tf_op jit(solution)/shard_map/all_to_all | solution.py:657
  46.7 1.7 %coadd.1 = f32[1,512,512]{2,1,0:T(8,128)} custom-call(bf16[16,272,128]{2,1,0:T(8,128)(2,1)S(1)} %all_to_all.5.got), custom_call_target="tpu_custom_call" | custom-call | tf_op jit(solution)/shard_map/coadd/pallas_call | solution.py:629
Async XLA Ops:
  1.7 9.2 %collective-permute-start = (f32[104,512]{1,0:T(8,128)}, f32[104,512]{1,0:T(8,128)S(1)}, u32[]{:S(2)}, u32[]{:S(2)}) collective-permute-start(f32[104,512]{1,0:T(8,128)} %get-tuple-element.31), channel_id=1, source_target_pairs={{0,1},{1,2},{2,3},{3,4},{4,5},{5,6},{6,7},{7,8},{8,9},{9,10},{10,1... | collective-permute-start | bytes 638984 | tf_op jit(solution)/shard_map/ppermute | solution.py:652
  2.2 0.7 %copy-start.7 = (f32[4,2,2,5]{3,2,1,0:T(2,128)S(1)}, f32[4,2,2,5]{3,2,1,0:T(2,128)}, u32[]{:S(2)}) copy-start(f32[4,2,2,5]{3,2,1,0:T(2,128)} %get-tuple-element.21.affine) | copy-start | bytes 964
  2.9 0.8 %copy-start.5 = (f32[5,3,4,9]{3,2,1,0:T(4,128)S(1)}, f32[5,3,4,9]{3,2,1,0:T(4,128)}, u32[]{:S(2)}) copy-start(f32[5,3,4,9]{3,2,1,0:T(4,128)} %get-tuple-element.20.psf) | copy-start | bytes 6484
  2.9 0.8 %copy-start.6 = (f32[9,2,11]{2,1,0:T(2,128)S(1)}, f32[9,2,11]{2,1,0:T(2,128)}, u32[]{:S(2)}) copy-start(f32[9,2,11]{2,1,0:T(2,128)} %get-tuple-element.19.taps) | copy-start | bytes 2380
  3.6 1.4 %copy-start = (f32[4,128,512]{2,1,0:T(8,128)S(1)}, f32[4,128,512]{2,1,0:T(8,128)}, u32[]{:S(2)}) copy-start(f32[4,128,512]{2,1,0:T(8,128)} %image.3) | copy-start | bytes 3145732
  3.6 1.4 %copy-start.1 = (bf16[512,512]{1,0:T(8,128)(2,1)S(1)}, bf16[512,512]{1,0:T(8,128)(2,1)}, u32[]{:S(2)}) copy-start(bf16[512,512]{1,0:T(8,128)(2,1)} %constant.4.clone.sort) | copy-start | bytes 1572868
  3.6 1.4 %copy-start.3 = (s32[1,16,1]{1,2,0:T(1,128)S(1)}, s32[1,16,1]{1,2,0:T(1,128)}, u32[]{:S(2)}) copy-start(s32[1,16,1]{1,2,0:T(1,128)} %param.15) | copy-start | bytes 196
  3.6 1.4 %copy-start.4 = (s32[16]{0:T(128)S(1)}, s32[16]{0:T(128)}, u32[]{:S(2)}) copy-start(s32[16]{0:T(128)} %param.17) | copy-start | bytes 196
  3.6 1.4 %copy-start.8 = (bf16[4,5]{1,0:T(4,128)(2,1)S(1)}, bf16[4,5]{1,0:T(4,128)(2,1)}, u32[]{:S(2)}) copy-start(bf16[4,5]{1,0:T(4,128)(2,1)} %weight.1) | copy-start | bytes 124
  3.6 1.4 %copy-start.9 = (s32[1,16]{1,0:T(1,128)S(1)}, s32[1,16]{1,0:T(1,128)}, u32[]{:S(2)}) copy-start(s32[1,16]{1,0:T(1,128)} %slot.1) | copy-start | bytes 196
  5.1 5.8 %copy-start.2 = (bf16[512,512]{1,0:T(8,128)(2,1)S(1)}, bf16[512,512]{1,0:T(8,128)(2,1)}, u32[]{:S(2)}) copy-start(bf16[512,512]{1,0:T(8,128)(2,1)} %constant.5.clone.unsort) | copy-start | bytes 1572868

commit v17 on v16

--- a/solution.py
+++ b/solution.py
@@ -3,7 +3,6 @@
 
 import jax
 import jax.numpy as jnp
-import numpy as np
 from jax import lax
 from jax.experimental import pallas as pl
 from jax.experimental.pallas import tpu as pltpu
@@ -37,7 +36,8 @@
 OWN_FIRST = 1
 FREE_FIRST = 2
 HALVES = 2
-TOGETHER = 2
+MATCHED = 4
+WARPED = 1
 ROWS = BLOCK // HALVES
 WINDOW = ROWS + STRIP
 BODY = BLOCK - TAIL
@@ -74,13 +74,21 @@
     return lax.broadcasted_iota(jnp.int32, shape, dim)
 
 
-def deinterleave():
-    order = np.arange(WIDTH).reshape(LANES, LANE_BLOCKS).T.reshape(-1)
-    return (np.arange(WIDTH)[:, None] == order[None, :]).astype(np.float32)
-
-
 def column_at(lane):
     return lane % LANES * LANE_BLOCKS + lane // LANES
+
+
+def order_kernel(sort, unsort):
+    square = (WIDTH, WIDTH)
+    one, none = jnp.ones((), F32), jnp.zeros((), F32)
+    goes = iota(square, 0) == column_at(iota((1, WIDTH), 1))
+    sort[...] = jnp.where(goes, one, none).astype(BF16)
+    comes = iota(square, 1) == column_at(iota((WIDTH, 1), 0))
+    unsort[...] = jnp.where(comes, one, none).astype(BF16)
+
+
+def orders():
+    return small_kernel(order_kernel, "orders", [], [((WIDTH, WIDTH), BF16)] * 2)
 
 
 def lane_block(x, v):
@@ -135,50 +143,43 @@
     return (own, before), (quarter > 0) & (band > 0)
 
 
-def collect_kernel(images, patch, *refs):
-    count = (len(refs) - 3) // 2
-    small, head, copies_out, numbers, sems = (
-        refs[:count], refs[count], refs[count + 1 : 2 * count + 1], refs[-2], refs[-1]
-    )
+def collect_kernel(images, patch, head, numbers, line, sems):
     copies = [
         pltpu.make_async_copy(
             images.at[v, pl.ds(BLOCK - GOT, GOT)], head.at[pl.ds(v * GOT, GOT)], sems.at[v]
         )
         for v in range(V)
     ]
-    copies += [
-        pltpu.make_async_copy(a, b, sems.at[V + 1 + n])
-        for n, (a, b) in enumerate(zip(small, copies_out))
-    ]
     names = pltpu.make_async_copy(patch, numbers, sems.at[V])
     names.start()
     for copy in copies:
         copy.start()
-    head[V * GOT :] = jnp.zeros((8, WIDTH), F32)
+    line[...] = jnp.zeros_like(line)
     names.wait()
-    head[V * GOT : V * GOT + 1, : V * BLKC] = numbers[...].astype(F32)
-    for copy in copies:
+    line[0:1, : V * BLKC] = numbers[...].astype(F32)
+    last = pltpu.make_async_copy(line, head.at[pl.ds(V * GOT, 8)], sems.at[V + 1])
+    last.start()
+    for copy in copies + [last]:
         copy.wait()
 
 
-def collect(images, patch, small):
+def collect(images, patch):
     hbm = pl.BlockSpec(memory_space=pl.ANY)
-    vmem = pl.BlockSpec(memory_space=pltpu.VMEM)
     return pl.pallas_call(
         collect_kernel,
-        in_specs=[hbm] * (2 + len(small)),
-        out_specs=[vmem] * (1 + len(small)),
-        out_shape=[jax.ShapeDtypeStruct((V * GOT + 8, WIDTH), F32)]
-        + [jax.ShapeDtypeStruct(x.shape, x.dtype) for x in small],
+        in_specs=[hbm] * 2,
+        out_specs=hbm,
+        out_shape=jax.ShapeDtypeStruct((V * GOT + 8, WIDTH), F32),
         scratch_shapes=[
             pltpu.VMEM(patch.shape, jnp.int32),
-            pltpu.SemaphoreType.DMA((V + 1 + len(small),)),
+            pltpu.VMEM((8, WIDTH), F32),
+            pltpu.SemaphoreType.DMA((V + 2,)),
         ],
         name="collect",
-    )(images, patch, *small)
-
-
-def lanczos_kernel(devices, affine, rows_out, cols_out):
+    )(images, patch)
+
+
+def lanczos_weights(devices, affine, cols_out):
     bands, same = whereabouts(devices)
     lane = iota((1, LANES), 1)
     lanes = iota((8, WIDTH), 1)
@@ -191,6 +192,7 @@
     offset = iota((8, LANES), 0) - WARP
     crosses = (lane + offset >= TAIL) != (lane >= TAIL)
     keep = (offset <= WARP) & (same | jnp.logical_not(crosses))
+    by_row = []
     for visit in range(V):
         shifts = []
         for n, (ccd, top_row) in enumerate(bands):
@@ -204,12 +206,14 @@
             cols_out[n * V + visit] = jnp.where(within, lanczos(col_shift - step.astype(F32)), 0.0)
         shift = jnp.where(lane < TAIL, shifts[1], shifts[0])
         weights = jnp.where(keep, lanczos(shift - offset.astype(F32)), 0.0)
-        rows_out[visit] = jnp.concatenate([weights, jnp.zeros((LANES - 8, LANES), F32)], axis=0).T
+        by_row.append(jnp.concatenate([weights, jnp.zeros((LANES - 8, LANES), F32)], axis=0).T)
+    return by_row
 
 
 def prepare_kernel(
-    devices, taps, psf, row_weights, high_level, step_level, slope, rows_high, rows_low
+    devices, taps, psf, affine, high_level, step_level, slope, rows_high, rows_low, cols_out
 ):
+    row_weights = lanczos_weights(devices, affine, cols_out)
     bands, _ = whereabouts(devices)
     band_lane = iota((1, BAND), 1)
     seg = band_lane // STEP
@@ -245,12 +249,12 @@
         row_part = iota((STRIP, 1), 0).astype(F32) * (1.0 / STRIP)
         for u in range(TAPS):
             at = slice(u * STRIP, (u + 1) * STRIP)
-            x = staircase(jnp.broadcast_to(const[u : u + 1], (STRIP, BAND)), 0)
+            one = jnp.broadcast_to(const[u : u + 1], (STRIP, BAND))
+            x, tail = staircase(one[:, :LANES], 0), staircase(one[:, LANES:], 0)
             y = staircase(jnp.broadcast_to(by_row[u : u + 1, :LANES], (STRIP, LANES)), 0)
-            tail = x[:, LANES:]
             high = tail.astype(BF16).astype(F32)
             slope[n * V + visit, at] = jnp.where(low_band[:, LANES:], tail - high, high).astype(BF16)
-            x = x[:, :LANES] + row_part * y
+            x = x + row_part * y
             high = jnp.where(lane < 3 * STEP, jnp.round(x), x.astype(BF16).astype(F32))
             high_level[n * V + visit, at] = jnp.where(low_lanes, x - high, high)
             high = jnp.round(y)
@@ -285,23 +289,17 @@
 
 
 def prepare(taps, psf, affine, devices):
-    row_weights, col_weights = small_kernel(
-        functools.partial(lanczos_kernel, devices), "lanczos_weights",
-        [affine],
-        [((V, BLOCK, LANES), F32), ((2 * V, 8, WIDTH), F32)],
-    )
-    matrices = small_kernel(
-        functools.partial(prepare_kernel, devices), "matrices",
-        [taps, psf, row_weights],
+    return small_kernel(
+        functools.partial(prepare_kernel, devices), "matrices", [taps, psf, affine],
         [
             ((2 * V, TAPS * STRIP, LANES), F32),
             ((2 * V, TAPS * STRIP, LANES), F32),
             ((2 * V, TAPS * STRIP, BAND - LANES), BF16),
             ((V, BLOCK, LANES), BF16),
             ((V, BLOCK, LANES), BF16),
+            ((2 * V, 8, WIDTH), F32),
         ],
     )
-    return [*matrices, col_weights]
 
 
 def sorted_rows(raw, sort):
@@ -378,10 +376,10 @@
 
     open_row = FREE_FIRST * STRIP - GOT
     seen = OPEN - STRIP
-    terms[:, :, seen:] = jnp.zeros((TOGETHER, 4, STRIP, WIDTH), BF16)
+    terms[:, :, seen:] = jnp.zeros((MATCHED, 4, STRIP, WIDTH), BF16)
 
     def some_visits(turn, _):
-        visits = [turn * TOGETHER + i for i in range(TOGETHER)]
+        visits = [turn * MATCHED + i for i in range(MATCHED)]
         for i, visit in enumerate(visits):
             rows = sorted_rows(image[visit, open_row : open_row + seen], sort[...])
             for h, value in enumerate(rows):
@@ -395,7 +393,7 @@
                 )
         return 0
 
-    lax.fori_loop(0, V // TOGETHER, some_visits, 0)
+    lax.fori_loop(0, V // MATCHED, some_visits, 0)
 
 
 def warp_kernel(
@@ -423,7 +421,7 @@
     past_sees = jnp.where(foreign, 1.0, both)
 
     def some_visits(turn, _):
-        visits = [turn * TOGETHER + i for i in range(TOGETHER)]
+        visits = [turn * WARPED + i for i in range(WARPED)]
         for i, visit in enumerate(visits):
             tail = pl.ds(pl.multiple_of(visit * GOT, 8), GOT)
             raw = jnp.concatenate([above[tail], image[visit, : seam - GOT]], axis=0)
@@ -501,13 +499,12 @@
                 out[to // CAP, rows] = piece[:TAIL]
         return 0
 
-    lax.fori_loop(0, V // TOGETHER, some_visits, 0)
-
-
-def warp(patch, slot, owner, weight, ready, images, above, devices):
+    lax.fori_loop(0, V // WARPED, some_visits, 0)
+
+
+def warp(patch, slot, owner, weight, ready, order, images, above, devices):
     vmem = pl.BlockSpec(memory_space=pltpu.VMEM)
-    order = deinterleave()
-    sort, unsort = jnp.asarray(order, BF16), jnp.asarray(order.T, BF16)
+    sort, unsort = order
     *matrices, rows_high, rows_low, col_weights = ready
     owner = owner.reshape(1, -1)
     args = [patch, slot, owner, weight, *matrices, sort, images]
@@ -521,7 +518,7 @@
             jax.ShapeDtypeStruct((V, 2, (STRIPS - FREE_FIRST) * STRIP, WIDTH), BF16),
         ],
         scratch_shapes=[
-            pltpu.VMEM((TOGETHER, 4, OPEN, WIDTH), BF16),
+            pltpu.VMEM((MATCHED, 4, OPEN, WIDTH), BF16),
         ],
         compiler_params=pltpu.CompilerParams(vmem_limit_bytes=32 << 20),
         cost_estimate=pl.CostEstimate(
@@ -540,10 +537,10 @@
         in_specs=[vmem] * len(args),
         out_specs=vmem,
         scratch_shapes=[
-            pltpu.VMEM((TOGETHER, 4, STRIP + STEP, WIDTH), BF16),
-            pltpu.VMEM((TOGETHER, 4, STRIP + STEP, WIDTH), BF16),
-            pltpu.VMEM((TOGETHER, 2, STRIP, WIDTH), BF16),
-            pltpu.VMEM((TOGETHER, 2, PAST_STRIPS * STRIP, WIDTH), BF16),
+            pltpu.VMEM((WARPED, 4, STRIP + STEP, WIDTH), BF16),
+            pltpu.VMEM((WARPED, 4, STRIP + STEP, WIDTH), BF16),
+            pltpu.VMEM((WARPED, 2, STRIP, WIDTH), BF16),
+            pltpu.VMEM((WARPED, 2, PAST_STRIPS * STRIP, WIDTH), BF16),
             pltpu.VMEM((8, LANES), jnp.int32),
             pltpu.SMEM((8, LANES), jnp.int32),
             pltpu.SemaphoreType.DMA(()),
@@ -645,14 +642,15 @@
 ):
     devices = lax.axis_size("ccd")
     patch = block_patch[:, :, 0]
-    head, taps, psf, affine = collect(
-        images, patch,
-        [basis_taps.transpose(1, 0, 2), psf_coef.transpose(1, 3, 0, 2), affine.transpose(0, 2, 3, 1)],
-    )
+    head = collect(images, patch)
     above = lax.ppermute(head, "ccd", [(i, (i + 1) % devices) for i in range(devices)])
-    ready = prepare(taps, psf, affine, devices)
+    order = orders()
+    ready = prepare(
+        basis_taps.transpose(1, 0, 2), psf_coef.transpose(1, 3, 0, 2), affine.transpose(0, 2, 3, 1),
+        devices,
+    )
     sent = warp(
-        patch, block_slot, patch_owner, visit_weight, ready, images, above, devices
+        patch, block_slot, patch_owner, visit_weight, ready, order, images, above, devices
     )
     got = lax.all_to_all(sent, "ccd", split_axis=0, concat_axis=0, tiled=True)
     return coadd(got)

time: 48.7 us -> 55.1 us (1.13)
  Pallas kernels: 11.2 us -> 17.9 us
  waiting for transfers between devices: 2.99 us -> 4.26 us
  local copies, waits for them, and re-layouts: 0.95 us -> 0.05 us
  blocking collectives: 32.6 us -> 32 us
    pallas_call x1, Pallas kernels: 1.65 us -> 7.11 us  [collect(): pl.pallas_call(collect_kernel, in_specs=[hbm] * 2, out_specs=hbm, out_sha...]
    pallas_call x1, Pallas kernels: 3.19 us -> 4.81 us  [warp(): pl.pallas_call(warp_kernel, in_specs=[vmem] * len(args), out_specs=vmem,...]
    ppermute x1, waiting for transfers between devices: 2.99 us -> 4.26 us  [shards(): lax.ppermute(head, 'ccd', [(i, (i + 1) % devices) for i in range(devices)])]
    unnamed x20 -> x16, local copies, waits for them, and re-layouts: 0.95 us -> 0.05 us
    pallas_call x1, Pallas kernels: 2.79 us -> 2.1 us  [warp(): pl.pallas_call(match_kernel, in_specs=[vmem] * len(args), out_specs=[vmem...]
    all_to_all x1, blocking collectives: 32.6 us -> 32 us  [shards(): got = lax.all_to_all(sent, 'ccd', split_axis=0, concat_axis=0, tiled=True)]
  transfers between devices with their start and end apart: 1 -> 1, of which waited for: 1 -> 1; matrix products, arithmetic and copies ran while one was open for 0% -> 0% of each run, Pallas kernels for 10% -> 8%
where the time goes in v17:
time: 55.1 us; the launch traced here: 54.9 us
  blocking collectives  32 us (58%)
  Pallas kernels  17.9 us (32%)
  waiting for transfers between devices  4.26 us (8%)
    all_to_all x1, blocking collectives, shards(): got = lax.all_to_all(sent, 'ccd', split_axis=0, concat_axis=0, tiled=True)  32 us
    pallas_call x1, Pallas kernels, collect(): pl.pallas_call(collect_kernel, in_specs=[hbm] * 2, out_specs=hbm, out_sha...  7.11 us
    pallas_call x1, Pallas kernels, warp(): pl.pallas_call(warp_kernel, in_specs=[vmem] * len(args), out_specs=vmem,...  4.81 us
    ppermute x1, waiting for transfers between devices, shards(): lax.ppermute(head, 'ccd', [(i, (i + 1) % devices) for i in range(devices)])  4.26 us
    pallas_call x2, Pallas kernels, small_kernel(): pl.pallas_call(body, in_specs=[vmem] * len(args), out_specs=[vmem] * len(...  2.22 us
    pallas_call x1, Pallas kernels, warp(): pl.pallas_call(match_kernel, in_specs=[vmem] * len(args), out_specs=[vmem...  2.1 us
    pallas_call x1, Pallas kernels, coadd(): pl.pallas_call(coadd_kernel, in_specs=[pl.BlockSpec(memory_space=pltpu.VM...  1.67 us
  transfers between devices with their start and end apart: 1, of which 1 were waited for; matrix products, arithmetic and copies ran while one was open for 0% of the time, Pallas kernels for 8%

profile of v17, /device:TPU:0, one launch (start us, length us, event | category | flops | bytes accessed | tf_op | source)
XLA Modules:
  0.0 54.9 jit_solution(15181842545166841001)
XLA Ops:
  0.0 7.1 %collect.1 = f32[104,512]{1,0:T(8,128)} custom-call(f32[4,128,512]{2,1,0:T(8,128)} %image.3, s32[1,16]{1,0:T(1,128)} %bitcast.5), custom_call_target="tpu_custom_call" | custom-call | tf_op jit(solution)/shard_map/collect/pallas_call | solution.py:168
  7.1 0.0 copy-start.3
  7.1 0.0 copy-start.4
  7.1 0.0 copy-start.5
  7.2 0.5 collective-permute-start
  7.7 0.2 orders.1
  7.9 0.0 copy-done.3
  7.9 0.0 copy-done.4
  7.9 0.0 copy-done.5
  7.9 0.0 copy-start
  7.9 0.0 copy-start.1
  7.9 0.0 copy-start.2
  8.0 0.0 copy-start.6
  8.0 0.0 copy-start.7
  8.0 2.0 %matrices.1 = (f32[8,176,128]{2,1,0:T(8,128)S(1)}, f32[8,176,128]{2,1,0:T(8,128)S(1)}, bf16[8,176,128]{2,1,0:T(8,128)(2,1)S(1)}, bf16[4,128,128]{2,1,0:T(8,128)(...) custom-call(f32[9,2,11]{2,1,0:T(2,128)S(1)} %bitcast.10, f32[5,3,4,9]{3,2,1,0:T(4,128)S(1)} %bitcast.9, ...), custom_call_target="tpu_custom_call" | custom-call | flops 1073741824 | bytes 1048576 | tf_op jit(solution)/shard_map/matrices/pallas_call | solution.py:280
  10.0 0.0 copy-done
  10.0 0.0 copy-done.1
  10.0 0.0 copy-done.2
  10.0 0.0 copy-done.6
  10.0 0.0 copy-done.7
  10.0 2.1 %match.1 = (s32[1,16]{1,0:T(1,128)S(1)}, f32[16,128]{1,0:T(8,128)S(1)}, bf16[4,2,112,512]{3,2,1,0:T(8,128)(2,1)S(1)}) custom-call(s32[1,16]{1,0:T(1,128)S(1)} %bitcast.6, s32[1,16]{1,0:T(1,128)S(1)} %copy-done.7, s32[1,16]{1,0:T(1,128)S(1)} %bitcast.7, bf16[4,5]{1,0:T(4,128)(2,1)S(1)} %copy-done.6, f32[8,176,128]{2,1,0:T(8,128)S(1)} %get-tuple-element.16.high_level, ...), custom_call_target="tpu_custom_call" | custom-call | flops 1291845632 | bytes 1572864 | tf_op jit(solution)/shard_map/match/pallas_call | solution.py:511
  12.1 4.3 %collective-permute-done.above = f32[104,512]{1,0:T(8,128)S(1)} collective-permute-done((f32[104,512]{1,0:T(8,128)}, f32[104,512]{1,0:T(8,128)S(1)}, u32[]{:S(2)}, u32[]{:S(2)}) %collective-permute-start) | collective-permute-done | bytes 213024 | tf_op jit(solution)/shard_map/ppermute | solution.py:646
  16.4 4.8 %warp.1 = bf16[16,272,128]{2,1,0:T(8,128)(2,1)S(1)} custom-call(s32[1,16]{1,0:T(1,128)S(1)} %bitcast.8, s32[1,16]{1,0:T(1,128)S(1)} %get-tuple-element.20.places, f32[16,128]{1,0:T(8,128)S(1)} %get-tuple-element.21.label, f32[8,176,128]{2,1,0:T(8,128)S(1)} %get-tuple-element.16.high_level, f32[8,176,128]{2,1,0:T(8,128)S(1)} %get-tuple-element.17.step_level, ...), custom_call_target="tpu_custom_call" | custom-call | flops 1660944384 | bytes 1572864 | tf_op jit(solution)/shard_map/warp/pallas_call | solution.py:535
  21.2 32.0 %all_to_all.5.got = bf16[16,272,128]{2,1,0:T(8,128)(2,1)S(1)} all-to-all(bf16[16,272,128]{2,1,0:T(8,128)(2,1)S(1)} %warp.1), channel_id=1, replica_groups=mesh['group'=2,'ccd'=16] {'ccd'}, dimensions={0} | all-to-all | bytes 2228224 | tf_op jit(solution)/shard_map/all_to_all | solution.py:655
  53.2 1.7 %coadd.1 = f32[1,512,512]{2,1,0:T(8,128)} custom-call(bf16[16,272,128]{2,1,0:T(8,128)(2,1)S(1)} %all_to_all.5.got), custom_call_target="tpu_custom_call" | custom-call | tf_op jit(solution)/shard_map/coadd/pallas_call | solution.py:626
Async XLA Ops:
  7.1 0.8 %copy-start.3 = (f32[4,5,9,3]{2,0,3,1:T(4,128)S(1)}, f32[4,5,9,3]{2,0,3,1:T(4,128)}, u32[]{:S(2)}) copy-start(f32[4,5,9,3]{2,0,3,1:T(4,128)} %param.10) | copy-start | bytes 6484
  7.1 0.8 %copy-start.4 = (f32[2,9,11]{2,0,1:T(2,128)S(1)}, f32[2,9,11]{2,0,1:T(2,128)}, u32[]{:S(2)}) copy-start(f32[2,9,11]{2,0,1:T(2,128)} %param.9) | copy-start | bytes 2380
  7.1 0.8 %copy-start.5 = (f32[4,5,2,2]{1,3,2,0:T(2,128)S(1)}, f32[4,5,2,2]{1,3,2,0:T(2,128)}, u32[]{:S(2)}) copy-start(f32[4,5,2,2]{1,3,2,0:T(2,128)} %param.11) | copy-start | bytes 964
  7.2 9.2 %collective-permute-start = (f32[104,512]{1,0:T(8,128)}, f32[104,512]{1,0:T(8,128)S(1)}, u32[]{:S(2)}, u32[]{:S(2)}) collective-permute-start(f32[104,512]{1,0:T(8,128)} %collect.1), channel_id=1, source_target_pairs={{0,1},{1,2},{2,3},{3,4},{4,5},{5,6},{6,7},{7,8},{8,9},{9,10},{10,1... | collective-permute-start | bytes 638984 | tf_op jit(solution)/shard_map/ppermute | solution.py:646
  7.9 2.1 %copy-start = (f32[4,128,512]{2,1,0:T(8,128)S(1)}, f32[4,128,512]{2,1,0:T(8,128)}, u32[]{:S(2)}) copy-start(f32[4,128,512]{2,1,0:T(8,128)} %image.3) | copy-start | bytes 3145732
  7.9 2.1 %copy-start.1 = (s32[1,16,1]{1,2,0:T(1,128)S(1)}, s32[1,16,1]{1,2,0:T(1,128)}, u32[]{:S(2)}) copy-start(s32[1,16,1]{1,2,0:T(1,128)} %param.13) | copy-start | bytes 196
  7.9 2.1 %copy-start.2 = (s32[16]{0:T(128)S(1)}, s32[16]{0:T(128)}, u32[]{:S(2)}) copy-start(s32[16]{0:T(128)} %param.15) | copy-start | bytes 196
  8.0 2.1 %copy-start.6 = (bf16[4,5]{1,0:T(4,128)(2,1)S(1)}, bf16[4,5]{1,0:T(4,128)(2,1)}, u32[]{:S(2)}) copy-start(bf16[4,5]{1,0:T(4,128)(2,1)} %weight.1) | copy-start | bytes 124
  8.0 2.1 %copy-start.7 = (s32[1,16]{1,0:T(1,128)S(1)}, s32[1,16]{1,0:T(1,128)}, u32[]{:S(2)}) copy-start(s32[1,16]{1,0:T(1,128)} %slot.1) | copy-start | bytes 196

commit v18 on v17

--- a/solution.py
+++ b/solution.py
@@ -37,7 +37,7 @@
 FREE_FIRST = 2
 HALVES = 2
 MATCHED = 4
-WARPED = 1
+WARPED = 4
 ROWS = BLOCK // HALVES
 WINDOW = ROWS + STRIP
 BODY = BLOCK - TAIL
@@ -143,7 +143,7 @@
     return (own, before), (quarter > 0) & (band > 0)
 
 
-def collect_kernel(images, patch, head, numbers, line, sems):
+def collect_kernel(images, patch, head, numbers, sems):
     copies = [
         pltpu.make_async_copy(
             images.at[v, pl.ds(BLOCK - GOT, GOT)], head.at[pl.ds(v * GOT, GOT)], sems.at[v]
@@ -154,27 +154,20 @@
     names.start()
     for copy in copies:
         copy.start()
-    line[...] = jnp.zeros_like(line)
+    head[V * GOT :] = jnp.zeros((8, WIDTH), F32)
     names.wait()
-    line[0:1, : V * BLKC] = numbers[...].astype(F32)
-    last = pltpu.make_async_copy(line, head.at[pl.ds(V * GOT, 8)], sems.at[V + 1])
-    last.start()
-    for copy in copies + [last]:
+    head[V * GOT : V * GOT + 1, : V * BLKC] = numbers[...].astype(F32)
+    for copy in copies:
         copy.wait()
 
 
 def collect(images, patch):
-    hbm = pl.BlockSpec(memory_space=pl.ANY)
     return pl.pallas_call(
         collect_kernel,
-        in_specs=[hbm] * 2,
-        out_specs=hbm,
+        in_specs=[pl.BlockSpec(memory_space=pl.ANY)] * 2,
+        out_specs=pl.BlockSpec(memory_space=pltpu.VMEM),
         out_shape=jax.ShapeDtypeStruct((V * GOT + 8, WIDTH), F32),
-        scratch_shapes=[
-            pltpu.VMEM(patch.shape, jnp.int32),
-            pltpu.VMEM((8, WIDTH), F32),
-            pltpu.SemaphoreType.DMA((V + 2,)),
-        ],
+        scratch_shapes=[pltpu.VMEM(patch.shape, jnp.int32), pltpu.SemaphoreType.DMA((V + 1,))],
         name="collect",
     )(images, patch)
 

time: 55.1 us -> 47.7 us (0.87)
  Pallas kernels: 17.9 us -> 10.4 us
    pallas_call x1, Pallas kernels: 7.11 us -> 1.61 us  [collect(): pl.pallas_call(collect_kernel, in_specs=[pl.BlockSpec(memory_space=pl.ANY...]
    pallas_call x1, Pallas kernels: 4.81 us -> 2.84 us  [warp(): pl.pallas_call(warp_kernel, in_specs=[vmem] * len(args), out_specs=vmem,...]
  transfers between devices with their start and end apart: 1 -> 1, of which waited for: 1 -> 1; matrix products, arithmetic and copies ran while one was open for 0% -> 0% of each run, Pallas kernels for 8% -> 9%
where the time goes in v18:
time: 47.7 us; the launch traced here: 47.4 us
  blocking collectives  32 us (67%)
  Pallas kernels  10.4 us (22%)
  waiting for transfers between devices  4.25 us (9%)
  starting transfers between devices  0.5 us (1%)
    all_to_all x1, blocking collectives, shards(): got = lax.all_to_all(sent, 'ccd', split_axis=0, concat_axis=0, tiled=True)  32 us
    ppermute x1, waiting for transfers between devices, shards(): lax.ppermute(head, 'ccd', [(i, (i + 1) % devices) for i in range(devices)])  4.25 us
    pallas_call x1, Pallas kernels, warp(): pl.pallas_call(warp_kernel, in_specs=[vmem] * len(args), out_specs=vmem,...  2.84 us
    pallas_call x2, Pallas kernels, small_kernel(): pl.pallas_call(body, in_specs=[vmem] * len(args), out_specs=[vmem] * len(...  2.22 us
    pallas_call x1, Pallas kernels, warp(): pl.pallas_call(match_kernel, in_specs=[vmem] * len(args), out_specs=[vmem...  2.1 us
    pallas_call x1, Pallas kernels, coadd(): pl.pallas_call(coadd_kernel, in_specs=[pl.BlockSpec(memory_space=pltpu.VM...  1.67 us
    pallas_call x1, Pallas kernels, collect(): pl.pallas_call(collect_kernel, in_specs=[pl.BlockSpec(memory_space=pl.ANY...  1.61 us
  transfers between devices with their start and end apart: 1, of which 1 were waited for; matrix products, arithmetic and copies ran while one was open for 0% of the time, Pallas kernels for 9%

profile of v18, /device:TPU:0, one launch (start us, length us, event | category | flops | bytes accessed | tf_op | source)
XLA Modules:
  0.0 47.4 jit_solution(13401980839231209394)
XLA Ops:
  0.0 1.6 %collect.1 = f32[104,512]{1,0:T(8,128)} custom-call(f32[4,128,512]{2,1,0:T(8,128)} %image.3, s32[1,16]{1,0:T(1,128)} %bitcast.5), custom_call_target="tpu_custom_call" | custom-call | tf_op jit(solution)/shard_map/collect/pallas_call | solution.py:165
  1.6 0.0 copy-start.3
  1.6 0.0 copy-start.4
  1.6 0.0 copy-start.5
  1.7 0.5 %collective-permute-start = (f32[104,512]{1,0:T(8,128)}, f32[104,512]{1,0:T(8,128)S(1)}, u32[]{:S(2)}, u32[]{:S(2)}) collective-permute-start(f32[104,512]{1,0:T(8,128)} %collect.1), channel_id=1, source_target_pairs={{0,1},{1,2},{2,3},{3,4},{4,5},{5,6},{6,7},{7,8},{8,9},{9,10},{10,1... | collective-permute-start | bytes 638984 | tf_op jit(solution)/shard_map/ppermute | solution.py:639
  2.2 0.2 orders.1
  2.4 0.0 copy-done.3
  2.4 0.0 copy-done.4
  2.4 0.0 copy-done.5
  2.4 0.0 copy-start
  2.4 0.0 copy-start.1
  2.4 0.0 copy-start.2
  2.5 0.0 copy-start.6
  2.5 0.0 copy-start.7
  2.5 2.0 %matrices.1 = (f32[8,176,128]{2,1,0:T(8,128)S(1)}, f32[8,176,128]{2,1,0:T(8,128)S(1)}, bf16[8,176,128]{2,1,0:T(8,128)(2,1)S(1)}, bf16[4,128,128]{2,1,0:T(8,128)(...) custom-call(f32[9,2,11]{2,1,0:T(2,128)S(1)} %bitcast.10, f32[5,3,4,9]{3,2,1,0:T(4,128)S(1)} %bitcast.9, ...), custom_call_target="tpu_custom_call" | custom-call | flops 1073741824 | bytes 1048576 | tf_op jit(solution)/shard_map/matrices/pallas_call | solution.py:273
  4.5 0.0 copy-done
  4.5 0.0 copy-done.1
  4.5 0.0 copy-done.2
  4.5 0.0 copy-done.6
  4.5 0.0 copy-done.7
  4.5 2.1 %match.1 = (s32[1,16]{1,0:T(1,128)S(1)}, f32[16,128]{1,0:T(8,128)S(1)}, bf16[4,2,112,512]{3,2,1,0:T(8,128)(2,1)S(1)}) custom-call(s32[1,16]{1,0:T(1,128)S(1)} %bitcast.6, s32[1,16]{1,0:T(1,128)S(1)} %copy-done.7, s32[1,16]{1,0:T(1,128)S(1)} %bitcast.7, bf16[4,5]{1,0:T(4,128)(2,1)S(1)} %copy-done.6, f32[8,176,128]{2,1,0:T(8,128)S(1)} %get-tuple-element.16.high_level, ...), custom_call_target="tpu_custom_call" | custom-call | flops 1291845632 | bytes 1572864 | tf_op jit(solution)/shard_map/match/pallas_call | solution.py:504
  6.6 4.3 %collective-permute-done.above = f32[104,512]{1,0:T(8,128)S(1)} collective-permute-done((f32[104,512]{1,0:T(8,128)}, f32[104,512]{1,0:T(8,128)S(1)}, u32[]{:S(2)}, u32[]{:S(2)}) %collective-permute-start) | collective-permute-done | bytes 213024 | tf_op jit(solution)/shard_map/ppermute | solution.py:639
  10.9 2.8 %warp.1 = bf16[16,272,128]{2,1,0:T(8,128)(2,1)S(1)} custom-call(s32[1,16]{1,0:T(1,128)S(1)} %bitcast.8, s32[1,16]{1,0:T(1,128)S(1)} %get-tuple-element.20.places, f32[16,128]{1,0:T(8,128)S(1)} %get-tuple-element.21.label, f32[8,176,128]{2,1,0:T(8,128)S(1)} %get-tuple-element.16.high_level, f32[8,176,128]{2,1,0:T(8,128)S(1)} %get-tuple-element.17.step_level, ...), custom_call_target="tpu_custom_call" | custom-call | flops 1660944384 | bytes 1572864 | tf_op jit(solution)/shard_map/warp/pallas_call | solution.py:528
  13.7 32.0 %all_to_all.5.got = bf16[16,272,128]{2,1,0:T(8,128)(2,1)S(1)} all-to-all(bf16[16,272,128]{2,1,0:T(8,128)(2,1)S(1)} %warp.1), channel_id=1, replica_groups=mesh['group'=2,'ccd'=16] {'ccd'}, dimensions={0} | all-to-all | bytes 2228224 | tf_op jit(solution)/shard_map/all_to_all | solution.py:648
  45.8 1.7 %coadd.1 = f32[1,512,512]{2,1,0:T(8,128)} custom-call(bf16[16,272,128]{2,1,0:T(8,128)(2,1)S(1)} %all_to_all.5.got), custom_call_target="tpu_custom_call" | custom-call | tf_op jit(solution)/shard_map/coadd/pallas_call | solution.py:619
Async XLA Ops:
  1.6 0.8 %copy-start.3 = (f32[4,5,9,3]{2,0,3,1:T(4,128)S(1)}, f32[4,5,9,3]{2,0,3,1:T(4,128)}, u32[]{:S(2)}) copy-start(f32[4,5,9,3]{2,0,3,1:T(4,128)} %param.10) | copy-start | bytes 6484
  1.6 0.8 %copy-start.4 = (f32[2,9,11]{2,0,1:T(2,128)S(1)}, f32[2,9,11]{2,0,1:T(2,128)}, u32[]{:S(2)}) copy-start(f32[2,9,11]{2,0,1:T(2,128)} %param.9) | copy-start | bytes 2380
  1.6 0.8 %copy-start.5 = (f32[4,5,2,2]{1,3,2,0:T(2,128)S(1)}, f32[4,5,2,2]{1,3,2,0:T(2,128)}, u32[]{:S(2)}) copy-start(f32[4,5,2,2]{1,3,2,0:T(2,128)} %param.11) | copy-start | bytes 964
  1.7 9.2 %collective-permute-start = (f32[104,512]{1,0:T(8,128)}, f32[104,512]{1,0:T(8,128)S(1)}, u32[]{:S(2)}, u32[]{:S(2)}) collective-permute-start(f32[104,512]{1,0:T(8,128)} %collect.1), channel_id=1, source_target_pairs={{0,1},{1,2},{2,3},{3,4},{4,5},{5,6},{6,7},{7,8},{8,9},{9,10},{10,1... | collective-permute-start | bytes 638984 | tf_op jit(solution)/shard_map/ppermute | solution.py:639
  2.4 2.1 %copy-start = (f32[4,128,512]{2,1,0:T(8,128)S(1)}, f32[4,128,512]{2,1,0:T(8,128)}, u32[]{:S(2)}) copy-start(f32[4,128,512]{2,1,0:T(8,128)} %image.3) | copy-start | bytes 3145732
  2.4 2.1 %copy-start.1 = (s32[1,16,1]{1,2,0:T(1,128)S(1)}, s32[1,16,1]{1,2,0:T(1,128)}, u32[]{:S(2)}) copy-start(s32[1,16,1]{1,2,0:T(1,128)} %param.13) | copy-start | bytes 196
  2.4 2.1 %copy-start.2 = (s32[16]{0:T(128)S(1)}, s32[16]{0:T(128)}, u32[]{:S(2)}) copy-start(s32[16]{0:T(128)} %param.15) | copy-start | bytes 196
  2.5 2.1 %copy-start.6 = (bf16[4,5]{1,0:T(4,128)(2,1)S(1)}, bf16[4,5]{1,0:T(4,128)(2,1)}, u32[]{:S(2)}) copy-start(bf16[4,5]{1,0:T(4,128)(2,1)} %weight.1) | copy-start | bytes 124
  2.5 2.1 %copy-start.7 = (s32[1,16]{1,0:T(1,128)S(1)}, s32[1,16]{1,0:T(1,128)}, u32[]{:S(2)}) copy-start(s32[1,16]{1,0:T(1,128)} %slot.1) | copy-start | bytes 196

commit v19 on v18

--- a/solution.py
+++ b/solution.py
@@ -1,5 +1,4 @@
 import functools
-import itertools
 
 import jax
 import jax.numpy as jnp
@@ -43,7 +42,7 @@
 BODY = BLOCK - TAIL
 GOT = TAIL + RIM
 OPEN = (STRIPS - 1) * STRIP + STEP - FREE_FIRST * STRIP
-LABEL = 16
+LABEL = 8
 F32 = jnp.float32
 BF16 = jnp.bfloat16
 
@@ -185,21 +184,32 @@
     offset = iota((8, LANES), 0) - WARP
     crosses = (lane + offset >= TAIL) != (lane >= TAIL)
     keep = (offset <= WARP) & (same | jnp.logical_not(crosses))
+    def terms_of(n, visit):
+        here = iota((1, 1, affine.shape[3]), 2) == bands[n][0]
+        return jnp.sum(jnp.where(here, affine[visit], 0.0), axis=2, keepdims=True)
+
+    def columns(n, visit):
+        a = terms_of(n, visit)
+        col_shift = a[1, 0:1] + a[1, 1:2] * (col - (WIDTH - 1) / 2.0) / WIDTH
+        cols_out[n * V + visit] = jnp.where(within, lanczos(col_shift - step.astype(F32)), 0.0)
+
     by_row = []
     for visit in range(V):
+        columns(0, visit)
         shifts = []
-        for n, (ccd, top_row) in enumerate(bands):
-            a = jnp.sum(
-                jnp.where(iota((1, 1, affine.shape[3]), 2) == ccd, affine[visit], 0.0),
-                axis=2, keepdims=True,
-            )
+        for n, (_, top_row) in enumerate(bands):
+            a = terms_of(n, visit)
             row = (top_row + lane).astype(F32)
             shifts.append(a[0, 0:1] + a[0, 1:2] * (row - (HEIGHT - 1) / 2.0) / HEIGHT)
-            col_shift = a[1, 0:1] + a[1, 1:2] * (col - (WIDTH - 1) / 2.0) / WIDTH
-            cols_out[n * V + visit] = jnp.where(within, lanczos(col_shift - step.astype(F32)), 0.0)
         shift = jnp.where(lane < TAIL, shifts[1], shifts[0])
         weights = jnp.where(keep, lanczos(shift - offset.astype(F32)), 0.0)
         by_row.append(jnp.concatenate([weights, jnp.zeros((LANES - 8, LANES), F32)], axis=0).T)
+
+    @pl.when(jnp.logical_not(same))
+    def _():
+        for visit in range(V):
+            columns(1, visit)
+
     return by_row
 
 
@@ -207,7 +217,7 @@
     devices, taps, psf, affine, high_level, step_level, slope, rows_high, rows_low, cols_out
 ):
     row_weights = lanczos_weights(devices, affine, cols_out)
-    bands, _ = whereabouts(devices)
+    bands, same = whereabouts(devices)
     band_lane = iota((1, BAND), 1)
     seg = band_lane // STEP
     lane = iota((1, LANES), 1)
@@ -216,8 +226,7 @@
     row_taps = dot_exact(taps[:, 0], onehot.astype(F32), ((1,), (0,)))
     eye = (iota((TAPS, STRIP), 0) == iota((TAPS, STRIP), 1)).astype(F32)
     turned_taps = dot_exact(eye, taps[:, 1], ((0,), (1,)))
-    units = []
-    for n, visit in itertools.product(range(2), range(V)):
+    def make(n, visit):
         ccd, top_row = bands[n]
         lhs = jnp.concatenate(
             [turned_taps * psf[ccd, c, visit : visit + 1, :] for c in range(3)], axis=0
@@ -234,7 +243,6 @@
         reach = per_strip * (STRIPS - MIDDLE)
         largest = jnp.max(jnp.abs(const) + reach * jnp.abs(by_row), axis=(0, 1), keepdims=True)
         unit = jnp.maximum(largest, 1e-30) * (1.0 / 200.0)
-        units.append(unit)
         const = const / unit
         by_row = (by_row * per_strip) / unit
         low_lanes = (lane // STEP) % 3 == 2
@@ -252,20 +260,24 @@
             high_level[n * V + visit, at] = jnp.where(low_lanes, x - high, high)
             high = jnp.round(y)
             step_level[n * V + visit, at] = jnp.where(low_lanes, y - high, high)
+        return unit
+
+    def put(visit, at, matrix):
+        high = matrix.astype(BF16)
+        rows_high[visit, at] = high
+        rows_low[visit, at] = (matrix - high.astype(F32)).astype(BF16)
 
     for visit in range(V):
-        weights = row_weights[visit]
-        matrix = jnp.concatenate(
-            [
-                staircase(weights[:TAIL] * units[V + visit], 0),
-                staircase(weights[TAIL:ROWS] * units[visit], PAST_STRIPS * STRIP),
-                staircase(weights[ROWS:] * units[visit], 0),
-            ],
-            axis=0,
-        )
-        high = matrix.astype(BF16)
-        rows_high[visit] = high
-        rows_low[visit] = (matrix - high.astype(F32)).astype(BF16)
+        weights = row_weights[visit] * make(0, visit)
+        put(visit, slice(0, TAIL), staircase(weights[:TAIL], 0))
+        put(visit, slice(TAIL, ROWS), staircase(weights[TAIL:ROWS], PAST_STRIPS * STRIP))
+        put(visit, slice(ROWS, BLOCK), staircase(weights[ROWS:], 0))
+
+    @pl.when(jnp.logical_not(same))
+    def _():
+        for visit in range(V):
+            weights = row_weights[visit][:TAIL] * make(1, visit)
+            put(visit, slice(0, TAIL), staircase(weights, 0))
 
 
 def small_kernel(body, name, args, shapes):
@@ -344,9 +356,36 @@
     return to, rank
 
 
+def warp_rows(high, low, first, second, weights, unsort):
+    lane = iota((1, LANES), 1)
+
+    def filled(x):
+        return jnp.concatenate([x, jnp.zeros((LANES - x.shape[0], WIDTH), BF16)], axis=0)
+
+    first = filled(first)
+    total = jnp.dot(
+        jnp.concatenate([high, high], axis=1),
+        jnp.concatenate([first, filled(second)], axis=0),
+        preferred_element_type=F32,
+    )
+    total = total + jnp.dot(low, first, preferred_element_type=F32)
+    parts = []
+    for rows, cols in weights:
+        some = total[rows]
+        blocks = lane_sum(
+            lambda s, v, w: lane_block(cols[s : s + 1], v) * lane_block(some, w),
+            lane, 2 * WARP + 1, True,
+        )
+        parts.append(jnp.concatenate(blocks, axis=1).astype(BF16))
+    return jnp.dot(
+        jnp.concatenate(parts, axis=0), unsort, preferred_element_type=F32
+    ).astype(BF16)
+
+
 def match_kernel(
-    patch, slot, owner, weight, high_level, step_level, slope, sort, image,
-    places, label, matched_terms, terms,
+    patch, slot, owner, weight, high_level, step_level, slope, rows_high, rows_low, col_weights,
+    sort, unsort, image,
+    places, label, matched_out, second_half, terms, matched_terms,
 ):
     ((ccd, _), _), _ = whereabouts(label.shape[0])
     to, rank = route(patch[...], owner[...])
@@ -381,9 +420,17 @@
             first = (k - FREE_FIRST) * STRIP
             for i, visit in enumerate(visits):
                 at = slice(first, first + STRIP)
-                matched_terms[visit, 0, at], matched_terms[visit, 1, at] = match_strip(
+                matched_terms[i, 0, at], matched_terms[i, 1, at] = match_strip(
                     high_level[visit], step_level[visit], slope[visit], terms.at[i], first, k
                 )
+        half = slice(ROWS, BLOCK)
+        for i, visit in enumerate(visits):
+            matched_out[visit] = matched_terms[i, :, : WINDOW - FREE_FIRST * STRIP]
+            under = [matched_terms[i, term, ROWS - FREE_FIRST * STRIP :] for term in range(2)]
+            second_half[visit] = warp_rows(
+                rows_high[visit, half], rows_low[visit, half], *under,
+                [(slice(0, ROWS), col_weights[visit])], unsort[...],
+            )
         return 0
 
     lax.fori_loop(0, V // MATCHED, some_visits, 0)
@@ -391,7 +438,7 @@
 
 def warp_kernel(
     owner, places, label, high_level, step_level, slope, rows_high, rows_low, col_weights,
-    sort, unsort, image, above, matched_free, out,
+    sort, unsort, image, above, matched_free, second_half, out,
     own_terms, past_terms, own_matched, past_matched, both_places, place_of, place_sem,
 ):
     devices = label.shape[0]
@@ -410,6 +457,7 @@
     seam = STRIP + STEP
     foreign = iota((seam, 1), 0) < GOT
     both = jnp.where(same, 1.0, 0.0)
+    past = jnp.where(same, 0, V)
     own_sees = jnp.where(foreign, both, 1.0)
     past_sees = jnp.where(foreign, 1.0, both)
 
@@ -430,63 +478,39 @@
             for i, visit in enumerate(visits):
                 at = slice(k * STRIP, (k + 1) * STRIP)
                 past_matched[i, 0, at], past_matched[i, 1, at] = match_strip(
-                    high_level[V + visit], step_level[V + visit], slope[V + visit],
+                    high_level[past + visit], step_level[past + visit], slope[past + visit],
                     past_terms.at[i], k * STRIP, k,
                 )
-
-        warped = []
-        for i, visit in enumerate(visits):
-            halves = []
-            for h in range(HALVES):
-                at = slice(h * ROWS, (h + 1) * ROWS)
-                high, low = rows_high[visit, at], rows_low[visit, at]
-                free = FREE_FIRST * STRIP
-
-                def under(term):
-                    if h == 0:
-                        parts = [
-                            past_matched[i, term],
-                            own_matched[i, term],
-                            matched_free[visit, term, : WINDOW - free],
-                        ]
-                    else:
-                        parts = [matched_free[visit, term, ROWS - free :]]
-                    left = LANES - sum([x.shape[0] for x in parts])
-                    return jnp.concatenate(parts + [jnp.zeros((left, WIDTH), BF16)], axis=0)
-
-                first = under(0)
-                total = jnp.dot(
-                    jnp.concatenate([high, high], axis=1),
-                    jnp.concatenate([first, under(1)], axis=0),
-                    preferred_element_type=F32,
-                )
-                halves.append(total + jnp.dot(low, first, preferred_element_type=F32))
-            warped.append(jnp.concatenate(halves, axis=0))
 
         @pl.when(turn == 0)
         def _():
             place_copy.wait()
 
+        half = slice(0, ROWS)
         for i, visit in enumerate(visits):
-            parts = []
-            for rows, weights in (
-                (slice(0, TAIL), col_weights[V + visit]),
-                (slice(TAIL, BLOCK), col_weights[visit]),
-            ):
-                some = warped[i][rows]
-                blocks = lane_sum(
-                    lambda s, v, w: lane_block(weights[s : s + 1], v) * lane_block(some, w),
-                    lane, 2 * WARP + 1, True,
+            under = [
+                jnp.concatenate(
+                    [past_matched[i, term], own_matched[i, term], matched_free[visit, term]], axis=0
                 )
-                parts.append(jnp.concatenate(blocks, axis=1).astype(BF16))
-            result = jnp.dot(
-                jnp.concatenate(parts, axis=0), unsort[...], preferred_element_type=F32
-            ).astype(BF16)
+                for term in range(2)
+            ]
+            result = warp_rows(
+                rows_high[visit, half], rows_low[visit, half], *under,
+                [
+                    (slice(0, TAIL), col_weights[past + visit]),
+                    (slice(TAIL, ROWS), col_weights[visit]),
+                ],
+                unsort[...],
+            )
+            rest = second_half[visit]
             for j in range(BLKC):
                 piece = lane_block(result, j)
                 to = place_of[0, visit * BLKC + j]
-                rows = pl.ds(pl.multiple_of(to % CAP * BODY, TAIL), BODY)
+                row = to % CAP * BODY
+                rows = pl.ds(pl.multiple_of(row, TAIL), ROWS - TAIL)
                 out[to // CAP, rows] = piece[TAIL:]
+                rows = pl.ds(pl.multiple_of(row + ROWS - TAIL, TAIL), BLOCK - ROWS)
+                out[to // CAP, rows] = lane_block(rest, j)
                 to = place_of[1, visit * BLKC + j]
                 rows = pl.ds(pl.multiple_of(CAP * BODY + to % CAP * TAIL, TAIL), TAIL)
                 out[to // CAP, rows] = piece[:TAIL]
@@ -500,18 +524,21 @@
     sort, unsort = order
     *matrices, rows_high, rows_low, col_weights = ready
     owner = owner.reshape(1, -1)
-    args = [patch, slot, owner, weight, *matrices, sort, images]
-    places, label, matched = pl.pallas_call(
+    ready = [*matrices, rows_high, rows_low, col_weights, sort, unsort, images]
+    args = [patch, slot, owner, weight, *ready]
+    places, label, matched, second_half = pl.pallas_call(
         match_kernel,
         in_specs=[vmem] * len(args),
-        out_specs=[vmem, vmem, vmem],
+        out_specs=[vmem] * 4,
         out_shape=[
             jax.ShapeDtypeStruct((1, V * BLKC), jnp.int32),
             jax.ShapeDtypeStruct((devices, LANES), F32),
-            jax.ShapeDtypeStruct((V, 2, (STRIPS - FREE_FIRST) * STRIP, WIDTH), BF16),
+            jax.ShapeDtypeStruct((V, 2, WINDOW - FREE_FIRST * STRIP, WIDTH), BF16),
+            jax.ShapeDtypeStruct((V, BLOCK - ROWS, WIDTH), BF16),
         ],
         scratch_shapes=[
             pltpu.VMEM((MATCHED, 4, OPEN, WIDTH), BF16),
+            pltpu.VMEM((MATCHED, 2, (STRIPS - FREE_FIRST) * STRIP, WIDTH), BF16),
         ],
         compiler_params=pltpu.CompilerParams(vmem_limit_bytes=32 << 20),
         cost_estimate=pl.CostEstimate(
@@ -521,10 +548,7 @@
         ),
         name="match",
     )(*args)
-    args = [
-        owner, places, label, *matrices, rows_high, rows_low, col_weights,
-        sort, unsort, images, above, matched,
-    ]
+    args = [owner, places, label, *ready, above, matched, second_half]
     return pl.pallas_call(
         warp_kernel,
         in_specs=[vmem] * len(args),

time: 47.7 us -> 48.2 us (1.010)
  Pallas kernels: 10.4 us -> 12.1 us
  waiting for transfers between devices: 4.25 us -> 2.73 us
    ppermute x1, waiting for transfers between devices: 4.25 us -> 2.73 us  [shards(): lax.ppermute(head, 'ccd', [(i, (i + 1) % devices) for i in range(devices)])]
    pallas_call x1, Pallas kernels: 2.1 us -> 3.31 us  [warp(): pl.pallas_call(match_kernel, in_specs=[vmem] * len(args), out_specs=[vmem...]
  transfers between devices with their start and end apart: 1 -> 1, of which waited for: 1 -> 1; matrix products, arithmetic and copies ran while one was open for 0% -> 0% of each run, Pallas kernels for 9% -> 12%
where the time goes in v19:
time: 48.2 us; the launch traced here: 47.9 us
  blocking collectives  32.4 us (67%)
  Pallas kernels  12.1 us (25%)
  waiting for transfers between devices  2.73 us (6%)
  starting transfers between devices  0.5 us (1%)
    all_to_all x1, blocking collectives, shards(): got = lax.all_to_all(sent, 'ccd', split_axis=0, concat_axis=0, tiled=True)  32.4 us
    pallas_call x1, Pallas kernels, warp(): pl.pallas_call(match_kernel, in_specs=[vmem] * len(args), out_specs=[vmem...  3.31 us
    pallas_call x1, Pallas kernels, warp(): pl.pallas_call(warp_kernel, in_specs=[vmem] * len(args), out_specs=vmem,...  2.93 us
    ppermute x1, waiting for transfers between devices, shards(): lax.ppermute(head, 'ccd', [(i, (i + 1) % devices) for i in range(devices)])  2.73 us
    pallas_call x2, Pallas kernels, small_kernel(): pl.pallas_call(body, in_specs=[vmem] * len(args), out_specs=[vmem] * len(...  2.55 us
    pallas_call x1, Pallas kernels, coadd(): pl.pallas_call(coadd_kernel, in_specs=[pl.BlockSpec(memory_space=pltpu.VM...  1.67 us
    pallas_call x1, Pallas kernels, collect(): pl.pallas_call(collect_kernel, in_specs=[pl.BlockSpec(memory_space=pl.ANY...  1.61 us
  transfers between devices with their start and end apart: 1, of which 1 were waited for; matrix products, arithmetic and copies ran while one was open for 0% of the time, Pallas kernels for 12%

profile of v19, /device:TPU:0, one launch (start us, length us, event | category | flops | bytes accessed | tf_op | source)
XLA Modules:
  0.0 47.9 jit_solution(4570700483978349804)
XLA Ops:
  0.0 1.6 %collect.1 = f32[104,512]{1,0:T(8,128)} custom-call(f32[4,128,512]{2,1,0:T(8,128)} %image.3, s32[1,16]{1,0:T(1,128)} %bitcast.5), custom_call_target="tpu_custom_call" | custom-call | tf_op jit(solution)/shard_map/collect/pallas_call | solution.py:164
  1.6 0.0 copy-start.3
  1.6 0.0 copy-start.4
  1.6 0.0 copy-start.5
  1.7 0.5 %collective-permute-start = (f32[104,512]{1,0:T(8,128)}, f32[104,512]{1,0:T(8,128)S(1)}, u32[]{:S(2)}, u32[]{:S(2)}) collective-permute-start(f32[104,512]{1,0:T(8,128)} %collect.1), channel_id=1, source_target_pairs={{0,1},{1,2},{2,3},{3,4},{4,5},{5,6},{6,7},{7,8},{8,9},{9,10},{10,1... | collective-permute-start | bytes 638984 | tf_op jit(solution)/shard_map/ppermute | solution.py:663
  2.2 0.2 orders.1
  2.4 0.0 copy-done.3
  2.4 0.0 copy-done.4
  2.4 0.0 copy-done.5
  2.4 0.0 copy-start
  2.4 0.0 copy-start.1
  2.4 0.0 copy-start.2
  2.5 0.0 copy-start.6
  2.5 0.0 copy-start.7
  2.5 2.3 %matrices.1 = (f32[8,176,128]{2,1,0:T(8,128)S(1)}, f32[8,176,128]{2,1,0:T(8,128)S(1)}, bf16[8,176,128]{2,1,0:T(8,128)(2,1)S(1)}, bf16[4,128,128]{2,1,0:T(8,128)(...) custom-call(f32[9,2,11]{2,1,0:T(2,128)S(1)} %bitcast.10, f32[5,3,4,9]{3,2,1,0:T(4,128)S(1)} %bitcast.9, ...), custom_call_target="tpu_custom_call" | custom-call | flops 1073741824 | bytes 1048576 | tf_op jit(solution)/shard_map/matrices/pallas_call | solution.py:285
  4.8 0.0 copy-done
  4.8 0.0 copy-done.1
  4.8 0.0 copy-done.2
  4.8 0.0 copy-done.6
  4.8 0.0 copy-done.7
  4.9 3.3 %match.1 = (s32[1,16]{1,0:T(1,128)S(1)}, f32[16,128]{1,0:T(8,128)S(1)}, bf16[4,2,48,512]{3,2,1,0:T(8,128)(2,1)S(1)}, bf16[4,64,512]{2,1,0:T(8,128)(2,1)S(1)}) custom-call(s32[1,16]{1,0:T(1,128)S(1)} %bitcast.6, s32[1,16]{1,0:T(1,128)S(1)} %copy-done.7, s32[1,16]{1,0:T(1,128)S(1)} %bitcast.7, bf16[4,5]{1,0:T(4,128)(2,1)S(1)} %copy-done.6, ...), custom_call_target="tpu_custom_call" | custom-call | flops 1291845632 | bytes 1572864 | tf_op jit(solution)/shard_map/match/pallas_call | solution.py:529
  8.2 2.7 %collective-permute-done.above = f32[104,512]{1,0:T(8,128)S(1)} collective-permute-done((f32[104,512]{1,0:T(8,128)}, f32[104,512]{1,0:T(8,128)S(1)}, u32[]{:S(2)}, u32[]{:S(2)}) %collective-permute-start) | collective-permute-done | bytes 213024 | tf_op jit(solution)/shard_map/ppermute | solution.py:663
  10.9 2.9 %warp.1 = bf16[16,264,128]{2,1,0:T(8,128)(2,1)S(1)} custom-call(s32[1,16]{1,0:T(1,128)S(1)} %bitcast.8, s32[1,16]{1,0:T(1,128)S(1)} %get-tuple-element.25.places, f32[16,128]{1,0:T(8,128)S(1)} %get-tuple-element.26.label, f32[8,176,128]{2,1,0:T(8,128)S(1)} %get-tuple-element.17.high_level, f32[8,176,128]{2,1,0:T(8,128)S(1)} %get-tuple-element.18.step_level, ...), custom_call_target="tpu_custom_call" | custom-call | flops 1660944384 | bytes 1572864 | tf_op jit(solution)/shard_map/warp/pallas_call | solution.py:552
  13.8 32.4 %all_to_all.5.got = bf16[16,264,128]{2,1,0:T(8,128)(2,1)S(1)} all-to-all(bf16[16,264,128]{2,1,0:T(8,128)(2,1)S(1)} %warp.1), channel_id=1, replica_groups=mesh['group'=2,'ccd'=16] {'ccd'}, dimensions={0} | all-to-all | bytes 2162688 | tf_op jit(solution)/shard_map/all_to_all | solution.py:672
  46.2 1.7 %coadd.1 = f32[1,512,512]{2,1,0:T(8,128)} custom-call(bf16[16,264,128]{2,1,0:T(8,128)(2,1)S(1)} %all_to_all.5.got), custom_call_target="tpu_custom_call" | custom-call | tf_op jit(solution)/shard_map/coadd/pallas_call | solution.py:643
Async XLA Ops:
  1.6 0.8 %copy-start.3 = (f32[4,5,9,3]{2,0,3,1:T(4,128)S(1)}, f32[4,5,9,3]{2,0,3,1:T(4,128)}, u32[]{:S(2)}) copy-start(f32[4,5,9,3]{2,0,3,1:T(4,128)} %param.10) | copy-start | bytes 6484
  1.6 0.8 %copy-start.4 = (f32[2,9,11]{2,0,1:T(2,128)S(1)}, f32[2,9,11]{2,0,1:T(2,128)}, u32[]{:S(2)}) copy-start(f32[2,9,11]{2,0,1:T(2,128)} %param.9) | copy-start | bytes 2380
  1.6 0.8 %copy-start.5 = (f32[4,5,2,2]{1,3,2,0:T(2,128)S(1)}, f32[4,5,2,2]{1,3,2,0:T(2,128)}, u32[]{:S(2)}) copy-start(f32[4,5,2,2]{1,3,2,0:T(2,128)} %param.11) | copy-start | bytes 964
  1.7 9.2 %collective-permute-start = (f32[104,512]{1,0:T(8,128)}, f32[104,512]{1,0:T(8,128)S(1)}, u32[]{:S(2)}, u32[]{:S(2)}) collective-permute-start(f32[104,512]{1,0:T(8,128)} %collect.1), channel_id=1, source_target_pairs={{0,1},{1,2},{2,3},{3,4},{4,5},{5,6},{6,7},{7,8},{8,9},{9,10},{10,1... | collective-permute-start | bytes 638984 | tf_op jit(solution)/shard_map/ppermute | solution.py:663
  2.4 2.4 %copy-start = (f32[4,128,512]{2,1,0:T(8,128)S(1)}, f32[4,128,512]{2,1,0:T(8,128)}, u32[]{:S(2)}) copy-start(f32[4,128,512]{2,1,0:T(8,128)} %image.3) | copy-start | bytes 3145732
  2.4 2.4 %copy-start.1 = (s32[1,16,1]{1,2,0:T(1,128)S(1)}, s32[1,16,1]{1,2,0:T(1,128)}, u32[]{:S(2)}) copy-start(s32[1,16,1]{1,2,0:T(1,128)} %param.13) | copy-start | bytes 196
  2.4 2.4 %copy-start.2 = (s32[16]{0:T(128)S(1)}, s32[16]{0:T(128)}, u32[]{:S(2)}) copy-start(s32[16]{0:T(128)} %param.15) | copy-start | bytes 196
  2.5 2.4 %copy-start.6 = (bf16[4,5]{1,0:T(4,128)(2,1)S(1)}, bf16[4,5]{1,0:T(4,128)(2,1)}, u32[]{:S(2)}) copy-start(bf16[4,5]{1,0:T(4,128)(2,1)} %weight.1) | copy-start | bytes 124
  2.5 2.4 %copy-start.7 = (s32[1,16]{1,0:T(1,128)S(1)}, s32[1,16]{1,0:T(1,128)}, u32[]{:S(2)}) copy-start(s32[1,16]{1,0:T(1,128)} %slot.1) | copy-start | bytes 196

commit v20 on v18

--- a/solution.py
+++ b/solution.py
@@ -1,5 +1,4 @@
 import functools
-import itertools
 
 import jax
 import jax.numpy as jnp
@@ -43,7 +42,7 @@
 BODY = BLOCK - TAIL
 GOT = TAIL + RIM
 OPEN = (STRIPS - 1) * STRIP + STEP - FREE_FIRST * STRIP
-LABEL = 16
+LABEL = 8
 F32 = jnp.float32
 BF16 = jnp.bfloat16
 
@@ -185,21 +184,32 @@
     offset = iota((8, LANES), 0) - WARP
     crosses = (lane + offset >= TAIL) != (lane >= TAIL)
     keep = (offset <= WARP) & (same | jnp.logical_not(crosses))
+    def terms_of(n, visit):
+        here = iota((1, 1, affine.shape[3]), 2) == bands[n][0]
+        return jnp.sum(jnp.where(here, affine[visit], 0.0), axis=2, keepdims=True)
+
+    def columns(n, visit):
+        a = terms_of(n, visit)
+        col_shift = a[1, 0:1] + a[1, 1:2] * (col - (WIDTH - 1) / 2.0) / WIDTH
+        cols_out[n * V + visit] = jnp.where(within, lanczos(col_shift - step.astype(F32)), 0.0)
+
     by_row = []
     for visit in range(V):
+        columns(0, visit)
         shifts = []
-        for n, (ccd, top_row) in enumerate(bands):
-            a = jnp.sum(
-                jnp.where(iota((1, 1, affine.shape[3]), 2) == ccd, affine[visit], 0.0),
-                axis=2, keepdims=True,
-            )
+        for n, (_, top_row) in enumerate(bands):
+            a = terms_of(n, visit)
             row = (top_row + lane).astype(F32)
             shifts.append(a[0, 0:1] + a[0, 1:2] * (row - (HEIGHT - 1) / 2.0) / HEIGHT)
-            col_shift = a[1, 0:1] + a[1, 1:2] * (col - (WIDTH - 1) / 2.0) / WIDTH
-            cols_out[n * V + visit] = jnp.where(within, lanczos(col_shift - step.astype(F32)), 0.0)
         shift = jnp.where(lane < TAIL, shifts[1], shifts[0])
         weights = jnp.where(keep, lanczos(shift - offset.astype(F32)), 0.0)
         by_row.append(jnp.concatenate([weights, jnp.zeros((LANES - 8, LANES), F32)], axis=0).T)
+
+    @pl.when(jnp.logical_not(same))
+    def _():
+        for visit in range(V):
+            columns(1, visit)
+
     return by_row
 
 
@@ -207,7 +217,7 @@
     devices, taps, psf, affine, high_level, step_level, slope, rows_high, rows_low, cols_out
 ):
     row_weights = lanczos_weights(devices, affine, cols_out)
-    bands, _ = whereabouts(devices)
+    bands, same = whereabouts(devices)
     band_lane = iota((1, BAND), 1)
     seg = band_lane // STEP
     lane = iota((1, LANES), 1)
@@ -216,8 +226,7 @@
     row_taps = dot_exact(taps[:, 0], onehot.astype(F32), ((1,), (0,)))
     eye = (iota((TAPS, STRIP), 0) == iota((TAPS, STRIP), 1)).astype(F32)
     turned_taps = dot_exact(eye, taps[:, 1], ((0,), (1,)))
-    units = []
-    for n, visit in itertools.product(range(2), range(V)):
+    def make(n, visit):
         ccd, top_row = bands[n]
         lhs = jnp.concatenate(
             [turned_taps * psf[ccd, c, visit : visit + 1, :] for c in range(3)], axis=0
@@ -234,7 +243,6 @@
         reach = per_strip * (STRIPS - MIDDLE)
         largest = jnp.max(jnp.abs(const) + reach * jnp.abs(by_row), axis=(0, 1), keepdims=True)
         unit = jnp.maximum(largest, 1e-30) * (1.0 / 200.0)
-        units.append(unit)
         const = const / unit
         by_row = (by_row * per_strip) / unit
         low_lanes = (lane // STEP) % 3 == 2
@@ -252,20 +260,24 @@
             high_level[n * V + visit, at] = jnp.where(low_lanes, x - high, high)
             high = jnp.round(y)
             step_level[n * V + visit, at] = jnp.where(low_lanes, y - high, high)
+        return unit
+
+    def put(visit, at, matrix):
+        high = matrix.astype(BF16)
+        rows_high[visit, at] = high
+        rows_low[visit, at] = (matrix - high.astype(F32)).astype(BF16)
 
     for visit in range(V):
-        weights = row_weights[visit]
-        matrix = jnp.concatenate(
-            [
-                staircase(weights[:TAIL] * units[V + visit], 0),
-                staircase(weights[TAIL:ROWS] * units[visit], PAST_STRIPS * STRIP),
-                staircase(weights[ROWS:] * units[visit], 0),
-            ],
-            axis=0,
-        )
-        high = matrix.astype(BF16)
-        rows_high[visit] = high
-        rows_low[visit] = (matrix - high.astype(F32)).astype(BF16)
+        weights = row_weights[visit] * make(0, visit)
+        put(visit, slice(0, TAIL), staircase(weights[:TAIL], 0))
+        put(visit, slice(TAIL, ROWS), staircase(weights[TAIL:ROWS], PAST_STRIPS * STRIP))
+        put(visit, slice(ROWS, BLOCK), staircase(weights[ROWS:], 0))
+
+    @pl.when(jnp.logical_not(same))
+    def _():
+        for visit in range(V):
+            weights = row_weights[visit][:TAIL] * make(1, visit)
+            put(visit, slice(0, TAIL), staircase(weights, 0))
 
 
 def small_kernel(body, name, args, shapes):
@@ -410,6 +422,7 @@
     seam = STRIP + STEP
     foreign = iota((seam, 1), 0) < GOT
     both = jnp.where(same, 1.0, 0.0)
+    past = jnp.where(same, 0, V)
     own_sees = jnp.where(foreign, both, 1.0)
     past_sees = jnp.where(foreign, 1.0, both)
 
@@ -430,7 +443,7 @@
             for i, visit in enumerate(visits):
                 at = slice(k * STRIP, (k + 1) * STRIP)
                 past_matched[i, 0, at], past_matched[i, 1, at] = match_strip(
-                    high_level[V + visit], step_level[V + visit], slope[V + visit],
+                    high_level[past + visit], step_level[past + visit], slope[past + visit],
                     past_terms.at[i], k * STRIP, k,
                 )
 
@@ -470,7 +483,7 @@
         for i, visit in enumerate(visits):
             parts = []
             for rows, weights in (
-                (slice(0, TAIL), col_weights[V + visit]),
+                (slice(0, TAIL), col_weights[past + visit]),
                 (slice(TAIL, BLOCK), col_weights[visit]),
             ):
                 some = warped[i][rows]

time: 47.7 us -> 47.1 us (0.987)
  blocking collectives: 32 us -> 31.5 us
    all_to_all x1, blocking collectives: 32 us -> 31.5 us  [shards(): got = lax.all_to_all(sent, 'ccd', split_axis=0, concat_axis=0, tiled=True)]
  transfers between devices with their start and end apart: 1 -> 1, of which waited for: 1 -> 1; matrix products, arithmetic and copies ran while one was open for 0% -> 0% of each run, Pallas kernels for 9% -> 10%
where the time goes in v20:
time: 47.1 us; the launch traced here: 46.9 us
  blocking collectives  31.5 us (67%)
  Pallas kernels  10.8 us (23%)
  waiting for transfers between devices  3.93 us (8%)
  starting transfers between devices  0.5 us (1%)
    all_to_all x1, blocking collectives, shards(): got = lax.all_to_all(sent, 'ccd', split_axis=0, concat_axis=0, tiled=True)  31.5 us
    ppermute x1, waiting for transfers between devices, shards(): lax.ppermute(head, 'ccd', [(i, (i + 1) % devices) for i in range(devices)])  3.93 us
    pallas_call x1, Pallas kernels, warp(): pl.pallas_call(warp_kernel, in_specs=[vmem] * len(args), out_specs=vmem,...  2.84 us
    pallas_call x2, Pallas kernels, small_kernel(): pl.pallas_call(body, in_specs=[vmem] * len(args), out_specs=[vmem] * len(...  2.55 us
    pallas_call x1, Pallas kernels, warp(): pl.pallas_call(match_kernel, in_specs=[vmem] * len(args), out_specs=[vmem...  2.1 us
    pallas_call x1, Pallas kernels, coadd(): pl.pallas_call(coadd_kernel, in_specs=[pl.BlockSpec(memory_space=pltpu.VM...  1.67 us
    pallas_call x1, Pallas kernels, collect(): pl.pallas_call(collect_kernel, in_specs=[pl.BlockSpec(memory_space=pl.ANY...  1.61 us
  transfers between devices with their start and end apart: 1, of which 1 were waited for; matrix products, arithmetic and copies ran while one was open for 0% of the time, Pallas kernels for 10%

profile of v20, /device:TPU:0, one launch (start us, length us, event | category | flops | bytes accessed | tf_op | source)
XLA Modules:
  0.0 46.9 jit_solution(2827975088856369678)
XLA Ops:
  0.0 1.6 %collect.1 = f32[104,512]{1,0:T(8,128)} custom-call(f32[4,128,512]{2,1,0:T(8,128)} %image.3, s32[1,16]{1,0:T(1,128)} %bitcast.5), custom_call_target="tpu_custom_call" | custom-call | tf_op jit(solution)/shard_map/collect/pallas_call | solution.py:164
  1.6 0.0 copy-start.3
  1.6 0.0 copy-start.4
  1.6 0.0 copy-start.5
  1.7 0.5 %collective-permute-start = (f32[104,512]{1,0:T(8,128)}, f32[104,512]{1,0:T(8,128)S(1)}, u32[]{:S(2)}, u32[]{:S(2)}) collective-permute-start(f32[104,512]{1,0:T(8,128)} %collect.1), channel_id=1, source_target_pairs={{0,1},{1,2},{2,3},{3,4},{4,5},{5,6},{6,7},{7,8},{8,9},{9,10},{10,1... | collective-permute-start | bytes 638984 | tf_op jit(solution)/shard_map/ppermute | solution.py:652
  2.2 0.2 orders.1
  2.4 0.0 copy-done.3
  2.4 0.0 copy-done.4
  2.4 0.0 copy-done.5
  2.4 0.0 copy-start
  2.4 0.0 copy-start.1
  2.4 0.0 copy-start.2
  2.5 0.0 copy-start.6
  2.5 0.0 copy-start.7
  2.5 2.3 %matrices.1 = (f32[8,176,128]{2,1,0:T(8,128)S(1)}, f32[8,176,128]{2,1,0:T(8,128)S(1)}, bf16[8,176,128]{2,1,0:T(8,128)(2,1)S(1)}, bf16[4,128,128]{2,1,0:T(8,128)(...) custom-call(f32[9,2,11]{2,1,0:T(2,128)S(1)} %bitcast.10, f32[5,3,4,9]{3,2,1,0:T(4,128)S(1)} %bitcast.9, ...), custom_call_target="tpu_custom_call" | custom-call | flops 1073741824 | bytes 1048576 | tf_op jit(solution)/shard_map/matrices/pallas_call | solution.py:285
  4.8 0.0 copy-done
  4.8 0.0 copy-done.1
  4.8 0.0 copy-done.2
  4.8 0.0 copy-done.6
  4.8 0.0 copy-done.7
  4.9 2.1 %match.1 = (s32[1,16]{1,0:T(1,128)S(1)}, f32[16,128]{1,0:T(8,128)S(1)}, bf16[4,2,112,512]{3,2,1,0:T(8,128)(2,1)S(1)}) custom-call(s32[1,16]{1,0:T(1,128)S(1)} %bitcast.6, s32[1,16]{1,0:T(1,128)S(1)} %copy-done.7, s32[1,16]{1,0:T(1,128)S(1)} %bitcast.7, bf16[4,5]{1,0:T(4,128)(2,1)S(1)} %copy-done.6, f32[8,176,128]{2,1,0:T(8,128)S(1)} %get-tuple-element.16.high_level, ...), custom_call_target="tpu_custom_call" | custom-call | flops 1291845632 | bytes 1572864 | tf_op jit(solution)/shard_map/match/pallas_call | solution.py:517
  7.0 3.9 %collective-permute-done.above = f32[104,512]{1,0:T(8,128)S(1)} collective-permute-done((f32[104,512]{1,0:T(8,128)}, f32[104,512]{1,0:T(8,128)S(1)}, u32[]{:S(2)}, u32[]{:S(2)}) %collective-permute-start) | collective-permute-done | bytes 213024 | tf_op jit(solution)/shard_map/ppermute | solution.py:652
  10.9 2.8 %warp.1 = bf16[16,264,128]{2,1,0:T(8,128)(2,1)S(1)} custom-call(s32[1,16]{1,0:T(1,128)S(1)} %bitcast.8, s32[1,16]{1,0:T(1,128)S(1)} %get-tuple-element.20.places, f32[16,128]{1,0:T(8,128)S(1)} %get-tuple-element.21.label, f32[8,176,128]{2,1,0:T(8,128)S(1)} %get-tuple-element.16.high_level, f32[8,176,128]{2,1,0:T(8,128)S(1)} %get-tuple-element.17.step_level, ...), custom_call_target="tpu_custom_call" | custom-call | flops 1660944384 | bytes 1572864 | tf_op jit(solution)/shard_map/warp/pallas_call | solution.py:541
  13.7 31.5 %all_to_all.5.got = bf16[16,264,128]{2,1,0:T(8,128)(2,1)S(1)} all-to-all(bf16[16,264,128]{2,1,0:T(8,128)(2,1)S(1)} %warp.1), channel_id=1, replica_groups=mesh['group'=2,'ccd'=16] {'ccd'}, dimensions={0} | all-to-all | bytes 2162688 | tf_op jit(solution)/shard_map/all_to_all | solution.py:661
  45.2 1.7 %coadd.1 = f32[1,512,512]{2,1,0:T(8,128)} custom-call(bf16[16,264,128]{2,1,0:T(8,128)(2,1)S(1)} %all_to_all.5.got), custom_call_target="tpu_custom_call" | custom-call | tf_op jit(solution)/shard_map/coadd/pallas_call | solution.py:632
Async XLA Ops:
  1.6 0.8 %copy-start.3 = (f32[4,5,9,3]{2,0,3,1:T(4,128)S(1)}, f32[4,5,9,3]{2,0,3,1:T(4,128)}, u32[]{:S(2)}) copy-start(f32[4,5,9,3]{2,0,3,1:T(4,128)} %param.10) | copy-start | bytes 6484
  1.6 0.8 %copy-start.4 = (f32[2,9,11]{2,0,1:T(2,128)S(1)}, f32[2,9,11]{2,0,1:T(2,128)}, u32[]{:S(2)}) copy-start(f32[2,9,11]{2,0,1:T(2,128)} %param.9) | copy-start | bytes 2380
  1.6 0.8 %copy-start.5 = (f32[4,5,2,2]{1,3,2,0:T(2,128)S(1)}, f32[4,5,2,2]{1,3,2,0:T(2,128)}, u32[]{:S(2)}) copy-start(f32[4,5,2,2]{1,3,2,0:T(2,128)} %param.11) | copy-start | bytes 964
  1.7 9.2 %collective-permute-start = (f32[104,512]{1,0:T(8,128)}, f32[104,512]{1,0:T(8,128)S(1)}, u32[]{:S(2)}, u32[]{:S(2)}) collective-permute-start(f32[104,512]{1,0:T(8,128)} %collect.1), channel_id=1, source_target_pairs={{0,1},{1,2},{2,3},{3,4},{4,5},{5,6},{6,7},{7,8},{8,9},{9,10},{10,1... | collective-permute-start | bytes 638984 | tf_op jit(solution)/shard_map/ppermute | solution.py:652
  2.4 2.4 %copy-start = (f32[4,128,512]{2,1,0:T(8,128)S(1)}, f32[4,128,512]{2,1,0:T(8,128)}, u32[]{:S(2)}) copy-start(f32[4,128,512]{2,1,0:T(8,128)} %image.3) | copy-start | bytes 3145732
  2.4 2.4 %copy-start.1 = (s32[1,16,1]{1,2,0:T(1,128)S(1)}, s32[1,16,1]{1,2,0:T(1,128)}, u32[]{:S(2)}) copy-start(s32[1,16,1]{1,2,0:T(1,128)} %param.13) | copy-start | bytes 196
  2.4 2.4 %copy-start.2 = (s32[16]{0:T(128)S(1)}, s32[16]{0:T(128)}, u32[]{:S(2)}) copy-start(s32[16]{0:T(128)} %param.15) | copy-start | bytes 196
  2.5 2.4 %copy-start.6 = (bf16[4,5]{1,0:T(4,128)(2,1)S(1)}, bf16[4,5]{1,0:T(4,128)(2,1)}, u32[]{:S(2)}) copy-start(bf16[4,5]{1,0:T(4,128)(2,1)} %weight.1) | copy-start | bytes 124
  2.5 2.4 %copy-start.7 = (s32[1,16]{1,0:T(1,128)S(1)}, s32[1,16]{1,0:T(1,128)}, u32[]{:S(2)}) copy-start(s32[1,16]{1,0:T(1,128)} %slot.1) | copy-start | bytes 196

commit v21 on v20

--- a/solution.py
+++ b/solution.py
@@ -383,7 +383,7 @@
     seen = OPEN - STRIP
     terms[:, :, seen:] = jnp.zeros((MATCHED, 4, STRIP, WIDTH), BF16)
 
-    def some_visits(turn, _):
+    def some_visits(turn):
         visits = [turn * MATCHED + i for i in range(MATCHED)]
         for i, visit in enumerate(visits):
             rows = sorted_rows(image[visit, open_row : open_row + seen], sort[...])
@@ -396,9 +396,9 @@
                 matched_terms[visit, 0, at], matched_terms[visit, 1, at] = match_strip(
                     high_level[visit], step_level[visit], slope[visit], terms.at[i], first, k
                 )
-        return 0
-
-    lax.fori_loop(0, V // MATCHED, some_visits, 0)
+
+    for turn in range(V // MATCHED):
+        some_visits(turn)
 
 
 def warp_kernel(
@@ -426,10 +426,10 @@
     own_sees = jnp.where(foreign, both, 1.0)
     past_sees = jnp.where(foreign, 1.0, both)
 
-    def some_visits(turn, _):
+    def some_visits(turn):
         visits = [turn * WARPED + i for i in range(WARPED)]
         for i, visit in enumerate(visits):
-            tail = pl.ds(pl.multiple_of(visit * GOT, 8), GOT)
+            tail = slice(visit * GOT, (visit + 1) * GOT)
             raw = jnp.concatenate([above[tail], image[visit, : seam - GOT]], axis=0)
             for h, value in enumerate(sorted_rows(raw, sort[...])):
                 own_terms[i, h] = (value * own_sees).astype(BF16)
@@ -476,10 +476,7 @@
                 halves.append(total + jnp.dot(low, first, preferred_element_type=F32))
             warped.append(jnp.concatenate(halves, axis=0))
 
-        @pl.when(turn == 0)
-        def _():
-            place_copy.wait()
-
+        finished = []
         for i, visit in enumerate(visits):
             parts = []
             for rows, weights in (
@@ -495,17 +492,22 @@
             result = jnp.dot(
                 jnp.concatenate(parts, axis=0), unsort[...], preferred_element_type=F32
             ).astype(BF16)
-            for j in range(BLKC):
-                piece = lane_block(result, j)
-                to = place_of[0, visit * BLKC + j]
-                rows = pl.ds(pl.multiple_of(to % CAP * BODY, TAIL), BODY)
-                out[to // CAP, rows] = piece[TAIL:]
-                to = place_of[1, visit * BLKC + j]
-                rows = pl.ds(pl.multiple_of(CAP * BODY + to % CAP * TAIL, TAIL), TAIL)
-                out[to // CAP, rows] = piece[:TAIL]
-        return 0
-
-    lax.fori_loop(0, V // WARPED, some_visits, 0)
+            finished.append(result)
+        return finished
+
+    finished = []
+    for turn in range(V // WARPED):
+        finished += some_visits(turn)
+    place_copy.wait()
+    for visit in range(V):
+        for j in range(BLKC):
+            piece = lane_block(finished[visit], j)
+            to = place_of[0, visit * BLKC + j]
+            rows = pl.ds(pl.multiple_of(to % CAP * BODY, TAIL), BODY)
+            out[to // CAP, rows] = piece[TAIL:]
+            to = place_of[1, visit * BLKC + j]
+            rows = pl.ds(pl.multiple_of(CAP * BODY + to % CAP * TAIL, TAIL), TAIL)
+            out[to // CAP, rows] = piece[:TAIL]
 
 
 def warp(patch, slot, owner, weight, ready, order, images, above, devices):

time: 47.1 us -> 47.1 us (level)
  no operation moved by 1% of the time
where the time goes in v21:
time: 47.1 us; the launch traced here: 46.8 us
  blocking collectives  31.5 us (67%)
  Pallas kernels  10.7 us (23%)
  waiting for transfers between devices  3.93 us (8%)
  starting transfers between devices  0.5 us (1%)
    all_to_all x1, blocking collectives, shards(): got = lax.all_to_all(sent, 'ccd', split_axis=0, concat_axis=0, tiled=True)  31.5 us
    ppermute x1, waiting for transfers between devices, shards(): lax.ppermute(head, 'ccd', [(i, (i + 1) % devices) for i in range(devices)])  3.93 us
    pallas_call x1, Pallas kernels, warp(): pl.pallas_call(warp_kernel, in_specs=[vmem] * len(args), out_specs=vmem,...  2.81 us
    pallas_call x2, Pallas kernels, small_kernel(): pl.pallas_call(body, in_specs=[vmem] * len(args), out_specs=[vmem] * len(...  2.55 us
    pallas_call x1, Pallas kernels, warp(): pl.pallas_call(match_kernel, in_specs=[vmem] * len(args), out_specs=[vmem...  2.1 us
    pallas_call x1, Pallas kernels, coadd(): pl.pallas_call(coadd_kernel, in_specs=[pl.BlockSpec(memory_space=pltpu.VM...  1.67 us
    pallas_call x1, Pallas kernels, collect(): pl.pallas_call(collect_kernel, in_specs=[pl.BlockSpec(memory_space=pl.ANY...  1.61 us
  transfers between devices with their start and end apart: 1, of which 1 were waited for; matrix products, arithmetic and copies ran while one was open for 0% of the time, Pallas kernels for 10%

profile of v21, /device:TPU:0, one launch (start us, length us, event | category | flops | bytes accessed | tf_op | source)
XLA Modules:
  0.0 46.8 jit_solution(2186612968769343621)
XLA Ops:
  0.0 1.6 %collect.1 = f32[104,512]{1,0:T(8,128)} custom-call(f32[4,128,512]{2,1,0:T(8,128)} %image.3, s32[1,16]{1,0:T(1,128)} %bitcast.5), custom_call_target="tpu_custom_call" | custom-call | tf_op jit(solution)/shard_map/collect/pallas_call | solution.py:164
  1.6 0.0 copy-start.3
  1.6 0.0 copy-start.4
  1.6 0.0 copy-start.5
  1.7 0.5 %collective-permute-start = (f32[104,512]{1,0:T(8,128)}, f32[104,512]{1,0:T(8,128)S(1)}, u32[]{:S(2)}, u32[]{:S(2)}) collective-permute-start(f32[104,512]{1,0:T(8,128)} %collect.1), channel_id=1, source_target_pairs={{0,1},{1,2},{2,3},{3,4},{4,5},{5,6},{6,7},{7,8},{8,9},{9,10},{10,1... | collective-permute-start | bytes 638984 | tf_op jit(solution)/shard_map/ppermute | solution.py:654
  2.2 0.2 orders.1
  2.4 0.0 copy-done.3
  2.4 0.0 copy-done.4
  2.4 0.0 copy-done.5
  2.4 0.0 copy-start
  2.4 0.0 copy-start.1
  2.4 0.0 copy-start.2
  2.5 0.0 copy-start.6
  2.5 0.0 copy-start.7
  2.5 2.3 %matrices.1 = (f32[8,176,128]{2,1,0:T(8,128)S(1)}, f32[8,176,128]{2,1,0:T(8,128)S(1)}, bf16[8,176,128]{2,1,0:T(8,128)(2,1)S(1)}, bf16[4,128,128]{2,1,0:T(8,128)(...) custom-call(f32[9,2,11]{2,1,0:T(2,128)S(1)} %bitcast.10, f32[5,3,4,9]{3,2,1,0:T(4,128)S(1)} %bitcast.9, ...), custom_call_target="tpu_custom_call" | custom-call | flops 1073741824 | bytes 1048576 | tf_op jit(solution)/shard_map/matrices/pallas_call | solution.py:285
  4.8 0.0 copy-done
  4.8 0.0 copy-done.1
  4.8 0.0 copy-done.2
  4.8 0.0 copy-done.6
  4.8 0.0 copy-done.7
  4.9 2.1 %match.1 = (s32[1,16]{1,0:T(1,128)S(1)}, f32[16,128]{1,0:T(8,128)S(1)}, bf16[4,2,112,512]{3,2,1,0:T(8,128)(2,1)S(1)}) custom-call(s32[1,16]{1,0:T(1,128)S(1)} %bitcast.6, s32[1,16]{1,0:T(1,128)S(1)} %copy-done.7, s32[1,16]{1,0:T(1,128)S(1)} %bitcast.7, bf16[4,5]{1,0:T(4,128)(2,1)S(1)} %copy-done.6, f32[8,176,128]{2,1,0:T(8,128)S(1)} %get-tuple-element.16.high_level, ...), custom_call_target="tpu_custom_call" | custom-call | flops 1291845632 | bytes 1572864 | tf_op jit(solution)/shard_map/match/pallas_call | solution.py:519
  7.0 3.9 %collective-permute-done.above = f32[104,512]{1,0:T(8,128)S(1)} collective-permute-done((f32[104,512]{1,0:T(8,128)}, f32[104,512]{1,0:T(8,128)S(1)}, u32[]{:S(2)}, u32[]{:S(2)}) %collective-permute-start) | collective-permute-done | bytes 213024 | tf_op jit(solution)/shard_map/ppermute | solution.py:654
  10.9 2.8 %warp.1 = bf16[16,264,128]{2,1,0:T(8,128)(2,1)S(1)} custom-call(s32[1,16]{1,0:T(1,128)S(1)} %bitcast.8, s32[1,16]{1,0:T(1,128)S(1)} %get-tuple-element.20.places, f32[16,128]{1,0:T(8,128)S(1)} %get-tuple-element.21.label, f32[8,176,128]{2,1,0:T(8,128)S(1)} %get-tuple-element.16.high_level, f32[8,176,128]{2,1,0:T(8,128)S(1)} %get-tuple-element.17.step_level, ...), custom_call_target="tpu_custom_call" | custom-call | flops 1660944384 | bytes 1572864 | tf_op jit(solution)/shard_map/warp/pallas_call | solution.py:543
  13.7 31.5 %all_to_all.5.got = bf16[16,264,128]{2,1,0:T(8,128)(2,1)S(1)} all-to-all(bf16[16,264,128]{2,1,0:T(8,128)(2,1)S(1)} %warp.1), channel_id=1, replica_groups=mesh['group'=2,'ccd'=16] {'ccd'}, dimensions={0} | all-to-all | bytes 2162688 | tf_op jit(solution)/shard_map/all_to_all | solution.py:663
  45.2 1.7 %coadd.1 = f32[1,512,512]{2,1,0:T(8,128)} custom-call(bf16[16,264,128]{2,1,0:T(8,128)(2,1)S(1)} %all_to_all.5.got), custom_call_target="tpu_custom_call" | custom-call | tf_op jit(solution)/shard_map/coadd/pallas_call | solution.py:634
Async XLA Ops:
  1.6 0.8 %copy-start.3 = (f32[4,5,9,3]{2,0,3,1:T(4,128)S(1)}, f32[4,5,9,3]{2,0,3,1:T(4,128)}, u32[]{:S(2)}) copy-start(f32[4,5,9,3]{2,0,3,1:T(4,128)} %param.10) | copy-start | bytes 6484
  1.6 0.8 %copy-start.4 = (f32[2,9,11]{2,0,1:T(2,128)S(1)}, f32[2,9,11]{2,0,1:T(2,128)}, u32[]{:S(2)}) copy-start(f32[2,9,11]{2,0,1:T(2,128)} %param.9) | copy-start | bytes 2380
  1.6 0.8 %copy-start.5 = (f32[4,5,2,2]{1,3,2,0:T(2,128)S(1)}, f32[4,5,2,2]{1,3,2,0:T(2,128)}, u32[]{:S(2)}) copy-start(f32[4,5,2,2]{1,3,2,0:T(2,128)} %param.11) | copy-start | bytes 964
  1.7 9.2 %collective-permute-start = (f32[104,512]{1,0:T(8,128)}, f32[104,512]{1,0:T(8,128)S(1)}, u32[]{:S(2)}, u32[]{:S(2)}) collective-permute-start(f32[104,512]{1,0:T(8,128)} %collect.1), channel_id=1, source_target_pairs={{0,1},{1,2},{2,3},{3,4},{4,5},{5,6},{6,7},{7,8},{8,9},{9,10},{10,1... | collective-permute-start | bytes 638984 | tf_op jit(solution)/shard_map/ppermute | solution.py:654
  2.4 2.4 %copy-start = (f32[4,128,512]{2,1,0:T(8,128)S(1)}, f32[4,128,512]{2,1,0:T(8,128)}, u32[]{:S(2)}) copy-start(f32[4,128,512]{2,1,0:T(8,128)} %image.3) | copy-start | bytes 3145732
  2.4 2.4 %copy-start.1 = (s32[1,16,1]{1,2,0:T(1,128)S(1)}, s32[1,16,1]{1,2,0:T(1,128)}, u32[]{:S(2)}) copy-start(s32[1,16,1]{1,2,0:T(1,128)} %param.13) | copy-start | bytes 196
  2.4 2.4 %copy-start.2 = (s32[16]{0:T(128)S(1)}, s32[16]{0:T(128)}, u32[]{:S(2)}) copy-start(s32[16]{0:T(128)} %param.15) | copy-start | bytes 196
  2.5 2.4 %copy-start.6 = (bf16[4,5]{1,0:T(4,128)(2,1)S(1)}, bf16[4,5]{1,0:T(4,128)(2,1)}, u32[]{:S(2)}) copy-start(bf16[4,5]{1,0:T(4,128)(2,1)} %weight.1) | copy-start | bytes 124
  2.5 2.4 %copy-start.7 = (s32[1,16]{1,0:T(1,128)S(1)}, s32[1,16]{1,0:T(1,128)}, u32[]{:S(2)}) copy-start(s32[1,16]{1,0:T(1,128)} %slot.1) | copy-start | bytes 196

commit v22 on v21

--- a/solution.py
+++ b/solution.py
@@ -385,10 +385,10 @@
 
     def some_visits(turn):
         visits = [turn * MATCHED + i for i in range(MATCHED)]
-        for i, visit in enumerate(visits):
-            rows = sorted_rows(image[visit, open_row : open_row + seen], sort[...])
-            for h, value in enumerate(rows):
-                terms[i, h, :seen] = value.astype(BF16)
+        raw = [image[visit, open_row : open_row + seen] for visit in visits]
+        for h, value in enumerate(sorted_rows(jnp.concatenate(raw, axis=0), sort[...])):
+            for i in range(MATCHED):
+                terms[i, h, :seen] = value[i * seen : (i + 1) * seen].astype(BF16)
         for k in range(FREE_FIRST, STRIPS):
             first = (k - FREE_FIRST) * STRIP
             for i, visit in enumerate(visits):
@@ -428,12 +428,14 @@
 
     def some_visits(turn):
         visits = [turn * WARPED + i for i in range(WARPED)]
-        for i, visit in enumerate(visits):
-            tail = slice(visit * GOT, (visit + 1) * GOT)
-            raw = jnp.concatenate([above[tail], image[visit, : seam - GOT]], axis=0)
-            for h, value in enumerate(sorted_rows(raw, sort[...])):
-                own_terms[i, h] = (value * own_sees).astype(BF16)
-                past_terms[i, h] = (value * past_sees).astype(BF16)
+        raw = []
+        for visit in visits:
+            raw += [above[visit * GOT : (visit + 1) * GOT], image[visit, : seam - GOT]]
+        for h, value in enumerate(sorted_rows(jnp.concatenate(raw, axis=0), sort[...])):
+            for i in range(WARPED):
+                rows = value[i * seam : (i + 1) * seam]
+                own_terms[i, h] = (rows * own_sees).astype(BF16)
+                past_terms[i, h] = (rows * past_sees).astype(BF16)
         for i, visit in enumerate(visits):
             own_matched[i, 0], own_matched[i, 1] = match_strip(
                 high_level[visit], step_level[visit], slope[visit],
@@ -476,9 +478,8 @@
                 halves.append(total + jnp.dot(low, first, preferred_element_type=F32))
             warped.append(jnp.concatenate(halves, axis=0))
 
-        finished = []
+        parts = []
         for i, visit in enumerate(visits):
-            parts = []
             for rows, weights in (
                 (slice(0, TAIL), col_weights[past + visit]),
                 (slice(TAIL, BLOCK), col_weights[visit]),
@@ -489,11 +490,10 @@
                     lane, 2 * WARP + 1, True,
                 )
                 parts.append(jnp.concatenate(blocks, axis=1).astype(BF16))
-            result = jnp.dot(
-                jnp.concatenate(parts, axis=0), unsort[...], preferred_element_type=F32
-            ).astype(BF16)
-            finished.append(result)
-        return finished
+        result = jnp.dot(
+            jnp.concatenate(parts, axis=0), unsort[...], preferred_element_type=F32
+        ).astype(BF16)
+        return [result[i * BLOCK : (i + 1) * BLOCK] for i in range(WARPED)]
 
     finished = []
     for turn in range(V // WARPED):

time: 47.1 us -> 47.1 us (level)
  no operation moved by 1% of the time
where the time goes in v22:
time: 47.1 us; the launch traced here: 46.8 us
  blocking collectives  31.5 us (67%)
  Pallas kernels  10.8 us (23%)
  waiting for transfers between devices  3.86 us (8%)
  starting transfers between devices  0.5 us (1%)
    all_to_all x1, blocking collectives, shards(): got = lax.all_to_all(sent, 'ccd', split_axis=0, concat_axis=0, tiled=True)  31.5 us
    ppermute x1, waiting for transfers between devices, shards(): lax.ppermute(head, 'ccd', [(i, (i + 1) % devices) for i in range(devices)])  3.86 us
    pallas_call x1, Pallas kernels, warp(): pl.pallas_call(warp_kernel, in_specs=[vmem] * len(args), out_specs=vmem,...  2.81 us
    pallas_call x2, Pallas kernels, small_kernel(): pl.pallas_call(body, in_specs=[vmem] * len(args), out_specs=[vmem] * len(...  2.55 us
    pallas_call x1, Pallas kernels, warp(): pl.pallas_call(match_kernel, in_specs=[vmem] * len(args), out_specs=[vmem...  2.17 us
    pallas_call x1, Pallas kernels, coadd(): pl.pallas_call(coadd_kernel, in_specs=[pl.BlockSpec(memory_space=pltpu.VM...  1.67 us
    pallas_call x1, Pallas kernels, collect(): pl.pallas_call(collect_kernel, in_specs=[pl.BlockSpec(memory_space=pl.ANY...  1.61 us
  transfers between devices with their start and end apart: 1, of which 1 were waited for; matrix products, arithmetic and copies ran while one was open for 0% of the time, Pallas kernels for 10%

profile of v22, /device:TPU:0, one launch (start us, length us, event | category | flops | bytes accessed | tf_op | source)
XLA Modules:
  0.0 46.8 jit_solution(9808782563875797239)
XLA Ops:
  0.0 1.6 %collect.1 = f32[104,512]{1,0:T(8,128)} custom-call(f32[4,128,512]{2,1,0:T(8,128)} %image.3, s32[1,16]{1,0:T(1,128)} %bitcast.5), custom_call_target="tpu_custom_call" | custom-call | tf_op jit(solution)/shard_map/collect/pallas_call | solution.py:164
  1.6 0.0 copy-start.3
  1.6 0.0 copy-start.4
  1.6 0.0 copy-start.5
  1.7 0.5 %collective-permute-start = (f32[104,512]{1,0:T(8,128)}, f32[104,512]{1,0:T(8,128)S(1)}, u32[]{:S(2)}, u32[]{:S(2)}) collective-permute-start(f32[104,512]{1,0:T(8,128)} %collect.1), channel_id=1, source_target_pairs={{0,1},{1,2},{2,3},{3,4},{4,5},{5,6},{6,7},{7,8},{8,9},{9,10},{10,1... | collective-permute-start | bytes 638984 | tf_op jit(solution)/shard_map/ppermute | solution.py:654
  2.2 0.2 orders.1
  2.4 0.0 copy-done.3
  2.4 0.0 copy-done.4
  2.4 0.0 copy-done.5
  2.4 0.0 copy-start
  2.4 0.0 copy-start.1
  2.4 0.0 copy-start.2
  2.5 0.0 copy-start.6
  2.5 0.0 copy-start.7
  2.5 2.3 %matrices.1 = (f32[8,176,128]{2,1,0:T(8,128)S(1)}, f32[8,176,128]{2,1,0:T(8,128)S(1)}, bf16[8,176,128]{2,1,0:T(8,128)(2,1)S(1)}, bf16[4,128,128]{2,1,0:T(8,128)(...) custom-call(f32[9,2,11]{2,1,0:T(2,128)S(1)} %bitcast.10, f32[5,3,4,9]{3,2,1,0:T(4,128)S(1)} %bitcast.9, ...), custom_call_target="tpu_custom_call" | custom-call | flops 1073741824 | bytes 1048576 | tf_op jit(solution)/shard_map/matrices/pallas_call | solution.py:285
  4.8 0.0 copy-done
  4.8 0.0 copy-done.1
  4.8 0.0 copy-done.2
  4.8 0.0 copy-done.6
  4.8 0.0 copy-done.7
  4.9 2.2 %match.1 = (s32[1,16]{1,0:T(1,128)S(1)}, f32[16,128]{1,0:T(8,128)S(1)}, bf16[4,2,112,512]{3,2,1,0:T(8,128)(2,1)S(1)}) custom-call(s32[1,16]{1,0:T(1,128)S(1)} %bitcast.6, s32[1,16]{1,0:T(1,128)S(1)} %copy-done.7, s32[1,16]{1,0:T(1,128)S(1)} %bitcast.7, bf16[4,5]{1,0:T(4,128)(2,1)S(1)} %copy-done.6, f32[8,176,128]{2,1,0:T(8,128)S(1)} %get-tuple-element.16.high_level, ...), custom_call_target="tpu_custom_call" | custom-call | flops 1291845632 | bytes 1572864 | tf_op jit(solution)/shard_map/match/pallas_call | solution.py:519
  7.0 3.9 %collective-permute-done.above = f32[104,512]{1,0:T(8,128)S(1)} collective-permute-done((f32[104,512]{1,0:T(8,128)}, f32[104,512]{1,0:T(8,128)S(1)}, u32[]{:S(2)}, u32[]{:S(2)}) %collective-permute-start) | collective-permute-done | bytes 213024 | tf_op jit(solution)/shard_map/ppermute | solution.py:654
  10.9 2.8 %warp.1 = bf16[16,264,128]{2,1,0:T(8,128)(2,1)S(1)} custom-call(s32[1,16]{1,0:T(1,128)S(1)} %bitcast.8, s32[1,16]{1,0:T(1,128)S(1)} %get-tuple-element.20.places, f32[16,128]{1,0:T(8,128)S(1)} %get-tuple-element.21.label, f32[8,176,128]{2,1,0:T(8,128)S(1)} %get-tuple-element.16.high_level, f32[8,176,128]{2,1,0:T(8,128)S(1)} %get-tuple-element.17.step_level, ...), custom_call_target="tpu_custom_call" | custom-call | flops 1660944384 | bytes 1572864 | tf_op jit(solution)/shard_map/warp/pallas_call | solution.py:543
  13.7 31.5 %all_to_all.5.got = bf16[16,264,128]{2,1,0:T(8,128)(2,1)S(1)} all-to-all(bf16[16,264,128]{2,1,0:T(8,128)(2,1)S(1)} %warp.1), channel_id=1, replica_groups=mesh['group'=2,'ccd'=16] {'ccd'}, dimensions={0} | all-to-all | bytes 2162688 | tf_op jit(solution)/shard_map/all_to_all | solution.py:663
  45.2 1.7 %coadd.1 = f32[1,512,512]{2,1,0:T(8,128)} custom-call(bf16[16,264,128]{2,1,0:T(8,128)(2,1)S(1)} %all_to_all.5.got), custom_call_target="tpu_custom_call" | custom-call | tf_op jit(solution)/shard_map/coadd/pallas_call | solution.py:634
Async XLA Ops:
  1.6 0.8 %copy-start.3 = (f32[4,5,9,3]{2,0,3,1:T(4,128)S(1)}, f32[4,5,9,3]{2,0,3,1:T(4,128)}, u32[]{:S(2)}) copy-start(f32[4,5,9,3]{2,0,3,1:T(4,128)} %param.10) | copy-start | bytes 6484
  1.6 0.8 %copy-start.4 = (f32[2,9,11]{2,0,1:T(2,128)S(1)}, f32[2,9,11]{2,0,1:T(2,128)}, u32[]{:S(2)}) copy-start(f32[2,9,11]{2,0,1:T(2,128)} %param.9) | copy-start | bytes 2380
  1.6 0.8 %copy-start.5 = (f32[4,5,2,2]{1,3,2,0:T(2,128)S(1)}, f32[4,5,2,2]{1,3,2,0:T(2,128)}, u32[]{:S(2)}) copy-start(f32[4,5,2,2]{1,3,2,0:T(2,128)} %param.11) | copy-start | bytes 964
  1.7 9.2 %collective-permute-start = (f32[104,512]{1,0:T(8,128)}, f32[104,512]{1,0:T(8,128)S(1)}, u32[]{:S(2)}, u32[]{:S(2)}) collective-permute-start(f32[104,512]{1,0:T(8,128)} %collect.1), channel_id=1, source_target_pairs={{0,1},{1,2},{2,3},{3,4},{4,5},{5,6},{6,7},{7,8},{8,9},{9,10},{10,1... | collective-permute-start | bytes 638984 | tf_op jit(solution)/shard_map/ppermute | solution.py:654
  2.4 2.4 %copy-start = (f32[4,128,512]{2,1,0:T(8,128)S(1)}, f32[4,128,512]{2,1,0:T(8,128)}, u32[]{:S(2)}) copy-start(f32[4,128,512]{2,1,0:T(8,128)} %image.3) | copy-start | bytes 3145732
  2.4 2.4 %copy-start.1 = (s32[1,16,1]{1,2,0:T(1,128)S(1)}, s32[1,16,1]{1,2,0:T(1,128)}, u32[]{:S(2)}) copy-start(s32[1,16,1]{1,2,0:T(1,128)} %param.13) | copy-start | bytes 196
  2.4 2.4 %copy-start.2 = (s32[16]{0:T(128)S(1)}, s32[16]{0:T(128)}, u32[]{:S(2)}) copy-start(s32[16]{0:T(128)} %param.15) | copy-start | bytes 196
  2.5 2.4 %copy-start.6 = (bf16[4,5]{1,0:T(4,128)(2,1)S(1)}, bf16[4,5]{1,0:T(4,128)(2,1)}, u32[]{:S(2)}) copy-start(bf16[4,5]{1,0:T(4,128)(2,1)} %weight.1) | copy-start | bytes 124
  2.5 2.4 %copy-start.7 = (s32[1,16]{1,0:T(1,128)S(1)}, s32[1,16]{1,0:T(1,128)}, u32[]{:S(2)}) copy-start(s32[1,16]{1,0:T(1,128)} %slot.1) | copy-start | bytes 196

commit v23 on v20

--- a/solution.py
+++ b/solution.py
@@ -42,7 +42,7 @@
 BODY = BLOCK - TAIL
 GOT = TAIL + RIM
 OPEN = (STRIPS - 1) * STRIP + STEP - FREE_FIRST * STRIP
-LABEL = 8
+LABEL = 16
 F32 = jnp.float32
 BF16 = jnp.bfloat16
 

time: 47.1 us -> 47.7 us (1.013)
  blocking collectives: 31.5 us -> 32 us
    all_to_all x1, blocking collectives: 31.5 us -> 32 us  [shards(): got = lax.all_to_all(sent, 'ccd', split_axis=0, concat_axis=0, tiled=True)]
where the time goes in v23:
time: 47.7 us; the launch traced here: 47.4 us
  blocking collectives  32 us (67%)
  Pallas kernels  10.8 us (23%)
  waiting for transfers between devices  3.93 us (8%)
  starting transfers between devices  0.5 us (1%)
    all_to_all x1, blocking collectives, shards(): got = lax.all_to_all(sent, 'ccd', split_axis=0, concat_axis=0, tiled=True)  32 us
    ppermute x1, waiting for transfers between devices, shards(): lax.ppermute(head, 'ccd', [(i, (i + 1) % devices) for i in range(devices)])  3.93 us
    pallas_call x1, Pallas kernels, warp(): pl.pallas_call(warp_kernel, in_specs=[vmem] * len(args), out_specs=vmem,...  2.84 us
    pallas_call x2, Pallas kernels, small_kernel(): pl.pallas_call(body, in_specs=[vmem] * len(args), out_specs=[vmem] * len(...  2.55 us
    pallas_call x1, Pallas kernels, warp(): pl.pallas_call(match_kernel, in_specs=[vmem] * len(args), out_specs=[vmem...  2.1 us
    pallas_call x1, Pallas kernels, coadd(): pl.pallas_call(coadd_kernel, in_specs=[pl.BlockSpec(memory_space=pltpu.VM...  1.67 us
    pallas_call x1, Pallas kernels, collect(): pl.pallas_call(collect_kernel, in_specs=[pl.BlockSpec(memory_space=pl.ANY...  1.61 us
  transfers between devices with their start and end apart: 1, of which 1 were waited for; matrix products, arithmetic and copies ran while one was open for 0% of the time, Pallas kernels for 10%

profile of v23, /device:TPU:0, one launch (start us, length us, event | category | flops | bytes accessed | tf_op | source)
XLA Modules:
  0.0 47.4 jit_solution(8373736697829565081)
XLA Ops:
  0.0 1.6 %collect.1 = f32[104,512]{1,0:T(8,128)} custom-call(f32[4,128,512]{2,1,0:T(8,128)} %image.3, s32[1,16]{1,0:T(1,128)} %bitcast.5), custom_call_target="tpu_custom_call" | custom-call | tf_op jit(solution)/shard_map/collect/pallas_call | solution.py:164
  1.6 0.0 copy-start.3
  1.6 0.0 copy-start.4
  1.6 0.0 copy-start.5
  1.7 0.5 %collective-permute-start = (f32[104,512]{1,0:T(8,128)}, f32[104,512]{1,0:T(8,128)S(1)}, u32[]{:S(2)}, u32[]{:S(2)}) collective-permute-start(f32[104,512]{1,0:T(8,128)} %collect.1), channel_id=1, source_target_pairs={{0,1},{1,2},{2,3},{3,4},{4,5},{5,6},{6,7},{7,8},{8,9},{9,10},{10,1... | collective-permute-start | bytes 638984 | tf_op jit(solution)/shard_map/ppermute | solution.py:652
  2.2 0.2 orders.1
  2.4 0.0 copy-done.3
  2.4 0.0 copy-done.4
  2.4 0.0 copy-done.5
  2.4 0.0 copy-start
  2.4 0.0 copy-start.1
  2.4 0.0 copy-start.2
  2.5 0.0 copy-start.6
  2.5 0.0 copy-start.7
  2.5 2.3 %matrices.1 = (f32[8,176,128]{2,1,0:T(8,128)S(1)}, f32[8,176,128]{2,1,0:T(8,128)S(1)}, bf16[8,176,128]{2,1,0:T(8,128)(2,1)S(1)}, bf16[4,128,128]{2,1,0:T(8,128)(...) custom-call(f32[9,2,11]{2,1,0:T(2,128)S(1)} %bitcast.10, f32[5,3,4,9]{3,2,1,0:T(4,128)S(1)} %bitcast.9, ...), custom_call_target="tpu_custom_call" | custom-call | flops 1073741824 | bytes 1048576 | tf_op jit(solution)/shard_map/matrices/pallas_call | solution.py:285
  4.8 0.0 copy-done
  4.8 0.0 copy-done.1
  4.8 0.0 copy-done.2
  4.8 0.0 copy-done.6
  4.8 0.0 copy-done.7
  4.9 2.1 %match.1 = (s32[1,16]{1,0:T(1,128)S(1)}, f32[16,128]{1,0:T(8,128)S(1)}, bf16[4,2,112,512]{3,2,1,0:T(8,128)(2,1)S(1)}) custom-call(s32[1,16]{1,0:T(1,128)S(1)} %bitcast.6, s32[1,16]{1,0:T(1,128)S(1)} %copy-done.7, s32[1,16]{1,0:T(1,128)S(1)} %bitcast.7, bf16[4,5]{1,0:T(4,128)(2,1)S(1)} %copy-done.6, f32[8,176,128]{2,1,0:T(8,128)S(1)} %get-tuple-element.16.high_level, ...), custom_call_target="tpu_custom_call" | custom-call | flops 1291845632 | bytes 1572864 | tf_op jit(solution)/shard_map/match/pallas_call | solution.py:517
  7.0 3.9 %collective-permute-done.above = f32[104,512]{1,0:T(8,128)S(1)} collective-permute-done((f32[104,512]{1,0:T(8,128)}, f32[104,512]{1,0:T(8,128)S(1)}, u32[]{:S(2)}, u32[]{:S(2)}) %collective-permute-start) | collective-permute-done | bytes 213024 | tf_op jit(solution)/shard_map/ppermute | solution.py:652
  10.9 2.8 %warp.1 = bf16[16,272,128]{2,1,0:T(8,128)(2,1)S(1)} custom-call(s32[1,16]{1,0:T(1,128)S(1)} %bitcast.8, s32[1,16]{1,0:T(1,128)S(1)} %get-tuple-element.20.places, f32[16,128]{1,0:T(8,128)S(1)} %get-tuple-element.21.label, f32[8,176,128]{2,1,0:T(8,128)S(1)} %get-tuple-element.16.high_level, f32[8,176,128]{2,1,0:T(8,128)S(1)} %get-tuple-element.17.step_level, ...), custom_call_target="tpu_custom_call" | custom-call | flops 1660944384 | bytes 1572864 | tf_op jit(solution)/shard_map/warp/pallas_call | solution.py:541
  13.7 32.0 %all_to_all.5.got = bf16[16,272,128]{2,1,0:T(8,128)(2,1)S(1)} all-to-all(bf16[16,272,128]{2,1,0:T(8,128)(2,1)S(1)} %warp.1), channel_id=1, replica_groups=mesh['group'=2,'ccd'=16] {'ccd'}, dimensions={0} | all-to-all | bytes 2228224 | tf_op jit(solution)/shard_map/all_to_all | solution.py:661
  45.8 1.7 %coadd.1 = f32[1,512,512]{2,1,0:T(8,128)} custom-call(bf16[16,272,128]{2,1,0:T(8,128)(2,1)S(1)} %all_to_all.5.got), custom_call_target="tpu_custom_call" | custom-call | tf_op jit(solution)/shard_map/coadd/pallas_call | solution.py:632
Async XLA Ops:
  1.6 0.8 %copy-start.3 = (f32[4,5,9,3]{2,0,3,1:T(4,128)S(1)}, f32[4,5,9,3]{2,0,3,1:T(4,128)}, u32[]{:S(2)}) copy-start(f32[4,5,9,3]{2,0,3,1:T(4,128)} %param.10) | copy-start | bytes 6484
  1.6 0.8 %copy-start.4 = (f32[2,9,11]{2,0,1:T(2,128)S(1)}, f32[2,9,11]{2,0,1:T(2,128)}, u32[]{:S(2)}) copy-start(f32[2,9,11]{2,0,1:T(2,128)} %param.9) | copy-start | bytes 2380
  1.6 0.8 %copy-start.5 = (f32[4,5,2,2]{1,3,2,0:T(2,128)S(1)}, f32[4,5,2,2]{1,3,2,0:T(2,128)}, u32[]{:S(2)}) copy-start(f32[4,5,2,2]{1,3,2,0:T(2,128)} %param.11) | copy-start | bytes 964
  1.7 9.2 %collective-permute-start = (f32[104,512]{1,0:T(8,128)}, f32[104,512]{1,0:T(8,128)S(1)}, u32[]{:S(2)}, u32[]{:S(2)}) collective-permute-start(f32[104,512]{1,0:T(8,128)} %collect.1), channel_id=1, source_target_pairs={{0,1},{1,2},{2,3},{3,4},{4,5},{5,6},{6,7},{7,8},{8,9},{9,10},{10,1... | collective-permute-start | bytes 638984 | tf_op jit(solution)/shard_map/ppermute | solution.py:652
  2.4 2.4 %copy-start = (f32[4,128,512]{2,1,0:T(8,128)S(1)}, f32[4,128,512]{2,1,0:T(8,128)}, u32[]{:S(2)}) copy-start(f32[4,128,512]{2,1,0:T(8,128)} %image.3) | copy-start | bytes 3145732
  2.4 2.4 %copy-start.1 = (s32[1,16,1]{1,2,0:T(1,128)S(1)}, s32[1,16,1]{1,2,0:T(1,128)}, u32[]{:S(2)}) copy-start(s32[1,16,1]{1,2,0:T(1,128)} %param.13) | copy-start | bytes 196
  2.4 2.4 %copy-start.2 = (s32[16]{0:T(128)S(1)}, s32[16]{0:T(128)}, u32[]{:S(2)}) copy-start(s32[16]{0:T(128)} %param.15) | copy-start | bytes 196
  2.5 2.4 %copy-start.6 = (bf16[4,5]{1,0:T(4,128)(2,1)S(1)}, bf16[4,5]{1,0:T(4,128)(2,1)}, u32[]{:S(2)}) copy-start(bf16[4,5]{1,0:T(4,128)(2,1)} %weight.1) | copy-start | bytes 124
  2.5 2.4 %copy-start.7 = (s32[1,16]{1,0:T(1,128)S(1)}, s32[1,16]{1,0:T(1,128)}, u32[]{:S(2)}) copy-start(s32[1,16]{1,0:T(1,128)} %slot.1) | copy-start | bytes 196

commit v24 on v23

--- a/solution.py
+++ b/solution.py
@@ -140,35 +140,6 @@
     own = ((band + SPLIT // 2) // SPLIT, quarter * BLOCK - TAIL)
     before = ((past + SPLIT // 2) // SPLIT, (past + SPLIT // 2) % SPLIT * BLOCK + BODY)
     return (own, before), (quarter > 0) & (band > 0)
-
-
-def collect_kernel(images, patch, head, numbers, sems):
-    copies = [
-        pltpu.make_async_copy(
-            images.at[v, pl.ds(BLOCK - GOT, GOT)], head.at[pl.ds(v * GOT, GOT)], sems.at[v]
-        )
-        for v in range(V)
-    ]
-    names = pltpu.make_async_copy(patch, numbers, sems.at[V])
-    names.start()
-    for copy in copies:
-        copy.start()
-    head[V * GOT :] = jnp.zeros((8, WIDTH), F32)
-    names.wait()
-    head[V * GOT : V * GOT + 1, : V * BLKC] = numbers[...].astype(F32)
-    for copy in copies:
-        copy.wait()
-
-
-def collect(images, patch):
-    return pl.pallas_call(
-        collect_kernel,
-        in_specs=[pl.BlockSpec(memory_space=pl.ANY)] * 2,
-        out_specs=pl.BlockSpec(memory_space=pltpu.VMEM),
-        out_shape=jax.ShapeDtypeStruct((V * GOT + 8, WIDTH), F32),
-        scratch_shapes=[pltpu.VMEM(patch.shape, jnp.int32), pltpu.SemaphoreType.DMA((V + 1,))],
-        name="collect",
-    )(images, patch)
 
 
 def lanczos_weights(devices, affine, cols_out):
@@ -648,7 +619,12 @@
 ):
     devices = lax.axis_size("ccd")
     patch = block_patch[:, :, 0]
-    head = collect(images, patch)
+    rows = V * GOT
+    names = lax.pad(
+        patch, jnp.zeros((), jnp.int32), ((rows, 7, 0), (0, WIDTH - V * BLKC, 0))
+    )
+    rims = images[:, BLOCK - GOT :].reshape(rows, WIDTH)
+    head = lax.pad(rims, jnp.zeros((), F32), ((0, 8, 0), (0, 0, 0))) + names.astype(F32)
     above = lax.ppermute(head, "ccd", [(i, (i + 1) % devices) for i in range(devices)])
     order = orders()
     ready = prepare(

time: 47.7 us -> 47.4 us (level)
  Pallas kernels: 10.8 us -> 9.16 us
  local copies, waits for them, and re-layouts: 0.05 us -> 0.99 us
  other arithmetic: 0 us -> 0.67 us
    pallas_call x1 -> x0, Pallas kernels: 1.61 us -> none  [collect(): pl.pallas_call(collect_kernel, in_specs=[pl.BlockSpec(memory_space=pl.ANY...]
    slice x0 -> x1, local copies, waits for them, and re-layouts: none -> 0.94 us  [shards(): rims = images[:, BLOCK - GOT:].reshape(rows, WIDTH)]
    add x0 -> x1, other arithmetic: none -> 0.67 us  [shards(): lax.pad(rims, jnp.zeros((), F32), ((0, 8, 0), (0, 0, 0)))]
where the time goes in v24:
time: 47.4 us; the launch traced here: 47.2 us
  blocking collectives  32 us (68%)
  Pallas kernels  9.16 us (19%)
  waiting for transfers between devices  3.72 us (8%)
  local copies, waits for them, and re-layouts  0.99 us (2%)
  other arithmetic  0.67 us (1%)
  starting transfers between devices  0.5 us (1%)
    all_to_all x1, blocking collectives, shards(): got = lax.all_to_all(sent, 'ccd', split_axis=0, concat_axis=0, tiled=True)  32 us
    ppermute x1, waiting for transfers between devices, shards(): lax.ppermute(head, 'ccd', [(i, (i + 1) % devices) for i in range(devices)])  3.72 us
    pallas_call x1, Pallas kernels, warp(): pl.pallas_call(warp_kernel, in_specs=[vmem] * len(args), out_specs=vmem,...  2.84 us
    pallas_call x2, Pallas kernels, small_kernel(): pl.pallas_call(body, in_specs=[vmem] * len(args), out_specs=[vmem] * len(...  2.55 us
    pallas_call x1, Pallas kernels, warp(): pl.pallas_call(match_kernel, in_specs=[vmem] * len(args), out_specs=[vmem...  2.1 us
    pallas_call x1, Pallas kernels, coadd(): pl.pallas_call(coadd_kernel, in_specs=[pl.BlockSpec(memory_space=pltpu.VM...  1.67 us
  transfers between devices with their start and end apart: 1, of which 1 were waited for; matrix products, arithmetic and copies ran while one was open for 0% of the time, Pallas kernels for 10%

profile of v24, /device:TPU:0, one launch (start us, length us, event | category | flops | bytes accessed | tf_op | source)
XLA Modules:
  0.0 47.2 jit_solution(11461149872267728054)
XLA Ops:
  0.0 0.9 %slice.3 = f32[4,24,512]{2,1,0:T(8,128)S(1)} slice(f32[4,128,512]{2,1,0:T(8,128)} %image.3), slice={[0:4], [104:128], [0:512]} | slice | bytes 393216 | tf_op jit(solution)/shard_map/slice | solution.py:626
  0.9 0.7 %convert_add_fusion = f32[104,512]{1,0:T(8,128)S(1)} fusion(s32[1,16]{1,0:T(1,128)} %bitcast.6, f32[96,512]{1,0:T(8,128)S(1)} %bitcast.13), kind=kLoop, calls=%fused_computation | loop fusion | flops 106496 | bytes 409664 | tf_op jit(solution)/shard_map/add | solution.py:627
  1.6 0.0 copy-start.3
  1.6 0.0 copy-start.4
  1.6 0.0 copy-start.5
  1.7 0.5 %collective-permute-start = (f32[104,512]{1,0:T(8,128)S(1)}, f32[104,512]{1,0:T(8,128)S(1)}, u32[]{:S(2)}, u32[]{:S(2)}) collective-permute-start(f32[104,512]{1,0:T(8,128)S(1)} %convert_add_fusion), channel_id=1, source_target_pairs={{0,1},{1,2},{2,3},{3,4},{4,5},{5,6},{6,7},{7,8},{8,9},{9,10},{10,1... | collective-permute-start | bytes 638984 | tf_op jit(solution)/shard_map/ppermute | solution.py:628
  2.2 0.2 orders.1
  2.4 0.0 copy-done.3
  2.4 0.0 copy-done.4
  2.4 0.0 copy-done.5
  2.4 0.0 copy-start
  2.4 0.0 copy-start.1
  2.4 0.0 copy-start.2
  2.5 0.0 copy-start.6
  2.5 0.0 copy-start.7
  2.5 2.3 %matrices.1 = (f32[8,176,128]{2,1,0:T(8,128)S(1)}, f32[8,176,128]{2,1,0:T(8,128)S(1)}, bf16[8,176,128]{2,1,0:T(8,128)(2,1)S(1)}, bf16[4,128,128]{2,1,0:T(8,128)(...) custom-call(f32[9,2,11]{2,1,0:T(2,128)S(1)} %bitcast.11, f32[5,3,4,9]{3,2,1,0:T(4,128)S(1)} %bitcast.10, ...), custom_call_target="tpu_custom_call" | custom-call | flops 1073741824 | bytes 1048576 | tf_op jit(solution)/shard_map/matrices/pallas_call | solution.py:256
  4.8 0.0 copy-done
  4.8 0.0 copy-done.1
  4.8 0.0 copy-done.2
  4.8 0.0 copy-done.6
  4.8 0.0 copy-done.7
  4.9 2.1 %match.1 = (s32[1,16]{1,0:T(1,128)S(1)}, f32[16,128]{1,0:T(8,128)S(1)}, bf16[4,2,112,512]{3,2,1,0:T(8,128)(2,1)S(1)}) custom-call(s32[1,16]{1,0:T(1,128)S(1)} %bitcast.7, s32[1,16]{1,0:T(1,128)S(1)} %copy-done.7, s32[1,16]{1,0:T(1,128)S(1)} %bitcast.8, bf16[4,5]{1,0:T(4,128)(2,1)S(1)} %copy-done.6, f32[8,176,128]{2,1,0:T(8,128)S(1)} %get-tuple-element.16.high_level, ...), custom_call_target="tpu_custom_call" | custom-call | flops 1291845632 | bytes 1572864 | tf_op jit(solution)/shard_map/match/pallas_call | solution.py:488
  7.0 3.7 %collective-permute-done.above = f32[104,512]{1,0:T(8,128)S(1)} collective-permute-done((f32[104,512]{1,0:T(8,128)S(1)}, f32[104,512]{1,0:T(8,128)S(1)}, u32[]{:S(2)}, u32[]{:S(2)}) %collective-permute-start) | collective-permute-done | bytes 213024 | tf_op jit(solution)/shard_map/ppermute | solution.py:628
  10.7 2.8 %warp.1 = bf16[16,272,128]{2,1,0:T(8,128)(2,1)S(1)} custom-call(s32[1,16]{1,0:T(1,128)S(1)} %bitcast.9, s32[1,16]{1,0:T(1,128)S(1)} %get-tuple-element.20.places, f32[16,128]{1,0:T(8,128)S(1)} %get-tuple-element.21.label, f32[8,176,128]{2,1,0:T(8,128)S(1)} %get-tuple-element.16.high_level, f32[8,176,128]{2,1,0:T(8,128)S(1)} %get-tuple-element.17.step_level, ...), custom_call_target="tpu_custom_call" | custom-call | flops 1660944384 | bytes 1572864 | tf_op jit(solution)/shard_map/warp/pallas_call | solution.py:512
  13.5 32.0 %all_to_all.5.got = bf16[16,272,128]{2,1,0:T(8,128)(2,1)S(1)} all-to-all(bf16[16,272,128]{2,1,0:T(8,128)(2,1)S(1)} %warp.1), channel_id=1, replica_groups=mesh['group'=2,'ccd'=16] {'ccd'}, dimensions={0} | all-to-all | bytes 2228224 | tf_op jit(solution)/shard_map/all_to_all | solution.py:637
  45.5 1.7 %coadd.1 = f32[1,512,512]{2,1,0:T(8,128)} custom-call(bf16[16,272,128]{2,1,0:T(8,128)(2,1)S(1)} %all_to_all.5.got), custom_call_target="tpu_custom_call" | custom-call | tf_op jit(solution)/shard_map/coadd/pallas_call | solution.py:603
Async XLA Ops:
  1.6 0.8 %copy-start.3 = (f32[4,5,9,3]{2,0,3,1:T(4,128)S(1)}, f32[4,5,9,3]{2,0,3,1:T(4,128)}, u32[]{:S(2)}) copy-start(f32[4,5,9,3]{2,0,3,1:T(4,128)} %param.10) | copy-start | bytes 6484
  1.6 0.8 %copy-start.4 = (f32[2,9,11]{2,0,1:T(2,128)S(1)}, f32[2,9,11]{2,0,1:T(2,128)}, u32[]{:S(2)}) copy-start(f32[2,9,11]{2,0,1:T(2,128)} %param.9) | copy-start | bytes 2380
  1.6 0.8 %copy-start.5 = (f32[4,5,2,2]{1,3,2,0:T(2,128)S(1)}, f32[4,5,2,2]{1,3,2,0:T(2,128)}, u32[]{:S(2)}) copy-start(f32[4,5,2,2]{1,3,2,0:T(2,128)} %param.11) | copy-start | bytes 964
  1.7 9.0 %collective-permute-start = (f32[104,512]{1,0:T(8,128)S(1)}, f32[104,512]{1,0:T(8,128)S(1)}, u32[]{:S(2)}, u32[]{:S(2)}) collective-permute-start(f32[104,512]{1,0:T(8,128)S(1)} %convert_add_fusion), channel_id=1, source_target_pairs={{0,1},{1,2},{2,3},{3,4},{4,5},{5,6},{6,7},{7,8},{8,9},{9,10},{10,1... | collective-permute-start | bytes 638984 | tf_op jit(solution)/shard_map/ppermute | solution.py:628
  2.4 2.4 %copy-start = (f32[4,128,512]{2,1,0:T(8,128)S(1)}, f32[4,128,512]{2,1,0:T(8,128)}, u32[]{:S(2)}) copy-start(f32[4,128,512]{2,1,0:T(8,128)} %image.3) | copy-start | bytes 3145732
  2.4 2.4 %copy-start.1 = (s32[1,16,1]{1,2,0:T(1,128)S(1)}, s32[1,16,1]{1,2,0:T(1,128)}, u32[]{:S(2)}) copy-start(s32[1,16,1]{1,2,0:T(1,128)} %param.13) | copy-start | bytes 196
  2.4 2.4 %copy-start.2 = (s32[16]{0:T(128)S(1)}, s32[16]{0:T(128)}, u32[]{:S(2)}) copy-start(s32[16]{0:T(128)} %param.15) | copy-start | bytes 196
  2.5 2.4 %copy-start.6 = (bf16[4,5]{1,0:T(4,128)(2,1)S(1)}, bf16[4,5]{1,0:T(4,128)(2,1)}, u32[]{:S(2)}) copy-start(bf16[4,5]{1,0:T(4,128)(2,1)} %weight.1) | copy-start | bytes 124
  2.5 2.4 %copy-start.7 = (s32[1,16]{1,0:T(1,128)S(1)}, s32[1,16]{1,0:T(1,128)}, u32[]{:S(2)}) copy-start(s32[1,16]{1,0:T(1,128)} %slot.1) | copy-start | bytes 196

commit v25 on v18

--- a/solution.py
+++ b/solution.py
@@ -143,7 +143,7 @@
     return (own, before), (quarter > 0) & (band > 0)
 
 
-def collect_kernel(images, patch, head, numbers, sems):
+def collect_kernel(images, patch, owner, head, numbers, owners, sems):
     copies = [
         pltpu.make_async_copy(
             images.at[v, pl.ds(BLOCK - GOT, GOT)], head.at[pl.ds(v * GOT, GOT)], sems.at[v]
@@ -152,24 +152,32 @@
     ]
     names = pltpu.make_async_copy(patch, numbers, sems.at[V])
     names.start()
+    named = pltpu.make_async_copy(owner, owners, sems.at[V + 1])
+    named.start()
     for copy in copies:
         copy.start()
     head[V * GOT :] = jnp.zeros((8, WIDTH), F32)
     names.wait()
-    head[V * GOT : V * GOT + 1, : V * BLKC] = numbers[...].astype(F32)
+    named.wait()
+    to, rank = route(numbers[...], owners[...])
+    head[V * GOT : V * GOT + 1, : V * BLKC] = (to * CAP + rank).astype(F32)
     for copy in copies:
         copy.wait()
 
 
-def collect(images, patch):
+def collect(images, patch, owner):
     return pl.pallas_call(
         collect_kernel,
-        in_specs=[pl.BlockSpec(memory_space=pl.ANY)] * 2,
+        in_specs=[pl.BlockSpec(memory_space=pl.ANY)] * 3,
         out_specs=pl.BlockSpec(memory_space=pltpu.VMEM),
         out_shape=jax.ShapeDtypeStruct((V * GOT + 8, WIDTH), F32),
-        scratch_shapes=[pltpu.VMEM(patch.shape, jnp.int32), pltpu.SemaphoreType.DMA((V + 1,))],
+        scratch_shapes=[
+            pltpu.VMEM(patch.shape, jnp.int32),
+            pltpu.VMEM(owner.shape, jnp.int32),
+            pltpu.SemaphoreType.DMA((V + 2,)),
+        ],
         name="collect",
-    )(images, patch)
+    )(images, patch, owner)
 
 
 def lanczos_weights(devices, affine, cols_out):
@@ -392,16 +400,17 @@
 def warp_kernel(
     owner, places, label, high_level, step_level, slope, rows_high, rows_low, col_weights,
     sort, unsort, image, above, matched_free, out,
-    own_terms, past_terms, own_matched, past_matched, both_places, place_of, place_sem,
+    own_terms, past_terms, own_matched, past_matched, both_places, place_of, past_place, place_sem,
 ):
     devices = label.shape[0]
     _, same = whereabouts(devices)
-    past_patch = above[V * GOT : V * GOT + 1, : V * BLKC].astype(jnp.int32)
-    to, rank = route(past_patch, owner[...])
     both_places[0:1, : V * BLKC] = places[...]
-    both_places[1:2, : V * BLKC] = to * CAP + rank
-    place_copy = pltpu.make_async_copy(both_places, place_of, place_sem)
+    place_copy = pltpu.make_async_copy(both_places, place_of, place_sem.at[0])
     place_copy.start()
+    past_copy = pltpu.make_async_copy(
+        above.at[pl.ds(V * GOT, 8), pl.ds(0, LANES)], past_place, place_sem.at[1]
+    )
+    past_copy.start()
     lane = iota((1, LANES), 1)
     out[:, CAP * BLOCK :] = jnp.broadcast_to(
         label[...].reshape(devices, 1, LANES), (devices, LABEL, LANES)
@@ -466,6 +475,7 @@
         @pl.when(turn == 0)
         def _():
             place_copy.wait()
+            past_copy.wait()
 
         for i, visit in enumerate(visits):
             parts = []
@@ -487,7 +497,7 @@
                 to = place_of[0, visit * BLKC + j]
                 rows = pl.ds(pl.multiple_of(to % CAP * BODY, TAIL), BODY)
                 out[to // CAP, rows] = piece[TAIL:]
-                to = place_of[1, visit * BLKC + j]
+                to = past_place[0, visit * BLKC + j].astype(jnp.int32)
                 rows = pl.ds(pl.multiple_of(CAP * BODY + to % CAP * TAIL, TAIL), TAIL)
                 out[to // CAP, rows] = piece[:TAIL]
         return 0
@@ -536,7 +546,8 @@
             pltpu.VMEM((WARPED, 2, PAST_STRIPS * STRIP, WIDTH), BF16),
             pltpu.VMEM((8, LANES), jnp.int32),
             pltpu.SMEM((8, LANES), jnp.int32),
-            pltpu.SemaphoreType.DMA(()),
+            pltpu.SMEM((8, LANES), F32),
+            pltpu.SemaphoreType.DMA((2,)),
         ],
         out_shape=jax.ShapeDtypeStruct((devices, CAP * BLOCK + LABEL, BLOCK), BF16),
         compiler_params=pltpu.CompilerParams(vmem_limit_bytes=32 << 20),
@@ -635,7 +646,7 @@
 ):
     devices = lax.axis_size("ccd")
     patch = block_patch[:, :, 0]
-    head = collect(images, patch)
+    head = collect(images, patch, patch_owner.reshape(1, -1))
     above = lax.ppermute(head, "ccd", [(i, (i + 1) % devices) for i in range(devices)])
     order = orders()
     ready = prepare(

time: 47.7 us -> 47.7 us (level)
  no operation moved by 1% of the time
where the time goes in v25:
time: 47.7 us; the launch traced here: 47.5 us
  blocking collectives  32 us (67%)
  Pallas kernels  10.5 us (22%)
  waiting for transfers between devices  4.28 us (9%)
  starting transfers between devices  0.5 us (1%)
    all_to_all x1, blocking collectives, shards(): got = lax.all_to_all(sent, 'ccd', split_axis=0, concat_axis=0, tiled=True)  32 us
    ppermute x1, waiting for transfers between devices, shards(): lax.ppermute(head, 'ccd', [(i, (i + 1) % devices) for i in range(devices)])  4.28 us
    pallas_call x1, Pallas kernels, warp(): pl.pallas_call(warp_kernel, in_specs=[vmem] * len(args), out_specs=vmem,...  2.85 us
    pallas_call x2, Pallas kernels, small_kernel(): pl.pallas_call(body, in_specs=[vmem] * len(args), out_specs=[vmem] * len(...  2.22 us
    pallas_call x1, Pallas kernels, warp(): pl.pallas_call(match_kernel, in_specs=[vmem] * len(args), out_specs=[vmem...  2.07 us
    pallas_call x1, Pallas kernels, coadd(): pl.pallas_call(coadd_kernel, in_specs=[pl.BlockSpec(memory_space=pltpu.VM...  1.67 us
    pallas_call x1, Pallas kernels, collect(): pl.pallas_call(collect_kernel, in_specs=[pl.BlockSpec(memory_space=pl.ANY...  1.63 us
  transfers between devices with their start and end apart: 1, of which 1 were waited for; matrix products, arithmetic and copies ran while one was open for 0% of the time, Pallas kernels for 9%

profile of v25, /device:TPU:0, one launch (start us, length us, event | category | flops | bytes accessed | tf_op | source)
XLA Modules:
  0.0 47.5 jit_solution(316724333214333520)
XLA Ops:
  0.0 1.6 %collect.1 = f32[104,512]{1,0:T(8,128)} custom-call(f32[4,128,512]{2,1,0:T(8,128)} %image.3, s32[1,16]{1,0:T(1,128)} %bitcast.8, s32[1,16]{1,0:T(1,128)} %bitcast.5), custom_call_target="tpu_custom_call" | custom-call | tf_op jit(solution)/shard_map/collect/pallas_call | solution.py:169
  1.6 0.0 copy-start.3
  1.7 0.0 copy-start.4
  1.7 0.0 copy-start.5
  1.7 0.5 %collective-permute-start = (f32[104,512]{1,0:T(8,128)}, f32[104,512]{1,0:T(8,128)S(1)}, u32[]{:S(2)}, u32[]{:S(2)}) collective-permute-start(f32[104,512]{1,0:T(8,128)} %collect.1), channel_id=1, source_target_pairs={{0,1},{1,2},{2,3},{3,4},{4,5},{5,6},{6,7},{7,8},{8,9},{9,10},{10,1... | collective-permute-start | bytes 638984 | tf_op jit(solution)/shard_map/ppermute | solution.py:650
  2.2 0.2 orders.1
  2.4 0.0 copy-done.3
  2.4 0.0 copy-done.4
  2.4 0.0 copy-done.5
  2.4 0.0 copy-start
  2.5 0.0 copy-start.1
  2.5 0.0 copy-start.2
  2.5 0.0 copy-start.6
  2.5 0.0 copy-start.7
  2.5 2.0 %matrices.1 = (f32[8,176,128]{2,1,0:T(8,128)S(1)}, f32[8,176,128]{2,1,0:T(8,128)S(1)}, bf16[8,176,128]{2,1,0:T(8,128)(2,1)S(1)}, bf16[4,128,128]{2,1,0:T(8,128)(...) custom-call(f32[9,2,11]{2,1,0:T(2,128)S(1)} %bitcast.11, f32[5,3,4,9]{3,2,1,0:T(4,128)S(1)} %bitcast.10, ...), custom_call_target="tpu_custom_call" | custom-call | flops 1073741824 | bytes 1048576 | tf_op jit(solution)/shard_map/matrices/pallas_call | solution.py:281
  4.5 0.0 copy-done
  4.5 0.0 copy-done.1
  4.5 0.0 copy-done.2
  4.5 0.0 copy-done.6
  4.5 0.0 copy-done.7
  4.6 2.1 %match.1 = (s32[1,16]{1,0:T(1,128)S(1)}, f32[16,128]{1,0:T(8,128)S(1)}, bf16[4,2,112,512]{3,2,1,0:T(8,128)(2,1)S(1)}) custom-call(s32[1,16]{1,0:T(1,128)S(1)} %bitcast.9, s32[1,16]{1,0:T(1,128)S(1)} %copy-done.7, s32[1,16]{1,0:T(1,128)S(1)} %bitcast.6, bf16[4,5]{1,0:T(4,128)(2,1)S(1)} %copy-done.6, f32[8,176,128]{2,1,0:T(8,128)S(1)} %get-tuple-element.16.high_level, ...), custom_call_target="tpu_custom_call" | custom-call | flops 1291845632 | bytes 1572864 | tf_op jit(solution)/shard_map/match/pallas_call | solution.py:514
  6.6 4.3 %collective-permute-done.above = f32[104,512]{1,0:T(8,128)S(1)} collective-permute-done((f32[104,512]{1,0:T(8,128)}, f32[104,512]{1,0:T(8,128)S(1)}, u32[]{:S(2)}, u32[]{:S(2)}) %collective-permute-start) | collective-permute-done | bytes 213024 | tf_op jit(solution)/shard_map/ppermute | solution.py:650
  10.9 2.9 %warp.1 = bf16[16,272,128]{2,1,0:T(8,128)(2,1)S(1)} custom-call(s32[1,16]{1,0:T(1,128)S(1)} %bitcast.7, s32[1,16]{1,0:T(1,128)S(1)} %get-tuple-element.20.places, f32[16,128]{1,0:T(8,128)S(1)} %get-tuple-element.21.label, f32[8,176,128]{2,1,0:T(8,128)S(1)} %get-tuple-element.16.high_level, f32[8,176,128]{2,1,0:T(8,128)S(1)} %get-tuple-element.17.step_level, ...), custom_call_target="tpu_custom_call" | custom-call | flops 1660944384 | bytes 1572864 | tf_op jit(solution)/shard_map/warp/pallas_call | solution.py:538
  13.8 32.0 %all_to_all.5.got = bf16[16,272,128]{2,1,0:T(8,128)(2,1)S(1)} all-to-all(bf16[16,272,128]{2,1,0:T(8,128)(2,1)S(1)} %warp.1), channel_id=1, replica_groups=mesh['group'=2,'ccd'=16] {'ccd'}, dimensions={0} | all-to-all | bytes 2228224 | tf_op jit(solution)/shard_map/all_to_all | solution.py:659
  45.8 1.7 %coadd.1 = f32[1,512,512]{2,1,0:T(8,128)} custom-call(bf16[16,272,128]{2,1,0:T(8,128)(2,1)S(1)} %all_to_all.5.got), custom_call_target="tpu_custom_call" | custom-call | tf_op jit(solution)/shard_map/coadd/pallas_call | solution.py:630
Async XLA Ops:
  1.6 0.8 %copy-start.3 = (f32[4,5,9,3]{2,0,3,1:T(4,128)S(1)}, f32[4,5,9,3]{2,0,3,1:T(4,128)}, u32[]{:S(2)}) copy-start(f32[4,5,9,3]{2,0,3,1:T(4,128)} %param.10) | copy-start | bytes 6484
  1.7 0.8 %copy-start.4 = (f32[2,9,11]{2,0,1:T(2,128)S(1)}, f32[2,9,11]{2,0,1:T(2,128)}, u32[]{:S(2)}) copy-start(f32[2,9,11]{2,0,1:T(2,128)} %param.9) | copy-start | bytes 2380
  1.7 0.8 %copy-start.5 = (f32[4,5,2,2]{1,3,2,0:T(2,128)S(1)}, f32[4,5,2,2]{1,3,2,0:T(2,128)}, u32[]{:S(2)}) copy-start(f32[4,5,2,2]{1,3,2,0:T(2,128)} %param.11) | copy-start | bytes 964
  1.7 9.2 %collective-permute-start = (f32[104,512]{1,0:T(8,128)}, f32[104,512]{1,0:T(8,128)S(1)}, u32[]{:S(2)}, u32[]{:S(2)}) collective-permute-start(f32[104,512]{1,0:T(8,128)} %collect.1), channel_id=1, source_target_pairs={{0,1},{1,2},{2,3},{3,4},{4,5},{5,6},{6,7},{7,8},{8,9},{9,10},{10,1... | collective-permute-start | bytes 638984 | tf_op jit(solution)/shard_map/ppermute | solution.py:650
  2.4 2.1 %copy-start = (f32[4,128,512]{2,1,0:T(8,128)S(1)}, f32[4,128,512]{2,1,0:T(8,128)}, u32[]{:S(2)}) copy-start(f32[4,128,512]{2,1,0:T(8,128)} %image.3) | copy-start | bytes 3145732
  2.5 2.1 %copy-start.1 = (s32[16]{0:T(128)S(1)}, s32[16]{0:T(128)}, u32[]{:S(2)}) copy-start(s32[16]{0:T(128)} %param.15) | copy-start | bytes 196
  2.5 2.1 %copy-start.2 = (s32[1,16,1]{1,2,0:T(1,128)S(1)}, s32[1,16,1]{1,2,0:T(1,128)}, u32[]{:S(2)}) copy-start(s32[1,16,1]{1,2,0:T(1,128)} %param.13) | copy-start | bytes 196
  2.5 2.1 %copy-start.6 = (bf16[4,5]{1,0:T(4,128)(2,1)S(1)}, bf16[4,5]{1,0:T(4,128)(2,1)}, u32[]{:S(2)}) copy-start(bf16[4,5]{1,0:T(4,128)(2,1)} %weight.1) | copy-start | bytes 124
  2.5 2.1 %copy-start.7 = (s32[1,16]{1,0:T(1,128)S(1)}, s32[1,16]{1,0:T(1,128)}, u32[]{:S(2)}) copy-start(s32[1,16]{1,0:T(1,128)} %slot.1) | copy-start | bytes 196

commit v26 on v18

--- a/solution.py
+++ b/solution.py
@@ -584,13 +584,13 @@
         return jnp.where(taken[s, r], got[device, first : first + STRIP], jnp.zeros((), BF16))
 
     copies = []
-    for pair in range(BLOCK // STRIP // 2):
+    for pair in range(BLOCK // STRIP // 4):
         columns = jnp.concatenate(
             [
                 jnp.concatenate(
                     [tile(s, r, k) for s in range(devices) for r in range(CAP)], axis=0
                 )
-                for k in (2 * pair, 2 * pair + 1)
+                for k in range(4 * pair, 4 * pair + 4)
             ],
             axis=1,
         )
@@ -598,10 +598,10 @@
         for c in range(CELLS):
             part = result[c * STRIP : (c + 1) * STRIP]
             lanes = slice(c % PSIDE * BLOCK, (c % PSIDE + 1) * BLOCK)
-            for n in range(2):
-                first = (2 * pair + n) * STRIP
+            for n in range(4):
+                first = (4 * pair + n) * STRIP
                 total[c // PSIDE, first : first + STRIP, lanes] = lane_block(part, n)
-        size = 2 * STRIP
+        size = 4 * STRIP
         for line in range(PSIDE):
             copies.append(
                 pltpu.make_async_copy(
@@ -623,7 +623,7 @@
         out_shape=jax.ShapeDtypeStruct((1, PSIDE * BLOCK, PSIDE * BLOCK), F32),
         scratch_shapes=[
             pltpu.VMEM((PSIDE, BLOCK, WIDTH), F32),
-            pltpu.SemaphoreType.DMA((BLOCK // STRIP // 2, PSIDE)),
+            pltpu.SemaphoreType.DMA((BLOCK // STRIP // 4, PSIDE)),
         ],
         compiler_params=pltpu.CompilerParams(vmem_limit_bytes=32 << 20),
         name="coadd",

time: 47.7 us -> 47.6 us (level)
  no operation moved by 1% of the time
where the time goes in v26:
time: 47.6 us; the launch traced here: 47.4 us
  blocking collectives  32 us (67%)
  Pallas kernels  10.4 us (22%)
  waiting for transfers between devices  4.25 us (9%)
  starting transfers between devices  0.5 us (1%)
    all_to_all x1, blocking collectives, shards(): got = lax.all_to_all(sent, 'ccd', split_axis=0, concat_axis=0, tiled=True)  32 us
    ppermute x1, waiting for transfers between devices, shards(): lax.ppermute(head, 'ccd', [(i, (i + 1) % devices) for i in range(devices)])  4.25 us
    pallas_call x1, Pallas kernels, warp(): pl.pallas_call(warp_kernel, in_specs=[vmem] * len(args), out_specs=vmem,...  2.84 us
    pallas_call x2, Pallas kernels, small_kernel(): pl.pallas_call(body, in_specs=[vmem] * len(args), out_specs=[vmem] * len(...  2.22 us
    pallas_call x1, Pallas kernels, warp(): pl.pallas_call(match_kernel, in_specs=[vmem] * len(args), out_specs=[vmem...  2.1 us
    pallas_call x1, Pallas kernels, collect(): pl.pallas_call(collect_kernel, in_specs=[pl.BlockSpec(memory_space=pl.ANY...  1.61 us
    pallas_call x1, Pallas kernels, coadd(): pl.pallas_call(coadd_kernel, in_specs=[pl.BlockSpec(memory_space=pltpu.VM...  1.61 us
  transfers between devices with their start and end apart: 1, of which 1 were waited for; matrix products, arithmetic and copies ran while one was open for 0% of the time, Pallas kernels for 9%

profile of v26, /device:TPU:0, one launch (start us, length us, event | category | flops | bytes accessed | tf_op | source)
XLA Modules:
  0.0 47.4 jit_solution(640852578239071897)
XLA Ops:
  0.0 1.6 %collect.1 = f32[104,512]{1,0:T(8,128)} custom-call(f32[4,128,512]{2,1,0:T(8,128)} %image.3, s32[1,16]{1,0:T(1,128)} %bitcast.5), custom_call_target="tpu_custom_call" | custom-call | tf_op jit(solution)/shard_map/collect/pallas_call | solution.py:165
  1.6 0.0 copy-start.3
  1.6 0.0 copy-start.4
  1.6 0.0 copy-start.5
  1.7 0.5 %collective-permute-start = (f32[104,512]{1,0:T(8,128)}, f32[104,512]{1,0:T(8,128)S(1)}, u32[]{:S(2)}, u32[]{:S(2)}) collective-permute-start(f32[104,512]{1,0:T(8,128)} %collect.1), channel_id=1, source_target_pairs={{0,1},{1,2},{2,3},{3,4},{4,5},{5,6},{6,7},{7,8},{8,9},{9,10},{10,1... | collective-permute-start | bytes 638984 | tf_op jit(solution)/shard_map/ppermute | solution.py:639
  2.2 0.2 orders.1
  2.4 0.0 copy-done.3
  2.4 0.0 copy-done.4
  2.4 0.0 copy-done.5
  2.4 0.0 copy-start
  2.4 0.0 copy-start.1
  2.4 0.0 copy-start.2
  2.5 0.0 copy-start.6
  2.5 0.0 copy-start.7
  2.5 2.0 %matrices.1 = (f32[8,176,128]{2,1,0:T(8,128)S(1)}, f32[8,176,128]{2,1,0:T(8,128)S(1)}, bf16[8,176,128]{2,1,0:T(8,128)(2,1)S(1)}, bf16[4,128,128]{2,1,0:T(8,128)(...) custom-call(f32[9,2,11]{2,1,0:T(2,128)S(1)} %bitcast.10, f32[5,3,4,9]{3,2,1,0:T(4,128)S(1)} %bitcast.9, ...), custom_call_target="tpu_custom_call" | custom-call | flops 1073741824 | bytes 1048576 | tf_op jit(solution)/shard_map/matrices/pallas_call | solution.py:273
  4.5 0.0 copy-done
  4.5 0.0 copy-done.1
  4.5 0.0 copy-done.2
  4.5 0.0 copy-done.6
  4.5 0.0 copy-done.7
  4.5 2.1 %match.1 = (s32[1,16]{1,0:T(1,128)S(1)}, f32[16,128]{1,0:T(8,128)S(1)}, bf16[4,2,112,512]{3,2,1,0:T(8,128)(2,1)S(1)}) custom-call(s32[1,16]{1,0:T(1,128)S(1)} %bitcast.6, s32[1,16]{1,0:T(1,128)S(1)} %copy-done.7, s32[1,16]{1,0:T(1,128)S(1)} %bitcast.7, bf16[4,5]{1,0:T(4,128)(2,1)S(1)} %copy-done.6, f32[8,176,128]{2,1,0:T(8,128)S(1)} %get-tuple-element.16.high_level, ...), custom_call_target="tpu_custom_call" | custom-call | flops 1291845632 | bytes 1572864 | tf_op jit(solution)/shard_map/match/pallas_call | solution.py:504
  6.6 4.3 %collective-permute-done.above = f32[104,512]{1,0:T(8,128)S(1)} collective-permute-done((f32[104,512]{1,0:T(8,128)}, f32[104,512]{1,0:T(8,128)S(1)}, u32[]{:S(2)}, u32[]{:S(2)}) %collective-permute-start) | collective-permute-done | bytes 213024 | tf_op jit(solution)/shard_map/ppermute | solution.py:639
  10.9 2.8 %warp.1 = bf16[16,272,128]{2,1,0:T(8,128)(2,1)S(1)} custom-call(s32[1,16]{1,0:T(1,128)S(1)} %bitcast.8, s32[1,16]{1,0:T(1,128)S(1)} %get-tuple-element.20.places, f32[16,128]{1,0:T(8,128)S(1)} %get-tuple-element.21.label, f32[8,176,128]{2,1,0:T(8,128)S(1)} %get-tuple-element.16.high_level, f32[8,176,128]{2,1,0:T(8,128)S(1)} %get-tuple-element.17.step_level, ...), custom_call_target="tpu_custom_call" | custom-call | flops 1660944384 | bytes 1572864 | tf_op jit(solution)/shard_map/warp/pallas_call | solution.py:528
  13.7 32.0 %all_to_all.5.got = bf16[16,272,128]{2,1,0:T(8,128)(2,1)S(1)} all-to-all(bf16[16,272,128]{2,1,0:T(8,128)(2,1)S(1)} %warp.1), channel_id=1, replica_groups=mesh['group'=2,'ccd'=16] {'ccd'}, dimensions={0} | all-to-all | bytes 2228224 | tf_op jit(solution)/shard_map/all_to_all | solution.py:648
  45.8 1.6 %coadd.1 = f32[1,512,512]{2,1,0:T(8,128)} custom-call(bf16[16,272,128]{2,1,0:T(8,128)(2,1)S(1)} %all_to_all.5.got), custom_call_target="tpu_custom_call" | custom-call | tf_op jit(solution)/shard_map/coadd/pallas_call | solution.py:619
Async XLA Ops:
  1.6 0.8 %copy-start.3 = (f32[4,5,9,3]{2,0,3,1:T(4,128)S(1)}, f32[4,5,9,3]{2,0,3,1:T(4,128)}, u32[]{:S(2)}) copy-start(f32[4,5,9,3]{2,0,3,1:T(4,128)} %param.10) | copy-start | bytes 6484
  1.6 0.8 %copy-start.4 = (f32[2,9,11]{2,0,1:T(2,128)S(1)}, f32[2,9,11]{2,0,1:T(2,128)}, u32[]{:S(2)}) copy-start(f32[2,9,11]{2,0,1:T(2,128)} %param.9) | copy-start | bytes 2380
  1.6 0.8 %copy-start.5 = (f32[4,5,2,2]{1,3,2,0:T(2,128)S(1)}, f32[4,5,2,2]{1,3,2,0:T(2,128)}, u32[]{:S(2)}) copy-start(f32[4,5,2,2]{1,3,2,0:T(2,128)} %param.11) | copy-start | bytes 964
  1.7 9.2 %collective-permute-start = (f32[104,512]{1,0:T(8,128)}, f32[104,512]{1,0:T(8,128)S(1)}, u32[]{:S(2)}, u32[]{:S(2)}) collective-permute-start(f32[104,512]{1,0:T(8,128)} %collect.1), channel_id=1, source_target_pairs={{0,1},{1,2},{2,3},{3,4},{4,5},{5,6},{6,7},{7,8},{8,9},{9,10},{10,1... | collective-permute-start | bytes 638984 | tf_op jit(solution)/shard_map/ppermute | solution.py:639
  2.4 2.1 %copy-start = (f32[4,128,512]{2,1,0:T(8,128)S(1)}, f32[4,128,512]{2,1,0:T(8,128)}, u32[]{:S(2)}) copy-start(f32[4,128,512]{2,1,0:T(8,128)} %image.3) | copy-start | bytes 3145732
  2.4 2.1 %copy-start.1 = (s32[1,16,1]{1,2,0:T(1,128)S(1)}, s32[1,16,1]{1,2,0:T(1,128)}, u32[]{:S(2)}) copy-start(s32[1,16,1]{1,2,0:T(1,128)} %param.13) | copy-start | bytes 196
  2.4 2.1 %copy-start.2 = (s32[16]{0:T(128)S(1)}, s32[16]{0:T(128)}, u32[]{:S(2)}) copy-start(s32[16]{0:T(128)} %param.15) | copy-start | bytes 196
  2.5 2.1 %copy-start.6 = (bf16[4,5]{1,0:T(4,128)(2,1)S(1)}, bf16[4,5]{1,0:T(4,128)(2,1)}, u32[]{:S(2)}) copy-start(bf16[4,5]{1,0:T(4,128)(2,1)} %weight.1) | copy-start | bytes 124
  2.5 2.1 %copy-start.7 = (s32[1,16]{1,0:T(1,128)S(1)}, s32[1,16]{1,0:T(1,128)}, u32[]{:S(2)}) copy-start(s32[1,16]{1,0:T(1,128)} %slot.1) | copy-start | bytes 196
